TPU v7x, 32 devices: a whole 2x2x4 slice. The times are simulated.
32 devices in a mesh: delay: 4 (over x, core), surface: 8 (over z, y).
Axes of the slice: x: 2, y: 2, z: 4, core: 2. Of those that a mesh axis runs over, the one named last changes fastest.
Arguments:
- lagged_block_entries: bfloat16 [4, 32, 16, 128, 128], P('delay', 'surface'), may hold values from -0.0625 to 0.0625
- pattern: int32 [4, 32, 16], P('delay', 'surface'), may hold values from 0 to 31, as said below
- diagonal_block_inverses: bfloat16 [32, 128, 128], P('surface'), may hold values from -0.5 to 0.5
- excitation: bfloat16 [6, 4096, 128], P(None, 'surface'), may hold values from -6 to 6
- history: float32 [4, 4096, 128], P('delay', 'surface'), may hold values from -6 to 6
Outputs:
- currents: bfloat16 [6, 4096, 128], P(None, 'surface')
- accum: float32 [4, 4096, 128], P('delay', 'surface')
Inputs may be any that keep to these rules, and one draw needn't show every extreme that they name: `pattern`: in each row block i and lag, the 16 column block indices are distinct, and each names a block of the five groups of 4 blocks around i: block j lies in group floor(j / 4), and the groups g - 2 .. g + 2 around i's group g are counted cyclically over all 32 blocks.
All inputs are finite; a program needn't handle non-finite values.
Results may differ from a plain program's by a relative error of at most 0.0095.
Values may be sent and summed in bfloat16 or wider, within the bound.
No kernel may reach another device: no remote copies, remote signals or barrier semaphores. Data moves between devices by JAX's collectives and lax.ppermute only.
A program may use at most 64 MiB of HBM per device.

v0:
```python
import jax
import jax.numpy as jnp
from jax import lax
from jax.sharding import PartitionSpec as P


def from_root(block, axis, holder):
    block = jnp.where(lax.axis_index(axis) == holder, block, jnp.zeros_like(block))
    return lax.psum(block, axis)


def shifted(value, axis, steps):
    count = lax.axis_size(axis)
    first, last = (max(0, -steps), min(count, count - steps))
    return lax.ppermute(value, axis, [(source, source + steps) for source in range(first, last)])


def shifted_2(value, axis, steps):
    count = lax.axis_size(axis)
    pairs = [(source, (source + steps) % count) for source in range(count)]
    return lax.ppermute(value, axis, pairs)


def block_solve(inverse, rhs):
    block_tiles, size = (inverse.shape[0], inverse.shape[1])
    shaped = rhs.reshape(block_tiles, size, rhs.shape[1])
    fresh = jnp.einsum("ibc,icr->ibr", inverse, shaped, preferred_element_type=jnp.float32)
    return fresh.astype(jnp.bfloat16).reshape(rhs.shape)


def per_device(lagged_block_entries, pattern, diagonal_block_inverses, excitation, history):
    period_length = lax.axis_size("surface")
    position = lax.axis_index("surface")
    block_tiles, slots, size = (
        lagged_block_entries.shape[1],
        lagged_block_entries.shape[2],
        lagged_block_entries.shape[3],
    )
    rows, columns = (excitation.shape[1], excitation.shape[2])
    all_blocks = block_tiles * period_length
    local_index = ((pattern[0] - (position - 2) * block_tiles) % all_blocks).reshape(-1)
    accum = history[0]
    output_currents = []
    for step in range(excitation.shape[0]):
        rhs = (excitation[step].astype(jnp.float32) - accum).astype(jnp.bfloat16)
        current = from_root(block_solve(diagonal_block_inverses, rhs), "delay", 0)
        moved = shifted(accum, "delay", -1)
        received = {}
        for hop in (2, 1, -1, -2):
            received[hop] = shifted_2(current, "surface", hop)
        window = jnp.concatenate(
            [received[2], received[1], current, received[-1], received[-2]], axis=0
        )
        window = window.reshape(5 * block_tiles, size, columns)
        selected_entries = jnp.take(window, local_index, axis=0).reshape(
            block_tiles, slots, size, columns
        )
        product = jnp.einsum(
            "dhxp,dhpl->dxl",
            lagged_block_entries[0],
            selected_entries,
            preferred_element_type=jnp.float32,
        )
        accum = moved + product.reshape(rows, columns)
        output_currents.append(current)
    return (jnp.stack(output_currents), accum[None])


def solution(mesh):
    placed = (
        P("delay", "surface", None, None, None),
        P("delay", "surface", None),
        P("surface", None, None),
        P(None, "surface", None),
        P("delay", "surface", None),
    )
    return jax.shard_map(
        per_device,
        mesh=mesh,
        in_specs=placed,
        out_specs=(P(None, "surface", None), P("delay", "surface", None)),
        check_vma=False,
    )
```

profile of v0, /device:TPU:0, one launch (start us, length us, event | category | flops | bytes accessed | tf_op | source)
XLA Modules:
  0.0 331.6 jit_solution(7050259363842964755)
XLA Ops:
  12.3 32.7 %all-reduce.7.cloned.1.call-done = bf16[512,128]{1,0:T(8,128)(2,1)} async-done(((bf16[512,128]{1,0:T(8,128)(2,1)}), bf16[512,128]{1,0:T(8,128)(2,1)}) %all-reduce.7.cloned.1.call-update) | async-done | bytes 131088 | tf_op jit(solution)/shard_map/psum | solution.py:9
  48.1 3.2 collective-permute-start.3
  53.3 3.2 collective-permute-done.2
  57.5 2.2 gather_fusion
  59.7 1.8 broadcast_select_fusion.5
  64.2 29.8 %all-reduce.9.cloned.1.call-done = bf16[512,128]{1,0:T(8,128)(2,1)} async-done(((bf16[512,128]{1,0:T(8,128)(2,1)}), bf16[512,128]{1,0:T(8,128)(2,1)}) %all-reduce.9.cloned.1.call-update) | async-done | bytes 131088 | tf_op jit(solution)/shard_map/psum | solution.py:9
  98.2 3.3 collective-permute-start.8
  102.1 2.0 collective-permute-done.7
  106.1 2.3 collective-permute-done.9
  108.5 2.2 gather_fusion.1
  110.6 1.8 broadcast_select_fusion.4
  115.2 31.9 %all-reduce.11.cloned.1.call-done = bf16[512,128]{1,0:T(8,128)(2,1)} async-done(((bf16[512,128]{1,0:T(8,128)(2,1)}), bf16[512,128]{1,0:T(8,128)(2,1)}) %all-reduce.11.cloned.1.call-update) | async-done | bytes 131088 | tf_op jit(solution)/shard_map/psum | solution.py:9
  151.4 3.3 collective-permute-start.13
  155.2 2.0 collective-permute-done.12
  159.3 2.3 collective-permute-done.14
  161.6 2.2 gather_fusion.2
  163.8 1.8 broadcast_select_fusion.3
  168.9 31.0 %all-reduce.13.cloned.1.call-done = bf16[512,128]{1,0:T(8,128)(2,1)} async-done(((bf16[512,128]{1,0:T(8,128)(2,1)}), bf16[512,128]{1,0:T(8,128)(2,1)}) %all-reduce.13.cloned.1.call-update) | async-done | bytes 131088 | tf_op jit(solution)/shard_map/psum | solution.py:9
  204.8 3.3 collective-permute-start.18
  212.7 2.4 collective-permute-done.19
  215.1 2.2 gather_fusion.3
  217.2 1.8 broadcast_select_fusion.2
  222.4 31.0 %all-reduce.15.cloned.1.call-done = bf16[512,128]{1,0:T(8,128)(2,1)} async-done(((bf16[512,128]{1,0:T(8,128)(2,1)}), bf16[512,128]{1,0:T(8,128)(2,1)}) %all-reduce.15.cloned.1.call-update) | async-done | bytes 131088 | tf_op jit(solution)/shard_map/psum | solution.py:9
  258.3 3.3 collective-permute-start.23
  266.1 2.4 collective-permute-done.24
  268.5 2.2 gather_fusion.4
  270.7 1.8 broadcast_select_fusion.1
  277.1 29.8 %all-reduce.17.cloned.1.call-done = bf16[512,128]{1,0:T(8,128)(2,1)} async-done(((bf16[512,128]{1,0:T(8,128)(2,1)}), bf16[512,128]{1,0:T(8,128)(2,1)}) %all-reduce.17.cloned.1.call-update) | async-done | bytes 131088 | tf_op jit(solution)/shard_map/psum | solution.py:9
  309.8 3.2 collective-permute-start.28
  315.2 3.1 collective-permute-done.27
  319.3 2.2 gather_fusion.5
  321.5 1.8 broadcast_select_fusion
  (131 shorter events, 67.5 us)
Async XLA Ops:
  7.2 37.9 %all-reduce.7.cloned.1.call-start = ((), (), s32[]{:S(2)}) async-start(), calls=%async_computation | async-start | bytes 262144 | tf_op jit(solution)/shard_map/psum | solution.py:9
  10.2 83.8 %all-reduce.9.cloned.1.call-start = ((), (), s32[]{:S(2)}) async-start(), calls=%async_computation.1 | async-start | bytes 262144 | tf_op jit(solution)/shard_map/psum | solution.py:9
  10.2 52.1 %collective-permute-start = (f32[512,128]{1,0:T(8,128)}, f32[512,128]{1,0:T(8,128)S(1)}, u32[]{:S(2)}, u32[]{:S(2)}) collective-permute-start(f32[512,128]{1,0:T(8,128)} %bitcast.168), channel_id=1, source_target_pairs={{8,0},{16,8},{24,16},{9,1},{17,9},{25,17},{10,2},{18,10},{26,18},{... | collective-permute-start | bytes 786440 | tf_op jit(solution)/shard_map/ppermute | solution.py:15
  45.0 8.2 %collective-permute-start.1 = (bf16[512,128]{1,0:T(8,128)(2,1)}, bf16[512,128]{1,0:T(8,128)(2,1)S(1)}, u32[]{:S(2)}, u32[]{:S(2)}) collective-permute-start(bf16[512,128]{1,0:T(8,128)(2,1)} %all-reduce.7.cloned.1.call-done), channel_id=1, source_target_pairs={{0,2},{1,3},{2,4},{3,5},{4,6},{5,7},{6,0},{7,1},{8,10},{9,11},{10,... | collective-permute-start | bytes 393224 | tf_op jit(solution)/shard_map/ppermute | solution.py:21
  46.5 9.9 %collective-permute-start.2 = (bf16[512,128]{1,0:T(8,128)(2,1)}, bf16[512,128]{1,0:T(8,128)(2,1)S(1)}, u32[]{:S(2)}, u32[]{:S(2)}) collective-permute-start(bf16[512,128]{1,0:T(8,128)(2,1)} %all-reduce.7.cloned.1.call-done), channel_id=1, source_target_pairs={{0,1},{1,2},{2,3},{3,4},{4,5},{5,6},{6,7},{7,0},{8,9},{9,10},{10,1... | collective-permute-start | bytes 393224 | tf_op jit(solution)/shard_map/ppermute | solution.py:21
  48.1 9.4 %collective-permute-start.3 = (bf16[512,128]{1,0:T(8,128)(2,1)}, bf16[512,128]{1,0:T(8,128)(2,1)S(1)}, u32[]{:S(2)}, u32[]{:S(2)}) collective-permute-start(bf16[512,128]{1,0:T(8,128)(2,1)} %all-reduce.7.cloned.1.call-done), channel_id=1, source_target_pairs={{0,7},{1,0},{2,1},{3,2},{4,3},{5,4},{6,5},{7,6},{8,15},{9,8},{10,9... | collective-permute-start | bytes 393224 | tf_op jit(solution)/shard_map/ppermute | solution.py:21
  64.1 83.0 %all-reduce.11.cloned.1.call-start = ((), (), s32[]{:S(2)}) async-start(), calls=%async_computation.2 | async-start | bytes 262144 | tf_op jit(solution)/shard_map/psum | solution.py:9
  94.0 8.1 %collective-permute-start.6 = (bf16[512,128]{1,0:T(8,128)(2,1)}, bf16[512,128]{1,0:T(8,128)(2,1)S(1)}, u32[]{:S(2)}, u32[]{:S(2)}) collective-permute-start(bf16[512,128]{1,0:T(8,128)(2,1)} %all-reduce.9.cloned.1.call-done), channel_id=1, source_target_pairs={{0,2},{1,3},{2,4},{3,5},{4,6},{5,7},{6,0},{7,1},{8,10},{9,11},{10,... | collective-permute-start | bytes 393224 | tf_op jit(solution)/shard_map/ppermute | solution.py:21
  95.5 8.6 %collective-permute-start.7 = (bf16[512,128]{1,0:T(8,128)(2,1)}, bf16[512,128]{1,0:T(8,128)(2,1)S(1)}, u32[]{:S(2)}, u32[]{:S(2)}) collective-permute-start(bf16[512,128]{1,0:T(8,128)(2,1)} %all-reduce.9.cloned.1.call-done), channel_id=1, source_target_pairs={{0,1},{1,2},{2,3},{3,4},{4,5},{5,6},{6,7},{7,0},{8,9},{9,10},{10,1... | collective-permute-start | bytes 393224 | tf_op jit(solution)/shard_map/ppermute | solution.py:21
  96.9 16.3 %collective-permute-start.5 = (f32[512,128]{1,0:T(8,128)S(1)}, f32[512,128]{1,0:T(8,128)}, u32[]{:S(2)}, u32[]{:S(2)}) collective-permute-start(f32[512,128]{1,0:T(8,128)S(1)} %get-tuple-element.12), channel_id=1, source_target_pairs={{8,0},{16,8},{24,16},{9,1},{17,9},{25,17},{10,2},{18,10},{26,18},{... | collective-permute-start | bytes 786440 | tf_op jit(solution)/shard_map/ppermute | solution.py:15
  98.2 7.9 %collective-permute-start.8 = (bf16[512,128]{1,0:T(8,128)(2,1)}, bf16[512,128]{1,0:T(8,128)(2,1)S(1)}, u32[]{:S(2)}, u32[]{:S(2)}) collective-permute-start(bf16[512,128]{1,0:T(8,128)(2,1)} %all-reduce.9.cloned.1.call-done), channel_id=1, source_target_pairs={{0,7},{1,0},{2,1},{3,2},{4,3},{5,4},{6,5},{7,6},{8,15},{9,8},{10,9... | collective-permute-start | bytes 393224 | tf_op jit(solution)/shard_map/ppermute | solution.py:21
  115.2 84.8 %all-reduce.13.cloned.1.call-start = ((), (), s32[]{:S(2)}) async-start(), calls=%async_computation.3 | async-start | bytes 262144 | tf_op jit(solution)/shard_map/psum | solution.py:9
  147.1 8.1 %collective-permute-start.11 = (bf16[512,128]{1,0:T(8,128)(2,1)}, bf16[512,128]{1,0:T(8,128)(2,1)S(1)}, u32[]{:S(2)}, u32[]{:S(2)}) collective-permute-start(bf16[512,128]{1,0:T(8,128)(2,1)} %all-reduce.11.cloned.1.call-done), channel_id=1, source_target_pairs={{0,2},{1,3},{2,4},{3,5},{4,6},{5,7},{6,0},{7,1},{8,10},{9,11},{10,... | collective-permute-start | bytes 393224 | tf_op jit(solution)/shard_map/ppermute | solution.py:21
  148.6 8.6 %collective-permute-start.12 = (bf16[512,128]{1,0:T(8,128)(2,1)}, bf16[512,128]{1,0:T(8,128)(2,1)S(1)}, u32[]{:S(2)}, u32[]{:S(2)}) collective-permute-start(bf16[512,128]{1,0:T(8,128)(2,1)} %all-reduce.11.cloned.1.call-done), channel_id=1, source_target_pairs={{0,1},{1,2},{2,3},{3,4},{4,5},{5,6},{6,7},{7,0},{8,9},{9,10},{10,1... | collective-permute-start | bytes 393224 | tf_op jit(solution)/shard_map/ppermute | solution.py:21
  150.1 16.3 %collective-permute-start.10 = (f32[512,128]{1,0:T(8,128)S(1)}, f32[512,128]{1,0:T(8,128)S(1)}, u32[]{:S(2)}, u32[]{:S(2)}) collective-permute-start(f32[512,128]{1,0:T(8,128)S(1)} %get-tuple-element.10), channel_id=1, source_target_pairs={{8,0},{16,8},{24,16},{9,1},{17,9},{25,17},{10,2},{18,10},{26,18},{... | collective-permute-start | bytes 786440 | tf_op jit(solution)/shard_map/ppermute | solution.py:15
  151.4 7.9 %collective-permute-start.13 = (bf16[512,128]{1,0:T(8,128)(2,1)}, bf16[512,128]{1,0:T(8,128)(2,1)S(1)}, u32[]{:S(2)}, u32[]{:S(2)}) collective-permute-start(bf16[512,128]{1,0:T(8,128)(2,1)} %all-reduce.11.cloned.1.call-done), channel_id=1, source_target_pairs={{0,7},{1,0},{2,1},{3,2},{4,3},{5,4},{6,5},{7,6},{8,15},{9,8},{10,9... | collective-permute-start | bytes 393224 | tf_op jit(solution)/shard_map/ppermute | solution.py:21
  154.7 6.9 %collective-permute-start.14 = (bf16[512,128]{1,0:T(8,128)(2,1)}, bf16[512,128]{1,0:T(8,128)(2,1)S(1)}, u32[]{:S(2)}, u32[]{:S(2)}) collective-permute-start(bf16[512,128]{1,0:T(8,128)(2,1)} %all-reduce.11.cloned.1.call-done), channel_id=1, source_target_pairs={{0,6},{1,7},{2,0},{3,1},{4,2},{5,3},{6,4},{7,5},{8,14},{9,15},{10,... | collective-permute-start | bytes 393224 | tf_op jit(solution)/shard_map/ppermute | solution.py:21
  168.2 85.2 %all-reduce.15.cloned.1.call-start = ((), (), s32[]{:S(2)}) async-start(), calls=%async_computation.4 | async-start | bytes 262144 | tf_op jit(solution)/shard_map/psum | solution.py:9
  199.9 8.8 %collective-permute-start.16 = (bf16[512,128]{1,0:T(8,128)(2,1)}, bf16[512,128]{1,0:T(8,128)(2,1)S(1)}, u32[]{:S(2)}, u32[]{:S(2)}) collective-permute-start(bf16[512,128]{1,0:T(8,128)(2,1)} %all-reduce.13.cloned.1.call-done), channel_id=1, source_target_pairs={{0,2},{1,3},{2,4},{3,5},{4,6},{5,7},{6,0},{7,1},{8,10},{9,11},{10,... | collective-permute-start | bytes 393224 | tf_op jit(solution)/shard_map/ppermute | solution.py:21
  201.4 8.6 %collective-permute-start.17 = (bf16[512,128]{1,0:T(8,128)(2,1)}, bf16[512,128]{1,0:T(8,128)(2,1)S(1)}, u32[]{:S(2)}, u32[]{:S(2)}) collective-permute-start(bf16[512,128]{1,0:T(8,128)(2,1)} %all-reduce.13.cloned.1.call-done), channel_id=1, source_target_pairs={{0,1},{1,2},{2,3},{3,4},{4,5},{5,6},{6,7},{7,0},{8,9},{9,10},{10,1... | collective-permute-start | bytes 393224 | tf_op jit(solution)/shard_map/ppermute | solution.py:21
  203.5 16.3 %collective-permute-start.15 = (f32[512,128]{1,0:T(8,128)S(1)}, f32[512,128]{1,0:T(8,128)S(1)}, u32[]{:S(2)}, u32[]{:S(2)}) collective-permute-start(f32[512,128]{1,0:T(8,128)S(1)} %get-tuple-element.8), channel_id=1, source_target_pairs={{8,0},{16,8},{24,16},{9,1},{17,9},{25,17},{10,2},{18,10},{26,18},{... | collective-permute-start | bytes 786440 | tf_op jit(solution)/shard_map/ppermute | solution.py:15
  204.8 7.8 %collective-permute-start.18 = (bf16[512,128]{1,0:T(8,128)(2,1)}, bf16[512,128]{1,0:T(8,128)(2,1)S(1)}, u32[]{:S(2)}, u32[]{:S(2)}) collective-permute-start(bf16[512,128]{1,0:T(8,128)(2,1)} %all-reduce.13.cloned.1.call-done), channel_id=1, source_target_pairs={{0,7},{1,0},{2,1},{3,2},{4,3},{5,4},{6,5},{7,6},{8,15},{9,8},{10,9... | collective-permute-start | bytes 393224 | tf_op jit(solution)/shard_map/ppermute | solution.py:21
  208.1 6.9 %collective-permute-start.19 = (bf16[512,128]{1,0:T(8,128)(2,1)}, bf16[512,128]{1,0:T(8,128)(2,1)S(1)}, u32[]{:S(2)}, u32[]{:S(2)}) collective-permute-start(bf16[512,128]{1,0:T(8,128)(2,1)} %all-reduce.13.cloned.1.call-done), channel_id=1, source_target_pairs={{0,6},{1,7},{2,0},{3,1},{4,2},{5,3},{6,4},{7,5},{8,14},{9,15},{10,... | collective-permute-start | bytes 393224 | tf_op jit(solution)/shard_map/ppermute | solution.py:21
  221.7 85.2 %all-reduce.17.cloned.1.call-start = ((), (), s32[]{:S(2)}) async-start(), calls=%async_computation.5 | async-start | bytes 262144 | tf_op jit(solution)/shard_map/psum | solution.py:9
  253.4 8.8 %collective-permute-start.21 = (bf16[512,128]{1,0:T(8,128)(2,1)}, bf16[512,128]{1,0:T(8,128)(2,1)S(1)}, u32[]{:S(2)}, u32[]{:S(2)}) collective-permute-start(bf16[512,128]{1,0:T(8,128)(2,1)} %all-reduce.15.cloned.1.call-done), channel_id=1, source_target_pairs={{0,2},{1,3},{2,4},{3,5},{4,6},{5,7},{6,0},{7,1},{8,10},{9,11},{10,... | collective-permute-start | bytes 393224 | tf_op jit(solution)/shard_map/ppermute | solution.py:21
  254.9 8.6 %collective-permute-start.22 = (bf16[512,128]{1,0:T(8,128)(2,1)}, bf16[512,128]{1,0:T(8,128)(2,1)S(1)}, u32[]{:S(2)}, u32[]{:S(2)}) collective-permute-start(bf16[512,128]{1,0:T(8,128)(2,1)} %all-reduce.15.cloned.1.call-done), channel_id=1, source_target_pairs={{0,1},{1,2},{2,3},{3,4},{4,5},{5,6},{6,7},{7,0},{8,9},{9,10},{10,1... | collective-permute-start | bytes 393224 | tf_op jit(solution)/shard_map/ppermute | solution.py:21
  257.0 16.3 %collective-permute-start.20 = (f32[512,128]{1,0:T(8,128)S(1)}, f32[512,128]{1,0:T(8,128)S(1)}, u32[]{:S(2)}, u32[]{:S(2)}) collective-permute-start(f32[512,128]{1,0:T(8,128)S(1)} %get-tuple-element.6), channel_id=1, source_target_pairs={{8,0},{16,8},{24,16},{9,1},{17,9},{25,17},{10,2},{18,10},{26,18},{... | collective-permute-start | bytes 786440 | tf_op jit(solution)/shard_map/ppermute | solution.py:15
  258.3 7.8 %collective-permute-start.23 = (bf16[512,128]{1,0:T(8,128)(2,1)}, bf16[512,128]{1,0:T(8,128)(2,1)S(1)}, u32[]{:S(2)}, u32[]{:S(2)}) collective-permute-start(bf16[512,128]{1,0:T(8,128)(2,1)} %all-reduce.15.cloned.1.call-done), channel_id=1, source_target_pairs={{0,7},{1,0},{2,1},{3,2},{4,3},{5,4},{6,5},{7,6},{8,15},{9,8},{10,9... | collective-permute-start | bytes 393224 | tf_op jit(solution)/shard_map/ppermute | solution.py:21
  275.8 48.3 %collective-permute-start.25 = (f32[512,128]{1,0:T(8,128)S(1)}, f32[512,128]{1,0:T(8,128)S(1)}, u32[]{:S(2)}, u32[]{:S(2)}) collective-permute-start(f32[512,128]{1,0:T(8,128)S(1)} %get-tuple-element.4), channel_id=1, source_target_pairs={{8,0},{16,8},{24,16},{9,1},{17,9},{25,17},{10,2},{18,10},{26,18},{... | collective-permute-start | bytes 786440 | tf_op jit(solution)/shard_map/ppermute | solution.py:15
  306.8 8.4 %collective-permute-start.26 = (bf16[512,128]{1,0:T(8,128)(2,1)}, bf16[512,128]{1,0:T(8,128)(2,1)S(1)}, u32[]{:S(2)}, u32[]{:S(2)}) collective-permute-start(bf16[512,128]{1,0:T(8,128)(2,1)} %all-reduce.17.cloned.1.call-done), channel_id=1, source_target_pairs={{0,2},{1,3},{2,4},{3,5},{4,6},{5,7},{6,0},{7,1},{8,10},{9,11},{10,... | collective-permute-start | bytes 393224 | tf_op jit(solution)/shard_map/ppermute | solution.py:21
  308.3 10.0 %collective-permute-start.27 = (bf16[512,128]{1,0:T(8,128)(2,1)}, bf16[512,128]{1,0:T(8,128)(2,1)S(1)}, u32[]{:S(2)}, u32[]{:S(2)}) collective-permute-start(bf16[512,128]{1,0:T(8,128)(2,1)} %all-reduce.17.cloned.1.call-done), channel_id=1, source_target_pairs={{0,1},{1,2},{2,3},{3,4},{4,5},{5,6},{6,7},{7,0},{8,9},{9,10},{10,1... | collective-permute-start | bytes 393224 | tf_op jit(solution)/shard_map/ppermute | solution.py:21
  309.8 9.4 %collective-permute-start.28 = (bf16[512,128]{1,0:T(8,128)(2,1)}, bf16[512,128]{1,0:T(8,128)(2,1)S(1)}, u32[]{:S(2)}, u32[]{:S(2)}) collective-permute-start(bf16[512,128]{1,0:T(8,128)(2,1)} %all-reduce.17.cloned.1.call-done), channel_id=1, source_target_pairs={{0,7},{1,0},{2,1},{3,2},{4,3},{5,4},{6,5},{7,6},{8,15},{9,8},{10,9... | collective-permute-start | bytes 393224 | tf_op jit(solution)/shard_map/ppermute | solution.py:21
  (11 other events, 164.5 us)
Sparse Core Ops, SparseCore 0:
  10.9 34.0 all-reduce.6
  64.2 29.7 all-reduce.8
  115.3 31.8 all-reduce.10
  168.3 31.5 all-reduce.12
  221.8 31.5 all-reduce.14
  275.2 31.5 all-reduce.16
where the time goes:
time: 332 us
  waiting for transfers between devices  216 us (65%)
  starting transfers between devices  48.7 us (15%)
  local copies, waits for them, and re-layouts  24 us (7%)
  other arithmetic  18.5 us (6%)
  between operations  14.6 us (4%)
  matrix products  10.3 us (3%)
    psum x6, waiting for transfers between devices, from_root(): return lax.psum(block, axis)  186 us
    ppermute x24, starting transfers between devices, shifted_2(): return lax.ppermute(value, axis, pairs)  40.8 us
    ppermute x24, waiting for transfers between devices, shifted_2(): return lax.ppermute(value, axis, pairs)  29.2 us
    gather x6, local copies, waits for them, and re-layouts, per_device(): jnp.take(window, local_index, axis=0)  13.1 us
    select_n x6, other arithmetic, per_device(): jnp.take(window, local_index, axis=0)  11 us
    unnamed x43, local copies, waits for them, and re-layouts  9.18 us
    ppermute x6, starting transfers between devices, shifted(): lax.ppermute(value, axis, [(source, source + steps) for source in range(f...  7.69 us
  transfers between devices with their start and end apart: 36, of which 21 were waited for; matrix products, arithmetic and copies ran while one was open for 12% of the time, Pallas kernels for 0%

commit v1 on v0

v1 whole, which is shorter than its diff:
```python
import functools

import jax
import jax.numpy as jnp
from jax import lax
from jax.experimental import pallas as pl
from jax.experimental.pallas import tpu as pltpu
from jax.sharding import PartitionSpec as P

F32 = jnp.float32
BF16 = jnp.bfloat16
AXES = ("delay", "surface")
VMEM = pl.BlockSpec(memory_space=pltpu.VMEM)
SMEM = pl.BlockSpec(memory_space=pltpu.SMEM)


def dot(a, b):
    return jnp.dot(a, b, preferred_element_type=F32)


def call(body, outs, flops, args):
    moved = sum(a.size * a.dtype.itemsize for a in args)
    return pl.pallas_call(
        body,
        out_shape=outs,
        in_specs=[SMEM] + [VMEM] * (len(args) - 1),
        out_specs=tuple(VMEM for _ in outs),
        cost_estimate=pl.CostEstimate(flops=flops, bytes_accessed=moved, transcendentals=0),
        compiler_params=pltpu.CompilerParams(vmem_limit_bytes=24 * 1024 * 1024),
    )(*args)


def spread_body(slots, slot_ref, entries_ref, keep_ref, send_ref):
    row = pl.program_id(0)
    size = entries_ref.shape[-1]
    count = keep_ref.shape[1] // size
    for out_ref, first in ((keep_ref, 0), (send_ref, count)):
        for j in range(count):
            slot = slot_ref[row, first + j]
            columns = slice(j * size, (j + 1) * size)

            @pl.when(slot < slots)
            def _():
                out_ref[:, columns] = entries_ref[0, jnp.minimum(slot, slots - 1)]

            @pl.when(slot >= slots)
            def _():
                out_ref[:, columns] = jnp.zeros((out_ref.shape[0], size), out_ref.dtype)


def spread(entries, slot):
    blocks, slots, size, _ = entries.shape
    width = slot.shape[1] // 2 * size
    out = jax.ShapeDtypeStruct((blocks * size, width), entries.dtype)
    return pl.pallas_call(
        functools.partial(spread_body, slots),
        grid_spec=pltpu.PrefetchScalarGridSpec(
            num_scalar_prefetch=1,
            grid=(blocks,),
            in_specs=[pl.BlockSpec((1, slots, size, size), lambda i, s: (i, 0, 0, 0))],
            out_specs=[pl.BlockSpec((size, width), lambda i, s: (i, 0))] * 2,
        ),
        out_shape=(out, out),
        compiler_params=pltpu.CompilerParams(vmem_limit_bytes=24 * 1024 * 1024),
    )(slot, entries)


def own_half(flags, current_ref):
    rows = current_ref.shape[0] // 2
    return current_ref[pl.ds(pl.multiple_of(flags[0] * rows, rows), rows), :]


def early_body(flags, near_ref, far_ref, now_ref, first_ref, second_ref, before_ref, out_ref):
    rows = now_ref.shape[0]
    out_ref[...] = (
        dot(near_ref[:, 2 * rows :], own_half(flags, now_ref))
        + dot(far_ref[:, :rows], first_ref[...])
        + dot(far_ref[:, rows : 2 * rows], second_ref[...])
        + dot(far_ref[:, 2 * rows :], own_half(flags, before_ref))
    )


def early_first_body(flags, near_ref, now_ref, out_ref):
    rows = now_ref.shape[0]
    out_ref[...] = dot(near_ref[:, 2 * rows :], own_half(flags, now_ref))


def late_body(flags, near_ref, first_ref, second_ref, early_ref, out_ref):
    rows = first_ref.shape[0]
    out_ref[...] = (
        early_ref[...]
        + dot(near_ref[:, :rows], first_ref[...])
        + dot(near_ref[:, rows : 2 * rows], second_ref[...])
    )


def late_final_body(
    flags, near_ref, far_ref, now_ref, first_ref, second_ref, early_ref, keep_ref, send_ref
):
    rows = first_ref.shape[0]
    even = (
        early_ref[...]
        + dot(near_ref[:, :rows], first_ref[...])
        + dot(near_ref[:, rows : 2 * rows], second_ref[...])
    )
    odd = (
        dot(far_ref[:, :rows], first_ref[...])
        + dot(far_ref[:, rows : 2 * rows], second_ref[...])
        + dot(far_ref[:, 2 * rows :], own_half(flags, now_ref))
    )
    ends = flags[2] == 1
    second_core = flags[0] == 1
    keep_ref[...] = jnp.where(ends & second_core, odd, even)
    send_ref[...] = jnp.where(ends & ~second_core, odd, even)


def solve(inverse_ref, rhs, out_ref, keep, other):
    size = inverse_ref.shape[1]
    for i in range(inverse_ref.shape[0]):
        rows = slice(i * size, (i + 1) * size)
        fresh = dot(inverse_ref[i], rhs[rows]).astype(BF16)
        out_ref[rows, :] = jnp.where(keep, fresh, other[rows])


def start_body(flags, inverse_ref, excitation_ref, history_ref, out_ref):
    rhs = (excitation_ref[...].astype(F32) - history_ref[...]).astype(BF16)
    solve(inverse_ref, rhs, out_ref, flags[1] == 0, jnp.zeros_like(rhs))


def next_body(
    special, flags, inverse_ref, excitation_ref, mine_ref, other_ref, field_in_ref,
    current_in_ref, *rest
):
    *history, out_ref, field_ref = rest
    came = jnp.where(flags[3] == 1, 0.0, field_in_ref[...].astype(F32))
    if special:
        came = jnp.where(flags[4] == 1, history[0][...], came)
    field = mine_ref[...] + other_ref[...] + came
    rhs = (excitation_ref[...].astype(F32) - field).astype(BF16)
    first_pair = flags[1] == 0
    solve(inverse_ref, rhs, out_ref, first_pair, current_in_ref)
    field_ref[...] = field.astype(BF16)


def per_device(lagged_block_entries, pattern, diagonal_block_inverses, excitation, history):
    lags, groups = lax.axis_size("delay"), lax.axis_size("surface")
    lag, position = lax.axis_index("delay"), lax.axis_index("surface")
    core, pair, pairs = lag % 2, lag // 2, lags // 2
    entries = lagged_block_entries[0]
    blocks, slots, size, _ = entries.shape
    steps, rows, columns = excitation.shape

    def device(d, s):
        return d * groups + s

    def everyone(move):
        return [
            (device(d, s), device(*move(d, s))) for d in range(lags) for s in range(groups)
        ]

    def swapped(value):
        return lax.ppermute(value, AXES, everyone(lambda d, s: (d ^ 1, s)))

    def pair_moved(value, hop):
        return lax.ppermute(value, AXES, everyone(lambda d, s: ((d + 2 * hop) % lags, s)))

    def halo(value, hop):
        return lax.ppermute(
            value, AXES, everyone(lambda d, s: (d, (s + (hop if d % 2 == 0 else -hop)) % groups))
        )

    other_history = swapped(history[0])
    even_history = jnp.where(core == 0, history[0], other_history)
    odd_history = jnp.where(core == 0, other_history, history[0])

    span = list(range(blocks))
    half = blocks // 2
    before = [blocks + j for j in span] + span + [2 * blocks + j for j in span[:half]]
    after = (
        [3 * blocks + j for j in span]
        + [4 * blocks + j for j in span]
        + [2 * blocks + j for j in span[half:]]
    )
    order = jnp.where(
        core == 0,
        jnp.array(before + after, jnp.int32),
        jnp.array(after + before, jnp.int32),
    )
    local = (pattern[0] - (position - 2) * blocks) % (blocks * groups)
    match = local[:, :, None] == order[None, None, :]
    slot = jnp.min(
        jnp.where(match, jnp.arange(slots, dtype=jnp.int32)[None, :, None], slots), axis=1
    )
    kept, sent = spread(entries, slot)
    got = swapped(sent)
    near = jnp.where(core == 0, kept, got)
    far = jnp.where(core == 0, got, kept)

    def flags(step):
        return jnp.stack(
            [
                core,
                pair,
                (pair == step - (steps - 1)).astype(jnp.int32),
                (pair == pairs - 1).astype(jnp.int32),
                ((pair == step) | (pair == step + 1)).astype(jnp.int32),
            ]
        ).astype(jnp.int32)

    field_shape = jax.ShapeDtypeStruct((rows, columns), F32)
    current_shape = jax.ShapeDtypeStruct((rows, columns), BF16)
    unit = 2 * rows * columns
    (current,) = call(
        start_body,
        (current_shape,),
        unit * size,
        [flags(0), diagonal_block_inverses, excitation[0], even_history],
    )
    field = jnp.zeros((rows, columns), BF16)
    seen = []
    previous = None
    result = jnp.zeros((rows, columns), F32)
    for step in range(steps + pairs - 1):
        seen.append(current)
        mark = flags(step)
        first, second = halo(current, 1), halo(current, 2)
        if pairs == 2:
            current_in = field_in = pair_moved(jnp.where(pair == 0, current, field), 1)
        else:
            current_in, field_in = pair_moved(current, 1), pair_moved(field, -1)
        if previous is None:
            (early,) = call(
                early_first_body, (field_shape,), unit * rows // 2, [mark, near, current]
            )
        else:
            (early,) = call(
                early_body, (field_shape,), unit * rows * 3, [mark, near, far, current, *previous]
            )
        if step < steps - 1:
            (mine,) = call(
                late_body, (field_shape,), unit * rows * 2, [mark, near, first, second, early]
            )
            other = swapped(mine)
        else:
            mine, send = call(
                late_final_body,
                (field_shape, field_shape),
                unit * rows * 5,
                [mark, near, far, current, first, second, early],
            )
            other = swapped(send)
        came = jnp.where(pair == pairs - 1, 0.0, field_in.astype(F32))
        if step >= steps - 1:
            last = pair == step - (steps - 1)
            result = jnp.where(last, mine + other + jnp.where(core == 0, came, 0.0), result)
            result = jnp.where(
                (core == 1) & (pair == step - steps), result + came, result
            )
        previous = (first, second, current)
        if step < steps + pairs - 2:
            special = step < pairs
            extra = []
            if special:
                extra = [jnp.where(pair == step, odd_history, even_history)]
            current, field = call(
                functools.partial(next_body, special),
                (current_shape, current_shape),
                unit * size,
                [
                    mark,
                    diagonal_block_inverses,
                    excitation[min(step + 1, steps - 1)],
                    mine,
                    other,
                    field_in,
                    current_in,
                ]
                + extra,
            )
    out = []
    for step in range(steps):
        value = seen[step]
        for later in range(1, pairs):
            value = jnp.where(pair == later, seen[step + later], value)
        out.append(value)
    return (jnp.stack(out), result[None])


def solution(mesh):
    placed = (
        P("delay", "surface", None, None, None),
        P("delay", "surface", None),
        P("surface", None, None),
        P(None, "surface", None),
        P("delay", "surface", None),
    )
    return jax.shard_map(
        per_device,
        mesh=mesh,
        in_specs=placed,
        out_specs=(P(None, "surface", None), P("delay", "surface", None)),
        check_vma=False,
    )
```

time: 332 us -> 135 us (0.41)
  waiting for transfers between devices: 216 us -> 66.2 us
  Pallas kernels: 0 us -> 25 us
  starting transfers between devices: 48.7 us -> 25.3 us
  between operations: 14.6 us -> 1.06 us
  other arithmetic: 18.5 us -> 5.63 us
  local copies, waits for them, and re-layouts: 24 us -> 11.7 us
  matrix products: 10.3 us -> 0 us
    psum x6 -> x0, waiting for transfers between devices: 186 us -> none  [from_root(): return lax.psum(block, axis)]
    ppermute x30, waiting for transfers between devices: 29.2 us -> 66.2 us  [the longest x14 34.8 us: halo(): lax.ppermute(value, AXES, everyone(lambda d, s: (d, (s + (hop if d % 2 ==...]
    pallas_call x0 -> x22, Pallas kernels: none -> 25 us  [the longest x21 23 us: call(): pl.pallas_call(body, out_shape=outs, in_specs=[SMEM] + [VMEM] * (len(args...]
    ppermute x30, starting transfers between devices: 48.4 us -> 25.3 us  [the longest x14 13.4 us: halo(): lax.ppermute(value, AXES, everyone(lambda d, s: (d, (s + (hop if d % 2 ==...]
    gather x6 -> x0, local copies, waits for them, and re-layouts: 13.1 us -> none  [per_device(): jnp.take(window, local_index, axis=0)]
    dot_general x12 -> x0, matrix products: 10.3 us -> none  [the longest x6 5.92 us: block_solve(): jnp.einsum('ibc,icr->ibr', inverse, shaped, preferred_element_type=jnp.fl...]
    select_n x6 -> x11, other arithmetic: 11 us -> 4.37 us  [the longest x1 1.49 us: per_device(): far = jnp.where(core == 0, got, kept)]
    convert_element_type x6 -> x0, other arithmetic: 6 us -> none  [per_device(): rhs = (excitation[step].astype(jnp.float32) - accum).astype(jnp.bfloat16)]
  transfers between devices with their start and end apart: 36 -> 30, of which waited for: 21 -> 22; matrix products, arithmetic and copies ran while one was open for 12% -> 4% of each run, Pallas kernels for 0% -> 7%
where the time goes in v1:
time: 135 us
  waiting for transfers between devices  66.2 us (49%)
  starting transfers between devices  25.3 us (19%)
  Pallas kernels  25 us (19%)
  local copies, waits for them, and re-layouts  11.7 us (9%)
  other arithmetic  5.63 us (4%)
    ppermute x14, waiting for transfers between devices, halo(): lax.ppermute(value, AXES, everyone(lambda d, s: (d, (s + (hop if d % 2 ==...  34.8 us
    ppermute x7, waiting for transfers between devices, pair_moved(): lax.ppermute(value, AXES, everyone(lambda d, s: ((d + 2 * hop) % lags, s)))  30.6 us
    pallas_call x21, Pallas kernels, call(): pl.pallas_call(body, out_shape=outs, in_specs=[SMEM] + [VMEM] * (len(args...  23 us
    ppermute x14, starting transfers between devices, halo(): lax.ppermute(value, AXES, everyone(lambda d, s: (d, (s + (hop if d % 2 ==...  13.4 us
    ppermute x7, starting transfers between devices, pair_moved(): lax.ppermute(value, AXES, everyone(lambda d, s: ((d + 2 * hop) % lags, s)))  10.9 us
    unnamed x46, local copies, waits for them, and re-layouts  9.16 us
  transfers between devices with their start and end apart: 30, of which 22 were waited for; matrix products, arithmetic and copies ran while one was open for 4% of the time, Pallas kernels for 7%

profile of v1, /device:TPU:0, one launch (start us, length us, event | category | flops | bytes accessed | tf_op | source)
XLA Modules:
  0.0 134.9 jit_solution(8862425056343423142)
XLA Ops:
  2.1 1.6 %copy-done.1 = bf16[1,4,16,128,128]{4,3,2,1,0:T(8,128)(2,1)S(1)} copy-done((bf16[1,4,16,128,128]{4,3,2,1,0:T(8,128)(2,1)S(1)}, bf16[1,4,16,128,128]{4,3,2,1,0:T(8,128)(2,1)}, u32[]{:S(2)}) %copy-start.1) | copy-done | bytes 2097176
  3.7 2.0 %shard_map.86 = (bf16[512,1280]{1,0:T(8,128)(2,1)S(1)}, bf16[512,1280]{1,0:T(8,128)(2,1)S(1)}) custom-call(s32[4,20]{1,0:T(4,128)S(1)} %select_reduce_fusion.slot_ref, bf16[4,16,128,128]{3,2,1,0:T(8,128)(2,1)S(1)} %bitcast.55), custom_call_target="tpu_custom_call" | custom-call | tf_op jit(solution)/shard_map/pallas_call | solution.py:55
  7.4 2.0 %slice_bitcast_fusion = (bf16[512,128]{1,0:T(8,128)(2,1)S(1)}, bf16[512,128]{1,0:T(8,128)(2,1)}, bf16[512,128]{1,0:T(8,128)(2,1)S(1)}, bf16[512,128]{1,0:T(8,128...) fusion(bf16[6,512,128]{2,1,0:T(8,128)(2,1)} %param.10), kind=kLoop, calls=%fused_computation.12 | loop fusion | bytes 1572864 | tf_op jit(solution)/shard_map/squeeze | solution.py:272
  11.7 2.6 %collective-permute-start.2 = (bf16[512,128]{1,0:T(8,128)(2,1)S(1)}, bf16[512,128]{1,0:T(8,128)(2,1)S(1)}, u32[]{:S(2)}, u32[]{:S(2)}) collective-permute-start(bf16[512,128]{1,0:T(8,128)(2,1)S(1)} %shard_map.87.now_ref.before_ref), channel_id=1, source_target_pairs={{0,1},{1,2},{2,3},{3,4},{4,5},{5,6},{6,7},{7,0},{8,15},{9,8},{10,9... | collective-permute-start | bytes 393224 | tf_op jit(solution)/shard_map/ppermute | solution.py:168
  14.3 1.6 %collective-permute-start.3 = (bf16[512,128]{1,0:T(8,128)(2,1)S(1)}, bf16[512,128]{1,0:T(8,128)(2,1)S(1)}, u32[]{:S(2)}, u32[]{:S(2)}) collective-permute-start(bf16[512,128]{1,0:T(8,128)(2,1)S(1)} %shard_map.87.now_ref.before_ref), channel_id=1, source_target_pairs={{0,2},{1,3},{2,4},{3,5},{4,6},{5,7},{6,0},{7,1},{8,14},{9,15},{10,... | collective-permute-start | bytes 393224 | tf_op jit(solution)/shard_map/ppermute | solution.py:168
  15.9 1.5 %broadcast_select_fusion = (bf16[512,1280]{1,0:T(8,128)(2,1)S(1)}, bf16[512,1280]{1,0:T(8,128)(2,1)S(1)}) fusion(bf16[512,1280]{1,0:T(8,128)(2,1)} %collective-permute-done, bf16[512,1280]{1,0:T(8,128)(2,1)S(1)} %copy-done.3, pred[]{:T(512)S(6)} %eq.43), kind=kLoop, calls=%fused_computation | loop fusion | flops 1310720 | bytes 5242881 | tf_op jit(solution)/shard_map/jit(_where)/select_n | solution.py:197
  18.2 3.5 %collective-permute-done.2.first_ref = bf16[512,128]{1,0:T(8,128)(2,1)S(1)} collective-permute-done((bf16[512,128]{1,0:T(8,128)(2,1)S(1)}, bf16[512,128]{1,0:T(8,128)(2,1)S(1)}, u32[]{:S(2)}, u32[]{:S(2)}) %collective-permute-start.2) | collective-permute-done | bytes 131104 | tf_op jit(solution)/shard_map/ppermute | solution.py:168
  23.7 1.6 %collective-permute-start.5 = (bf16[512,128]{1,0:T(8,128)(2,1)S(1)}, bf16[512,128]{1,0:T(8,128)(2,1)S(1)}, u32[]{:S(2)}, u32[]{:S(2)}) collective-permute-start(bf16[512,128]{1,0:T(8,128)(2,1)S(1)} %broadcast_select_fusion.9), channel_id=1, source_target_pairs={{0,16},{1,17},{2,18},{3,19},{4,20},{5,21},{6,22},{7,23},{8,24},{9,... | collective-permute-start | bytes 393224 | tf_op jit(solution)/shard_map/ppermute | solution.py:165
  25.2 4.3 %collective-permute-done.5.field_in_ref.current_in_ref = bf16[512,128]{1,0:T(8,128)(2,1)S(1)} collective-permute-done((bf16[512,128]{1,0:T(8,128)(2,1)S(1)}, bf16[512,128]{1,0:T(8,128)(2,1)S(1)}, u32[]{:S(2)}, u32[]{:S(2)}) %collective-permute-start.5) | collective-permute-done | bytes 131104 | tf_op jit(solution)/shard_map/ppermute | solution.py:165
  35.2 3.8 %collective-permute-done.6.first_ref = bf16[512,128]{1,0:T(8,128)(2,1)} collective-permute-done((bf16[512,128]{1,0:T(8,128)(2,1)S(1)}, bf16[512,128]{1,0:T(8,128)(2,1)}, u32[]{:S(2)}, u32[]{:S(2)}) %collective-permute-start.6) | collective-permute-done | bytes 131104 | tf_op jit(solution)/shard_map/ppermute | solution.py:168
  40.6 1.6 %collective-permute-start.9 = (bf16[512,128]{1,0:T(8,128)(2,1)S(1)}, bf16[512,128]{1,0:T(8,128)(2,1)S(1)}, u32[]{:S(2)}, u32[]{:S(2)}) collective-permute-start(bf16[512,128]{1,0:T(8,128)(2,1)S(1)} %broadcast_select_fusion.7), channel_id=1, source_target_pairs={{0,16},{1,17},{2,18},{3,19},{4,20},{5,21},{6,22},{7,23},{8,24},{9,... | collective-permute-start | bytes 393224 | tf_op jit(solution)/shard_map/ppermute | solution.py:165
  42.2 4.3 %collective-permute-done.9.field_in_ref.current_in_ref = bf16[512,128]{1,0:T(8,128)(2,1)S(1)} collective-permute-done((bf16[512,128]{1,0:T(8,128)(2,1)S(1)}, bf16[512,128]{1,0:T(8,128)(2,1)S(1)}, u32[]{:S(2)}, u32[]{:S(2)}) %collective-permute-start.9) | collective-permute-done | bytes 131104 | tf_op jit(solution)/shard_map/ppermute | solution.py:165
  48.0 1.9 %collective-permute-start.10 = (bf16[512,128]{1,0:T(8,128)(2,1)S(1)}, bf16[512,128]{1,0:T(8,128)(2,1)S(1)}, u32[]{:S(2)}, u32[]{:S(2)}) collective-permute-start(bf16[512,128]{1,0:T(8,128)(2,1)S(1)} %get-tuple-element.24.now_ref.before_ref), channel_id=1, source_target_pairs={{0,1},{1,2},{2,3},{3,4},{4,5},{5,6},{6,7},{7,0},{8,15},{9,8},{10,9... | collective-permute-start | bytes 393224 | tf_op jit(solution)/shard_map/ppermute | solution.py:168
  50.1 1.5 %shard_map.94.early_ref = f32[512,128]{1,0:T(8,128)S(1)} custom-call(s32[5]{0:T(128)S(1)} %stack.177.flags, bf16[512,1280]{1,0:T(8,128)(2,1)S(1)} %get-tuple-element.39.near_ref, bf16[512,1280]{1,0:T(8,128)(2,1)S(1)} %get-tuple-element.38.far_ref, bf16[512,128]{1,0:T(8,128)(2,1)S(1)} %get-tuple-element.24.now_ref.before_ref, ...), custom_call_target="tpu_custom_call" | custom-call | flops 201326592 | bytes 3145748 | tf_op jit(solution)/shard_map/pallas_call | solution.py:23
  51.7 4.0 %collective-permute-done.10.first_ref = bf16[512,128]{1,0:T(8,128)(2,1)S(1)} collective-permute-done((bf16[512,128]{1,0:T(8,128)(2,1)S(1)}, bf16[512,128]{1,0:T(8,128)(2,1)S(1)}, u32[]{:S(2)}, u32[]{:S(2)}) %collective-permute-start.10) | collective-permute-done | bytes 131104 | tf_op jit(solution)/shard_map/ppermute | solution.py:168
  57.9 1.6 %collective-permute-start.13 = (bf16[512,128]{1,0:T(8,128)(2,1)S(1)}, bf16[512,128]{1,0:T(8,128)(2,1)S(1)}, u32[]{:S(2)}, u32[]{:S(2)}) collective-permute-start(bf16[512,128]{1,0:T(8,128)(2,1)S(1)} %broadcast_select_fusion.6), channel_id=1, source_target_pairs={{0,16},{1,17},{2,18},{3,19},{4,20},{5,21},{6,22},{7,23},{8,24},{9,... | collective-permute-start | bytes 393224 | tf_op jit(solution)/shard_map/ppermute | solution.py:165
  59.5 4.4 %collective-permute-done.13.field_in_ref.current_in_ref = bf16[512,128]{1,0:T(8,128)(2,1)S(1)} collective-permute-done((bf16[512,128]{1,0:T(8,128)(2,1)S(1)}, bf16[512,128]{1,0:T(8,128)(2,1)S(1)}, u32[]{:S(2)}, u32[]{:S(2)}) %collective-permute-start.13) | collective-permute-done | bytes 131104 | tf_op jit(solution)/shard_map/ppermute | solution.py:165
  69.2 4.2 %collective-permute-done.14.first_ref = bf16[512,128]{1,0:T(8,128)(2,1)S(1)} collective-permute-done((bf16[512,128]{1,0:T(8,128)(2,1)S(1)}, bf16[512,128]{1,0:T(8,128)(2,1)S(1)}, u32[]{:S(2)}, u32[]{:S(2)}) %collective-permute-start.14) | collective-permute-done | bytes 131104 | tf_op jit(solution)/shard_map/ppermute | solution.py:168
  73.6 2.1 %shard_map.98.mine_ref = f32[512,128]{1,0:T(8,128)} custom-call(s32[5]{0:T(128)S(1)} %stack.183.flags, bf16[512,1280]{1,0:T(8,128)(2,1)S(1)} %get-tuple-element.39.near_ref, bf16[512,128]{1,0:T(8,128)(2,1)S(1)} %collective-permute-done.14.first_ref, bf16[512,128]{1,0:T(8,128)(2,1)} %collective-permute-done.15.second_ref, f32[512,128]{1,0:T(8,128)S(1)} %shard_map.97.early_ref), custom_call_target="tpu_custom_call" | custom-call | flops 134217728 | bytes 1835028 | tf_op jit(solution)/shard_map/pallas_call | solution.py:23
  76.3 1.5 %collective-permute-start.17 = (bf16[512,128]{1,0:T(8,128)(2,1)}, bf16[512,128]{1,0:T(8,128)(2,1)}, u32[]{:S(2)}, u32[]{:S(2)}) collective-permute-start(bf16[512,128]{1,0:T(8,128)(2,1)} %broadcast_select_fusion.5), channel_id=1, source_target_pairs={{0,16},{1,17},{2,18},{3,19},{4,20},{5,21},{6,22},{7,23},{8,24},{9,... | collective-permute-start | bytes 393224 | tf_op jit(solution)/shard_map/ppermute | solution.py:165
  78.1 4.5 %collective-permute-done.17.field_in_ref.current_in_ref = bf16[512,128]{1,0:T(8,128)(2,1)} collective-permute-done((bf16[512,128]{1,0:T(8,128)(2,1)}, bf16[512,128]{1,0:T(8,128)(2,1)}, u32[]{:S(2)}, u32[]{:S(2)}) %collective-permute-start.17) | collective-permute-done | bytes 131104 | tf_op jit(solution)/shard_map/ppermute | solution.py:165
  84.8 1.9 %collective-permute-start.18 = (bf16[512,128]{1,0:T(8,128)(2,1)S(1)}, bf16[512,128]{1,0:T(8,128)(2,1)S(1)}, u32[]{:S(2)}, u32[]{:S(2)}) collective-permute-start(bf16[512,128]{1,0:T(8,128)(2,1)S(1)} %get-tuple-element.28.now_ref.before_ref), channel_id=1, source_target_pairs={{0,1},{1,2},{2,3},{3,4},{4,5},{5,6},{6,7},{7,0},{8,15},{9,8},{10,9... | collective-permute-start | bytes 393224 | tf_op jit(solution)/shard_map/ppermute | solution.py:168
  88.4 4.1 %collective-permute-done.18.first_ref = bf16[512,128]{1,0:T(8,128)(2,1)S(1)} collective-permute-done((bf16[512,128]{1,0:T(8,128)(2,1)S(1)}, bf16[512,128]{1,0:T(8,128)(2,1)S(1)}, u32[]{:S(2)}, u32[]{:S(2)}) %collective-permute-start.18) | collective-permute-done | bytes 131104 | tf_op jit(solution)/shard_map/ppermute | solution.py:168
  94.8 1.6 %collective-permute-start.21 = (bf16[512,128]{1,0:T(8,128)(2,1)S(1)}, bf16[512,128]{1,0:T(8,128)(2,1)S(1)}, u32[]{:S(2)}, u32[]{:S(2)}) collective-permute-start(bf16[512,128]{1,0:T(8,128)(2,1)S(1)} %broadcast_select_fusion.4), channel_id=1, source_target_pairs={{0,16},{1,17},{2,18},{3,19},{4,20},{5,21},{6,22},{7,23},{8,24},{9,... | collective-permute-start | bytes 393224 | tf_op jit(solution)/shard_map/ppermute | solution.py:165
  96.4 4.3 %collective-permute-done.21.field_in_ref.current_in_ref = bf16[512,128]{1,0:T(8,128)(2,1)S(1)} collective-permute-done((bf16[512,128]{1,0:T(8,128)(2,1)S(1)}, bf16[512,128]{1,0:T(8,128)(2,1)S(1)}, u32[]{:S(2)}, u32[]{:S(2)}) %collective-permute-start.21) | collective-permute-done | bytes 131104 | tf_op jit(solution)/shard_map/ppermute | solution.py:165
  103.5 6.1 %collective-permute-done.22.first_ref = bf16[512,128]{1,0:T(8,128)(2,1)S(1)} collective-permute-done((bf16[512,128]{1,0:T(8,128)(2,1)S(1)}, bf16[512,128]{1,0:T(8,128)(2,1)S(1)}, u32[]{:S(2)}, u32[]{:S(2)}) %collective-permute-start.22) | collective-permute-done | bytes 131104 | tf_op jit(solution)/shard_map/ppermute | solution.py:168
  111.1 1.6 %collective-permute-start.25 = (bf16[512,128]{1,0:T(8,128)(2,1)S(1)}, bf16[512,128]{1,0:T(8,128)(2,1)S(1)}, u32[]{:S(2)}, u32[]{:S(2)}) collective-permute-start(bf16[512,128]{1,0:T(8,128)(2,1)S(1)} %broadcast_select_fusion.3), channel_id=1, source_target_pairs={{0,16},{1,17},{2,18},{3,19},{4,20},{5,21},{6,22},{7,23},{8,24},{9,... | collective-permute-start | bytes 393224 | tf_op jit(solution)/shard_map/ppermute | solution.py:165
  112.7 4.3 %collective-permute-done.25.field_in_ref.current_in_ref = bf16[512,128]{1,0:T(8,128)(2,1)S(1)} collective-permute-done((bf16[512,128]{1,0:T(8,128)(2,1)S(1)}, bf16[512,128]{1,0:T(8,128)(2,1)S(1)}, u32[]{:S(2)}, u32[]{:S(2)}) %collective-permute-start.25) | collective-permute-done | bytes 131104 | tf_op jit(solution)/shard_map/ppermute | solution.py:165
  117.8 1.9 %collective-permute-start.26 = (bf16[512,128]{1,0:T(8,128)(2,1)S(1)}, bf16[512,128]{1,0:T(8,128)(2,1)S(1)}, u32[]{:S(2)}, u32[]{:S(2)}) collective-permute-start(bf16[512,128]{1,0:T(8,128)(2,1)S(1)} %get-tuple-element.34.now_ref), channel_id=1, source_target_pairs={{0,1},{1,2},{2,3},{3,4},{4,5},{5,6},{6,7},{7,0},{8,15},{9,8},{10,9... | collective-permute-start | bytes 393224 | tf_op jit(solution)/shard_map/ppermute | solution.py:168
  121.1 4.5 %collective-permute-done.26.first_ref = bf16[512,128]{1,0:T(8,128)(2,1)S(1)} collective-permute-done((bf16[512,128]{1,0:T(8,128)(2,1)S(1)}, bf16[512,128]{1,0:T(8,128)(2,1)S(1)}, u32[]{:S(2)}, u32[]{:S(2)}) %collective-permute-start.26) | collective-permute-done | bytes 131104 | tf_op jit(solution)/shard_map/ppermute | solution.py:168
  128.1 1.6 %collective-permute-start.29 = (bf16[512,128]{1,0:T(8,128)(2,1)S(1)}, bf16[512,128]{1,0:T(8,128)(2,1)S(1)}, u32[]{:S(2)}, u32[]{:S(2)}) collective-permute-start(bf16[512,128]{1,0:T(8,128)(2,1)S(1)} %broadcast_select_fusion.2), channel_id=1, source_target_pairs={{0,16},{1,17},{2,18},{3,19},{4,20},{5,21},{6,22},{7,23},{8,24},{9,... | collective-permute-start | bytes 393224 | tf_op jit(solution)/shard_map/ppermute | solution.py:165
  129.8 4.3 %collective-permute-done.29 = bf16[512,128]{1,0:T(8,128)(2,1)S(1)} collective-permute-done((bf16[512,128]{1,0:T(8,128)(2,1)S(1)}, bf16[512,128]{1,0:T(8,128)(2,1)S(1)}, u32[]{:S(2)}, u32[]{:S(2)}) %collective-permute-start.29) | collective-permute-done | bytes 131104 | tf_op jit(solution)/shard_map/ppermute | solution.py:165
  (123 shorter events, 41.6 us)
Async XLA Ops:
  6.8 9.1 %collective-permute-start = (bf16[512,1280]{1,0:T(8,128)(2,1)S(1)}, bf16[512,1280]{1,0:T(8,128)(2,1)}, u32[]{:S(2)}, u32[]{:S(2)}) collective-permute-start(bf16[512,1280]{1,0:T(8,128)(2,1)S(1)} %get-tuple-element.21), channel_id=1, source_target_pairs={{0,8},{1,9},{2,10},{3,11},{4,12},{5,13},{6,14},{7,15},{8,0},{9,1},... | collective-permute-start | bytes 3932168 | tf_op jit(solution)/shard_map/ppermute | solution.py:162
  7.2 3.0 %collective-permute-start.1 = (f32[512,128]{1,0:T(8,128)S(1)}, f32[512,128]{1,0:T(8,128)S(1)}, u32[]{:S(2)}, u32[]{:S(2)}) collective-permute-start(f32[512,128]{1,0:T(8,128)S(1)} %bitcast.56), channel_id=1, source_target_pairs={{0,8},{1,9},{2,10},{3,11},{4,12},{5,13},{6,14},{7,15},{8,0},{9,1},... | collective-permute-start | bytes 786440 | tf_op jit(solution)/shard_map/ppermute | solution.py:162
  11.7 10.0 %collective-permute-start.2 = (bf16[512,128]{1,0:T(8,128)(2,1)S(1)}, bf16[512,128]{1,0:T(8,128)(2,1)S(1)}, u32[]{:S(2)}, u32[]{:S(2)}) collective-permute-start(bf16[512,128]{1,0:T(8,128)(2,1)S(1)} %shard_map.87.now_ref.before_ref), channel_id=1, source_target_pairs={{0,1},{1,2},{2,3},{3,4},{4,5},{5,6},{6,7},{7,0},{8,15},{9,8},{10,9... | collective-permute-start | bytes 393224 | tf_op jit(solution)/shard_map/ppermute | solution.py:168
  14.3 8.2 %collective-permute-start.3 = (bf16[512,128]{1,0:T(8,128)(2,1)S(1)}, bf16[512,128]{1,0:T(8,128)(2,1)S(1)}, u32[]{:S(2)}, u32[]{:S(2)}) collective-permute-start(bf16[512,128]{1,0:T(8,128)(2,1)S(1)} %shard_map.87.now_ref.before_ref), channel_id=1, source_target_pairs={{0,2},{1,3},{2,4},{3,5},{4,6},{5,7},{6,0},{7,1},{8,14},{9,15},{10,... | collective-permute-start | bytes 393224 | tf_op jit(solution)/shard_map/ppermute | solution.py:168
  23.5 6.1 %collective-permute-start.4 = (f32[512,128]{1,0:T(8,128)S(1)}, f32[512,128]{1,0:T(8,128)S(1)}, u32[]{:S(2)}, u32[]{:S(2)}) collective-permute-start(f32[512,128]{1,0:T(8,128)S(1)} %shard_map.89.mine_ref), channel_id=1, source_target_pairs={{0,8},{1,9},{2,10},{3,11},{4,12},{5,13},{6,14},{7,15},{8,0},{9,1},... | collective-permute-start | bytes 786440 | tf_op jit(solution)/shard_map/ppermute | solution.py:162
  23.7 5.9 %collective-permute-start.5 = (bf16[512,128]{1,0:T(8,128)(2,1)S(1)}, bf16[512,128]{1,0:T(8,128)(2,1)S(1)}, u32[]{:S(2)}, u32[]{:S(2)}) collective-permute-start(bf16[512,128]{1,0:T(8,128)(2,1)S(1)} %broadcast_select_fusion.9), channel_id=1, source_target_pairs={{0,16},{1,17},{2,18},{3,19},{4,20},{5,21},{6,22},{7,23},{8,24},{9,... | collective-permute-start | bytes 393224 | tf_op jit(solution)/shard_map/ppermute | solution.py:165
  31.0 8.0 %collective-permute-start.6 = (bf16[512,128]{1,0:T(8,128)(2,1)S(1)}, bf16[512,128]{1,0:T(8,128)(2,1)}, u32[]{:S(2)}, u32[]{:S(2)}) collective-permute-start(bf16[512,128]{1,0:T(8,128)(2,1)S(1)} %get-tuple-element.22.now_ref.before_ref), channel_id=1, source_target_pairs={{0,1},{1,2},{2,3},{3,4},{4,5},{5,6},{6,7},{7,0},{8,15},{9,8},{10,9... | collective-permute-start | bytes 393224 | tf_op jit(solution)/shard_map/ppermute | solution.py:168
  32.2 6.9 %collective-permute-start.7 = (bf16[512,128]{1,0:T(8,128)(2,1)S(1)}, bf16[512,128]{1,0:T(8,128)(2,1)}, u32[]{:S(2)}, u32[]{:S(2)}) collective-permute-start(bf16[512,128]{1,0:T(8,128)(2,1)S(1)} %get-tuple-element.22.now_ref.before_ref), channel_id=1, source_target_pairs={{0,2},{1,3},{2,4},{3,5},{4,6},{5,7},{6,0},{7,1},{8,14},{9,15},{10,... | collective-permute-start | bytes 393224 | tf_op jit(solution)/shard_map/ppermute | solution.py:168
  35.2 11.4 %copy-start.4 = (f32[512,128]{1,0:T(8,128)S(1)}, f32[512,128]{1,0:T(8,128)}, u32[]{:S(2)}) copy-start(f32[512,128]{1,0:T(8,128)} %get-tuple-element.46.rest_0_) | copy-start | bytes 786436
  40.5 6.1 %collective-permute-start.8 = (f32[512,128]{1,0:T(8,128)S(1)}, f32[512,128]{1,0:T(8,128)S(1)}, u32[]{:S(2)}, u32[]{:S(2)}) collective-permute-start(f32[512,128]{1,0:T(8,128)S(1)} %shard_map.92.mine_ref), channel_id=1, source_target_pairs={{0,8},{1,9},{2,10},{3,11},{4,12},{5,13},{6,14},{7,15},{8,0},{9,1},... | collective-permute-start | bytes 786440 | tf_op jit(solution)/shard_map/ppermute | solution.py:162
  40.6 6.0 %collective-permute-start.9 = (bf16[512,128]{1,0:T(8,128)(2,1)S(1)}, bf16[512,128]{1,0:T(8,128)(2,1)S(1)}, u32[]{:S(2)}, u32[]{:S(2)}) collective-permute-start(bf16[512,128]{1,0:T(8,128)(2,1)S(1)} %broadcast_select_fusion.7), channel_id=1, source_target_pairs={{0,16},{1,17},{2,18},{3,19},{4,20},{5,21},{6,22},{7,23},{8,24},{9,... | collective-permute-start | bytes 393224 | tf_op jit(solution)/shard_map/ppermute | solution.py:165
  48.0 7.7 %collective-permute-start.10 = (bf16[512,128]{1,0:T(8,128)(2,1)S(1)}, bf16[512,128]{1,0:T(8,128)(2,1)S(1)}, u32[]{:S(2)}, u32[]{:S(2)}) collective-permute-start(bf16[512,128]{1,0:T(8,128)(2,1)S(1)} %get-tuple-element.24.now_ref.before_ref), channel_id=1, source_target_pairs={{0,1},{1,2},{2,3},{3,4},{4,5},{5,6},{6,7},{7,0},{8,15},{9,8},{10,9... | collective-permute-start | bytes 393224 | tf_op jit(solution)/shard_map/ppermute | solution.py:168
  49.9 6.9 %collective-permute-start.11 = (bf16[512,128]{1,0:T(8,128)(2,1)S(1)}, bf16[512,128]{1,0:T(8,128)(2,1)S(1)}, u32[]{:S(2)}, u32[]{:S(2)}) collective-permute-start(bf16[512,128]{1,0:T(8,128)(2,1)S(1)} %get-tuple-element.24.now_ref.before_ref), channel_id=1, source_target_pairs={{0,2},{1,3},{2,4},{3,5},{4,6},{5,7},{6,0},{7,1},{8,14},{9,15},{10,... | collective-permute-start | bytes 393224 | tf_op jit(solution)/shard_map/ppermute | solution.py:168
  51.7 12.2 %copy-start.14 = (bf16[512,128]{1,0:T(8,128)(2,1)S(1)}, bf16[512,128]{1,0:T(8,128)(2,1)}, u32[]{:S(2)}) copy-start(bf16[512,128]{1,0:T(8,128)(2,1)} %get-tuple-element.41.excitation_ref) | copy-start | bytes 393220
  57.8 6.1 %collective-permute-start.12 = (f32[512,128]{1,0:T(8,128)S(1)}, f32[512,128]{1,0:T(8,128)S(1)}, u32[]{:S(2)}, u32[]{:S(2)}) collective-permute-start(f32[512,128]{1,0:T(8,128)S(1)} %shard_map.95.mine_ref), channel_id=1, source_target_pairs={{0,8},{1,9},{2,10},{3,11},{4,12},{5,13},{6,14},{7,15},{8,0},{9,1},... | collective-permute-start | bytes 786440 | tf_op jit(solution)/shard_map/ppermute | solution.py:162
  57.9 6.0 %collective-permute-start.13 = (bf16[512,128]{1,0:T(8,128)(2,1)S(1)}, bf16[512,128]{1,0:T(8,128)(2,1)S(1)}, u32[]{:S(2)}, u32[]{:S(2)}) collective-permute-start(bf16[512,128]{1,0:T(8,128)(2,1)S(1)} %broadcast_select_fusion.6), channel_id=1, source_target_pairs={{0,16},{1,17},{2,18},{3,19},{4,20},{5,21},{6,22},{7,23},{8,24},{9,... | collective-permute-start | bytes 393224 | tf_op jit(solution)/shard_map/ppermute | solution.py:165
  65.3 8.1 %collective-permute-start.14 = (bf16[512,128]{1,0:T(8,128)(2,1)S(1)}, bf16[512,128]{1,0:T(8,128)(2,1)S(1)}, u32[]{:S(2)}, u32[]{:S(2)}) collective-permute-start(bf16[512,128]{1,0:T(8,128)(2,1)S(1)} %get-tuple-element.26.now_ref.before_ref), channel_id=1, source_target_pairs={{0,1},{1,2},{2,3},{3,4},{4,5},{5,6},{6,7},{7,0},{8,15},{9,8},{10,9... | collective-permute-start | bytes 393224 | tf_op jit(solution)/shard_map/ppermute | solution.py:168
  66.1 7.5 %collective-permute-start.15 = (bf16[512,128]{1,0:T(8,128)(2,1)S(1)}, bf16[512,128]{1,0:T(8,128)(2,1)}, u32[]{:S(2)}, u32[]{:S(2)}) collective-permute-start(bf16[512,128]{1,0:T(8,128)(2,1)S(1)} %get-tuple-element.26.now_ref.before_ref), channel_id=1, source_target_pairs={{0,2},{1,3},{2,4},{3,5},{4,6},{5,7},{6,0},{7,1},{8,14},{9,15},{10,... | collective-permute-start | bytes 393224 | tf_op jit(solution)/shard_map/ppermute | solution.py:168
  75.7 6.9 %collective-permute-start.16 = (f32[512,128]{1,0:T(8,128)}, f32[512,128]{1,0:T(8,128)}, u32[]{:S(2)}, u32[]{:S(2)}) collective-permute-start(f32[512,128]{1,0:T(8,128)} %shard_map.98.mine_ref), channel_id=1, source_target_pairs={{0,8},{1,9},{2,10},{3,11},{4,12},{5,13},{6,14},{7,15},{8,0},{9,1},... | collective-permute-start | bytes 786440 | tf_op jit(solution)/shard_map/ppermute | solution.py:162
  76.3 6.2 %collective-permute-start.17 = (bf16[512,128]{1,0:T(8,128)(2,1)}, bf16[512,128]{1,0:T(8,128)(2,1)}, u32[]{:S(2)}, u32[]{:S(2)}) collective-permute-start(bf16[512,128]{1,0:T(8,128)(2,1)} %broadcast_select_fusion.5), channel_id=1, source_target_pairs={{0,16},{1,17},{2,18},{3,19},{4,20},{5,21},{6,22},{7,23},{8,24},{9,... | collective-permute-start | bytes 393224 | tf_op jit(solution)/shard_map/ppermute | solution.py:165
  84.8 7.7 %collective-permute-start.18 = (bf16[512,128]{1,0:T(8,128)(2,1)S(1)}, bf16[512,128]{1,0:T(8,128)(2,1)S(1)}, u32[]{:S(2)}, u32[]{:S(2)}) collective-permute-start(bf16[512,128]{1,0:T(8,128)(2,1)S(1)} %get-tuple-element.28.now_ref.before_ref), channel_id=1, source_target_pairs={{0,1},{1,2},{2,3},{3,4},{4,5},{5,6},{6,7},{7,0},{8,15},{9,8},{10,9... | collective-permute-start | bytes 393224 | tf_op jit(solution)/shard_map/ppermute | solution.py:168
  86.7 6.9 %collective-permute-start.19 = (bf16[512,128]{1,0:T(8,128)(2,1)S(1)}, bf16[512,128]{1,0:T(8,128)(2,1)S(1)}, u32[]{:S(2)}, u32[]{:S(2)}) collective-permute-start(bf16[512,128]{1,0:T(8,128)(2,1)S(1)} %get-tuple-element.28.now_ref.before_ref), channel_id=1, source_target_pairs={{0,2},{1,3},{2,4},{3,5},{4,6},{5,7},{6,0},{7,1},{8,14},{9,15},{10,... | collective-permute-start | bytes 393224 | tf_op jit(solution)/shard_map/ppermute | solution.py:168
  94.6 6.1 %collective-permute-start.20 = (f32[512,128]{1,0:T(8,128)S(1)}, f32[512,128]{1,0:T(8,128)S(1)}, u32[]{:S(2)}, u32[]{:S(2)}) collective-permute-start(f32[512,128]{1,0:T(8,128)S(1)} %shard_map.101.mine_ref), channel_id=1, source_target_pairs={{0,8},{1,9},{2,10},{3,11},{4,12},{5,13},{6,14},{7,15},{8,0},{9,1},... | collective-permute-start | bytes 786440 | tf_op jit(solution)/shard_map/ppermute | solution.py:162
  94.8 6.0 %collective-permute-start.21 = (bf16[512,128]{1,0:T(8,128)(2,1)S(1)}, bf16[512,128]{1,0:T(8,128)(2,1)S(1)}, u32[]{:S(2)}, u32[]{:S(2)}) collective-permute-start(bf16[512,128]{1,0:T(8,128)(2,1)S(1)} %broadcast_select_fusion.4), channel_id=1, source_target_pairs={{0,16},{1,17},{2,18},{3,19},{4,20},{5,21},{6,22},{7,23},{8,24},{9,... | collective-permute-start | bytes 393224 | tf_op jit(solution)/shard_map/ppermute | solution.py:165
  101.5 8.2 %collective-permute-start.22 = (bf16[512,128]{1,0:T(8,128)(2,1)S(1)}, bf16[512,128]{1,0:T(8,128)(2,1)S(1)}, u32[]{:S(2)}, u32[]{:S(2)}) collective-permute-start(bf16[512,128]{1,0:T(8,128)(2,1)S(1)} %get-tuple-element.30.now_ref.before_ref), channel_id=1, source_target_pairs={{0,1},{1,2},{2,3},{3,4},{4,5},{5,6},{6,7},{7,0},{8,15},{9,8},{10,9... | collective-permute-start | bytes 393224 | tf_op jit(solution)/shard_map/ppermute | solution.py:168
  102.3 7.4 %collective-permute-start.23 = (bf16[512,128]{1,0:T(8,128)(2,1)S(1)}, bf16[512,128]{1,0:T(8,128)(2,1)S(1)}, u32[]{:S(2)}, u32[]{:S(2)}) collective-permute-start(bf16[512,128]{1,0:T(8,128)(2,1)S(1)} %get-tuple-element.30.now_ref.before_ref), channel_id=1, source_target_pairs={{0,2},{1,3},{2,4},{3,5},{4,6},{5,7},{6,0},{7,1},{8,14},{9,15},{10,... | collective-permute-start | bytes 393224 | tf_op jit(solution)/shard_map/ppermute | solution.py:168
  111.0 6.1 %collective-permute-start.24 = (f32[512,128]{1,0:T(8,128)S(1)}, f32[512,128]{1,0:T(8,128)S(1)}, u32[]{:S(2)}, u32[]{:S(2)}) collective-permute-start(f32[512,128]{1,0:T(8,128)S(1)} %get-tuple-element.32), channel_id=1, source_target_pairs={{0,8},{1,9},{2,10},{3,11},{4,12},{5,13},{6,14},{7,15},{8,0},{9,1},... | collective-permute-start | bytes 786440 | tf_op jit(solution)/shard_map/ppermute | solution.py:162
  111.1 6.0 %collective-permute-start.25 = (bf16[512,128]{1,0:T(8,128)(2,1)S(1)}, bf16[512,128]{1,0:T(8,128)(2,1)S(1)}, u32[]{:S(2)}, u32[]{:S(2)}) collective-permute-start(bf16[512,128]{1,0:T(8,128)(2,1)S(1)} %broadcast_select_fusion.3), channel_id=1, source_target_pairs={{0,16},{1,17},{2,18},{3,19},{4,20},{5,21},{6,22},{7,23},{8,24},{9,... | collective-permute-start | bytes 393224 | tf_op jit(solution)/shard_map/ppermute | solution.py:165
  117.8 7.7 %collective-permute-start.26 = (bf16[512,128]{1,0:T(8,128)(2,1)S(1)}, bf16[512,128]{1,0:T(8,128)(2,1)S(1)}, u32[]{:S(2)}, u32[]{:S(2)}) collective-permute-start(bf16[512,128]{1,0:T(8,128)(2,1)S(1)} %get-tuple-element.34.now_ref), channel_id=1, source_target_pairs={{0,1},{1,2},{2,3},{3,4},{4,5},{5,6},{6,7},{7,0},{8,15},{9,8},{10,9... | collective-permute-start | bytes 393224 | tf_op jit(solution)/shard_map/ppermute | solution.py:168
  119.8 6.9 %collective-permute-start.27 = (bf16[512,128]{1,0:T(8,128)(2,1)S(1)}, bf16[512,128]{1,0:T(8,128)(2,1)S(1)}, u32[]{:S(2)}, u32[]{:S(2)}) collective-permute-start(bf16[512,128]{1,0:T(8,128)(2,1)S(1)} %get-tuple-element.34.now_ref), channel_id=1, source_target_pairs={{0,2},{1,3},{2,4},{3,5},{4,6},{5,7},{6,0},{7,1},{8,14},{9,15},{10,... | collective-permute-start | bytes 393224 | tf_op jit(solution)/shard_map/ppermute | solution.py:168
  128.0 6.1 %collective-permute-start.28 = (f32[512,128]{1,0:T(8,128)S(1)}, f32[512,128]{1,0:T(8,128)S(1)}, u32[]{:S(2)}, u32[]{:S(2)}) collective-permute-start(f32[512,128]{1,0:T(8,128)S(1)} %get-tuple-element.36), channel_id=1, source_target_pairs={{0,8},{1,9},{2,10},{3,11},{4,12},{5,13},{6,14},{7,15},{8,0},{9,1},... | collective-permute-start | bytes 786440 | tf_op jit(solution)/shard_map/ppermute | solution.py:162
  128.1 6.0 %collective-permute-start.29 = (bf16[512,128]{1,0:T(8,128)(2,1)S(1)}, bf16[512,128]{1,0:T(8,128)(2,1)S(1)}, u32[]{:S(2)}, u32[]{:S(2)}) collective-permute-start(bf16[512,128]{1,0:T(8,128)(2,1)S(1)} %broadcast_select_fusion.2), channel_id=1, source_target_pairs={{0,16},{1,17},{2,18},{3,19},{4,20},{5,21},{6,22},{7,23},{8,24},{9,... | collective-permute-start | bytes 393224 | tf_op jit(solution)/shard_map/ppermute | solution.py:165
  (21 other events, 77.8 us)

commit v2 on v1

v2 whole, which is shorter than its diff:
```python
import functools

import jax
import jax.numpy as jnp
from jax import lax
from jax.experimental import pallas as pl
from jax.experimental.pallas import tpu as pltpu
from jax.sharding import PartitionSpec as P

F32 = jnp.float32
BF16 = jnp.bfloat16
AXES = ("delay", "surface")
VMEM = pl.BlockSpec(memory_space=pltpu.VMEM)
MIB = 1024 * 1024


def dot(a, b):
    return jnp.dot(a, b, preferred_element_type=F32)


def place():
    lag = lax.axis_index("delay")
    return lax.rem(lag, 2), lax.div(lag, 2)


def call(body, outs, flops, args):
    moved = sum(a.size * a.dtype.itemsize for a in args)
    return pl.pallas_call(
        body,
        out_shape=tuple(outs),
        in_specs=[VMEM] * len(args),
        out_specs=tuple(VMEM for _ in outs),
        cost_estimate=pl.CostEstimate(flops=flops, bytes_accessed=moved, transcendentals=0),
        compiler_params=pltpu.CompilerParams(vmem_limit_bytes=8 * MIB),
    )(*args)


def spread_body(groups, pattern_ref, entries_ref, after_ref, keep_ref, send_ref):
    del after_ref
    core, _ = place()
    row = pl.program_id(0)
    blocks = pl.num_programs(0)
    slots, size = entries_ref.shape[1], entries_ref.shape[2]
    total = blocks * groups
    base = (lax.axis_index("surface") - 2) * blocks
    keep_ref[...] = jnp.zeros_like(keep_ref)
    send_ref[...] = jnp.zeros_like(send_ref)
    for slot in range(slots):
        j = lax.rem(pattern_ref[row, slot] - base + total, total)
        first = j < 2 * blocks + blocks // 2
        column = jnp.where(
            j < blocks,
            j + blocks,
            jnp.where(
                j < 2 * blocks,
                j - blocks,
                jnp.where(first, j, jnp.where(j < 3 * blocks, j - blocks // 2, j - 3 * blocks)),
            ),
        )
        columns = pl.ds(pl.multiple_of(column * size, size), size)
        mine = first == (core == 0)

        @pl.when(mine)
        def _():
            keep_ref[:, columns] = entries_ref[0, slot]

        @pl.when(jnp.logical_not(mine))
        def _():
            send_ref[:, columns] = entries_ref[0, slot]


def spread(entries, pattern, groups, after):
    blocks, slots, size, _ = entries.shape
    width = (2 * blocks + blocks // 2) * size
    out = jax.ShapeDtypeStruct((blocks * size, width), entries.dtype)
    return pl.pallas_call(
        functools.partial(spread_body, groups),
        grid_spec=pltpu.PrefetchScalarGridSpec(
            num_scalar_prefetch=1,
            grid=(blocks,),
            in_specs=[
                pl.BlockSpec((1, slots, size, size), lambda i, s: (i, 0, 0, 0)),
                pl.BlockSpec(memory_space=pl.ANY),
            ],
            out_specs=[pl.BlockSpec((size, width), lambda i, s: (i, 0))] * 2,
        ),
        out_shape=(out, out),
        compiler_params=pltpu.CompilerParams(vmem_limit_bytes=8 * MIB),
    )(pattern, entries, after)


def own_half(current_ref):
    core, _ = place()
    rows = current_ref.shape[0] // 2
    return current_ref[pl.ds(pl.multiple_of(core * rows, rows), rows), :]


def early_body(near_ref, far_ref, now_ref, first_ref, second_ref, before_ref, out_ref):
    rows = now_ref.shape[0]
    out_ref[...] = (
        dot(near_ref[:, 2 * rows :], own_half(now_ref))
        + dot(far_ref[:, :rows], first_ref[...])
        + dot(far_ref[:, rows : 2 * rows], second_ref[...])
        + dot(far_ref[:, 2 * rows :], own_half(before_ref))
    )


def early_first_body(near_ref, now_ref, out_ref):
    rows = now_ref.shape[0]
    out_ref[...] = dot(near_ref[:, 2 * rows :], own_half(now_ref))


def came(step, pairs, field_ref, history):
    core, pair = place()
    value = 0.0
    if step > 0:
        value = jnp.where(pair == pairs - 1, 0.0, field_ref[...].astype(F32))
    if history:
        odd_ref, even_ref = history
        value = jnp.where(
            pair == step, odd_ref[...], jnp.where(pair == step + 1, even_ref[...], value)
        )
    return jnp.where(core == 0, value, 0.0)


def late_body(step, pairs, near_ref, first_ref, second_ref, early_ref, field_ref, *rest):
    *history, out_ref = rest
    rows = first_ref.shape[0]
    out_ref[...] = (
        early_ref[...]
        + came(step, pairs, field_ref, history)
        + dot(near_ref[:, :rows], first_ref[...])
        + dot(near_ref[:, rows : 2 * rows], second_ref[...])
    )


def late_final_body(
    step, steps, pairs, near_ref, first_ref, second_ref, early_ref, field_ref, far_ref, now_ref, *rest
):
    *history, keep_ref, send_ref = rest
    core, pair = place()
    rows = first_ref.shape[0]
    even = (
        early_ref[...]
        + came(step, pairs, field_ref, history)
        + dot(near_ref[:, :rows], first_ref[...])
        + dot(near_ref[:, rows : 2 * rows], second_ref[...])
    )
    odd = (
        dot(far_ref[:, :rows], first_ref[...])
        + dot(far_ref[:, rows : 2 * rows], second_ref[...])
        + dot(far_ref[:, 2 * rows :], own_half(now_ref))
    )
    ends = pair == step - (steps - 1)
    keep_ref[...] = jnp.where(jnp.logical_and(ends, core == 1), odd, even)
    send_ref[...] = jnp.where(jnp.logical_and(ends, core == 0), odd, even)


def solve(inverse_ref, rhs, out_ref, keep, other):
    size = inverse_ref.shape[1]
    fresh = []
    for i in range(inverse_ref.shape[0]):
        rows = slice(i * size, (i + 1) * size)
        block = dot(inverse_ref[i], rhs[rows]).astype(BF16)
        fresh.append(jnp.where(keep, block, other[rows]))
        out_ref[rows, :] = fresh[-1]
    return fresh


def start_body(inverse_ref, excitation_ref, history_ref, out_ref):
    _, pair = place()
    rhs = (excitation_ref[...].astype(F32) - history_ref[...]).astype(BF16)
    solve(inverse_ref, rhs, out_ref, pair == 0, jnp.zeros_like(rhs))


def next_body(pairs, inverse_ref, excitation_ref, mine_ref, other_ref, came_ref, out_ref, field_ref):
    _, pair = place()
    field = mine_ref[...] + other_ref[...]
    rhs = (excitation_ref[...].astype(F32) - field).astype(BF16)
    first_pair = pair == 0
    fresh = solve(inverse_ref, rhs, out_ref, first_pair, came_ref)
    if pairs == 2:
        size = inverse_ref.shape[1]
        for i, block in enumerate(fresh):
            rows = slice(i * size, (i + 1) * size)
            field_ref[rows, :] = jnp.where(first_pair, block, field[rows].astype(BF16))
    else:
        field_ref[...] = field.astype(BF16)


def per_device(lagged_block_entries, pattern, diagonal_block_inverses, excitation, history):
    lags, groups = lax.axis_size("delay"), lax.axis_size("surface")
    core, pair = place()
    pairs = lags // 2
    entries = lagged_block_entries[0]
    blocks, slots, size, _ = entries.shape
    steps, rows, columns = excitation.shape

    def device(d, s):
        return d * groups + s

    def everyone(move):
        return [
            (device(d, s), device(*move(d, s))) for d in range(lags) for s in range(groups)
        ]

    def swapped(value):
        return lax.ppermute(value, AXES, everyone(lambda d, s: (d ^ 1, s)))

    def pair_moved(value, hop):
        return lax.ppermute(value, AXES, everyone(lambda d, s: ((d + 2 * hop) % lags, s)))

    def halo(value, hop):
        return lax.ppermute(
            value, AXES, everyone(lambda d, s: (d, (s + (hop if d % 2 == 0 else -hop)) % groups))
        )

    other_history = swapped(history[0])
    even_history = jnp.where(core == 0, history[0], other_history)
    odd_history = jnp.where(core == 0, other_history, history[0])

    field_shape = jax.ShapeDtypeStruct((rows, columns), F32)
    current_shape = jax.ShapeDtypeStruct((rows, columns), BF16)
    unit = 2 * rows * columns
    (current,) = call(
        start_body,
        [current_shape],
        unit * size,
        [diagonal_block_inverses, excitation[0], even_history],
    )
    kept, sent = spread(entries, pattern[0], groups, current)
    got = swapped(sent)
    near = jnp.where(core == 0, kept, got)
    far = jnp.where(core == 0, got, kept)

    going = current
    seen = []
    previous = None
    result = jnp.zeros((rows, columns), F32)
    for step in range(steps + pairs - 1):
        seen.append(current)
        first, second = halo(current, 1), halo(current, 2)
        if pairs == 2:
            current_in = field_in = pair_moved(going, 1)
        else:
            current_in, field_in = pair_moved(current, 1), pair_moved(going, -1)
        if previous is None:
            (early,) = call(early_first_body, [field_shape], unit * rows // 2, [near, current])
        else:
            (early,) = call(
                early_body, [field_shape], unit * rows * 3, [near, far, current, *previous]
            )
        received = [near, first, second, early, field_in]
        extra = [odd_history, even_history] if step < pairs else []
        if step < steps - 1:
            (mine,) = call(
                functools.partial(late_body, step, pairs),
                [field_shape],
                unit * rows * 2,
                received + extra,
            )
            other = swapped(mine)
            came_in = current_in
            current, going = call(
                functools.partial(next_body, pairs),
                [current_shape, current_shape],
                unit * size,
                [diagonal_block_inverses, excitation[step + 1], mine, other, came_in],
            )
        else:
            mine, send = call(
                functools.partial(late_final_body, step, steps, pairs),
                [field_shape, field_shape],
                unit * rows * 5,
                received + [far, current] + extra,
            )
            field = mine + swapped(send)
            last_in = jnp.where(pair == pairs - 1, 0.0, field_in.astype(F32))
            result = jnp.where(pair == step - (steps - 1), field, result)
            result = jnp.where((core == 1) & (pair == step - steps), result + last_in, result)
            previous = (first, second, current)
            current, going = current_in, field.astype(BF16)
        previous = (first, second, seen[-1])
    out = []
    for step in range(steps):
        value = seen[step]
        for later in range(1, pairs):
            value = jnp.where(pair == later, seen[step + later], value)
        out.append(value)
    return (jnp.stack(out), result[None])


def solution(mesh):
    placed = (
        P("delay", "surface", None, None, None),
        P("delay", "surface", None),
        P("surface", None, None),
        P(None, "surface", None),
        P("delay", "surface", None),
    )
    return jax.shard_map(
        per_device,
        mesh=mesh,
        in_specs=placed,
        out_specs=(P(None, "surface", None), P("delay", "surface", None)),
        check_vma=False,
    )
```

time: 135 us -> 86.8 us (0.64)
  waiting for transfers between devices: 66.2 us -> 42.7 us
  Pallas kernels: 25 us -> 12.6 us
  local copies, waits for them, and re-layouts: 11.7 us -> 2.68 us
  other arithmetic: 5.63 us -> 1.38 us
    ppermute x7, waiting for transfers between devices: 30.6 us -> 3.7 us  [pair_moved(): lax.ppermute(value, AXES, everyone(lambda d, s: ((d + 2 * hop) % lags, s)))]
    pallas_call x22 -> x21, Pallas kernels: 25 us -> 12.6 us  [the longest x20 10.3 us: call(): pl.pallas_call(body, out_shape=tuple(outs), in_specs=[VMEM] * len(args),...]
    ppermute x9, waiting for transfers between devices: 0.86 us -> 9.24 us  [swapped(): return lax.ppermute(value, AXES, everyone(lambda d, s: (d ^ 1, s)))]
    unnamed x46 -> x22, local copies, waits for them, and re-layouts: 9.16 us -> 1.28 us
    ppermute x14, waiting for transfers between devices: 34.8 us -> 29.8 us  [halo(): lax.ppermute(value, AXES, everyone(lambda d, s: (d, (s + (hop if d % 2 ==...]
    select_n x10 -> x1, other arithmetic: 2.88 us -> 0.04 us  [per_device(): odd_history = jnp.where(core == 0, other_history, history[0])]
  transfers between devices with their start and end apart: 30 -> 30, of which waited for: 22 -> 21; matrix products, arithmetic and copies ran while one was open for 4% -> 2% of each run, Pallas kernels for 7% -> 4%
where the time goes in v2:
time: 86.8 us; the launch traced here: 86.6 us
  waiting for transfers between devices  42.7 us (49%)
  starting transfers between devices  26.3 us (30%)
  Pallas kernels  12.6 us (15%)
  local copies, waits for them, and re-layouts  2.68 us (3%)
  other arithmetic  1.38 us (2%)
  between operations  0.95 us (1%)
    ppermute x14, waiting for transfers between devices, halo(): lax.ppermute(value, AXES, everyone(lambda d, s: (d, (s + (hop if d % 2 ==...  29.8 us
    ppermute x14, starting transfers between devices, halo(): lax.ppermute(value, AXES, everyone(lambda d, s: (d, (s + (hop if d % 2 ==...  14.7 us
    ppermute x7, starting transfers between devices, pair_moved(): lax.ppermute(value, AXES, everyone(lambda d, s: ((d + 2 * hop) % lags, s)))  10.4 us
    pallas_call x20, Pallas kernels, call(): pl.pallas_call(body, out_shape=tuple(outs), in_specs=[VMEM] * len(args),...  10.3 us
    ppermute x9, waiting for transfers between devices, swapped(): return lax.ppermute(value, AXES, everyone(lambda d, s: (d ^ 1, s)))  9.24 us
    ppermute x7, waiting for transfers between devices, pair_moved(): lax.ppermute(value, AXES, everyone(lambda d, s: ((d + 2 * hop) % lags, s)))  3.7 us
    pallas_call x1, Pallas kernels, spread(): pl.pallas_call(functools.partial(spread_body, groups), grid_spec=pltpu.Pr...  2.31 us
  transfers between devices with their start and end apart: 30, of which 21 were waited for; matrix products, arithmetic and copies ran while one was open for 2% of the time, Pallas kernels for 4%

profile of v2, /device:TPU:0, one launch (start us, length us, event | category | flops | bytes accessed | tf_op | source)
XLA Modules:
  0.0 86.6 jit_solution(1289474203457083330)
XLA Ops:
  1.2 1.4 %slice_bitcast_fusion = (bf16[512,128]{1,0:T(8,128)(2,1)S(1)}, bf16[512,128]{1,0:T(8,128)(2,1)S(1)}, bf16[512,128]{1,0:T(8,128)(2,1)S(1)}, bf16[512,128]{1,0:T(8...) fusion(bf16[6,512,128]{2,1,0:T(8,128)(2,1)} %param.8), kind=kLoop, calls=%fused_computation.12 | loop fusion | bytes 1572864 | tf_op jit(solution)/shard_map/squeeze | solution.py:268
  3.2 2.3 %shard_map.69 = (bf16[512,1280]{1,0:T(8,128)(2,1)S(1)}, bf16[512,1280]{1,0:T(8,128)(2,1)S(1)}) custom-call(s32[4,16]{1,0:T(4,128)S(1)} %bitcast.32, bf16[4,16,128,128]{3,2,1,0:T(8,128)(2,1)S(1)} %bitcast.31, bf16[512,128]{1,0:T(8,128)(2,1)S(1)} %shard_map.68.after_ref.now_ref.before_ref), custom_call_target="tpu_custom_call" | custom-call | tf_op jit(solution)/shard_map/pallas_call | solution.py:76
  5.6 3.0 %collective-permute-start.2 = (bf16[512,128]{1,0:T(8,128)(2,1)S(1)}, bf16[512,128]{1,0:T(8,128)(2,1)S(1)}, u32[]{:S(2)}, u32[]{:S(2)}) collective-permute-start(bf16[512,128]{1,0:T(8,128)(2,1)S(1)} %shard_map.68.after_ref.now_ref.before_ref), channel_id=1, source_target_pairs={{0,1},{1,2},{2,3},{3,4},{4,5},{5,6},{6,7},{7,0},{8,15},{9,8},{10,9... | collective-permute-start | bytes 393224 | tf_op jit(solution)/shard_map/ppermute | solution.py:214
  8.6 1.6 %collective-permute-start.3 = (bf16[512,128]{1,0:T(8,128)(2,1)S(1)}, bf16[512,128]{1,0:T(8,128)(2,1)S(1)}, u32[]{:S(2)}, u32[]{:S(2)}) collective-permute-start(bf16[512,128]{1,0:T(8,128)(2,1)S(1)} %shard_map.68.after_ref.now_ref.before_ref), channel_id=1, source_target_pairs={{0,2},{1,3},{2,4},{3,5},{4,6},{5,7},{6,0},{7,1},{8,14},{9,15},{10,... | collective-permute-start | bytes 393224 | tf_op jit(solution)/shard_map/ppermute | solution.py:214
  10.2 1.5 %collective-permute-start.4 = (bf16[512,128]{1,0:T(8,128)(2,1)S(1)}, bf16[512,128]{1,0:T(8,128)(2,1)S(1)}, u32[]{:S(2)}, u32[]{:S(2)}) collective-permute-start(bf16[512,128]{1,0:T(8,128)(2,1)S(1)} %shard_map.68.after_ref.now_ref.before_ref), channel_id=1, source_target_pairs={{0,16},{1,17},{2,18},{3,19},{4,20},{5,21},{6,22},{7,23},{8,24},{9,... | collective-permute-start | bytes 393224 | tf_op jit(solution)/shard_map/ppermute | solution.py:211
  12.1 3.7 %collective-permute-done.2.first_ref = bf16[512,128]{1,0:T(8,128)(2,1)S(1)} collective-permute-done((bf16[512,128]{1,0:T(8,128)(2,1)S(1)}, bf16[512,128]{1,0:T(8,128)(2,1)S(1)}, u32[]{:S(2)}, u32[]{:S(2)}) %collective-permute-start.2) | collective-permute-done | bytes 131104 | tf_op jit(solution)/shard_map/ppermute | solution.py:214
  15.7 1.0 %collective-permute-done.3.second_ref = bf16[512,128]{1,0:T(8,128)(2,1)S(1)} collective-permute-done((bf16[512,128]{1,0:T(8,128)(2,1)S(1)}, bf16[512,128]{1,0:T(8,128)(2,1)S(1)}, u32[]{:S(2)}, u32[]{:S(2)}) %collective-permute-start.3) | collective-permute-done | bytes 131104 | tf_op jit(solution)/shard_map/ppermute | solution.py:214
  17.4 1.4 %collective-permute-done.5.other_ref = f32[512,128]{1,0:T(8,128)S(1)} collective-permute-done((f32[512,128]{1,0:T(8,128)S(1)}, f32[512,128]{1,0:T(8,128)S(1)}, u32[]{:S(2)}, u32[]{:S(2)}) %collective-permute-start.5) | collective-permute-done | bytes 262176 | tf_op jit(solution)/shard_map/ppermute | solution.py:208
  20.5 1.5 %collective-permute-start.8 = (bf16[512,128]{1,0:T(8,128)(2,1)S(1)}, bf16[512,128]{1,0:T(8,128)(2,1)S(1)}, u32[]{:S(2)}, u32[]{:S(2)}) collective-permute-start(bf16[512,128]{1,0:T(8,128)(2,1)S(1)} %get-tuple-element.21), channel_id=1, source_target_pairs={{0,16},{1,17},{2,18},{3,19},{4,20},{5,21},{6,22},{7,23},{8,24},{9,... | collective-permute-start | bytes 393224 | tf_op jit(solution)/shard_map/ppermute | solution.py:211
  22.6 4.8 %collective-permute-done.6.first_ref = bf16[512,128]{1,0:T(8,128)(2,1)S(1)} collective-permute-done((bf16[512,128]{1,0:T(8,128)(2,1)S(1)}, bf16[512,128]{1,0:T(8,128)(2,1)S(1)}, u32[]{:S(2)}, u32[]{:S(2)}) %collective-permute-start.6) | collective-permute-done | bytes 131104 | tf_op jit(solution)/shard_map/ppermute | solution.py:214
  28.0 1.5 %collective-permute-done.9.other_ref = f32[512,128]{1,0:T(8,128)S(1)} collective-permute-done((f32[512,128]{1,0:T(8,128)S(1)}, f32[512,128]{1,0:T(8,128)S(1)}, u32[]{:S(2)}, u32[]{:S(2)}) %collective-permute-start.9) | collective-permute-done | bytes 262176 | tf_op jit(solution)/shard_map/ppermute | solution.py:208
  29.8 1.9 %collective-permute-start.10 = (bf16[512,128]{1,0:T(8,128)(2,1)S(1)}, bf16[512,128]{1,0:T(8,128)(2,1)S(1)}, u32[]{:S(2)}, u32[]{:S(2)}) collective-permute-start(bf16[512,128]{1,0:T(8,128)(2,1)S(1)} %get-tuple-element.22.now_ref.before_ref), channel_id=1, source_target_pairs={{0,1},{1,2},{2,3},{3,4},{4,5},{5,6},{6,7},{7,0},{8,15},{9,8},{10,9... | collective-permute-start | bytes 393224 | tf_op jit(solution)/shard_map/ppermute | solution.py:214
  32.1 1.5 %collective-permute-start.12 = (bf16[512,128]{1,0:T(8,128)(2,1)S(1)}, bf16[512,128]{1,0:T(8,128)(2,1)S(1)}, u32[]{:S(2)}, u32[]{:S(2)}) collective-permute-start(bf16[512,128]{1,0:T(8,128)(2,1)S(1)} %get-tuple-element.23), channel_id=1, source_target_pairs={{0,16},{1,17},{2,18},{3,19},{4,20},{5,21},{6,22},{7,23},{8,24},{9,... | collective-permute-start | bytes 393224 | tf_op jit(solution)/shard_map/ppermute | solution.py:211
  34.2 3.3 %collective-permute-done.10.first_ref = bf16[512,128]{1,0:T(8,128)(2,1)S(1)} collective-permute-done((bf16[512,128]{1,0:T(8,128)(2,1)S(1)}, bf16[512,128]{1,0:T(8,128)(2,1)S(1)}, u32[]{:S(2)}, u32[]{:S(2)}) %collective-permute-start.10) | collective-permute-done | bytes 131104 | tf_op jit(solution)/shard_map/ppermute | solution.py:214
  37.5 1.2 %collective-permute-done.11.second_ref = bf16[512,128]{1,0:T(8,128)(2,1)S(1)} collective-permute-done((bf16[512,128]{1,0:T(8,128)(2,1)S(1)}, bf16[512,128]{1,0:T(8,128)(2,1)S(1)}, u32[]{:S(2)}, u32[]{:S(2)}) %collective-permute-start.11) | collective-permute-done | bytes 131104 | tf_op jit(solution)/shard_map/ppermute | solution.py:214
  39.2 1.5 %collective-permute-done.13.other_ref = f32[512,128]{1,0:T(8,128)S(1)} collective-permute-done((f32[512,128]{1,0:T(8,128)S(1)}, f32[512,128]{1,0:T(8,128)S(1)}, u32[]{:S(2)}, u32[]{:S(2)}) %collective-permute-start.13) | collective-permute-done | bytes 262176 | tf_op jit(solution)/shard_map/ppermute | solution.py:208
  41.8 1.5 %collective-permute-start.16 = (bf16[512,128]{1,0:T(8,128)(2,1)S(1)}, bf16[512,128]{1,0:T(8,128)(2,1)S(1)}, u32[]{:S(2)}, u32[]{:S(2)}) collective-permute-start(bf16[512,128]{1,0:T(8,128)(2,1)S(1)} %get-tuple-element.25), channel_id=1, source_target_pairs={{0,16},{1,17},{2,18},{3,19},{4,20},{5,21},{6,22},{7,23},{8,24},{9,... | collective-permute-start | bytes 393224 | tf_op jit(solution)/shard_map/ppermute | solution.py:211
  43.9 4.8 %collective-permute-done.14.first_ref = bf16[512,128]{1,0:T(8,128)(2,1)S(1)} collective-permute-done((bf16[512,128]{1,0:T(8,128)(2,1)S(1)}, bf16[512,128]{1,0:T(8,128)(2,1)S(1)}, u32[]{:S(2)}, u32[]{:S(2)}) %collective-permute-start.14) | collective-permute-done | bytes 131104 | tf_op jit(solution)/shard_map/ppermute | solution.py:214
  49.5 1.5 %collective-permute-done.17.other_ref = f32[512,128]{1,0:T(8,128)S(1)} collective-permute-done((f32[512,128]{1,0:T(8,128)S(1)}, f32[512,128]{1,0:T(8,128)S(1)}, u32[]{:S(2)}, u32[]{:S(2)}) %collective-permute-start.17) | collective-permute-done | bytes 262176 | tf_op jit(solution)/shard_map/ppermute | solution.py:208
  51.2 1.7 %collective-permute-start.18 = (bf16[512,128]{1,0:T(8,128)(2,1)S(1)}, bf16[512,128]{1,0:T(8,128)(2,1)S(1)}, u32[]{:S(2)}, u32[]{:S(2)}) collective-permute-start(bf16[512,128]{1,0:T(8,128)(2,1)S(1)} %get-tuple-element.26.now_ref.before_ref), channel_id=1, source_target_pairs={{0,1},{1,2},{2,3},{3,4},{4,5},{5,6},{6,7},{7,0},{8,15},{9,8},{10,9... | collective-permute-start | bytes 393224 | tf_op jit(solution)/shard_map/ppermute | solution.py:214
  53.3 1.5 %collective-permute-start.20 = (bf16[512,128]{1,0:T(8,128)(2,1)S(1)}, bf16[512,128]{1,0:T(8,128)(2,1)S(1)}, u32[]{:S(2)}, u32[]{:S(2)}) collective-permute-start(bf16[512,128]{1,0:T(8,128)(2,1)S(1)} %get-tuple-element.27), channel_id=1, source_target_pairs={{0,16},{1,17},{2,18},{3,19},{4,20},{5,21},{6,22},{7,23},{8,24},{9,... | collective-permute-start | bytes 393224 | tf_op jit(solution)/shard_map/ppermute | solution.py:211
  55.4 3.8 %collective-permute-done.18.first_ref = bf16[512,128]{1,0:T(8,128)(2,1)S(1)} collective-permute-done((bf16[512,128]{1,0:T(8,128)(2,1)S(1)}, bf16[512,128]{1,0:T(8,128)(2,1)S(1)}, u32[]{:S(2)}, u32[]{:S(2)}) %collective-permute-start.18) | collective-permute-done | bytes 131104 | tf_op jit(solution)/shard_map/ppermute | solution.py:214
  60.0 1.1 %shard_map.83.mine_ref = f32[512,128]{1,0:T(8,128)} custom-call(bf16[512,1280]{1,0:T(8,128)(2,1)S(1)} %get-tuple-element.35.near_ref, bf16[512,128]{1,0:T(8,128)(2,1)S(1)} %collective-permute-done.18.first_ref, bf16[512,128]{1,0:T(8,128)(2,1)S(1)} %collective-permute-done.19.second_ref, f32[512,128]{1,0:T(8,128)S(1)} %shard_map.82.early_ref, ...), custom_call_target="tpu_custom_call" | custom-call | flops 134217728 | bytes 1966080 | tf_op jit(solution)/shard_map/pallas_call | solution.py:28
  61.3 1.8 %collective-permute-done.21.other_ref = f32[512,128]{1,0:T(8,128)} collective-permute-done((f32[512,128]{1,0:T(8,128)}, f32[512,128]{1,0:T(8,128)}, u32[]{:S(2)}, u32[]{:S(2)}) %collective-permute-start.21) | collective-permute-done | bytes 262176 | tf_op jit(solution)/shard_map/ppermute | solution.py:208
  64.0 1.3 %shard_map.84 = (bf16[512,128]{1,0:T(8,128)(2,1)S(1)}, bf16[512,128]{1,0:T(8,128)(2,1)S(1)}) custom-call(bf16[4,128,128]{2,1,0:T(8,128)(2,1)S(1)} %copy-done, bf16[512,128]{1,0:T(8,128)(2,1)S(1)} %get-tuple-element.36.excitation_ref, f32[512,128]{1,0:T(8,128)} %shard_map.83.mine_ref, f32[512,128]{1,0:T(8,128)} %collective-permute-done.21.other_ref, ...), custom_call_target="tpu_custom_call" | custom-call | flops 16777216 | bytes 917504 | tf_op jit(solution)/shard_map/pallas_call | solution.py:28
  65.3 1.2 %collective-permute-start.25 = (bf16[512,128]{1,0:T(8,128)(2,1)S(1)}, bf16[512,128]{1,0:T(8,128)(2,1)S(1)}, u32[]{:S(2)}, u32[]{:S(2)}) collective-permute-start(bf16[512,128]{1,0:T(8,128)(2,1)S(1)} %get-tuple-element.28.before_ref.now_ref), channel_id=1, source_target_pairs={{0,1},{1,2},{2,3},{3,4},{4,5},{5,6},{6,7},{7,0},{8,15},{9,8},{10,9... | collective-permute-start | bytes 393224 | tf_op jit(solution)/shard_map/ppermute | solution.py:214
  66.5 1.5 %collective-permute-start.22 = (bf16[512,128]{1,0:T(8,128)(2,1)S(1)}, bf16[512,128]{1,0:T(8,128)(2,1)S(1)}, u32[]{:S(2)}, u32[]{:S(2)}) collective-permute-start(bf16[512,128]{1,0:T(8,128)(2,1)S(1)} %get-tuple-element.29), channel_id=1, source_target_pairs={{0,16},{1,17},{2,18},{3,19},{4,20},{5,21},{6,22},{7,23},{8,24},{9,... | collective-permute-start | bytes 393224 | tf_op jit(solution)/shard_map/ppermute | solution.py:211
  68.6 3.7 %collective-permute-done.22.now_ref.field_ref = bf16[512,128]{1,0:T(8,128)(2,1)S(1)} collective-permute-done((bf16[512,128]{1,0:T(8,128)(2,1)S(1)}, bf16[512,128]{1,0:T(8,128)(2,1)S(1)}, u32[]{:S(2)}, u32[]{:S(2)}) %collective-permute-start.22) | collective-permute-done | bytes 131104 | tf_op jit(solution)/shard_map/ppermute | solution.py:211
  74.4 1.6 %collective-permute-start.23 = (bf16[512,128]{1,0:T(8,128)(2,1)S(1)}, bf16[512,128]{1,0:T(8,128)(2,1)S(1)}, u32[]{:S(2)}, u32[]{:S(2)}) collective-permute-start(bf16[512,128]{1,0:T(8,128)(2,1)S(1)} %collective-permute-done.22.now_ref.field_ref), channel_id=1, source_target_pairs={{0,1},{1,2},{2,3},{3,4},{4,5},{5,6},{6,7},{7,0},{8,15},{9,8},{10,9... | collective-permute-start | bytes 393224 | tf_op jit(solution)/shard_map/ppermute | solution.py:214
  76.5 1.4 %collective-permute-start.28 = (bf16[512,128]{1,0:T(8,128)(2,1)S(1)}, bf16[512,128]{1,0:T(8,128)(2,1)S(1)}, u32[]{:S(2)}, u32[]{:S(2)}) collective-permute-start(bf16[512,128]{1,0:T(8,128)(2,1)S(1)} %add_convert_fusion), channel_id=1, source_target_pairs={{0,16},{1,17},{2,18},{3,19},{4,20},{5,21},{6,22},{7,23},{8,24},{9,... | collective-permute-start | bytes 393224 | tf_op jit(solution)/shard_map/ppermute | solution.py:211
  78.6 4.3 %collective-permute-done.23.first_ref = bf16[512,128]{1,0:T(8,128)(2,1)S(1)} collective-permute-done((bf16[512,128]{1,0:T(8,128)(2,1)S(1)}, bf16[512,128]{1,0:T(8,128)(2,1)S(1)}, u32[]{:S(2)}, u32[]{:S(2)}) %collective-permute-start.23) | collective-permute-done | bytes 131104 | tf_op jit(solution)/shard_map/ppermute | solution.py:214
  84.4 1.4 %collective-permute-done.29 = f32[512,128]{1,0:T(8,128)S(1)} collective-permute-done((f32[512,128]{1,0:T(8,128)S(1)}, f32[512,128]{1,0:T(8,128)S(1)}, u32[]{:S(2)}, u32[]{:S(2)}) %collective-permute-start.29) | collective-permute-done | bytes 262176 | tf_op jit(solution)/shard_map/ppermute | solution.py:208
  (82 shorter events, 18.4 us)
Async XLA Ops:
  0.6 1.9 %collective-permute-start = (f32[512,128]{1,0:T(8,128)}, f32[512,128]{1,0:T(8,128)S(1)}, u32[]{:S(2)}, u32[]{:S(2)}) collective-permute-start(f32[512,128]{1,0:T(8,128)} %bitcast.33), channel_id=1, source_target_pairs={{0,8},{1,9},{2,10},{3,11},{4,12},{5,13},{6,14},{7,15},{8,0},{9,1},... | collective-permute-start | bytes 786440 | tf_op jit(solution)/shard_map/ppermute | solution.py:208
  5.5 6.2 %collective-permute-start.1 = (bf16[512,1280]{1,0:T(8,128)(2,1)S(1)}, bf16[512,1280]{1,0:T(8,128)(2,1)S(1)}, u32[]{:S(2)}, u32[]{:S(2)}) collective-permute-start(bf16[512,1280]{1,0:T(8,128)(2,1)S(1)} %get-tuple-element.19), channel_id=1, source_target_pairs={{0,8},{1,9},{2,10},{3,11},{4,12},{5,13},{6,14},{7,15},{8,0},{9,1},... | collective-permute-start | bytes 3932168 | tf_op jit(solution)/shard_map/ppermute | solution.py:208
  5.6 10.1 %collective-permute-start.2 = (bf16[512,128]{1,0:T(8,128)(2,1)S(1)}, bf16[512,128]{1,0:T(8,128)(2,1)S(1)}, u32[]{:S(2)}, u32[]{:S(2)}) collective-permute-start(bf16[512,128]{1,0:T(8,128)(2,1)S(1)} %shard_map.68.after_ref.now_ref.before_ref), channel_id=1, source_target_pairs={{0,1},{1,2},{2,3},{3,4},{4,5},{5,6},{6,7},{7,0},{8,15},{9,8},{10,9... | collective-permute-start | bytes 393224 | tf_op jit(solution)/shard_map/ppermute | solution.py:214
  8.6 8.2 %collective-permute-start.3 = (bf16[512,128]{1,0:T(8,128)(2,1)S(1)}, bf16[512,128]{1,0:T(8,128)(2,1)S(1)}, u32[]{:S(2)}, u32[]{:S(2)}) collective-permute-start(bf16[512,128]{1,0:T(8,128)(2,1)S(1)} %shard_map.68.after_ref.now_ref.before_ref), channel_id=1, source_target_pairs={{0,2},{1,3},{2,4},{3,5},{4,6},{5,7},{6,0},{7,1},{8,14},{9,15},{10,... | collective-permute-start | bytes 393224 | tf_op jit(solution)/shard_map/ppermute | solution.py:214
  10.2 6.6 %collective-permute-start.4 = (bf16[512,128]{1,0:T(8,128)(2,1)S(1)}, bf16[512,128]{1,0:T(8,128)(2,1)S(1)}, u32[]{:S(2)}, u32[]{:S(2)}) collective-permute-start(bf16[512,128]{1,0:T(8,128)(2,1)S(1)} %shard_map.68.after_ref.now_ref.before_ref), channel_id=1, source_target_pairs={{0,16},{1,17},{2,18},{3,19},{4,20},{5,21},{6,22},{7,23},{8,24},{9,... | collective-permute-start | bytes 393224 | tf_op jit(solution)/shard_map/ppermute | solution.py:211
  17.2 1.6 %collective-permute-start.5 = (f32[512,128]{1,0:T(8,128)S(1)}, f32[512,128]{1,0:T(8,128)S(1)}, u32[]{:S(2)}, u32[]{:S(2)}) collective-permute-start(f32[512,128]{1,0:T(8,128)S(1)} %shard_map.71.mine_ref), channel_id=1, source_target_pairs={{0,8},{1,9},{2,10},{3,11},{4,12},{5,13},{6,14},{7,15},{8,0},{9,1},... | collective-permute-start | bytes 786440 | tf_op jit(solution)/shard_map/ppermute | solution.py:208
  19.0 8.4 %collective-permute-start.6 = (bf16[512,128]{1,0:T(8,128)(2,1)S(1)}, bf16[512,128]{1,0:T(8,128)(2,1)S(1)}, u32[]{:S(2)}, u32[]{:S(2)}) collective-permute-start(bf16[512,128]{1,0:T(8,128)(2,1)S(1)} %get-tuple-element.20.now_ref.before_ref), channel_id=1, source_target_pairs={{0,1},{1,2},{2,3},{3,4},{4,5},{5,6},{6,7},{7,0},{8,15},{9,8},{10,9... | collective-permute-start | bytes 393224 | tf_op jit(solution)/shard_map/ppermute | solution.py:214
  20.0 7.5 %collective-permute-start.7 = (bf16[512,128]{1,0:T(8,128)(2,1)S(1)}, bf16[512,128]{1,0:T(8,128)(2,1)S(1)}, u32[]{:S(2)}, u32[]{:S(2)}) collective-permute-start(bf16[512,128]{1,0:T(8,128)(2,1)S(1)} %get-tuple-element.20.now_ref.before_ref), channel_id=1, source_target_pairs={{0,2},{1,3},{2,4},{3,5},{4,6},{5,7},{6,0},{7,1},{8,14},{9,15},{10,... | collective-permute-start | bytes 393224 | tf_op jit(solution)/shard_map/ppermute | solution.py:214
  20.5 7.0 %collective-permute-start.8 = (bf16[512,128]{1,0:T(8,128)(2,1)S(1)}, bf16[512,128]{1,0:T(8,128)(2,1)S(1)}, u32[]{:S(2)}, u32[]{:S(2)}) collective-permute-start(bf16[512,128]{1,0:T(8,128)(2,1)S(1)} %get-tuple-element.21), channel_id=1, source_target_pairs={{0,16},{1,17},{2,18},{3,19},{4,20},{5,21},{6,22},{7,23},{8,24},{9,... | collective-permute-start | bytes 393224 | tf_op jit(solution)/shard_map/ppermute | solution.py:211
  28.0 1.6 %collective-permute-start.9 = (f32[512,128]{1,0:T(8,128)S(1)}, f32[512,128]{1,0:T(8,128)S(1)}, u32[]{:S(2)}, u32[]{:S(2)}) collective-permute-start(f32[512,128]{1,0:T(8,128)S(1)} %shard_map.74.mine_ref), channel_id=1, source_target_pairs={{0,8},{1,9},{2,10},{3,11},{4,12},{5,13},{6,14},{7,15},{8,0},{9,1},... | collective-permute-start | bytes 786440 | tf_op jit(solution)/shard_map/ppermute | solution.py:208
  29.8 7.7 %collective-permute-start.10 = (bf16[512,128]{1,0:T(8,128)(2,1)S(1)}, bf16[512,128]{1,0:T(8,128)(2,1)S(1)}, u32[]{:S(2)}, u32[]{:S(2)}) collective-permute-start(bf16[512,128]{1,0:T(8,128)(2,1)S(1)} %get-tuple-element.22.now_ref.before_ref), channel_id=1, source_target_pairs={{0,1},{1,2},{2,3},{3,4},{4,5},{5,6},{6,7},{7,0},{8,15},{9,8},{10,9... | collective-permute-start | bytes 393224 | tf_op jit(solution)/shard_map/ppermute | solution.py:214
  31.7 7.0 %collective-permute-start.11 = (bf16[512,128]{1,0:T(8,128)(2,1)S(1)}, bf16[512,128]{1,0:T(8,128)(2,1)S(1)}, u32[]{:S(2)}, u32[]{:S(2)}) collective-permute-start(bf16[512,128]{1,0:T(8,128)(2,1)S(1)} %get-tuple-element.22.now_ref.before_ref), channel_id=1, source_target_pairs={{0,2},{1,3},{2,4},{3,5},{4,6},{5,7},{6,0},{7,1},{8,14},{9,15},{10,... | collective-permute-start | bytes 393224 | tf_op jit(solution)/shard_map/ppermute | solution.py:214
  32.1 6.5 %collective-permute-start.12 = (bf16[512,128]{1,0:T(8,128)(2,1)S(1)}, bf16[512,128]{1,0:T(8,128)(2,1)S(1)}, u32[]{:S(2)}, u32[]{:S(2)}) collective-permute-start(bf16[512,128]{1,0:T(8,128)(2,1)S(1)} %get-tuple-element.23), channel_id=1, source_target_pairs={{0,16},{1,17},{2,18},{3,19},{4,20},{5,21},{6,22},{7,23},{8,24},{9,... | collective-permute-start | bytes 393224 | tf_op jit(solution)/shard_map/ppermute | solution.py:211
  39.1 1.6 %collective-permute-start.13 = (f32[512,128]{1,0:T(8,128)S(1)}, f32[512,128]{1,0:T(8,128)S(1)}, u32[]{:S(2)}, u32[]{:S(2)}) collective-permute-start(f32[512,128]{1,0:T(8,128)S(1)} %shard_map.77.mine_ref), channel_id=1, source_target_pairs={{0,8},{1,9},{2,10},{3,11},{4,12},{5,13},{6,14},{7,15},{8,0},{9,1},... | collective-permute-start | bytes 786440 | tf_op jit(solution)/shard_map/ppermute | solution.py:208
  40.9 7.7 %collective-permute-start.14 = (bf16[512,128]{1,0:T(8,128)(2,1)S(1)}, bf16[512,128]{1,0:T(8,128)(2,1)S(1)}, u32[]{:S(2)}, u32[]{:S(2)}) collective-permute-start(bf16[512,128]{1,0:T(8,128)(2,1)S(1)} %get-tuple-element.24.now_ref.before_ref), channel_id=1, source_target_pairs={{0,1},{1,2},{2,3},{3,4},{4,5},{5,6},{6,7},{7,0},{8,15},{9,8},{10,9... | collective-permute-start | bytes 393224 | tf_op jit(solution)/shard_map/ppermute | solution.py:214
  41.7 7.2 %collective-permute-start.15 = (bf16[512,128]{1,0:T(8,128)(2,1)S(1)}, bf16[512,128]{1,0:T(8,128)(2,1)S(1)}, u32[]{:S(2)}, u32[]{:S(2)}) collective-permute-start(bf16[512,128]{1,0:T(8,128)(2,1)S(1)} %get-tuple-element.24.now_ref.before_ref), channel_id=1, source_target_pairs={{0,2},{1,3},{2,4},{3,5},{4,6},{5,7},{6,0},{7,1},{8,14},{9,15},{10,... | collective-permute-start | bytes 393224 | tf_op jit(solution)/shard_map/ppermute | solution.py:214
  41.8 7.1 %collective-permute-start.16 = (bf16[512,128]{1,0:T(8,128)(2,1)S(1)}, bf16[512,128]{1,0:T(8,128)(2,1)S(1)}, u32[]{:S(2)}, u32[]{:S(2)}) collective-permute-start(bf16[512,128]{1,0:T(8,128)(2,1)S(1)} %get-tuple-element.25), channel_id=1, source_target_pairs={{0,16},{1,17},{2,18},{3,19},{4,20},{5,21},{6,22},{7,23},{8,24},{9,... | collective-permute-start | bytes 393224 | tf_op jit(solution)/shard_map/ppermute | solution.py:211
  49.4 1.6 %collective-permute-start.17 = (f32[512,128]{1,0:T(8,128)S(1)}, f32[512,128]{1,0:T(8,128)S(1)}, u32[]{:S(2)}, u32[]{:S(2)}) collective-permute-start(f32[512,128]{1,0:T(8,128)S(1)} %shard_map.80.mine_ref), channel_id=1, source_target_pairs={{0,8},{1,9},{2,10},{3,11},{4,12},{5,13},{6,14},{7,15},{8,0},{9,1},... | collective-permute-start | bytes 786440 | tf_op jit(solution)/shard_map/ppermute | solution.py:208
  51.2 8.0 %collective-permute-start.18 = (bf16[512,128]{1,0:T(8,128)(2,1)S(1)}, bf16[512,128]{1,0:T(8,128)(2,1)S(1)}, u32[]{:S(2)}, u32[]{:S(2)}) collective-permute-start(bf16[512,128]{1,0:T(8,128)(2,1)S(1)} %get-tuple-element.26.now_ref.before_ref), channel_id=1, source_target_pairs={{0,1},{1,2},{2,3},{3,4},{4,5},{5,6},{6,7},{7,0},{8,15},{9,8},{10,9... | collective-permute-start | bytes 393224 | tf_op jit(solution)/shard_map/ppermute | solution.py:214
  52.9 7.1 %collective-permute-start.19 = (bf16[512,128]{1,0:T(8,128)(2,1)S(1)}, bf16[512,128]{1,0:T(8,128)(2,1)S(1)}, u32[]{:S(2)}, u32[]{:S(2)}) collective-permute-start(bf16[512,128]{1,0:T(8,128)(2,1)S(1)} %get-tuple-element.26.now_ref.before_ref), channel_id=1, source_target_pairs={{0,2},{1,3},{2,4},{3,5},{4,6},{5,7},{6,0},{7,1},{8,14},{9,15},{10,... | collective-permute-start | bytes 393224 | tf_op jit(solution)/shard_map/ppermute | solution.py:214
  53.3 6.7 %collective-permute-start.20 = (bf16[512,128]{1,0:T(8,128)(2,1)S(1)}, bf16[512,128]{1,0:T(8,128)(2,1)S(1)}, u32[]{:S(2)}, u32[]{:S(2)}) collective-permute-start(bf16[512,128]{1,0:T(8,128)(2,1)S(1)} %get-tuple-element.27), channel_id=1, source_target_pairs={{0,16},{1,17},{2,18},{3,19},{4,20},{5,21},{6,22},{7,23},{8,24},{9,... | collective-permute-start | bytes 393224 | tf_op jit(solution)/shard_map/ppermute | solution.py:211
  61.2 1.9 %collective-permute-start.21 = (f32[512,128]{1,0:T(8,128)}, f32[512,128]{1,0:T(8,128)}, u32[]{:S(2)}, u32[]{:S(2)}) collective-permute-start(f32[512,128]{1,0:T(8,128)} %shard_map.83.mine_ref), channel_id=1, source_target_pairs={{0,8},{1,9},{2,10},{3,11},{4,12},{5,13},{6,14},{7,15},{8,0},{9,1},... | collective-permute-start | bytes 786440 | tf_op jit(solution)/shard_map/ppermute | solution.py:208
  64.0 4.0 %copy-start.5 = (bf16[512,128]{1,0:T(8,128)(2,1)S(1)}, bf16[512,128]{1,0:T(8,128)(2,1)}, u32[]{:S(2)}) copy-start(bf16[512,128]{1,0:T(8,128)(2,1)} %copy-done.4) | copy-start | bytes 393220
  64.0 4.0 %copy-start.7 = (bf16[512,128]{1,0:T(8,128)(2,1)S(1)}, bf16[512,128]{1,0:T(8,128)(2,1)}, u32[]{:S(2)}) copy-start(bf16[512,128]{1,0:T(8,128)(2,1)} %copy-done.6) | copy-start | bytes 393220
  65.3 7.7 %collective-permute-start.25 = (bf16[512,128]{1,0:T(8,128)(2,1)S(1)}, bf16[512,128]{1,0:T(8,128)(2,1)S(1)}, u32[]{:S(2)}, u32[]{:S(2)}) collective-permute-start(bf16[512,128]{1,0:T(8,128)(2,1)S(1)} %get-tuple-element.28.before_ref.now_ref), channel_id=1, source_target_pairs={{0,1},{1,2},{2,3},{3,4},{4,5},{5,6},{6,7},{7,0},{8,15},{9,8},{10,9... | collective-permute-start | bytes 393224 | tf_op jit(solution)/shard_map/ppermute | solution.py:214
  66.5 7.0 %collective-permute-start.26 = (bf16[512,128]{1,0:T(8,128)(2,1)S(1)}, bf16[512,128]{1,0:T(8,128)(2,1)S(1)}, u32[]{:S(2)}, u32[]{:S(2)}) collective-permute-start(bf16[512,128]{1,0:T(8,128)(2,1)S(1)} %get-tuple-element.28.before_ref.now_ref), channel_id=1, source_target_pairs={{0,2},{1,3},{2,4},{3,5},{4,6},{5,7},{6,0},{7,1},{8,14},{9,15},{10,... | collective-permute-start | bytes 393224 | tf_op jit(solution)/shard_map/ppermute | solution.py:214
  66.5 5.8 %collective-permute-start.22 = (bf16[512,128]{1,0:T(8,128)(2,1)S(1)}, bf16[512,128]{1,0:T(8,128)(2,1)S(1)}, u32[]{:S(2)}, u32[]{:S(2)}) collective-permute-start(bf16[512,128]{1,0:T(8,128)(2,1)S(1)} %get-tuple-element.29), channel_id=1, source_target_pairs={{0,16},{1,17},{2,18},{3,19},{4,20},{5,21},{6,22},{7,23},{8,24},{9,... | collective-permute-start | bytes 393224 | tf_op jit(solution)/shard_map/ppermute | solution.py:211
  74.2 2.3 %collective-permute-start.27 = (f32[512,128]{1,0:T(8,128)S(1)}, f32[512,128]{1,0:T(8,128)S(1)}, u32[]{:S(2)}, u32[]{:S(2)}) collective-permute-start(f32[512,128]{1,0:T(8,128)S(1)} %get-tuple-element.31), channel_id=1, source_target_pairs={{0,8},{1,9},{2,10},{3,11},{4,12},{5,13},{6,14},{7,15},{8,0},{9,1},... | collective-permute-start | bytes 786440 | tf_op jit(solution)/shard_map/ppermute | solution.py:208
  74.4 8.5 %collective-permute-start.23 = (bf16[512,128]{1,0:T(8,128)(2,1)S(1)}, bf16[512,128]{1,0:T(8,128)(2,1)S(1)}, u32[]{:S(2)}, u32[]{:S(2)}) collective-permute-start(bf16[512,128]{1,0:T(8,128)(2,1)S(1)} %collective-permute-done.22.now_ref.field_ref), channel_id=1, source_target_pairs={{0,1},{1,2},{2,3},{3,4},{4,5},{5,6},{6,7},{7,0},{8,15},{9,8},{10,9... | collective-permute-start | bytes 393224 | tf_op jit(solution)/shard_map/ppermute | solution.py:214
  76.0 7.4 %collective-permute-start.24 = (bf16[512,128]{1,0:T(8,128)(2,1)S(1)}, bf16[512,128]{1,0:T(8,128)(2,1)S(1)}, u32[]{:S(2)}, u32[]{:S(2)}) collective-permute-start(bf16[512,128]{1,0:T(8,128)(2,1)S(1)} %collective-permute-done.22.now_ref.field_ref), channel_id=1, source_target_pairs={{0,2},{1,3},{2,4},{3,5},{4,6},{5,7},{6,0},{7,1},{8,14},{9,15},{10,... | collective-permute-start | bytes 393224 | tf_op jit(solution)/shard_map/ppermute | solution.py:214
  76.5 6.9 %collective-permute-start.28 = (bf16[512,128]{1,0:T(8,128)(2,1)S(1)}, bf16[512,128]{1,0:T(8,128)(2,1)S(1)}, u32[]{:S(2)}, u32[]{:S(2)}) collective-permute-start(bf16[512,128]{1,0:T(8,128)(2,1)S(1)} %add_convert_fusion), channel_id=1, source_target_pairs={{0,16},{1,17},{2,18},{3,19},{4,20},{5,21},{6,22},{7,23},{8,24},{9,... | collective-permute-start | bytes 393224 | tf_op jit(solution)/shard_map/ppermute | solution.py:211
  84.2 1.6 %collective-permute-start.29 = (f32[512,128]{1,0:T(8,128)S(1)}, f32[512,128]{1,0:T(8,128)S(1)}, u32[]{:S(2)}, u32[]{:S(2)}) collective-permute-start(f32[512,128]{1,0:T(8,128)S(1)} %get-tuple-element.33), channel_id=1, source_target_pairs={{0,8},{1,9},{2,10},{3,11},{4,12},{5,13},{6,14},{7,15},{8,0},{9,1},... | collective-permute-start | bytes 786440 | tf_op jit(solution)/shard_map/ppermute | solution.py:208
  (9 other events, 14.9 us)

commit v3 on v2

v3 whole, which is shorter than its diff:
```python
import functools

import jax
import jax.numpy as jnp
from jax import lax
from jax.experimental import pallas as pl
from jax.experimental.pallas import tpu as pltpu
from jax.sharding import PartitionSpec as P

F32 = jnp.float32
BF16 = jnp.bfloat16
AXES = ("delay", "surface")
VMEM = pl.BlockSpec(memory_space=pltpu.VMEM)
MIB = 1024 * 1024


def dot(a, b):
    return jnp.dot(a, b, preferred_element_type=F32)


def place():
    lag = lax.axis_index("delay")
    return lax.rem(lag, 2), lax.div(lag, 2)


COST = pl.CostEstimate(flops=1, bytes_accessed=1, transcendentals=0)


def call(body, outs, args):
    return pl.pallas_call(
        body,
        out_shape=tuple(outs),
        in_specs=[VMEM] * len(args),
        out_specs=tuple(VMEM for _ in outs),
        cost_estimate=COST,
        compiler_params=pltpu.CompilerParams(vmem_limit_bytes=8 * MIB),
    )(*args)


def choose(*cases):
    *pairs, value = cases
    for when, other in reversed(pairs):
        value = jnp.where(when, other, value)
    return value


def far_next(s, count):
    return choose((s == 0, count - 2), (s == 1, count - 1), (s == count - 1, 0), s - 1)


def far_last(s, count):
    return choose((s == 0, count - 1), (s == count - 2, 0), (s == count - 1, 1), s + 1)


def close_next(s, count):
    even = lax.rem(s, 2) == 0
    return choose((s == 1, 0), (s == count - 2, count - 1), (even, s + 2), s - 2)


def close_last(s, count):
    even = lax.rem(s, 2) == 0
    return choose((s == 0, 1), (s == count - 1, count - 2), (even, s - 2), s + 2)


def tour(far, count):
    if far:
        return [0] + list(range(count - 2, 0, -1)) + [count - 1]
    return list(range(0, count, 2)) + list(range(count - 1, 0, -2))


def spread_body(groups, pattern_ref, entries_ref, out_ref):
    core, _ = place()
    row = pl.program_id(0)
    blocks = pl.num_programs(0)
    slots, size = entries_ref.shape[1], entries_ref.shape[2]
    here = lax.axis_index("surface")
    brought = (
        (far_last(here, groups), 0, 0),
        (close_last(here, groups), 0, blocks),
        (far_next(here, groups), 1, 0),
        (close_next(here, groups), 1, blocks),
    )
    out_ref[...] = jnp.zeros_like(out_ref)
    for slot in range(slots):
        block = pattern_ref[row, slot]
        group = lax.div(block, blocks)
        within = block - group * blocks
        second = within >= blocks // 2
        half = jnp.where(second, 1, 0)
        column = 2 * blocks + jnp.where(second, within - blocks // 2, within)
        for source, side, first in brought:
            half = jnp.where(group == source, side, half)
            column = jnp.where(group == source, first + within, column)
        columns = pl.ds(pl.multiple_of(column * size, size), size)
        out_ref[jnp.where(half == core, 0, 1), :, columns] = entries_ref[0, slot]


def spread(entries, pattern, groups):
    blocks, slots, size, _ = entries.shape
    width = (2 * blocks + blocks // 2) * size
    return pl.pallas_call(
        functools.partial(spread_body, groups),
        grid_spec=pltpu.PrefetchScalarGridSpec(
            num_scalar_prefetch=1,
            grid=(blocks,),
            in_specs=[pl.BlockSpec((1, slots, size, size), lambda i, s: (i, 0, 0, 0))],
            out_specs=pl.BlockSpec((2, size, width), lambda i, s: (0, i, 0)),
        ),
        out_shape=jax.ShapeDtypeStruct((2, blocks * size, width), entries.dtype),
        cost_estimate=COST,
        compiler_params=pltpu.CompilerParams(vmem_limit_bytes=8 * MIB),
    )(pattern, entries)


def own_half(current_ref):
    core, _ = place()
    rows = current_ref.shape[0] // 2
    return current_ref[pl.ds(pl.multiple_of(core * rows, rows), rows), :]


def early_body(near_ref, second_ref, now_ref, *rest):
    *last, out_ref = rest
    rows = now_ref.shape[0]
    total = dot(near_ref[:, rows : 2 * rows], second_ref[...])
    total += dot(near_ref[:, 2 * rows :], own_half(now_ref))
    if last:
        far_ref, first_ref, second_ref, before_ref = last
        total += dot(far_ref[:, :rows], first_ref[...])
        total += dot(far_ref[:, rows : 2 * rows], second_ref[...])
        total += dot(far_ref[:, 2 * rows :], own_half(before_ref))
    out_ref[...] = total


def came(step, pairs, field_ref, history):
    core, pair = place()
    value = 0.0
    if step > 0:
        value = jnp.where(pair == pairs - 1, 0.0, field_ref[...].astype(F32))
    if history:
        odd_ref, even_ref = history
        value = jnp.where(
            pair == step, odd_ref[...], jnp.where(pair == step + 1, even_ref[...], value)
        )
    return jnp.where(core == 0, value, 0.0)


def late_body(step, pairs, near_ref, first_ref, early_ref, field_ref, *rest):
    *history, out_ref = rest
    rows = first_ref.shape[0]
    out_ref[...] = (
        early_ref[...]
        + came(step, pairs, field_ref, history)
        + dot(near_ref[:, :rows], first_ref[...])
    )


def late_final_body(
    step, steps, pairs, near_ref, first_ref, early_ref, field_ref, far_ref, second_ref, now_ref, *rest
):
    *history, keep_ref, send_ref = rest
    core, pair = place()
    rows = first_ref.shape[0]
    even = (
        early_ref[...]
        + came(step, pairs, field_ref, history)
        + dot(near_ref[:, :rows], first_ref[...])
    )
    odd = (
        dot(far_ref[:, :rows], first_ref[...])
        + dot(far_ref[:, rows : 2 * rows], second_ref[...])
        + dot(far_ref[:, 2 * rows :], own_half(now_ref))
    )
    ends = pair == step - (steps - 1)
    keep_ref[...] = jnp.where(jnp.logical_and(ends, core == 1), odd, even)
    send_ref[...] = jnp.where(jnp.logical_and(ends, core == 0), odd, even)


def solve(inverse_ref, rhs, out_ref, keep, other):
    size = inverse_ref.shape[1]
    fresh = []
    for i in range(inverse_ref.shape[0]):
        rows = slice(i * size, (i + 1) * size)
        block = dot(inverse_ref[i], rhs[rows]).astype(BF16)
        fresh.append(jnp.where(keep, block, other[rows]))
        out_ref[rows, :] = fresh[-1]
    return fresh


def start_body(inverse_ref, excitation_ref, history_ref, out_ref):
    _, pair = place()
    rhs = (excitation_ref[0].astype(F32) - history_ref[...]).astype(BF16)
    solve(inverse_ref, rhs, out_ref, pair == 0, jnp.zeros_like(rhs))


def next_body(step, pairs, inverse_ref, excitation_ref, mine_ref, other_ref, came_ref, out_ref, field_ref):
    _, pair = place()
    field = mine_ref[...] + other_ref[...]
    rhs = (excitation_ref[step + 1].astype(F32) - field).astype(BF16)
    first_pair = pair == 0
    fresh = solve(inverse_ref, rhs, out_ref, first_pair, came_ref)
    if pairs == 2:
        size = inverse_ref.shape[1]
        for i, block in enumerate(fresh):
            rows = slice(i * size, (i + 1) * size)
            field_ref[rows, :] = jnp.where(first_pair, block, field[rows].astype(BF16))
    else:
        field_ref[...] = field.astype(BF16)


def per_device(lagged_block_entries, pattern, diagonal_block_inverses, excitation, history):
    lags, groups = lax.axis_size("delay"), lax.axis_size("surface")
    core, pair = place()
    pairs = lags // 2
    entries = lagged_block_entries[0]
    blocks, slots, size, _ = entries.shape
    steps, rows, columns = excitation.shape

    def device(d, s):
        return d * groups + s

    def everyone(move):
        return [
            (device(d, s), device(*move(d, s))) for d in range(lags) for s in range(groups)
        ]

    def swapped(value):
        return lax.ppermute(value, AXES, everyone(lambda d, s: (d ^ 1, s)))

    def pair_moved(value, hop):
        return lax.ppermute(value, AXES, everyone(lambda d, s: ((d + 2 * hop) % lags, s)))

    def halo(value, far):
        order = tour(far, groups)
        following = dict(zip(order, order[1:] + order[:1]))
        preceding = {t: s for s, t in following.items()}
        return lax.ppermute(
            value,
            AXES,
            everyone(lambda d, s: (d, following[s] if d % 2 == 0 else preceding[s])),
        )

    other_history = swapped(history[0])
    even_history = jnp.where(core == 0, history[0], other_history)
    odd_history = jnp.where(core == 0, other_history, history[0])

    field_shape = jax.ShapeDtypeStruct((rows, columns), F32)
    current_shape = jax.ShapeDtypeStruct((rows, columns), BF16)
    (current,) = call(
        start_body, [current_shape], [diagonal_block_inverses, excitation, even_history]
    )
    both = spread(entries, pattern[0], groups)
    kept, got = both[0], swapped(both[1])
    near = jnp.where(core == 0, kept, got)
    far = jnp.where(core == 0, got, kept)

    going = current
    seen = []
    previous = None
    result = jnp.zeros((rows, columns), F32)
    for step in range(steps + pairs - 1):
        seen.append(current)
        first, second = halo(current, True), halo(current, False)
        if pairs == 2:
            current_in = field_in = pair_moved(going, 1)
        else:
            current_in, field_in = pair_moved(current, 1), pair_moved(going, -1)
        last = [far, *previous] if previous else []
        (early,) = call(early_body, [field_shape], [near, second, current] + last)
        received = [near, first, early, field_in]
        extra = [odd_history, even_history] if step < pairs else []
        previous = (first, second, current)
        if step < steps - 1:
            (mine,) = call(
                functools.partial(late_body, step, pairs), [field_shape], received + extra
            )
            current, going = call(
                functools.partial(next_body, step, pairs),
                [current_shape, current_shape],
                [diagonal_block_inverses, excitation, mine, swapped(mine), current_in],
            )
        else:
            mine, send = call(
                functools.partial(late_final_body, step, steps, pairs),
                [field_shape, field_shape],
                received + [far, second, current] + extra,
            )
            field = mine + swapped(send)
            last_in = jnp.where(pair == pairs - 1, 0.0, field_in.astype(F32))
            result = jnp.where(pair == step - (steps - 1), field, result)
            result = jnp.where((core == 1) & (pair == step - steps), result + last_in, result)
            current, going = current_in, field.astype(BF16)
    out = []
    for step in range(steps):
        value = seen[step]
        for later in range(1, pairs):
            value = jnp.where(pair == later, seen[step + later], value)
        out.append(value)
    return (jnp.stack(out), result[None])


def solution(mesh):
    placed = (
        P("delay", "surface", None, None, None),
        P("delay", "surface", None),
        P("surface", None, None),
        P(None, "surface", None),
        P("delay", "surface", None),
    )
    return jax.shard_map(
        per_device,
        mesh=mesh,
        in_specs=placed,
        out_specs=(P(None, "surface", None), P("delay", "surface", None)),
        check_vma=False,
    )
```

time: 86.8 us -> 92.4 us (1.065)
  starting transfers between devices: 26.3 us -> 32.2 us
  waiting for transfers between devices: 42.7 us -> 37.6 us
  other arithmetic: 1.38 us -> 4.06 us
  local copies, waits for them, and re-layouts: 2.68 us -> 5.25 us
    ppermute x14, starting transfers between devices: 14.7 us -> 20.6 us  [halo(): lax.ppermute(value, AXES, everyone(lambda d, s: (d, following[s] if d % 2...]
    ppermute x14, waiting for transfers between devices: 29.8 us -> 25 us  [halo(): lax.ppermute(value, AXES, everyone(lambda d, s: (d, following[s] if d % 2...]
    ppermute x7, waiting for transfers between devices: 3.7 us -> 0.32 us  [pair_moved(): lax.ppermute(value, AXES, everyone(lambda d, s: ((d + 2 * hop) % lags, s)))]
    ppermute x9, waiting for transfers between devices: 9.24 us -> 12.3 us  [swapped(): return lax.ppermute(value, AXES, everyone(lambda d, s: (d ^ 1, s)))]
    unnamed x22 -> x44, local copies, waits for them, and re-layouts: 1.28 us -> 4.07 us
    select_n x1, other arithmetic: 0.17 us -> 1.88 us  [per_device(): far = jnp.where(core == 0, got, kept)]
    select_n x1, other arithmetic: 0.04 us -> 0.99 us  [per_device(): odd_history = jnp.where(core == 0, other_history, history[0])]
  transfers between devices with their start and end apart: 30 -> 30, of which waited for: 21 -> 20; matrix products, arithmetic and copies ran while one was open for 2% -> 4% of each run, Pallas kernels for 4% -> 5%
where the time goes in v3:
time: 92.4 us; the launch traced here: 92.1 us
  waiting for transfers between devices  37.6 us (41%)
  starting transfers between devices  32.2 us (35%)
  Pallas kernels  11.9 us (13%)
  local copies, waits for them, and re-layouts  5.25 us (6%)
  other arithmetic  4.06 us (4%)
  between operations  1.06 us (1%)
    ppermute x14, waiting for transfers between devices, halo(): lax.ppermute(value, AXES, everyone(lambda d, s: (d, following[s] if d % 2...  25 us
    ppermute x14, starting transfers between devices, halo(): lax.ppermute(value, AXES, everyone(lambda d, s: (d, following[s] if d % 2...  20.6 us
    ppermute x9, waiting for transfers between devices, swapped(): return lax.ppermute(value, AXES, everyone(lambda d, s: (d ^ 1, s)))  12.3 us
    ppermute x7, starting transfers between devices, pair_moved(): lax.ppermute(value, AXES, everyone(lambda d, s: ((d + 2 * hop) % lags, s)))  10.5 us
    pallas_call x20, Pallas kernels, call(): pl.pallas_call(body, out_shape=tuple(outs), in_specs=[VMEM] * len(args),...  10.3 us
    unnamed x44, local copies, waits for them, and re-layouts  4.07 us
    select_n x1, other arithmetic, per_device(): far = jnp.where(core == 0, got, kept)  1.88 us
  transfers between devices with their start and end apart: 30, of which 20 were waited for; matrix products, arithmetic and copies ran while one was open for 4% of the time, Pallas kernels for 5%

profile of v3, /device:TPU:0, one launch (start us, length us, event | category | flops | bytes accessed | tf_op | source)
XLA Modules:
  0.0 92.1 jit_solution(1387797012642281115)
XLA Ops:
  0.6 1.6 %copy-done.13 = bf16[1,4,16,128,128]{4,3,2,1,0:T(8,128)(2,1)S(1)} copy-done((bf16[1,4,16,128,128]{4,3,2,1,0:T(8,128)(2,1)S(1)}, bf16[1,4,16,128,128]{4,3,2,1,0:T(8,128)(2,1)}, u32[]{:S(2)}) %copy-start.13) | copy-done | bytes 2097176
  2.9 1.7 %shard_map.68 = bf16[2,512,1280]{2,1,0:T(8,128)(2,1)S(1)} custom-call(s32[4,16]{1,0:T(4,128)S(1)} %bitcast.28, bf16[4,16,128,128]{3,2,1,0:T(8,128)(2,1)S(1)} %bitcast.27), custom_call_target="tpu_custom_call" | custom-call | flops 1 | bytes 1 | tf_op jit(solution)/shard_map/pallas_call | solution.py:101
  7.0 3.1 %collective-permute-done.1 = f32[512,128]{1,0:T(8,128)S(1)} collective-permute-done((f32[512,128]{1,0:T(8,128)}, f32[512,128]{1,0:T(8,128)S(1)}, u32[]{:S(2)}, u32[]{:S(2)}) %collective-permute-start.1) | collective-permute-done | bytes 262176 | tf_op jit(solution)/shard_map/ppermute | solution.py:227
  11.3 2.7 %collective-permute-start.3 = (bf16[512,128]{1,0:T(8,128)(2,1)S(1)}, bf16[512,128]{1,0:T(8,128)(2,1)S(1)}, u32[]{:S(2)}, u32[]{:S(2)}) collective-permute-start(bf16[512,128]{1,0:T(8,128)(2,1)S(1)} %shard_map.69.now_ref.rest_3_), channel_id=1, source_target_pairs={{0,2},{1,0},{2,4},{3,1},{4,6},{5,3},{6,7},{7,5},{8,9},{9,11},{10,8... | collective-permute-start | bytes 393224 | tf_op jit(solution)/shard_map/ppermute | solution.py:236
  14.0 3.5 %collective-permute-start.2 = (bf16[512,128]{1,0:T(8,128)(2,1)S(1)}, bf16[512,128]{1,0:T(8,128)(2,1)S(1)}, u32[]{:S(2)}, u32[]{:S(2)}) collective-permute-start(bf16[512,128]{1,0:T(8,128)(2,1)S(1)} %shard_map.69.now_ref.rest_3_), channel_id=1, source_target_pairs={{0,6},{1,7},{2,1},{3,2},{4,3},{5,4},{6,5},{7,0},{8,15},{9,10},{10,... | collective-permute-start | bytes 393224 | tf_op jit(solution)/shard_map/ppermute | solution.py:236
  17.5 1.5 %collective-permute-start.4 = (bf16[512,128]{1,0:T(8,128)(2,1)S(1)}, bf16[512,128]{1,0:T(8,128)(2,1)S(1)}, u32[]{:S(2)}, u32[]{:S(2)}) collective-permute-start(bf16[512,128]{1,0:T(8,128)(2,1)S(1)} %shard_map.69.now_ref.rest_3_), channel_id=1, source_target_pairs={{0,16},{1,17},{2,18},{3,19},{4,20},{5,21},{6,22},{7,23},{8,24},{9,... | collective-permute-start | bytes 393224 | tf_op jit(solution)/shard_map/ppermute | solution.py:230
  19.0 1.9 %broadcast_select_fusion = (bf16[512,1280]{1,0:T(8,128)(2,1)S(1)}, bf16[512,1280]{1,0:T(8,128)(2,1)S(1)}) fusion(bf16[512,1280]{1,0:T(8,128)(2,1)} %collective-permute-done, pred[]{:T(512)S(6)} %eq.11, bf16[2,512,1280]{2,1,0:T(8,128)(2,1)} %copy-done.1), kind=kLoop, calls=%fused_computation.2 | loop fusion | flops 1310720 | bytes 5242881 | tf_op jit(solution)/shard_map/jit(_where)/select_n | solution.py:254
  21.3 1.9 %collective-permute-done.2.first_ref.rest_1_ = bf16[512,128]{1,0:T(8,128)(2,1)S(1)} collective-permute-done((bf16[512,128]{1,0:T(8,128)(2,1)S(1)}, bf16[512,128]{1,0:T(8,128)(2,1)S(1)}, u32[]{:S(2)}, u32[]{:S(2)}) %collective-permute-start.2) | collective-permute-done | bytes 131104 | tf_op jit(solution)/shard_map/ppermute | solution.py:236
  23.6 1.5 %collective-permute-done.5.other_ref = f32[512,128]{1,0:T(8,128)S(1)} collective-permute-done((f32[512,128]{1,0:T(8,128)S(1)}, f32[512,128]{1,0:T(8,128)S(1)}, u32[]{:S(2)}, u32[]{:S(2)}) %collective-permute-start.5) | collective-permute-done | bytes 262176 | tf_op jit(solution)/shard_map/ppermute | solution.py:227
  25.4 1.7 %collective-permute-start.6 = (bf16[512,128]{1,0:T(8,128)(2,1)S(1)}, bf16[512,128]{1,0:T(8,128)(2,1)S(1)}, u32[]{:S(2)}, u32[]{:S(2)}) collective-permute-start(bf16[512,128]{1,0:T(8,128)(2,1)S(1)} %get-tuple-element.16.now_ref.rest_3_), channel_id=1, source_target_pairs={{0,6},{1,7},{2,1},{3,2},{4,3},{5,4},{6,5},{7,0},{8,15},{9,10},{10,... | collective-permute-start | bytes 393224 | tf_op jit(solution)/shard_map/ppermute | solution.py:236
  27.0 1.5 %collective-permute-start.8 = (bf16[512,128]{1,0:T(8,128)(2,1)S(1)}, bf16[512,128]{1,0:T(8,128)(2,1)S(1)}, u32[]{:S(2)}, u32[]{:S(2)}) collective-permute-start(bf16[512,128]{1,0:T(8,128)(2,1)S(1)} %get-tuple-element.17), channel_id=1, source_target_pairs={{0,16},{1,17},{2,18},{3,19},{4,20},{5,21},{6,22},{7,23},{8,24},{9,... | collective-permute-start | bytes 393224 | tf_op jit(solution)/shard_map/ppermute | solution.py:230
  28.5 1.8 %collective-permute-done.7.second_ref.rest_2_ = bf16[512,128]{1,0:T(8,128)(2,1)S(1)} collective-permute-done((bf16[512,128]{1,0:T(8,128)(2,1)S(1)}, bf16[512,128]{1,0:T(8,128)(2,1)S(1)}, u32[]{:S(2)}, u32[]{:S(2)}) %collective-permute-start.7) | collective-permute-done | bytes 131104 | tf_op jit(solution)/shard_map/ppermute | solution.py:236
  31.0 2.0 %collective-permute-done.6.first_ref.rest_1_ = bf16[512,128]{1,0:T(8,128)(2,1)S(1)} collective-permute-done((bf16[512,128]{1,0:T(8,128)(2,1)S(1)}, bf16[512,128]{1,0:T(8,128)(2,1)S(1)}, u32[]{:S(2)}, u32[]{:S(2)}) %collective-permute-start.6) | collective-permute-done | bytes 131104 | tf_op jit(solution)/shard_map/ppermute | solution.py:236
  33.9 1.4 %collective-permute-done.9.other_ref = f32[512,128]{1,0:T(8,128)S(1)} collective-permute-done((f32[512,128]{1,0:T(8,128)S(1)}, f32[512,128]{1,0:T(8,128)S(1)}, u32[]{:S(2)}, u32[]{:S(2)}) %collective-permute-start.9) | collective-permute-done | bytes 262176 | tf_op jit(solution)/shard_map/ppermute | solution.py:227
  36.0 2.3 %collective-permute-start.10 = (bf16[512,128]{1,0:T(8,128)(2,1)S(1)}, bf16[512,128]{1,0:T(8,128)(2,1)S(1)}, u32[]{:S(2)}, u32[]{:S(2)}) collective-permute-start(bf16[512,128]{1,0:T(8,128)(2,1)S(1)} %get-tuple-element.18.now_ref.rest_3_), channel_id=1, source_target_pairs={{0,6},{1,7},{2,1},{3,2},{4,3},{5,4},{6,5},{7,0},{8,15},{9,10},{10,... | collective-permute-start | bytes 393224 | tf_op jit(solution)/shard_map/ppermute | solution.py:236
  38.3 1.5 %collective-permute-start.12 = (bf16[512,128]{1,0:T(8,128)(2,1)S(1)}, bf16[512,128]{1,0:T(8,128)(2,1)S(1)}, u32[]{:S(2)}, u32[]{:S(2)}) collective-permute-start(bf16[512,128]{1,0:T(8,128)(2,1)S(1)} %get-tuple-element.19), channel_id=1, source_target_pairs={{0,16},{1,17},{2,18},{3,19},{4,20},{5,21},{6,22},{7,23},{8,24},{9,... | collective-permute-start | bytes 393224 | tf_op jit(solution)/shard_map/ppermute | solution.py:230
  41.2 2.5 %collective-permute-done.10.first_ref.rest_1_ = bf16[512,128]{1,0:T(8,128)(2,1)S(1)} collective-permute-done((bf16[512,128]{1,0:T(8,128)(2,1)S(1)}, bf16[512,128]{1,0:T(8,128)(2,1)S(1)}, u32[]{:S(2)}, u32[]{:S(2)}) %collective-permute-start.10) | collective-permute-done | bytes 131104 | tf_op jit(solution)/shard_map/ppermute | solution.py:236
  44.1 1.5 %collective-permute-done.13.other_ref = f32[512,128]{1,0:T(8,128)S(1)} collective-permute-done((f32[512,128]{1,0:T(8,128)S(1)}, f32[512,128]{1,0:T(8,128)S(1)}, u32[]{:S(2)}, u32[]{:S(2)}) %collective-permute-start.13) | collective-permute-done | bytes 262176 | tf_op jit(solution)/shard_map/ppermute | solution.py:227
  46.2 2.2 %collective-permute-start.14 = (bf16[512,128]{1,0:T(8,128)(2,1)S(1)}, bf16[512,128]{1,0:T(8,128)(2,1)S(1)}, u32[]{:S(2)}, u32[]{:S(2)}) collective-permute-start(bf16[512,128]{1,0:T(8,128)(2,1)S(1)} %get-tuple-element.20.now_ref.rest_3_), channel_id=1, source_target_pairs={{0,6},{1,7},{2,1},{3,2},{4,3},{5,4},{6,5},{7,0},{8,15},{9,10},{10,... | collective-permute-start | bytes 393224 | tf_op jit(solution)/shard_map/ppermute | solution.py:236
  48.4 1.5 %collective-permute-start.16 = (bf16[512,128]{1,0:T(8,128)(2,1)S(1)}, bf16[512,128]{1,0:T(8,128)(2,1)S(1)}, u32[]{:S(2)}, u32[]{:S(2)}) collective-permute-start(bf16[512,128]{1,0:T(8,128)(2,1)S(1)} %get-tuple-element.21), channel_id=1, source_target_pairs={{0,16},{1,17},{2,18},{3,19},{4,20},{5,21},{6,22},{7,23},{8,24},{9,... | collective-permute-start | bytes 393224 | tf_op jit(solution)/shard_map/ppermute | solution.py:230
  51.5 3.0 %collective-permute-done.14.first_ref.rest_1_ = bf16[512,128]{1,0:T(8,128)(2,1)S(1)} collective-permute-done((bf16[512,128]{1,0:T(8,128)(2,1)S(1)}, bf16[512,128]{1,0:T(8,128)(2,1)S(1)}, u32[]{:S(2)}, u32[]{:S(2)}) %collective-permute-start.14) | collective-permute-done | bytes 131104 | tf_op jit(solution)/shard_map/ppermute | solution.py:236
  54.9 1.5 %collective-permute-done.17.other_ref = f32[512,128]{1,0:T(8,128)S(1)} collective-permute-done((f32[512,128]{1,0:T(8,128)S(1)}, f32[512,128]{1,0:T(8,128)S(1)}, u32[]{:S(2)}, u32[]{:S(2)}) %collective-permute-start.17) | collective-permute-done | bytes 262176 | tf_op jit(solution)/shard_map/ppermute | solution.py:227
  56.7 2.4 %collective-permute-start.18 = (bf16[512,128]{1,0:T(8,128)(2,1)S(1)}, bf16[512,128]{1,0:T(8,128)(2,1)S(1)}, u32[]{:S(2)}, u32[]{:S(2)}) collective-permute-start(bf16[512,128]{1,0:T(8,128)(2,1)S(1)} %get-tuple-element.22.now_ref.rest_3_), channel_id=1, source_target_pairs={{0,6},{1,7},{2,1},{3,2},{4,3},{5,4},{6,5},{7,0},{8,15},{9,10},{10,... | collective-permute-start | bytes 393224 | tf_op jit(solution)/shard_map/ppermute | solution.py:236
  59.1 1.5 %collective-permute-start.20 = (bf16[512,128]{1,0:T(8,128)(2,1)S(1)}, bf16[512,128]{1,0:T(8,128)(2,1)S(1)}, u32[]{:S(2)}, u32[]{:S(2)}) collective-permute-start(bf16[512,128]{1,0:T(8,128)(2,1)S(1)} %get-tuple-element.23), channel_id=1, source_target_pairs={{0,16},{1,17},{2,18},{3,19},{4,20},{5,21},{6,22},{7,23},{8,24},{9,... | collective-permute-start | bytes 393224 | tf_op jit(solution)/shard_map/ppermute | solution.py:230
  62.4 2.9 %collective-permute-done.18.first_ref.rest_1_ = bf16[512,128]{1,0:T(8,128)(2,1)S(1)} collective-permute-done((bf16[512,128]{1,0:T(8,128)(2,1)S(1)}, bf16[512,128]{1,0:T(8,128)(2,1)S(1)}, u32[]{:S(2)}, u32[]{:S(2)}) %collective-permute-start.18) | collective-permute-done | bytes 131104 | tf_op jit(solution)/shard_map/ppermute | solution.py:236
  66.3 1.8 %collective-permute-done.21.other_ref = f32[512,128]{1,0:T(8,128)} collective-permute-done((f32[512,128]{1,0:T(8,128)}, f32[512,128]{1,0:T(8,128)}, u32[]{:S(2)}, u32[]{:S(2)}) %collective-permute-start.21) | collective-permute-done | bytes 262176 | tf_op jit(solution)/shard_map/ppermute | solution.py:227
  70.3 1.8 %collective-permute-start.25 = (bf16[512,128]{1,0:T(8,128)(2,1)S(1)}, bf16[512,128]{1,0:T(8,128)(2,1)S(1)}, u32[]{:S(2)}, u32[]{:S(2)}) collective-permute-start(bf16[512,128]{1,0:T(8,128)(2,1)S(1)} %get-tuple-element.24.rest_3_.now_ref), channel_id=1, source_target_pairs={{0,6},{1,7},{2,1},{3,2},{4,3},{5,4},{6,5},{7,0},{8,15},{9,10},{10,... | collective-permute-start | bytes 393224 | tf_op jit(solution)/shard_map/ppermute | solution.py:236
  72.1 1.5 %collective-permute-start.22 = (bf16[512,128]{1,0:T(8,128)(2,1)S(1)}, bf16[512,128]{1,0:T(8,128)(2,1)S(1)}, u32[]{:S(2)}, u32[]{:S(2)}) collective-permute-start(bf16[512,128]{1,0:T(8,128)(2,1)S(1)} %get-tuple-element.25), channel_id=1, source_target_pairs={{0,16},{1,17},{2,18},{3,19},{4,20},{5,21},{6,22},{7,23},{8,24},{9,... | collective-permute-start | bytes 393224 | tf_op jit(solution)/shard_map/ppermute | solution.py:230
  73.6 4.8 %collective-permute-done.26.rest_2_.second_ref = bf16[512,128]{1,0:T(8,128)(2,1)S(1)} collective-permute-done((bf16[512,128]{1,0:T(8,128)(2,1)S(1)}, bf16[512,128]{1,0:T(8,128)(2,1)S(1)}, u32[]{:S(2)}, u32[]{:S(2)}) %collective-permute-start.26) | collective-permute-done | bytes 131104 | tf_op jit(solution)/shard_map/ppermute | solution.py:236
  81.1 2.1 %collective-permute-start.23 = (bf16[512,128]{1,0:T(8,128)(2,1)S(1)}, bf16[512,128]{1,0:T(8,128)(2,1)S(1)}, u32[]{:S(2)}, u32[]{:S(2)}) collective-permute-start(bf16[512,128]{1,0:T(8,128)(2,1)S(1)} %collective-permute-done.22.now_ref.field_ref), channel_id=1, source_target_pairs={{0,6},{1,7},{2,1},{3,2},{4,3},{5,4},{6,5},{7,0},{8,15},{9,10},{10,... | collective-permute-start | bytes 393224 | tf_op jit(solution)/shard_map/ppermute | solution.py:236
  83.2 1.6 %collective-permute-start.28 = (bf16[512,128]{1,0:T(8,128)(2,1)S(1)}, bf16[512,128]{1,0:T(8,128)(2,1)S(1)}, u32[]{:S(2)}, u32[]{:S(2)}) collective-permute-start(bf16[512,128]{1,0:T(8,128)(2,1)S(1)} %add_convert_fusion), channel_id=1, source_target_pairs={{0,16},{1,17},{2,18},{3,19},{4,20},{5,21},{6,22},{7,23},{8,24},{9,... | collective-permute-start | bytes 393224 | tf_op jit(solution)/shard_map/ppermute | solution.py:230
  85.9 3.1 %collective-permute-done.23.first_ref = bf16[512,128]{1,0:T(8,128)(2,1)S(1)} collective-permute-done((bf16[512,128]{1,0:T(8,128)(2,1)S(1)}, bf16[512,128]{1,0:T(8,128)(2,1)S(1)}, u32[]{:S(2)}, u32[]{:S(2)}) %collective-permute-start.23) | collective-permute-done | bytes 131104 | tf_op jit(solution)/shard_map/ppermute | solution.py:236
  (104 shorter events, 24.0 us)
Async XLA Ops:
  6.5 12.6 %collective-permute-start = (bf16[512,1280]{1,0:T(8,128)(2,1)}, bf16[512,1280]{1,0:T(8,128)(2,1)}, u32[]{:S(2)}, u32[]{:S(2)}) collective-permute-start(bf16[512,1280]{1,0:T(8,128)(2,1)} %slice_bitcast_fusion), channel_id=1, source_target_pairs={{0,8},{1,9},{2,10},{3,11},{4,12},{5,13},{6,14},{7,15},{8,0},{9,1},... | collective-permute-start | bytes 3932168 | tf_op jit(solution)/shard_map/ppermute | solution.py:227
  6.9 3.2 %collective-permute-start.1 = (f32[512,128]{1,0:T(8,128)}, f32[512,128]{1,0:T(8,128)S(1)}, u32[]{:S(2)}, u32[]{:S(2)}) collective-permute-start(f32[512,128]{1,0:T(8,128)} %bitcast.4), channel_id=1, source_target_pairs={{0,8},{1,9},{2,10},{3,11},{4,12},{5,13},{6,14},{7,15},{8,0},{9,1},... | collective-permute-start | bytes 786440 | tf_op jit(solution)/shard_map/ppermute | solution.py:227
  11.3 19.0 %copy-start.11 = (bf16[512,128]{1,0:T(8,128)(2,1)}, bf16[512,128]{1,0:T(8,128)(2,1)S(1)}, u32[]{:S(2)}) copy-start(bf16[512,128]{1,0:T(8,128)(2,1)S(1)} %shard_map.69.now_ref.rest_3_) | copy-start | bytes 393220
  11.3 9.6 %collective-permute-start.3 = (bf16[512,128]{1,0:T(8,128)(2,1)S(1)}, bf16[512,128]{1,0:T(8,128)(2,1)S(1)}, u32[]{:S(2)}, u32[]{:S(2)}) collective-permute-start(bf16[512,128]{1,0:T(8,128)(2,1)S(1)} %shard_map.69.now_ref.rest_3_), channel_id=1, source_target_pairs={{0,2},{1,0},{2,4},{3,1},{4,6},{5,3},{6,7},{7,5},{8,9},{9,11},{10,8... | collective-permute-start | bytes 393224 | tf_op jit(solution)/shard_map/ppermute | solution.py:236
  14.0 9.2 %collective-permute-start.2 = (bf16[512,128]{1,0:T(8,128)(2,1)S(1)}, bf16[512,128]{1,0:T(8,128)(2,1)S(1)}, u32[]{:S(2)}, u32[]{:S(2)}) collective-permute-start(bf16[512,128]{1,0:T(8,128)(2,1)S(1)} %shard_map.69.now_ref.rest_3_), channel_id=1, source_target_pairs={{0,6},{1,7},{2,1},{3,2},{4,3},{5,4},{6,5},{7,0},{8,15},{9,10},{10,... | collective-permute-start | bytes 393224 | tf_op jit(solution)/shard_map/ppermute | solution.py:236
  17.5 5.6 %collective-permute-start.4 = (bf16[512,128]{1,0:T(8,128)(2,1)S(1)}, bf16[512,128]{1,0:T(8,128)(2,1)S(1)}, u32[]{:S(2)}, u32[]{:S(2)}) collective-permute-start(bf16[512,128]{1,0:T(8,128)(2,1)S(1)} %shard_map.69.now_ref.rest_3_), channel_id=1, source_target_pairs={{0,16},{1,17},{2,18},{3,19},{4,20},{5,21},{6,22},{7,23},{8,24},{9,... | collective-permute-start | bytes 393224 | tf_op jit(solution)/shard_map/ppermute | solution.py:230
  23.5 1.6 %collective-permute-start.5 = (f32[512,128]{1,0:T(8,128)S(1)}, f32[512,128]{1,0:T(8,128)S(1)}, u32[]{:S(2)}, u32[]{:S(2)}) collective-permute-start(f32[512,128]{1,0:T(8,128)S(1)} %shard_map.71.mine_ref), channel_id=1, source_target_pairs={{0,8},{1,9},{2,10},{3,11},{4,12},{5,13},{6,14},{7,15},{8,0},{9,1},... | collective-permute-start | bytes 786440 | tf_op jit(solution)/shard_map/ppermute | solution.py:227
  25.3 5.0 %collective-permute-start.7 = (bf16[512,128]{1,0:T(8,128)(2,1)S(1)}, bf16[512,128]{1,0:T(8,128)(2,1)S(1)}, u32[]{:S(2)}, u32[]{:S(2)}) collective-permute-start(bf16[512,128]{1,0:T(8,128)(2,1)S(1)} %get-tuple-element.16.now_ref.rest_3_), channel_id=1, source_target_pairs={{0,2},{1,0},{2,4},{3,1},{4,6},{5,3},{6,7},{7,5},{8,9},{9,11},{10,8... | collective-permute-start | bytes 393224 | tf_op jit(solution)/shard_map/ppermute | solution.py:236
  25.4 7.7 %collective-permute-start.6 = (bf16[512,128]{1,0:T(8,128)(2,1)S(1)}, bf16[512,128]{1,0:T(8,128)(2,1)S(1)}, u32[]{:S(2)}, u32[]{:S(2)}) collective-permute-start(bf16[512,128]{1,0:T(8,128)(2,1)S(1)} %get-tuple-element.16.now_ref.rest_3_), channel_id=1, source_target_pairs={{0,6},{1,7},{2,1},{3,2},{4,3},{5,4},{6,5},{7,0},{8,15},{9,10},{10,... | collective-permute-start | bytes 393224 | tf_op jit(solution)/shard_map/ppermute | solution.py:236
  27.0 6.4 %collective-permute-start.8 = (bf16[512,128]{1,0:T(8,128)(2,1)S(1)}, bf16[512,128]{1,0:T(8,128)(2,1)S(1)}, u32[]{:S(2)}, u32[]{:S(2)}) collective-permute-start(bf16[512,128]{1,0:T(8,128)(2,1)S(1)} %get-tuple-element.17), channel_id=1, source_target_pairs={{0,16},{1,17},{2,18},{3,19},{4,20},{5,21},{6,22},{7,23},{8,24},{9,... | collective-permute-start | bytes 393224 | tf_op jit(solution)/shard_map/ppermute | solution.py:230
  33.7 1.6 %collective-permute-start.9 = (f32[512,128]{1,0:T(8,128)S(1)}, f32[512,128]{1,0:T(8,128)S(1)}, u32[]{:S(2)}, u32[]{:S(2)}) collective-permute-start(f32[512,128]{1,0:T(8,128)S(1)} %shard_map.74.mine_ref), channel_id=1, source_target_pairs={{0,8},{1,9},{2,10},{3,11},{4,12},{5,13},{6,14},{7,15},{8,0},{9,1},... | collective-permute-start | bytes 786440 | tf_op jit(solution)/shard_map/ppermute | solution.py:227
  35.5 5.0 %collective-permute-start.11 = (bf16[512,128]{1,0:T(8,128)(2,1)S(1)}, bf16[512,128]{1,0:T(8,128)(2,1)S(1)}, u32[]{:S(2)}, u32[]{:S(2)}) collective-permute-start(bf16[512,128]{1,0:T(8,128)(2,1)S(1)} %get-tuple-element.18.now_ref.rest_3_), channel_id=1, source_target_pairs={{0,2},{1,0},{2,4},{3,1},{4,6},{5,3},{6,7},{7,5},{8,9},{9,11},{10,8... | collective-permute-start | bytes 393224 | tf_op jit(solution)/shard_map/ppermute | solution.py:236
  36.0 7.7 %collective-permute-start.10 = (bf16[512,128]{1,0:T(8,128)(2,1)S(1)}, bf16[512,128]{1,0:T(8,128)(2,1)S(1)}, u32[]{:S(2)}, u32[]{:S(2)}) collective-permute-start(bf16[512,128]{1,0:T(8,128)(2,1)S(1)} %get-tuple-element.18.now_ref.rest_3_), channel_id=1, source_target_pairs={{0,6},{1,7},{2,1},{3,2},{4,3},{5,4},{6,5},{7,0},{8,15},{9,10},{10,... | collective-permute-start | bytes 393224 | tf_op jit(solution)/shard_map/ppermute | solution.py:236
  38.3 5.4 %collective-permute-start.12 = (bf16[512,128]{1,0:T(8,128)(2,1)S(1)}, bf16[512,128]{1,0:T(8,128)(2,1)S(1)}, u32[]{:S(2)}, u32[]{:S(2)}) collective-permute-start(bf16[512,128]{1,0:T(8,128)(2,1)S(1)} %get-tuple-element.19), channel_id=1, source_target_pairs={{0,16},{1,17},{2,18},{3,19},{4,20},{5,21},{6,22},{7,23},{8,24},{9,... | collective-permute-start | bytes 393224 | tf_op jit(solution)/shard_map/ppermute | solution.py:230
  44.0 1.6 %collective-permute-start.13 = (f32[512,128]{1,0:T(8,128)S(1)}, f32[512,128]{1,0:T(8,128)S(1)}, u32[]{:S(2)}, u32[]{:S(2)}) collective-permute-start(f32[512,128]{1,0:T(8,128)S(1)} %shard_map.77.mine_ref), channel_id=1, source_target_pairs={{0,8},{1,9},{2,10},{3,11},{4,12},{5,13},{6,14},{7,15},{8,0},{9,1},... | collective-permute-start | bytes 786440 | tf_op jit(solution)/shard_map/ppermute | solution.py:227
  45.8 15.9 %copy-start.7 = (bf16[512,128]{1,0:T(8,128)(2,1)}, bf16[512,128]{1,0:T(8,128)(2,1)S(1)}, u32[]{:S(2)}) copy-start(bf16[512,128]{1,0:T(8,128)(2,1)S(1)} %get-tuple-element.20.now_ref.rest_3_) | copy-start | bytes 393220
  45.8 5.0 %collective-permute-start.15 = (bf16[512,128]{1,0:T(8,128)(2,1)S(1)}, bf16[512,128]{1,0:T(8,128)(2,1)S(1)}, u32[]{:S(2)}, u32[]{:S(2)}) collective-permute-start(bf16[512,128]{1,0:T(8,128)(2,1)S(1)} %get-tuple-element.20.now_ref.rest_3_), channel_id=1, source_target_pairs={{0,2},{1,0},{2,4},{3,1},{4,6},{5,3},{6,7},{7,5},{8,9},{9,11},{10,8... | collective-permute-start | bytes 393224 | tf_op jit(solution)/shard_map/ppermute | solution.py:236
  46.2 8.4 %collective-permute-start.14 = (bf16[512,128]{1,0:T(8,128)(2,1)S(1)}, bf16[512,128]{1,0:T(8,128)(2,1)S(1)}, u32[]{:S(2)}, u32[]{:S(2)}) collective-permute-start(bf16[512,128]{1,0:T(8,128)(2,1)S(1)} %get-tuple-element.20.now_ref.rest_3_), channel_id=1, source_target_pairs={{0,6},{1,7},{2,1},{3,2},{4,3},{5,4},{6,5},{7,0},{8,15},{9,10},{10,... | collective-permute-start | bytes 393224 | tf_op jit(solution)/shard_map/ppermute | solution.py:236
  48.4 6.1 %collective-permute-start.16 = (bf16[512,128]{1,0:T(8,128)(2,1)S(1)}, bf16[512,128]{1,0:T(8,128)(2,1)S(1)}, u32[]{:S(2)}, u32[]{:S(2)}) collective-permute-start(bf16[512,128]{1,0:T(8,128)(2,1)S(1)} %get-tuple-element.21), channel_id=1, source_target_pairs={{0,16},{1,17},{2,18},{3,19},{4,20},{5,21},{6,22},{7,23},{8,24},{9,... | collective-permute-start | bytes 393224 | tf_op jit(solution)/shard_map/ppermute | solution.py:230
  54.8 1.6 %collective-permute-start.17 = (f32[512,128]{1,0:T(8,128)S(1)}, f32[512,128]{1,0:T(8,128)S(1)}, u32[]{:S(2)}, u32[]{:S(2)}) collective-permute-start(f32[512,128]{1,0:T(8,128)S(1)} %shard_map.80.mine_ref), channel_id=1, source_target_pairs={{0,8},{1,9},{2,10},{3,11},{4,12},{5,13},{6,14},{7,15},{8,0},{9,1},... | collective-permute-start | bytes 786440 | tf_op jit(solution)/shard_map/ppermute | solution.py:227
  56.6 5.0 %collective-permute-start.19 = (bf16[512,128]{1,0:T(8,128)(2,1)S(1)}, bf16[512,128]{1,0:T(8,128)(2,1)S(1)}, u32[]{:S(2)}, u32[]{:S(2)}) collective-permute-start(bf16[512,128]{1,0:T(8,128)(2,1)S(1)} %get-tuple-element.22.now_ref.rest_3_), channel_id=1, source_target_pairs={{0,2},{1,0},{2,4},{3,1},{4,6},{5,3},{6,7},{7,5},{8,9},{9,11},{10,8... | collective-permute-start | bytes 393224 | tf_op jit(solution)/shard_map/ppermute | solution.py:236
  56.7 8.5 %collective-permute-start.18 = (bf16[512,128]{1,0:T(8,128)(2,1)S(1)}, bf16[512,128]{1,0:T(8,128)(2,1)S(1)}, u32[]{:S(2)}, u32[]{:S(2)}) collective-permute-start(bf16[512,128]{1,0:T(8,128)(2,1)S(1)} %get-tuple-element.22.now_ref.rest_3_), channel_id=1, source_target_pairs={{0,6},{1,7},{2,1},{3,2},{4,3},{5,4},{6,5},{7,0},{8,15},{9,10},{10,... | collective-permute-start | bytes 393224 | tf_op jit(solution)/shard_map/ppermute | solution.py:236
  59.1 6.2 %collective-permute-start.20 = (bf16[512,128]{1,0:T(8,128)(2,1)S(1)}, bf16[512,128]{1,0:T(8,128)(2,1)S(1)}, u32[]{:S(2)}, u32[]{:S(2)}) collective-permute-start(bf16[512,128]{1,0:T(8,128)(2,1)S(1)} %get-tuple-element.23), channel_id=1, source_target_pairs={{0,16},{1,17},{2,18},{3,19},{4,20},{5,21},{6,22},{7,23},{8,24},{9,... | collective-permute-start | bytes 393224 | tf_op jit(solution)/shard_map/ppermute | solution.py:230
  66.3 1.9 %collective-permute-start.21 = (f32[512,128]{1,0:T(8,128)}, f32[512,128]{1,0:T(8,128)}, u32[]{:S(2)}, u32[]{:S(2)}) collective-permute-start(f32[512,128]{1,0:T(8,128)} %shard_map.83.mine_ref), channel_id=1, source_target_pairs={{0,8},{1,9},{2,10},{3,11},{4,12},{5,13},{6,14},{7,15},{8,0},{9,1},... | collective-permute-start | bytes 786440 | tf_op jit(solution)/shard_map/ppermute | solution.py:227
  70.3 8.9 %collective-permute-start.25 = (bf16[512,128]{1,0:T(8,128)(2,1)S(1)}, bf16[512,128]{1,0:T(8,128)(2,1)S(1)}, u32[]{:S(2)}, u32[]{:S(2)}) collective-permute-start(bf16[512,128]{1,0:T(8,128)(2,1)S(1)} %get-tuple-element.24.rest_3_.now_ref), channel_id=1, source_target_pairs={{0,6},{1,7},{2,1},{3,2},{4,3},{5,4},{6,5},{7,0},{8,15},{9,10},{10,... | collective-permute-start | bytes 393224 | tf_op jit(solution)/shard_map/ppermute | solution.py:236
  72.0 6.4 %collective-permute-start.26 = (bf16[512,128]{1,0:T(8,128)(2,1)S(1)}, bf16[512,128]{1,0:T(8,128)(2,1)S(1)}, u32[]{:S(2)}, u32[]{:S(2)}) collective-permute-start(bf16[512,128]{1,0:T(8,128)(2,1)S(1)} %get-tuple-element.24.rest_3_.now_ref), channel_id=1, source_target_pairs={{0,2},{1,0},{2,4},{3,1},{4,6},{5,3},{6,7},{7,5},{8,9},{9,11},{10,8... | collective-permute-start | bytes 393224 | tf_op jit(solution)/shard_map/ppermute | solution.py:236
  72.1 7.0 %collective-permute-start.22 = (bf16[512,128]{1,0:T(8,128)(2,1)S(1)}, bf16[512,128]{1,0:T(8,128)(2,1)S(1)}, u32[]{:S(2)}, u32[]{:S(2)}) collective-permute-start(bf16[512,128]{1,0:T(8,128)(2,1)S(1)} %get-tuple-element.25), channel_id=1, source_target_pairs={{0,16},{1,17},{2,18},{3,19},{4,20},{5,21},{6,22},{7,23},{8,24},{9,... | collective-permute-start | bytes 393224 | tf_op jit(solution)/shard_map/ppermute | solution.py:230
  79.8 3.4 %collective-permute-start.27 = (f32[512,128]{1,0:T(8,128)S(1)}, f32[512,128]{1,0:T(8,128)S(1)}, u32[]{:S(2)}, u32[]{:S(2)}) collective-permute-start(f32[512,128]{1,0:T(8,128)S(1)} %get-tuple-element.27), channel_id=1, source_target_pairs={{0,8},{1,9},{2,10},{3,11},{4,12},{5,13},{6,14},{7,15},{8,0},{9,1},... | collective-permute-start | bytes 786440 | tf_op jit(solution)/shard_map/ppermute | solution.py:227
  80.2 5.0 %collective-permute-start.24 = (bf16[512,128]{1,0:T(8,128)(2,1)S(1)}, bf16[512,128]{1,0:T(8,128)(2,1)S(1)}, u32[]{:S(2)}, u32[]{:S(2)}) collective-permute-start(bf16[512,128]{1,0:T(8,128)(2,1)S(1)} %collective-permute-done.22.now_ref.field_ref), channel_id=1, source_target_pairs={{0,2},{1,0},{2,4},{3,1},{4,6},{5,3},{6,7},{7,5},{8,9},{9,11},{10,8... | collective-permute-start | bytes 393224 | tf_op jit(solution)/shard_map/ppermute | solution.py:236
  81.1 7.9 %collective-permute-start.23 = (bf16[512,128]{1,0:T(8,128)(2,1)S(1)}, bf16[512,128]{1,0:T(8,128)(2,1)S(1)}, u32[]{:S(2)}, u32[]{:S(2)}) collective-permute-start(bf16[512,128]{1,0:T(8,128)(2,1)S(1)} %collective-permute-done.22.now_ref.field_ref), channel_id=1, source_target_pairs={{0,6},{1,7},{2,1},{3,2},{4,3},{5,4},{6,5},{7,0},{8,15},{9,10},{10,... | collective-permute-start | bytes 393224 | tf_op jit(solution)/shard_map/ppermute | solution.py:236
  83.2 5.8 %collective-permute-start.28 = (bf16[512,128]{1,0:T(8,128)(2,1)S(1)}, bf16[512,128]{1,0:T(8,128)(2,1)S(1)}, u32[]{:S(2)}, u32[]{:S(2)}) collective-permute-start(bf16[512,128]{1,0:T(8,128)(2,1)S(1)} %add_convert_fusion), channel_id=1, source_target_pairs={{0,16},{1,17},{2,18},{3,19},{4,20},{5,21},{6,22},{7,23},{8,24},{9,... | collective-permute-start | bytes 393224 | tf_op jit(solution)/shard_map/ppermute | solution.py:230
  89.7 1.6 %collective-permute-start.29 = (f32[512,128]{1,0:T(8,128)S(1)}, f32[512,128]{1,0:T(8,128)S(1)}, u32[]{:S(2)}, u32[]{:S(2)}) collective-permute-start(f32[512,128]{1,0:T(8,128)S(1)} %get-tuple-element.29), channel_id=1, source_target_pairs={{0,8},{1,9},{2,10},{3,11},{4,12},{5,13},{6,14},{7,15},{8,0},{9,1},... | collective-permute-start | bytes 786440 | tf_op jit(solution)/shard_map/ppermute | solution.py:227
  (20 other events, 112.2 us)

commit v4 on v3

v4 whole, which is shorter than its diff:
```python
import functools

import jax
import jax.numpy as jnp
from jax import lax
from jax.experimental import pallas as pl
from jax.experimental.pallas import tpu as pltpu
from jax.sharding import PartitionSpec as P

F32 = jnp.float32
BF16 = jnp.bfloat16
AXES = ("delay", "surface")
VMEM = pl.BlockSpec(memory_space=pltpu.VMEM)
MIB = 1024 * 1024


def dot(a, b):
    return jnp.dot(a, b, preferred_element_type=F32)


def place():
    lag = lax.axis_index("delay")
    return lax.rem(lag, 2), lax.div(lag, 2)


def cost(microseconds):
    moved = int(3.6e6 * microseconds)
    return pl.CostEstimate(flops=0, bytes_accessed=moved, transcendentals=0)


def call(body, outs, args, after=None, microseconds=0.5):
    specs = [VMEM] * len(args)
    if after is not None:
        args, specs = [after] + args, [pl.BlockSpec(memory_space=pl.ANY)] + specs
        body = functools.partial(skip_first, body)
    return pl.pallas_call(
        body,
        out_shape=tuple(outs),
        in_specs=specs,
        out_specs=tuple(VMEM for _ in outs),
        cost_estimate=cost(microseconds),
        compiler_params=pltpu.CompilerParams(vmem_limit_bytes=8 * MIB),
    )(*args)


def skip_first(body, _, *refs):
    body(*refs)


def choose(*cases):
    *pairs, value = cases
    for when, other in reversed(pairs):
        value = jnp.where(when, other, value)
    return value


def far_next(s, count):
    return choose((s == 0, count - 2), (s == 1, count - 1), (s == count - 1, 0), s - 1)


def far_last(s, count):
    return choose((s == 0, count - 1), (s == count - 2, 0), (s == count - 1, 1), s + 1)


def close_next(s, count):
    even = lax.rem(s, 2) == 0
    return choose((s == 1, 0), (s == count - 2, count - 1), (even, s + 2), s - 2)


def close_last(s, count):
    even = lax.rem(s, 2) == 0
    return choose((s == 0, 1), (s == count - 1, count - 2), (even, s - 2), s + 2)


def tour(far, count):
    if far:
        return [0] + list(range(count - 2, 0, -1)) + [count - 1]
    return list(range(0, count, 2)) + list(range(count - 1, 0, -2))


def spread_body(groups, pattern_ref, entries_ref, keep_ref, send_ref, here_ref, both_ref, sems):
    core, _ = place()
    blocks, slots, size, _ = entries_ref.shape
    copies = [
        pltpu.make_async_copy(entries_ref.at[row], here_ref.at[row], sems.at[row])
        for row in range(blocks)
    ]
    for copy in copies:
        copy.start()
    here = lax.axis_index("surface")
    brought = (
        (far_last(here, groups), 0, 0),
        (close_last(here, groups), 0, blocks),
        (far_next(here, groups), 1, 0),
        (close_next(here, groups), 1, blocks),
    )
    both_ref[...] = jnp.zeros_like(both_ref)
    for row in range(blocks):
        copies[row].wait()
        rows = slice(row * size, (row + 1) * size)
        for slot in range(slots):
            block = pattern_ref[row, slot]
            group = lax.div(block, blocks)
            within = block - group * blocks
            second = within >= blocks // 2
            half = jnp.where(second, 1, 0)
            column = 2 * blocks + jnp.where(second, within - blocks // 2, within)
            for source, side, first in brought:
                half = jnp.where(group == source, side, half)
                column = jnp.where(group == source, first + within, column)
            columns = pl.ds(pl.multiple_of(column * size, size), size)
            both_ref[jnp.where(half == core, 0, 1), rows, columns] = here_ref[row, slot]
        keep_ref[rows, :] = both_ref[0, rows, :]
        send_ref[rows, :] = both_ref[1, rows, :]


def spread(entries, pattern, groups):
    blocks, slots, size, _ = entries.shape
    shape = (blocks * size, (2 * blocks + blocks // 2) * size)
    out = jax.ShapeDtypeStruct(shape, entries.dtype)
    return pl.pallas_call(
        functools.partial(spread_body, groups),
        out_shape=(out, out),
        in_specs=[
            pl.BlockSpec(memory_space=pltpu.SMEM),
            pl.BlockSpec(memory_space=pltpu.HBM),
        ],
        out_specs=(VMEM, VMEM),
        scratch_shapes=[
            pltpu.VMEM(entries.shape, entries.dtype),
            pltpu.VMEM((2, *shape), entries.dtype),
            pltpu.SemaphoreType.DMA((blocks,)),
        ],
        cost_estimate=cost(4),
        compiler_params=pltpu.CompilerParams(vmem_limit_bytes=12 * MIB),
    )(pattern, entries)


def arrange_body(kept_ref, got_ref, near_ref, far_ref):
    core, _ = place()

    @pl.when(core == 0)
    def _():
        near_ref[...] = kept_ref[...]
        far_ref[...] = got_ref[...]

    @pl.when(core == 1)
    def _():
        near_ref[...] = got_ref[...]
        far_ref[...] = kept_ref[...]


def own_half(current_ref):
    core, _ = place()
    rows = current_ref.shape[0] // 2
    return current_ref[pl.ds(pl.multiple_of(core * rows, rows), rows), :]


def early_body(near_ref, now_ref, *rest):
    *last, out_ref = rest
    rows = now_ref.shape[0]
    total = dot(near_ref[:, 2 * rows :], own_half(now_ref))
    if last:
        far_ref, first_ref, second_ref, before_ref = last
        total += dot(far_ref[:, :rows], first_ref[...])
        total += dot(far_ref[:, rows : 2 * rows], second_ref[...])
        total += dot(far_ref[:, 2 * rows :], own_half(before_ref))
    out_ref[...] = total


def late_sum(step, pairs, near_ref, first_ref, second_ref, early_ref, field):
    core, pair = place()
    rows = first_ref.shape[0]
    total = early_ref[...]
    total += dot(near_ref[:, :rows], first_ref[...])
    total += dot(near_ref[:, rows : 2 * rows], second_ref[...])
    if not field:
        return total
    field_ref, *history = field
    value = jnp.where(pair == pairs - 1, 0.0, field_ref[...].astype(F32))
    if history:
        mine_ref, other_ref = history
        value = jnp.where(
            pair == step, other_ref[...], jnp.where(pair == step + 1, mine_ref[...], value)
        )
    return total + jnp.where(core == 0, value, 0.0)


def late_body(step, pairs, near_ref, first_ref, second_ref, early_ref, *rest):
    *field, out_ref = rest
    out_ref[...] = late_sum(step, pairs, near_ref, first_ref, second_ref, early_ref, field)


def late_final_body(
    step, steps, pairs, near_ref, first_ref, second_ref, early_ref, far_ref, now_ref, *rest
):
    *field, keep_ref, send_ref = rest
    core, pair = place()
    rows = first_ref.shape[0]
    even = late_sum(step, pairs, near_ref, first_ref, second_ref, early_ref, field)
    odd = (
        dot(far_ref[:, :rows], first_ref[...])
        + dot(far_ref[:, rows : 2 * rows], second_ref[...])
        + dot(far_ref[:, 2 * rows :], own_half(now_ref))
    )
    ends = pair == step - (steps - 1)
    keep_ref[...] = jnp.where(jnp.logical_and(ends, core == 1), odd, even)
    send_ref[...] = jnp.where(jnp.logical_and(ends, core == 0), odd, even)


def finish_body(step, steps, mine_ref, other_ref, *rest):
    *earlier, result_ref, field_ref = rest
    core, pair = place()
    field = mine_ref[...] + other_ref[...]
    field_ref[...] = field.astype(BF16)
    if earlier:
        before_ref, field_in_ref = earlier
        adds = jnp.logical_and(core == 1, pair == step - steps)
        before = before_ref[...] + jnp.where(adds, field_in_ref[...].astype(F32), 0.0)
        field = jnp.where(pair == step - (steps - 1), field, before)
    result_ref[...] = field


def collect_body(pairs, *refs):
    *seen, out_ref = refs
    _, pair = place()
    for step in range(out_ref.shape[0]):
        value = seen[step][...]
        for later in range(1, pairs):
            value = jnp.where(pair == later, seen[step + later][...], value)
        out_ref[step] = value


def solve(inverse_ref, rhs, out_ref, keep, other):
    size = inverse_ref.shape[1]
    fresh = []
    for i in range(inverse_ref.shape[0]):
        rows = slice(i * size, (i + 1) * size)
        block = dot(inverse_ref[i], rhs[rows]).astype(BF16)
        fresh.append(jnp.where(keep, block, other[rows]))
        out_ref[rows, :] = fresh[-1]
    return fresh


def start_body(inverse_ref, excitation_ref, history_ref, other_history_ref, out_ref):
    core, pair = place()
    history = jnp.where(core == 0, history_ref[...], other_history_ref[...])
    rhs = (excitation_ref[0].astype(F32) - history).astype(BF16)
    solve(inverse_ref, rhs, out_ref, pair == 0, jnp.zeros_like(rhs))


def next_body(step, pairs, inverse_ref, excitation_ref, mine_ref, other_ref, came_ref, out_ref, field_ref):
    _, pair = place()
    field = mine_ref[...] + other_ref[...]
    rhs = (excitation_ref[step + 1].astype(F32) - field).astype(BF16)
    first_pair = pair == 0
    fresh = solve(inverse_ref, rhs, out_ref, first_pair, came_ref)
    if pairs == 2:
        size = inverse_ref.shape[1]
        for i, block in enumerate(fresh):
            rows = slice(i * size, (i + 1) * size)
            field_ref[rows, :] = jnp.where(first_pair, block, field[rows].astype(BF16))
    else:
        field_ref[...] = field.astype(BF16)


def per_device(lagged_block_entries, pattern, diagonal_block_inverses, excitation, history):
    lags, groups = lax.axis_size("delay"), lax.axis_size("surface")
    pairs = lags // 2
    entries = lagged_block_entries[0]
    blocks, slots, size, _ = entries.shape
    steps, rows, columns = excitation.shape

    def device(d, s):
        return d * groups + s

    def everyone(move):
        return [
            (device(d, s), device(*move(d, s))) for d in range(lags) for s in range(groups)
        ]

    def swapped(value):
        return lax.ppermute(value, AXES, everyone(lambda d, s: (d ^ 1, s)))

    def pair_moved(value, hop):
        return lax.ppermute(value, AXES, everyone(lambda d, s: ((d + 2 * hop) % lags, s)))

    def halo(value, far):
        order = tour(far, groups)
        following = dict(zip(order, order[1:] + order[:1]))
        preceding = {t: s for s, t in following.items()}
        return lax.ppermute(
            value,
            AXES,
            everyone(lambda d, s: (d, following[s] if d % 2 == 0 else preceding[s])),
        )

    other_history = swapped(history[0])
    field_shape = jax.ShapeDtypeStruct((rows, columns), F32)
    current_shape = jax.ShapeDtypeStruct((rows, columns), BF16)
    kept, sent = spread(entries, pattern[0], groups)
    (current,) = call(
        start_body,
        [current_shape],
        [diagonal_block_inverses, excitation, history[0], other_history],
        after=kept,
    )
    matrix_shape = jax.ShapeDtypeStruct(kept.shape, kept.dtype)
    near, far = call(arrange_body, [matrix_shape, matrix_shape], [kept, swapped(sent)])

    going = current
    seen = []
    previous = []
    result = []
    out = None
    rounds = steps + pairs - 1
    for step in range(rounds):
        seen.append(current)
        if step == rounds - 1:
            (out,) = call(
                functools.partial(collect_body, pairs),
                [jax.ShapeDtypeStruct(excitation.shape, BF16)],
                seen,
            )
        first, second = halo(current, True), halo(current, False)
        if pairs == 2:
            current_in = field_in = pair_moved(going, 1)
        else:
            current_in, field_in = pair_moved(current, 1), pair_moved(going, -1)
        last = [far, *previous] if previous else []
        (early,) = call(early_body, [field_shape], [near, current] + last)
        received = [near, first, second, early]
        field = [field_in] if step < rounds - 1 else []
        if step < pairs:
            field += [history[0], other_history]
        previous = [first, second, current]
        if step < steps - 1:
            (mine,) = call(
                functools.partial(late_body, step, pairs), [field_shape], received + field
            )
            current, going = call(
                functools.partial(next_body, step, pairs),
                [current_shape, current_shape],
                [diagonal_block_inverses, excitation, mine, swapped(mine), current_in],
            )
        else:
            mine, send = call(
                functools.partial(late_final_body, step, steps, pairs),
                [field_shape, field_shape],
                received + [far, current] + field,
                after=out,
                microseconds=0.5 if out is None else 20,
            )
            result, going = call(
                functools.partial(finish_body, step, steps),
                [field_shape, current_shape],
                [mine, swapped(send)] + ([result, field_in] if step >= steps else []),
            )
            current = current_in
    return (out, result[None])


def solution(mesh):
    placed = (
        P("delay", "surface", None, None, None),
        P("delay", "surface", None),
        P("surface", None, None),
        P(None, "surface", None),
        P("delay", "surface", None),
    )
    return jax.shard_map(
        per_device,
        mesh=mesh,
        in_specs=placed,
        out_specs=(P(None, "surface", None), P("delay", "surface", None)),
        check_vma=False,
    )
```

time: 92.4 us -> 94.5 us (1.023)
  waiting for transfers between devices: 37.6 us -> 43.6 us
  other arithmetic: 4.06 us -> 0 us
  local copies, waits for them, and re-layouts: 5.25 us -> 3.5 us
  starting transfers between devices: 32.2 us -> 33.9 us
    ppermute x7, waiting for transfers between devices: 0.32 us -> 6.05 us  [pair_moved(): lax.ppermute(value, AXES, everyone(lambda d, s: ((d + 2 * hop) % lags, s)))]
    select_n x2 -> x0, other arithmetic: 2.87 us -> none  [the longest x1 1.88 us: per_device(): far = jnp.where(core == 0, got, kept)]
    ppermute x14, starting transfers between devices: 20.6 us -> 23.1 us  [halo(): lax.ppermute(value, AXES, everyone(lambda d, s: (d, following[s] if d % 2...]
    ppermute x14, waiting for transfers between devices: 25 us -> 27.1 us  [halo(): lax.ppermute(value, AXES, everyone(lambda d, s: (d, following[s] if d % 2...]
    ppermute x9, waiting for transfers between devices: 12.3 us -> 10.5 us  [swapped(): return lax.ppermute(value, AXES, everyone(lambda d, s: (d ^ 1, s)))]
    squeeze x1 -> x0, local copies, waits for them, and re-layouts: 1.18 us -> none  [per_device(): kept, got = (both[0], swapped(both[1]))]
    unnamed x44 -> x12, local copies, waits for them, and re-layouts: 4.07 us -> 3.5 us
    pallas_call x21 -> x25, Pallas kernels: 11.9 us -> 12.4 us  [the longest x24 10.6 us: call(): pl.pallas_call(body, out_shape=tuple(outs), in_specs=specs, out_specs=tup...]
  transfers between devices with their start and end apart: 30 -> 30, of which waited for: 20 -> 20; matrix products, arithmetic and copies ran while one was open for 4% -> 0% of each run, Pallas kernels for 5% -> 6%
where the time goes in v4:
time: 94.5 us; the launch traced here: 94.3 us
  waiting for transfers between devices  43.6 us (46%)
  starting transfers between devices  33.9 us (36%)
  Pallas kernels  12.4 us (13%)
  local copies, waits for them, and re-layouts  3.5 us (4%)
    ppermute x14, waiting for transfers between devices, halo(): lax.ppermute(value, AXES, everyone(lambda d, s: (d, following[s] if d % 2...  27.1 us
    ppermute x14, starting transfers between devices, halo(): lax.ppermute(value, AXES, everyone(lambda d, s: (d, following[s] if d % 2...  23.1 us
    pallas_call x24, Pallas kernels, call(): pl.pallas_call(body, out_shape=tuple(outs), in_specs=specs, out_specs=tup...  10.6 us
    ppermute x9, waiting for transfers between devices, swapped(): return lax.ppermute(value, AXES, everyone(lambda d, s: (d ^ 1, s)))  10.5 us
    ppermute x7, starting transfers between devices, pair_moved(): lax.ppermute(value, AXES, everyone(lambda d, s: ((d + 2 * hop) % lags, s)))  9.6 us
    ppermute x7, waiting for transfers between devices, pair_moved(): lax.ppermute(value, AXES, everyone(lambda d, s: ((d + 2 * hop) % lags, s)))  6.05 us
    unnamed x12, local copies, waits for them, and re-layouts  3.5 us
  transfers between devices with their start and end apart: 30, of which 20 were waited for; matrix products, arithmetic and copies ran while one was open for 0% of the time, Pallas kernels for 6%

profile of v4, /device:TPU:0, one launch (start us, length us, event | category | flops | bytes accessed | tf_op | source)
XLA Modules:
  0.0 94.3 jit_solution(3303416408969802893)
XLA Ops:
  0.7 1.7 %copy-done.4 = bf16[1,4,16,128,128]{4,3,2,1,0:T(8,128)(2,1)S(1)} copy-done((bf16[1,4,16,128,128]{4,3,2,1,0:T(8,128)(2,1)S(1)}, bf16[1,4,16,128,128]{4,3,2,1,0:T(8,128)(2,1)}, u32[]{:S(2)}) %copy-start.4) | copy-done | bytes 2097176
  3.0 1.8 %shard_map.68 = (bf16[512,1280]{1,0:T(8,128)(2,1)S(1)}, bf16[512,1280]{1,0:T(8,128)(2,1)S(1)}) custom-call(s32[4,16]{1,0:T(4,128)S(1)} %bitcast.9, bf16[4,16,128,128]{3,2,1,0:T(8,128)(2,1)S(1)} %bitcast.8), custom_call_target="tpu_custom_call" | custom-call | bytes 14400000 | tf_op jit(solution)/shard_map/pallas_call | solution.py:121
  5.4 2.9 %collective-permute-done.refs_3_.rest_2_ = f32[512,128]{1,0:T(8,128)S(1)} collective-permute-done((f32[512,128]{1,0:T(8,128)S(1)}, f32[512,128]{1,0:T(8,128)S(1)}, u32[]{:S(2)}, u32[]{:S(2)}) %collective-permute-start) | collective-permute-done | bytes 262176 | tf_op jit(solution)/shard_map/ppermute | solution.py:283
  8.6 5.0 %collective-permute-start.2 = (bf16[512,128]{1,0:T(8,128)(2,1)S(1)}, bf16[512,128]{1,0:T(8,128)(2,1)S(1)}, u32[]{:S(2)}, u32[]{:S(2)}) collective-permute-start(bf16[512,128]{1,0:T(8,128)(2,1)S(1)} %shard_map.69.now_ref.rest_3_.refs_0_), channel_id=1, source_target_pairs={{0,6},{1,7},{2,1},{3,2},{4,3},{5,4},{6,5},{7,0},{8,15},{9,10},{10,... | collective-permute-start | bytes 393224 | tf_op jit(solution)/shard_map/ppermute | solution.py:292
  13.6 1.5 %collective-permute-start.4 = (bf16[512,128]{1,0:T(8,128)(2,1)S(1)}, bf16[512,128]{1,0:T(8,128)(2,1)S(1)}, u32[]{:S(2)}, u32[]{:S(2)}) collective-permute-start(bf16[512,128]{1,0:T(8,128)(2,1)S(1)} %shard_map.69.now_ref.rest_3_.refs_0_), channel_id=1, source_target_pairs={{0,16},{1,17},{2,18},{3,19},{4,20},{5,21},{6,22},{7,23},{8,24},{9,... | collective-permute-start | bytes 393224 | tf_op jit(solution)/shard_map/ppermute | solution.py:286
  15.5 3.0 %collective-permute-done.2.first_ref.rest_1_ = bf16[512,128]{1,0:T(8,128)(2,1)S(1)} collective-permute-done((bf16[512,128]{1,0:T(8,128)(2,1)S(1)}, bf16[512,128]{1,0:T(8,128)(2,1)S(1)}, u32[]{:S(2)}, u32[]{:S(2)}) %collective-permute-start.2) | collective-permute-done | bytes 131104 | tf_op jit(solution)/shard_map/ppermute | solution.py:292
  20.4 1.5 %collective-permute-done.5.other_ref = f32[512,128]{1,0:T(8,128)S(1)} collective-permute-done((f32[512,128]{1,0:T(8,128)S(1)}, f32[512,128]{1,0:T(8,128)S(1)}, u32[]{:S(2)}, u32[]{:S(2)}) %collective-permute-start.5) | collective-permute-done | bytes 262176 | tf_op jit(solution)/shard_map/ppermute | solution.py:283
  22.1 3.0 %collective-permute-start.6 = (bf16[512,128]{1,0:T(8,128)(2,1)S(1)}, bf16[512,128]{1,0:T(8,128)(2,1)S(1)}, u32[]{:S(2)}, u32[]{:S(2)}) collective-permute-start(bf16[512,128]{1,0:T(8,128)(2,1)S(1)} %get-tuple-element.26.now_ref.rest_3_.refs_1_), channel_id=1, source_target_pairs={{0,6},{1,7},{2,1},{3,2},{4,3},{5,4},{6,5},{7,0},{8,15},{9,10},{10,... | collective-permute-start | bytes 393224 | tf_op jit(solution)/shard_map/ppermute | solution.py:292
  25.1 1.5 %collective-permute-start.8 = (bf16[512,128]{1,0:T(8,128)(2,1)S(1)}, bf16[512,128]{1,0:T(8,128)(2,1)S(1)}, u32[]{:S(2)}, u32[]{:S(2)}) collective-permute-start(bf16[512,128]{1,0:T(8,128)(2,1)S(1)} %get-tuple-element.28), channel_id=1, source_target_pairs={{0,16},{1,17},{2,18},{3,19},{4,20},{5,21},{6,22},{7,23},{8,24},{9,... | collective-permute-start | bytes 393224 | tf_op jit(solution)/shard_map/ppermute | solution.py:286
  27.2 2.8 %collective-permute-done.6.first_ref.rest_1_ = bf16[512,128]{1,0:T(8,128)(2,1)S(1)} collective-permute-done((bf16[512,128]{1,0:T(8,128)(2,1)S(1)}, bf16[512,128]{1,0:T(8,128)(2,1)S(1)}, u32[]{:S(2)}, u32[]{:S(2)}) %collective-permute-start.6) | collective-permute-done | bytes 131104 | tf_op jit(solution)/shard_map/ppermute | solution.py:292
  30.0 1.3 %collective-permute-done.7.second_ref.rest_2_ = bf16[512,128]{1,0:T(8,128)(2,1)S(1)} collective-permute-done((bf16[512,128]{1,0:T(8,128)(2,1)S(1)}, bf16[512,128]{1,0:T(8,128)(2,1)S(1)}, u32[]{:S(2)}, u32[]{:S(2)}) %collective-permute-start.7) | collective-permute-done | bytes 131104 | tf_op jit(solution)/shard_map/ppermute | solution.py:292
  31.8 1.5 %collective-permute-done.9.other_ref = f32[512,128]{1,0:T(8,128)S(1)} collective-permute-done((f32[512,128]{1,0:T(8,128)S(1)}, f32[512,128]{1,0:T(8,128)S(1)}, u32[]{:S(2)}, u32[]{:S(2)}) %collective-permute-start.9) | collective-permute-done | bytes 262176 | tf_op jit(solution)/shard_map/ppermute | solution.py:283
  33.5 1.8 %collective-permute-start.10 = (bf16[512,128]{1,0:T(8,128)(2,1)S(1)}, bf16[512,128]{1,0:T(8,128)(2,1)S(1)}, u32[]{:S(2)}, u32[]{:S(2)}) collective-permute-start(bf16[512,128]{1,0:T(8,128)(2,1)S(1)} %get-tuple-element.29.now_ref.rest_3_.refs_2_), channel_id=1, source_target_pairs={{0,6},{1,7},{2,1},{3,2},{4,3},{5,4},{6,5},{7,0},{8,15},{9,10},{10,... | collective-permute-start | bytes 393224 | tf_op jit(solution)/shard_map/ppermute | solution.py:292
  35.9 1.5 %collective-permute-start.12 = (bf16[512,128]{1,0:T(8,128)(2,1)S(1)}, bf16[512,128]{1,0:T(8,128)(2,1)S(1)}, u32[]{:S(2)}, u32[]{:S(2)}) collective-permute-start(bf16[512,128]{1,0:T(8,128)(2,1)S(1)} %get-tuple-element.30), channel_id=1, source_target_pairs={{0,16},{1,17},{2,18},{3,19},{4,20},{5,21},{6,22},{7,23},{8,24},{9,... | collective-permute-start | bytes 393224 | tf_op jit(solution)/shard_map/ppermute | solution.py:286
  37.9 3.5 %collective-permute-done.10.first_ref.rest_1_ = bf16[512,128]{1,0:T(8,128)(2,1)S(1)} collective-permute-done((bf16[512,128]{1,0:T(8,128)(2,1)S(1)}, bf16[512,128]{1,0:T(8,128)(2,1)S(1)}, u32[]{:S(2)}, u32[]{:S(2)}) %collective-permute-start.10) | collective-permute-done | bytes 131104 | tf_op jit(solution)/shard_map/ppermute | solution.py:292
  42.2 1.4 %collective-permute-done.13.other_ref = f32[512,128]{1,0:T(8,128)S(1)} collective-permute-done((f32[512,128]{1,0:T(8,128)S(1)}, f32[512,128]{1,0:T(8,128)S(1)}, u32[]{:S(2)}, u32[]{:S(2)}) %collective-permute-start.13) | collective-permute-done | bytes 262176 | tf_op jit(solution)/shard_map/ppermute | solution.py:283
  43.9 2.2 %collective-permute-start.14 = (bf16[512,128]{1,0:T(8,128)(2,1)S(1)}, bf16[512,128]{1,0:T(8,128)(2,1)S(1)}, u32[]{:S(2)}, u32[]{:S(2)}) collective-permute-start(bf16[512,128]{1,0:T(8,128)(2,1)S(1)} %get-tuple-element.31.now_ref.rest_3_.refs_3_), channel_id=1, source_target_pairs={{0,6},{1,7},{2,1},{3,2},{4,3},{5,4},{6,5},{7,0},{8,15},{9,10},{10,... | collective-permute-start | bytes 393224 | tf_op jit(solution)/shard_map/ppermute | solution.py:292
  47.0 1.5 %collective-permute-start.16 = (bf16[512,128]{1,0:T(8,128)(2,1)S(1)}, bf16[512,128]{1,0:T(8,128)(2,1)S(1)}, u32[]{:S(2)}, u32[]{:S(2)}) collective-permute-start(bf16[512,128]{1,0:T(8,128)(2,1)S(1)} %get-tuple-element.32), channel_id=1, source_target_pairs={{0,16},{1,17},{2,18},{3,19},{4,20},{5,21},{6,22},{7,23},{8,24},{9,... | collective-permute-start | bytes 393224 | tf_op jit(solution)/shard_map/ppermute | solution.py:286
  49.0 3.4 %collective-permute-done.14.first_ref.rest_1_ = bf16[512,128]{1,0:T(8,128)(2,1)S(1)} collective-permute-done((bf16[512,128]{1,0:T(8,128)(2,1)S(1)}, bf16[512,128]{1,0:T(8,128)(2,1)S(1)}, u32[]{:S(2)}, u32[]{:S(2)}) %collective-permute-start.14) | collective-permute-done | bytes 131104 | tf_op jit(solution)/shard_map/ppermute | solution.py:292
  53.0 1.5 %collective-permute-done.17.other_ref = f32[512,128]{1,0:T(8,128)S(1)} collective-permute-done((f32[512,128]{1,0:T(8,128)S(1)}, f32[512,128]{1,0:T(8,128)S(1)}, u32[]{:S(2)}, u32[]{:S(2)}) %collective-permute-start.17) | collective-permute-done | bytes 262176 | tf_op jit(solution)/shard_map/ppermute | solution.py:283
  54.7 2.3 %collective-permute-start.18 = (bf16[512,128]{1,0:T(8,128)(2,1)S(1)}, bf16[512,128]{1,0:T(8,128)(2,1)S(1)}, u32[]{:S(2)}, u32[]{:S(2)}) collective-permute-start(bf16[512,128]{1,0:T(8,128)(2,1)S(1)} %get-tuple-element.33.now_ref.refs_4_.rest_3_), channel_id=1, source_target_pairs={{0,6},{1,7},{2,1},{3,2},{4,3},{5,4},{6,5},{7,0},{8,15},{9,10},{10,... | collective-permute-start | bytes 393224 | tf_op jit(solution)/shard_map/ppermute | solution.py:292
  58.1 1.5 %collective-permute-start.20 = (bf16[512,128]{1,0:T(8,128)(2,1)S(1)}, bf16[512,128]{1,0:T(8,128)(2,1)S(1)}, u32[]{:S(2)}, u32[]{:S(2)}) collective-permute-start(bf16[512,128]{1,0:T(8,128)(2,1)S(1)} %get-tuple-element.34), channel_id=1, source_target_pairs={{0,16},{1,17},{2,18},{3,19},{4,20},{5,21},{6,22},{7,23},{8,24},{9,... | collective-permute-start | bytes 393224 | tf_op jit(solution)/shard_map/ppermute | solution.py:286
  60.2 3.4 %collective-permute-done.18.first_ref.rest_1_ = bf16[512,128]{1,0:T(8,128)(2,1)S(1)} collective-permute-done((bf16[512,128]{1,0:T(8,128)(2,1)S(1)}, bf16[512,128]{1,0:T(8,128)(2,1)S(1)}, u32[]{:S(2)}, u32[]{:S(2)}) %collective-permute-start.18) | collective-permute-done | bytes 131104 | tf_op jit(solution)/shard_map/ppermute | solution.py:292
  64.1 1.5 %collective-permute-done.21.other_ref = f32[512,128]{1,0:T(8,128)S(1)} collective-permute-done((f32[512,128]{1,0:T(8,128)S(1)}, f32[512,128]{1,0:T(8,128)S(1)}, u32[]{:S(2)}, u32[]{:S(2)}) %collective-permute-start.21) | collective-permute-done | bytes 262176 | tf_op jit(solution)/shard_map/ppermute | solution.py:283
  65.8 1.6 %collective-permute-start.22 = (bf16[512,128]{1,0:T(8,128)(2,1)S(1)}, bf16[512,128]{1,0:T(8,128)(2,1)S(1)}, u32[]{:S(2)}, u32[]{:S(2)}) collective-permute-start(bf16[512,128]{1,0:T(8,128)(2,1)S(1)} %get-tuple-element.36), channel_id=1, source_target_pairs={{0,16},{1,17},{2,18},{3,19},{4,20},{5,21},{6,22},{7,23},{8,24},{9,... | collective-permute-start | bytes 393224 | tf_op jit(solution)/shard_map/ppermute | solution.py:286
  67.4 2.1 %collective-permute-start.25 = (bf16[512,128]{1,0:T(8,128)(2,1)S(1)}, bf16[512,128]{1,0:T(8,128)(2,1)S(1)}, u32[]{:S(2)}, u32[]{:S(2)}) collective-permute-start(bf16[512,128]{1,0:T(8,128)(2,1)S(1)} %get-tuple-element.35.refs_5_.rest_3_.now_ref), channel_id=1, source_target_pairs={{0,6},{1,7},{2,1},{3,2},{4,3},{5,4},{6,5},{7,0},{8,15},{9,10},{10,... | collective-permute-start | bytes 393224 | tf_op jit(solution)/shard_map/ppermute | solution.py:292
  71.4 4.3 %collective-permute-done.25.rest_1_.first_ref = bf16[512,128]{1,0:T(8,128)(2,1)S(1)} collective-permute-done((bf16[512,128]{1,0:T(8,128)(2,1)S(1)}, bf16[512,128]{1,0:T(8,128)(2,1)S(1)}, u32[]{:S(2)}, u32[]{:S(2)}) %collective-permute-start.25) | collective-permute-done | bytes 131104 | tf_op jit(solution)/shard_map/ppermute | solution.py:292
  76.7 1.7 %collective-permute-start.23 = (bf16[512,128]{1,0:T(8,128)(2,1)S(1)}, bf16[512,128]{1,0:T(8,128)(2,1)S(1)}, u32[]{:S(2)}, u32[]{:S(2)}) collective-permute-start(bf16[512,128]{1,0:T(8,128)(2,1)S(1)} %collective-permute-done.22.refs_6_.now_ref.refs_5_.rest_0_), channel_id=1, source_target_pairs={{0,6},{1,7},{2,1},{3,2},{4,3},{5,4},{6,5},{7,0},{8,15},{9,10},{10,... | collective-permute-start | bytes 393224 | tf_op jit(solution)/shard_map/ppermute | solution.py:292
  78.4 1.3 %collective-permute-start.24 = (bf16[512,128]{1,0:T(8,128)(2,1)S(1)}, bf16[512,128]{1,0:T(8,128)(2,1)S(1)}, u32[]{:S(2)}, u32[]{:S(2)}) collective-permute-start(bf16[512,128]{1,0:T(8,128)(2,1)S(1)} %collective-permute-done.22.refs_6_.now_ref.refs_5_.rest_0_), channel_id=1, source_target_pairs={{0,2},{1,0},{2,4},{3,1},{4,6},{5,3},{6,7},{7,5},{8,9},{9,11},{10,8... | collective-permute-start | bytes 393224 | tf_op jit(solution)/shard_map/ppermute | solution.py:292
  81.4 4.1 %collective-permute-done.23.refs_1_ = bf16[512,128]{1,0:T(8,128)(2,1)S(1)} collective-permute-done((bf16[512,128]{1,0:T(8,128)(2,1)S(1)}, bf16[512,128]{1,0:T(8,128)(2,1)S(1)}, u32[]{:S(2)}, u32[]{:S(2)}) %collective-permute-start.23) | collective-permute-done | bytes 131104 | tf_op jit(solution)/shard_map/ppermute | solution.py:292
  85.5 1.1 %copy-done.2 = bf16[6,512,128]{2,1,0:T(8,128)(2,1)S(1)} copy-done((bf16[6,512,128]{2,1,0:T(8,128)(2,1)S(1)}, bf16[6,512,128]{2,1,0:T(8,128)(2,1)}, u32[]{:S(2)}) %copy-start.2) | copy-done | bytes 786456
  88.1 5.4 %collective-permute-done.29.rest_1_ = bf16[512,128]{1,0:T(8,128)(2,1)S(1)} collective-permute-done((bf16[512,128]{1,0:T(8,128)(2,1)S(1)}, bf16[512,128]{1,0:T(8,128)(2,1)S(1)}, u32[]{:S(2)}, u32[]{:S(2)}) %collective-permute-start.29) | collective-permute-done | bytes 131104 | tf_op jit(solution)/shard_map/ppermute | solution.py:286
  (65 shorter events, 18.6 us)
Async XLA Ops:
  0.6 7.7 %copy-start.1 = (bf16[4,128,128]{2,1,0:T(8,128)(2,1)S(1)}, bf16[4,128,128]{2,1,0:T(8,128)(2,1)}, u32[]{:S(2)}) copy-start(bf16[4,128,128]{2,1,0:T(8,128)(2,1)} %inverse_ref.9) | copy-start | bytes 393220
  0.7 7.7 %copy-start = (bf16[6,512,128]{2,1,0:T(8,128)(2,1)S(1)}, bf16[6,512,128]{2,1,0:T(8,128)(2,1)}, u32[]{:S(2)}) copy-start(bf16[6,512,128]{2,1,0:T(8,128)(2,1)} %excitation_ref.9) | copy-start | bytes 2359300
  4.8 10.3 %collective-permute-start.1 = (bf16[512,1280]{1,0:T(8,128)(2,1)S(1)}, bf16[512,1280]{1,0:T(8,128)(2,1)S(1)}, u32[]{:S(2)}, u32[]{:S(2)}) collective-permute-start(bf16[512,1280]{1,0:T(8,128)(2,1)S(1)} %get-tuple-element.24), channel_id=1, source_target_pairs={{0,8},{1,9},{2,10},{3,11},{4,12},{5,13},{6,14},{7,15},{8,0},{9,1},... | collective-permute-start | bytes 3932168 | tf_op jit(solution)/shard_map/ppermute | solution.py:283
  5.3 3.0 %collective-permute-start = (f32[512,128]{1,0:T(8,128)S(1)}, f32[512,128]{1,0:T(8,128)S(1)}, u32[]{:S(2)}, u32[]{:S(2)}) collective-permute-start(f32[512,128]{1,0:T(8,128)S(1)} %bitcast.4), channel_id=1, source_target_pairs={{0,8},{1,9},{2,10},{3,11},{4,12},{5,13},{6,14},{7,15},{8,0},{9,1},... | collective-permute-start | bytes 786440 | tf_op jit(solution)/shard_map/ppermute | solution.py:283
  8.6 10.0 %collective-permute-start.2 = (bf16[512,128]{1,0:T(8,128)(2,1)S(1)}, bf16[512,128]{1,0:T(8,128)(2,1)S(1)}, u32[]{:S(2)}, u32[]{:S(2)}) collective-permute-start(bf16[512,128]{1,0:T(8,128)(2,1)S(1)} %shard_map.69.now_ref.rest_3_.refs_0_), channel_id=1, source_target_pairs={{0,6},{1,7},{2,1},{3,2},{4,3},{5,4},{6,5},{7,0},{8,15},{9,10},{10,... | collective-permute-start | bytes 393224 | tf_op jit(solution)/shard_map/ppermute | solution.py:292
  13.6 5.9 %collective-permute-start.3 = (bf16[512,128]{1,0:T(8,128)(2,1)S(1)}, bf16[512,128]{1,0:T(8,128)(2,1)S(1)}, u32[]{:S(2)}, u32[]{:S(2)}) collective-permute-start(bf16[512,128]{1,0:T(8,128)(2,1)S(1)} %shard_map.69.now_ref.rest_3_.refs_0_), channel_id=1, source_target_pairs={{0,2},{1,0},{2,4},{3,1},{4,6},{5,3},{6,7},{7,5},{8,9},{9,11},{10,8... | collective-permute-start | bytes 393224 | tf_op jit(solution)/shard_map/ppermute | solution.py:292
  13.6 6.2 %collective-permute-start.4 = (bf16[512,128]{1,0:T(8,128)(2,1)S(1)}, bf16[512,128]{1,0:T(8,128)(2,1)S(1)}, u32[]{:S(2)}, u32[]{:S(2)}) collective-permute-start(bf16[512,128]{1,0:T(8,128)(2,1)S(1)} %shard_map.69.now_ref.rest_3_.refs_0_), channel_id=1, source_target_pairs={{0,16},{1,17},{2,18},{3,19},{4,20},{5,21},{6,22},{7,23},{8,24},{9,... | collective-permute-start | bytes 393224 | tf_op jit(solution)/shard_map/ppermute | solution.py:286
  20.3 1.6 %collective-permute-start.5 = (f32[512,128]{1,0:T(8,128)S(1)}, f32[512,128]{1,0:T(8,128)S(1)}, u32[]{:S(2)}, u32[]{:S(2)}) collective-permute-start(f32[512,128]{1,0:T(8,128)S(1)} %shard_map.72.mine_ref), channel_id=1, source_target_pairs={{0,8},{1,9},{2,10},{3,11},{4,12},{5,13},{6,14},{7,15},{8,0},{9,1},... | collective-permute-start | bytes 786440 | tf_op jit(solution)/shard_map/ppermute | solution.py:283
  22.1 7.9 %collective-permute-start.6 = (bf16[512,128]{1,0:T(8,128)(2,1)S(1)}, bf16[512,128]{1,0:T(8,128)(2,1)S(1)}, u32[]{:S(2)}, u32[]{:S(2)}) collective-permute-start(bf16[512,128]{1,0:T(8,128)(2,1)S(1)} %get-tuple-element.26.now_ref.rest_3_.refs_1_), channel_id=1, source_target_pairs={{0,6},{1,7},{2,1},{3,2},{4,3},{5,4},{6,5},{7,0},{8,15},{9,10},{10,... | collective-permute-start | bytes 393224 | tf_op jit(solution)/shard_map/ppermute | solution.py:292
  25.1 6.1 %collective-permute-start.7 = (bf16[512,128]{1,0:T(8,128)(2,1)S(1)}, bf16[512,128]{1,0:T(8,128)(2,1)S(1)}, u32[]{:S(2)}, u32[]{:S(2)}) collective-permute-start(bf16[512,128]{1,0:T(8,128)(2,1)S(1)} %get-tuple-element.26.now_ref.rest_3_.refs_1_), channel_id=1, source_target_pairs={{0,2},{1,0},{2,4},{3,1},{4,6},{5,3},{6,7},{7,5},{8,9},{9,11},{10,8... | collective-permute-start | bytes 393224 | tf_op jit(solution)/shard_map/ppermute | solution.py:292
  25.1 6.1 %collective-permute-start.8 = (bf16[512,128]{1,0:T(8,128)(2,1)S(1)}, bf16[512,128]{1,0:T(8,128)(2,1)S(1)}, u32[]{:S(2)}, u32[]{:S(2)}) collective-permute-start(bf16[512,128]{1,0:T(8,128)(2,1)S(1)} %get-tuple-element.28), channel_id=1, source_target_pairs={{0,16},{1,17},{2,18},{3,19},{4,20},{5,21},{6,22},{7,23},{8,24},{9,... | collective-permute-start | bytes 393224 | tf_op jit(solution)/shard_map/ppermute | solution.py:286
  31.7 1.6 %collective-permute-start.9 = (f32[512,128]{1,0:T(8,128)S(1)}, f32[512,128]{1,0:T(8,128)S(1)}, u32[]{:S(2)}, u32[]{:S(2)}) collective-permute-start(f32[512,128]{1,0:T(8,128)S(1)} %shard_map.75.mine_ref), channel_id=1, source_target_pairs={{0,8},{1,9},{2,10},{3,11},{4,12},{5,13},{6,14},{7,15},{8,0},{9,1},... | collective-permute-start | bytes 786440 | tf_op jit(solution)/shard_map/ppermute | solution.py:283
  33.5 8.0 %collective-permute-start.10 = (bf16[512,128]{1,0:T(8,128)(2,1)S(1)}, bf16[512,128]{1,0:T(8,128)(2,1)S(1)}, u32[]{:S(2)}, u32[]{:S(2)}) collective-permute-start(bf16[512,128]{1,0:T(8,128)(2,1)S(1)} %get-tuple-element.29.now_ref.rest_3_.refs_2_), channel_id=1, source_target_pairs={{0,6},{1,7},{2,1},{3,2},{4,3},{5,4},{6,5},{7,0},{8,15},{9,10},{10,... | collective-permute-start | bytes 393224 | tf_op jit(solution)/shard_map/ppermute | solution.py:292
  35.3 6.4 %collective-permute-start.11 = (bf16[512,128]{1,0:T(8,128)(2,1)S(1)}, bf16[512,128]{1,0:T(8,128)(2,1)S(1)}, u32[]{:S(2)}, u32[]{:S(2)}) collective-permute-start(bf16[512,128]{1,0:T(8,128)(2,1)S(1)} %get-tuple-element.29.now_ref.rest_3_.refs_2_), channel_id=1, source_target_pairs={{0,2},{1,0},{2,4},{3,1},{4,6},{5,3},{6,7},{7,5},{8,9},{9,11},{10,8... | collective-permute-start | bytes 393224 | tf_op jit(solution)/shard_map/ppermute | solution.py:292
  35.9 5.8 %collective-permute-start.12 = (bf16[512,128]{1,0:T(8,128)(2,1)S(1)}, bf16[512,128]{1,0:T(8,128)(2,1)S(1)}, u32[]{:S(2)}, u32[]{:S(2)}) collective-permute-start(bf16[512,128]{1,0:T(8,128)(2,1)S(1)} %get-tuple-element.30), channel_id=1, source_target_pairs={{0,16},{1,17},{2,18},{3,19},{4,20},{5,21},{6,22},{7,23},{8,24},{9,... | collective-permute-start | bytes 393224 | tf_op jit(solution)/shard_map/ppermute | solution.py:286
  42.1 1.6 %collective-permute-start.13 = (f32[512,128]{1,0:T(8,128)S(1)}, f32[512,128]{1,0:T(8,128)S(1)}, u32[]{:S(2)}, u32[]{:S(2)}) collective-permute-start(f32[512,128]{1,0:T(8,128)S(1)} %shard_map.78.mine_ref), channel_id=1, source_target_pairs={{0,8},{1,9},{2,10},{3,11},{4,12},{5,13},{6,14},{7,15},{8,0},{9,1},... | collective-permute-start | bytes 786440 | tf_op jit(solution)/shard_map/ppermute | solution.py:283
  43.9 8.6 %collective-permute-start.14 = (bf16[512,128]{1,0:T(8,128)(2,1)S(1)}, bf16[512,128]{1,0:T(8,128)(2,1)S(1)}, u32[]{:S(2)}, u32[]{:S(2)}) collective-permute-start(bf16[512,128]{1,0:T(8,128)(2,1)S(1)} %get-tuple-element.31.now_ref.rest_3_.refs_3_), channel_id=1, source_target_pairs={{0,6},{1,7},{2,1},{3,2},{4,3},{5,4},{6,5},{7,0},{8,15},{9,10},{10,... | collective-permute-start | bytes 393224 | tf_op jit(solution)/shard_map/ppermute | solution.py:292
  46.1 6.4 %collective-permute-start.15 = (bf16[512,128]{1,0:T(8,128)(2,1)S(1)}, bf16[512,128]{1,0:T(8,128)(2,1)S(1)}, u32[]{:S(2)}, u32[]{:S(2)}) collective-permute-start(bf16[512,128]{1,0:T(8,128)(2,1)S(1)} %get-tuple-element.31.now_ref.rest_3_.refs_3_), channel_id=1, source_target_pairs={{0,2},{1,0},{2,4},{3,1},{4,6},{5,3},{6,7},{7,5},{8,9},{9,11},{10,8... | collective-permute-start | bytes 393224 | tf_op jit(solution)/shard_map/ppermute | solution.py:292
  47.0 5.5 %collective-permute-start.16 = (bf16[512,128]{1,0:T(8,128)(2,1)S(1)}, bf16[512,128]{1,0:T(8,128)(2,1)S(1)}, u32[]{:S(2)}, u32[]{:S(2)}) collective-permute-start(bf16[512,128]{1,0:T(8,128)(2,1)S(1)} %get-tuple-element.32), channel_id=1, source_target_pairs={{0,16},{1,17},{2,18},{3,19},{4,20},{5,21},{6,22},{7,23},{8,24},{9,... | collective-permute-start | bytes 393224 | tf_op jit(solution)/shard_map/ppermute | solution.py:286
  52.9 1.6 %collective-permute-start.17 = (f32[512,128]{1,0:T(8,128)S(1)}, f32[512,128]{1,0:T(8,128)S(1)}, u32[]{:S(2)}, u32[]{:S(2)}) collective-permute-start(f32[512,128]{1,0:T(8,128)S(1)} %shard_map.81.mine_ref), channel_id=1, source_target_pairs={{0,8},{1,9},{2,10},{3,11},{4,12},{5,13},{6,14},{7,15},{8,0},{9,1},... | collective-permute-start | bytes 786440 | tf_op jit(solution)/shard_map/ppermute | solution.py:283
  54.7 8.8 %collective-permute-start.18 = (bf16[512,128]{1,0:T(8,128)(2,1)S(1)}, bf16[512,128]{1,0:T(8,128)(2,1)S(1)}, u32[]{:S(2)}, u32[]{:S(2)}) collective-permute-start(bf16[512,128]{1,0:T(8,128)(2,1)S(1)} %get-tuple-element.33.now_ref.refs_4_.rest_3_), channel_id=1, source_target_pairs={{0,6},{1,7},{2,1},{3,2},{4,3},{5,4},{6,5},{7,0},{8,15},{9,10},{10,... | collective-permute-start | bytes 393224 | tf_op jit(solution)/shard_map/ppermute | solution.py:292
  57.1 6.5 %collective-permute-start.19 = (bf16[512,128]{1,0:T(8,128)(2,1)S(1)}, bf16[512,128]{1,0:T(8,128)(2,1)S(1)}, u32[]{:S(2)}, u32[]{:S(2)}) collective-permute-start(bf16[512,128]{1,0:T(8,128)(2,1)S(1)} %get-tuple-element.33.now_ref.refs_4_.rest_3_), channel_id=1, source_target_pairs={{0,2},{1,0},{2,4},{3,1},{4,6},{5,3},{6,7},{7,5},{8,9},{9,11},{10,8... | collective-permute-start | bytes 393224 | tf_op jit(solution)/shard_map/ppermute | solution.py:292
  58.1 5.5 %collective-permute-start.20 = (bf16[512,128]{1,0:T(8,128)(2,1)S(1)}, bf16[512,128]{1,0:T(8,128)(2,1)S(1)}, u32[]{:S(2)}, u32[]{:S(2)}) collective-permute-start(bf16[512,128]{1,0:T(8,128)(2,1)S(1)} %get-tuple-element.34), channel_id=1, source_target_pairs={{0,16},{1,17},{2,18},{3,19},{4,20},{5,21},{6,22},{7,23},{8,24},{9,... | collective-permute-start | bytes 393224 | tf_op jit(solution)/shard_map/ppermute | solution.py:286
  64.0 1.6 %collective-permute-start.21 = (f32[512,128]{1,0:T(8,128)S(1)}, f32[512,128]{1,0:T(8,128)S(1)}, u32[]{:S(2)}, u32[]{:S(2)}) collective-permute-start(f32[512,128]{1,0:T(8,128)S(1)} %shard_map.84.mine_ref), channel_id=1, source_target_pairs={{0,8},{1,9},{2,10},{3,11},{4,12},{5,13},{6,14},{7,15},{8,0},{9,1},... | collective-permute-start | bytes 786440 | tf_op jit(solution)/shard_map/ppermute | solution.py:283
  65.8 5.6 %collective-permute-start.22 = (bf16[512,128]{1,0:T(8,128)(2,1)S(1)}, bf16[512,128]{1,0:T(8,128)(2,1)S(1)}, u32[]{:S(2)}, u32[]{:S(2)}) collective-permute-start(bf16[512,128]{1,0:T(8,128)(2,1)S(1)} %get-tuple-element.36), channel_id=1, source_target_pairs={{0,16},{1,17},{2,18},{3,19},{4,20},{5,21},{6,22},{7,23},{8,24},{9,... | collective-permute-start | bytes 393224 | tf_op jit(solution)/shard_map/ppermute | solution.py:286
  67.4 8.4 %collective-permute-start.25 = (bf16[512,128]{1,0:T(8,128)(2,1)S(1)}, bf16[512,128]{1,0:T(8,128)(2,1)S(1)}, u32[]{:S(2)}, u32[]{:S(2)}) collective-permute-start(bf16[512,128]{1,0:T(8,128)(2,1)S(1)} %get-tuple-element.35.refs_5_.rest_3_.now_ref), channel_id=1, source_target_pairs={{0,6},{1,7},{2,1},{3,2},{4,3},{5,4},{6,5},{7,0},{8,15},{9,10},{10,... | collective-permute-start | bytes 393224 | tf_op jit(solution)/shard_map/ppermute | solution.py:292
  69.5 6.4 %collective-permute-start.26 = (bf16[512,128]{1,0:T(8,128)(2,1)S(1)}, bf16[512,128]{1,0:T(8,128)(2,1)S(1)}, u32[]{:S(2)}, u32[]{:S(2)}) collective-permute-start(bf16[512,128]{1,0:T(8,128)(2,1)S(1)} %get-tuple-element.35.refs_5_.rest_3_.now_ref), channel_id=1, source_target_pairs={{0,2},{1,0},{2,4},{3,1},{4,6},{5,3},{6,7},{7,5},{8,9},{9,11},{10,8... | collective-permute-start | bytes 393224 | tf_op jit(solution)/shard_map/ppermute | solution.py:292
  76.6 10.9 %collective-permute-start.28 = (f32[512,128]{1,0:T(8,128)S(1)}, f32[512,128]{1,0:T(8,128)S(1)}, u32[]{:S(2)}, u32[]{:S(2)}) collective-permute-start(f32[512,128]{1,0:T(8,128)S(1)} %get-tuple-element.40), channel_id=1, source_target_pairs={{0,8},{1,9},{2,10},{3,11},{4,12},{5,13},{6,14},{7,15},{8,0},{9,1},... | collective-permute-start | bytes 786440 | tf_op jit(solution)/shard_map/ppermute | solution.py:283
  76.7 8.8 %collective-permute-start.23 = (bf16[512,128]{1,0:T(8,128)(2,1)S(1)}, bf16[512,128]{1,0:T(8,128)(2,1)S(1)}, u32[]{:S(2)}, u32[]{:S(2)}) collective-permute-start(bf16[512,128]{1,0:T(8,128)(2,1)S(1)} %collective-permute-done.22.refs_6_.now_ref.refs_5_.rest_0_), channel_id=1, source_target_pairs={{0,6},{1,7},{2,1},{3,2},{4,3},{5,4},{6,5},{7,0},{8,15},{9,10},{10,... | collective-permute-start | bytes 393224 | tf_op jit(solution)/shard_map/ppermute | solution.py:292
  78.4 7.1 %collective-permute-start.24 = (bf16[512,128]{1,0:T(8,128)(2,1)S(1)}, bf16[512,128]{1,0:T(8,128)(2,1)S(1)}, u32[]{:S(2)}, u32[]{:S(2)}) collective-permute-start(bf16[512,128]{1,0:T(8,128)(2,1)S(1)} %collective-permute-done.22.refs_6_.now_ref.refs_5_.rest_0_), channel_id=1, source_target_pairs={{0,2},{1,0},{2,4},{3,1},{4,6},{5,3},{6,7},{7,5},{8,9},{9,11},{10,8... | collective-permute-start | bytes 393224 | tf_op jit(solution)/shard_map/ppermute | solution.py:292
  87.4 6.1 %collective-permute-start.27 = (f32[512,128]{1,0:T(8,128)S(1)}, f32[512,128]{1,0:T(8,128)S(1)}, u32[]{:S(2)}, u32[]{:S(2)}) collective-permute-start(f32[512,128]{1,0:T(8,128)S(1)} %get-tuple-element.38), channel_id=1, source_target_pairs={{0,8},{1,9},{2,10},{3,11},{4,12},{5,13},{6,14},{7,15},{8,0},{9,1},... | collective-permute-start | bytes 786440 | tf_op jit(solution)/shard_map/ppermute | solution.py:283
  87.5 6.0 %collective-permute-start.29 = (bf16[512,128]{1,0:T(8,128)(2,1)S(1)}, bf16[512,128]{1,0:T(8,128)(2,1)S(1)}, u32[]{:S(2)}, u32[]{:S(2)}) collective-permute-start(bf16[512,128]{1,0:T(8,128)(2,1)S(1)} %get-tuple-element.42), channel_id=1, source_target_pairs={{0,16},{1,17},{2,18},{3,19},{4,20},{5,21},{6,22},{7,23},{8,24},{9,... | collective-permute-start | bytes 393224 | tf_op jit(solution)/shard_map/ppermute | solution.py:286
  (4 other events, 8.2 us)

commit v5 on v4

v5 whole, which is shorter than its diff:
```python
import functools

import jax
import jax.numpy as jnp
from jax import lax
from jax.experimental import pallas as pl
from jax.experimental.pallas import tpu as pltpu
from jax.sharding import PartitionSpec as P

F32 = jnp.float32
BF16 = jnp.bfloat16
AXES = ("delay", "surface")
VMEM = pl.BlockSpec(memory_space=pltpu.VMEM)
MIB = 1024 * 1024
TOKEN = jax.ShapeDtypeStruct((8, 128), F32)


def dot(a, b):
    return jnp.dot(a, b, preferred_element_type=F32)


def place():
    lag = lax.axis_index("delay")
    return lax.rem(lag, 2), lax.div(lag, 2)


def cost(microseconds):
    moved = int(3.6e6 * microseconds)
    return pl.CostEstimate(flops=0, bytes_accessed=moved, transcendentals=0)


def call(body, outs, args, after=None, microseconds=0.5):
    specs = [VMEM] * len(args)
    if after is not None:
        args, specs = [after] + args, [pl.BlockSpec(memory_space=pl.ANY)] + specs
        body = functools.partial(skip_first, body)
    return pl.pallas_call(
        body,
        out_shape=tuple(outs),
        in_specs=specs,
        out_specs=tuple(VMEM for _ in outs),
        cost_estimate=cost(microseconds),
        compiler_params=pltpu.CompilerParams(vmem_limit_bytes=8 * MIB),
    )(*args)


def skip_first(body, _, *refs):
    body(*refs)


def choose(*cases):
    *pairs, value = cases
    for when, other in reversed(pairs):
        value = jnp.where(when, other, value)
    return value


def far_next(s, count):
    return choose((s == 0, count - 2), (s == 1, count - 1), (s == count - 1, 0), s - 1)


def far_last(s, count):
    return choose((s == 0, count - 1), (s == count - 2, 0), (s == count - 1, 1), s + 1)


def close_next(s, count):
    even = lax.rem(s, 2) == 0
    return choose((s == 1, 0), (s == count - 2, count - 1), (even, s + 2), s - 2)


def close_last(s, count):
    even = lax.rem(s, 2) == 0
    return choose((s == 0, 1), (s == count - 1, count - 2), (even, s - 2), s + 2)


def tour(far, count):
    if far:
        return [0] + list(range(count - 2, 0, -1)) + [count - 1]
    return list(range(0, count, 2)) + list(range(count - 1, 0, -2))


def spread_body(groups, pattern_ref, entries_ref, keep_ref, own_ref, *rest):
    *send_refs, here_ref, all_ref, sems = rest
    core, _ = place()
    blocks, slots, size, _ = entries_ref.shape
    copies = [
        pltpu.make_async_copy(entries_ref.at[row], here_ref.at[row], sems.at[row])
        for row in range(blocks)
    ]
    for copy in copies:
        copy.start()
    here = lax.axis_index("surface")
    brought = (
        (far_last(here, groups), 0),
        (close_last(here, groups), 1),
        (far_next(here, groups), 2),
        (close_next(here, groups), 3),
    )
    mine = 2 * blocks * core
    all_ref[...] = jnp.zeros_like(all_ref)
    for row in range(blocks):
        copies[row].wait()
        rows = slice(row * size, (row + 1) * size)
        for slot in range(slots):
            block = pattern_ref[row, slot]
            group = lax.div(block, blocks)
            part = 4
            for source, number in brought:
                part = jnp.where(group == source, number, part)
            column = part * blocks + block - group * blocks
            columns = pl.ds(pl.multiple_of(column * size, size), size)
            all_ref[rows, columns] = here_ref[row, slot]
        width = 2 * blocks * size
        first = pl.ds(pl.multiple_of(core * width, width), width)
        second = pl.ds(pl.multiple_of((1 - core) * width, width), width)
        keep_ref[rows, :] = all_ref[rows, first]
        send_refs[row][...] = all_ref[rows, second]
        own_ref[rows, :] = all_ref[rows, 2 * width :]


def spread(entries, pattern, groups):
    blocks, slots, size, _ = entries.shape
    side = blocks * size

    def matrix(rows, columns):
        return jax.ShapeDtypeStruct((rows, columns), entries.dtype)

    return pl.pallas_call(
        functools.partial(spread_body, groups),
        out_shape=(matrix(side, 2 * side), matrix(side, side), *[matrix(size, 2 * side)] * blocks),
        in_specs=[
            pl.BlockSpec(memory_space=pltpu.SMEM),
            pl.BlockSpec(memory_space=pltpu.HBM),
        ],
        out_specs=(VMEM,) * (blocks + 2),
        scratch_shapes=[
            pltpu.VMEM(entries.shape, entries.dtype),
            pltpu.VMEM((side, 5 * side), entries.dtype),
            pltpu.SemaphoreType.DMA((blocks,)),
        ],
        cost_estimate=cost(4),
        compiler_params=pltpu.CompilerParams(vmem_limit_bytes=54 * MIB),
    )(pattern, entries)


def arrange_body(kept_ref, *rest):
    *got_refs, near_ref, far_ref = rest
    core, _ = place()

    def put(got_to_ref, kept_to_ref):
        kept_to_ref[...] = kept_ref[...]
        for i, got_ref in enumerate(got_refs):
            size = got_ref.shape[0]
            got_to_ref[i * size : (i + 1) * size, :] = got_ref[...]

    @pl.when(core == 0)
    def _():
        put(far_ref, near_ref)

    @pl.when(core == 1)
    def _():
        put(near_ref, far_ref)


def window(matrix_ref, first_ref, second_ref):
    rows = first_ref.shape[0]
    return dot(matrix_ref[:, :rows], first_ref[...]) + dot(matrix_ref[:, rows:], second_ref[...])


def early_body(own_ref, now_ref, *rest):
    *last, out_ref = rest
    core, _ = place()
    if last:
        far_ref, first_ref, second_ref, before_ref = last
        local = jnp.where(core == 0, now_ref[...], before_ref[...])
        out_ref[...] = dot(own_ref[...], local) + window(far_ref, first_ref, second_ref)
    else:
        local = jnp.where(core == 0, now_ref[...], jnp.zeros_like(now_ref))
        out_ref[...] = dot(own_ref[...], local)


def came(step, pairs, field_ref, history):
    core, pair = place()
    value = jnp.where(pair == pairs - 1, 0.0, field_ref[...].astype(F32))
    if history:
        mine_ref, other_ref = history
        past = jnp.where(pair == step, other_ref[...], mine_ref[...])
        special = jnp.logical_or(pair == step, pair == step + 1)
        value = jnp.where(special, jnp.where(core == 0, past, 0.0), value)
    return value


def late_body(step, pairs, near_ref, first_ref, second_ref, early_ref, field_ref, *rest):
    *history, out_ref = rest
    total = early_ref[...] + window(near_ref, first_ref, second_ref)
    out_ref[...] = (total + came(step, pairs, field_ref, history)).astype(BF16)


def last_body(near_ref, first_ref, second_ref, early_ref, far_ref, own_ref, now_ref, even_ref, odd_ref):
    core, _ = place()
    even_ref[...] = early_ref[...] + window(near_ref, first_ref, second_ref)
    local = jnp.where(core == 1, now_ref[...], jnp.zeros_like(now_ref))
    odd_ref[...] = window(far_ref, first_ref, second_ref) + dot(own_ref[...], local)


def share_body(step, steps, pairs, even_ref, odd_ref, field_ref, *rest):
    *history, keep_ref, send_ref, field_out_ref = rest
    core, pair = place()
    even = even_ref[...] + came(step, pairs, field_ref, history)
    odd = odd_ref[...]
    ended = pair == step - steps
    late = field_ref[...].astype(F32)
    keep_ref[...] = jnp.where(ended, late, jnp.where(core == 1, odd, even))
    send_ref[...] = jnp.where(ended, late, jnp.where(core == 0, odd, even)).astype(BF16)
    field_out_ref[...] = even.astype(BF16)


def finish_body(step, steps, mine_ref, other_ref, *rest):
    *earlier, result_ref = rest
    core, pair = place()
    field = mine_ref[...] + other_ref[...].astype(F32)
    if earlier:
        before = earlier[0][...]
        ended = pair == step - steps
        adds = jnp.logical_and(ended, core == 1)
        field = jnp.where(
            adds, before + field, jnp.where(pair == step - (steps - 1), field, before)
        )
    result_ref[...] = field


def collect_body(pairs, *refs):
    *seen, out_ref, token_ref = refs
    token_ref[...] = jnp.zeros_like(token_ref)
    _, pair = place()
    for step in range(out_ref.shape[0]):
        value = seen[step][...]
        for later in range(1, pairs):
            value = jnp.where(pair == later, seen[step + later][...], value)
        out_ref[step] = value


def solve(inverse_ref, rhs, out_ref, keep, other):
    size = inverse_ref.shape[1]
    fresh = []
    for i in range(inverse_ref.shape[0]):
        rows = slice(i * size, (i + 1) * size)
        block = dot(inverse_ref[i], rhs[rows]).astype(BF16)
        fresh.append(jnp.where(keep, block, other[rows]))
        out_ref[rows, :] = fresh[-1]
    return fresh


def first_history_body(history_ref, other_history_ref, out_ref):
    core, _ = place()
    out_ref[...] = jnp.where(core == 0, history_ref[...], other_history_ref[...])


def start_body(inverse_ref, excitation_ref, history_ref, out_ref):
    _, pair = place()
    rhs = (excitation_ref[0].astype(F32) - history_ref[...]).astype(BF16)
    solve(inverse_ref, rhs, out_ref, pair == 0, jnp.zeros_like(rhs))


def next_body(step, inverse_ref, excitation_ref, mine_ref, other_ref, came_ref, out_ref, going_ref):
    _, pair = place()
    field = mine_ref[...].astype(F32) + other_ref[...].astype(F32)
    rhs = (excitation_ref[step + 1].astype(F32) - field).astype(BF16)
    first_pair = pair == 0
    size = inverse_ref.shape[1]
    for i, block in enumerate(solve(inverse_ref, rhs, out_ref, first_pair, came_ref)):
        rows = slice(i * size, (i + 1) * size)
        going_ref[rows, :] = jnp.where(first_pair, block, mine_ref[rows, :])


def per_device(lagged_block_entries, pattern, diagonal_block_inverses, excitation, history):
    lags, groups = lax.axis_size("delay"), lax.axis_size("surface")
    pairs = lags // 2
    entries = lagged_block_entries[0]
    blocks, slots, size, _ = entries.shape
    steps, rows, columns = excitation.shape

    def device(d, s):
        return d * groups + s

    def everyone(move):
        return [
            (device(d, s), device(*move(d, s))) for d in range(lags) for s in range(groups)
        ]

    def swapped(value):
        return lax.ppermute(value, AXES, everyone(lambda d, s: (d ^ 1, s)))

    def pair_moved(value, hop):
        return lax.ppermute(value, AXES, everyone(lambda d, s: ((d + 2 * hop) % lags, s)))

    def halo(value, far):
        order = tour(far, groups)
        following = dict(zip(order, order[1:] + order[:1]))
        preceding = {t: s for s, t in following.items()}
        return lax.ppermute(
            value,
            AXES,
            everyone(lambda d, s: (d, following[s] if d % 2 == 0 else preceding[s])),
        )

    other_history = swapped(history[0])
    field_shape = jax.ShapeDtypeStruct((rows, columns), F32)
    current_shape = jax.ShapeDtypeStruct((rows, columns), BF16)
    kept, own, *sent = spread(entries, pattern[0], groups)
    (first_history,) = call(first_history_body, [field_shape], [history[0], other_history])
    (current,) = call(
        start_body,
        [current_shape],
        [diagonal_block_inverses, excitation, first_history],
    )
    matrix_shape = jax.ShapeDtypeStruct(kept.shape, kept.dtype)
    near, far = call(arrange_body, [matrix_shape, matrix_shape], [kept] + [swapped(part) for part in sent])

    going = field = current
    seen = []
    previous = []
    result = []
    out = collected = None
    rounds = steps + pairs - 1
    windows = None
    for step in range(rounds):
        seen.append(current)
        if step == rounds - 1:
            out, collected = call(
                functools.partial(collect_body, pairs),
                [jax.ShapeDtypeStruct(excitation.shape, BF16), TOKEN],
                seen,
            )
        first, second = windows or (halo(current, True), halo(current, False))
        if pairs == 2:
            current_in = field_in = pair_moved(going, 1)
        else:
            current_in, field_in = pair_moved(current, 1), pair_moved(field, -1)
        last = [far, *previous] if previous else []
        (early,) = call(early_body, [field_shape], [own, current] + last)
        received = [near, first, second, early]
        past = [history[0], other_history] if step < pairs else []
        previous = [first, second, current]
        if step < steps - 1:
            (field,) = call(
                functools.partial(late_body, step, pairs), [current_shape], received + [field_in] + past
            )
            current, going = call(
                functools.partial(next_body, step),
                [current_shape, current_shape],
                [diagonal_block_inverses, excitation, field, swapped(field), current_in],
            )
        else:
            if step < rounds - 1:
                windows = halo(current_in, True), halo(current_in, False)
            even, odd = call(
                last_body,
                [field_shape, field_shape],
                received + [far, own, current],
                after=collected,
                microseconds=0.5 if step < rounds - 1 else 20,
            )
            mine, send, field = call(
                functools.partial(share_body, step, steps, pairs),
                [field_shape, current_shape, current_shape],
                [even, odd, field_in] + past,
            )
            (result,) = call(
                functools.partial(finish_body, step, steps),
                [field_shape],
                [mine, swapped(send)] + ([result] if step >= steps else []),
            )
            current, going = current_in, field
    return (out, result[None])


def solution(mesh):
    placed = (
        P("delay", "surface", None, None, None),
        P("delay", "surface", None),
        P("surface", None, None),
        P(None, "surface", None),
        P("delay", "surface", None),
    )
    return jax.shard_map(
        per_device,
        mesh=mesh,
        in_specs=placed,
        out_specs=(P(None, "surface", None), P("delay", "surface", None)),
        check_vma=False,
    )
```

time: 94.5 us -> 82.4 us (0.87)
  waiting for transfers between devices: 43.6 us -> 36.4 us
  starting transfers between devices: 33.9 us -> 29.4 us
  local copies, waits for them, and re-layouts: 3.5 us -> 0.02 us
  Pallas kernels: 12.4 us -> 15.5 us
    unnamed x12 -> x10, local copies, waits for them, and re-layouts: 3.5 us -> 0.02 us
    ppermute x7, starting transfers between devices: 9.6 us -> 6.81 us  [pair_moved(): lax.ppermute(value, AXES, everyone(lambda d, s: ((d + 2 * hop) % lags, s)))]
    ppermute x14, waiting for transfers between devices: 27.1 us -> 24.5 us  [halo(): lax.ppermute(value, AXES, everyone(lambda d, s: (d, following[s] if d % 2...]
    ppermute x9 -> x12, waiting for transfers between devices: 10.5 us -> 7.9 us  [swapped(): return lax.ppermute(value, AXES, everyone(lambda d, s: (d ^ 1, s)))]
    ppermute x14, starting transfers between devices: 23.1 us -> 20.5 us  [halo(): lax.ppermute(value, AXES, everyone(lambda d, s: (d, following[s] if d % 2...]
    pallas_call x1, Pallas kernels: 1.79 us -> 3.86 us  [spread(): pl.pallas_call(functools.partial(spread_body, groups), out_shape=(matrix(...]
    ppermute x7, waiting for transfers between devices: 6.05 us -> 4 us  [pair_moved(): lax.ppermute(value, AXES, everyone(lambda d, s: ((d + 2 * hop) % lags, s)))]
    pallas_call x24 -> x27, Pallas kernels: 10.6 us -> 11.6 us  [call(): pl.pallas_call(body, out_shape=tuple(outs), in_specs=specs, out_specs=tup...]
  transfers between devices with their start and end apart: 30 -> 33, of which waited for: 20 -> 23; matrix products, arithmetic and copies ran while one was open for 0% -> 0% of each run, Pallas kernels for 6% -> 14%
where the time goes in v5:
time: 82.4 us; the launch traced here: 82.3 us
  waiting for transfers between devices  36.4 us (44%)
  starting transfers between devices  29.4 us (36%)
  Pallas kernels  15.5 us (19%)
  between operations  0.95 us (1%)
    ppermute x14, waiting for transfers between devices, halo(): lax.ppermute(value, AXES, everyone(lambda d, s: (d, following[s] if d % 2...  24.5 us
    ppermute x14, starting transfers between devices, halo(): lax.ppermute(value, AXES, everyone(lambda d, s: (d, following[s] if d % 2...  20.5 us
    pallas_call x27, Pallas kernels, call(): pl.pallas_call(body, out_shape=tuple(outs), in_specs=specs, out_specs=tup...  11.6 us
    ppermute x12, waiting for transfers between devices, swapped(): return lax.ppermute(value, AXES, everyone(lambda d, s: (d ^ 1, s)))  7.9 us
    ppermute x7, starting transfers between devices, pair_moved(): lax.ppermute(value, AXES, everyone(lambda d, s: ((d + 2 * hop) % lags, s)))  6.81 us
    ppermute x7, waiting for transfers between devices, pair_moved(): lax.ppermute(value, AXES, everyone(lambda d, s: ((d + 2 * hop) % lags, s)))  4 us
    pallas_call x1, Pallas kernels, spread(): pl.pallas_call(functools.partial(spread_body, groups), out_shape=(matrix(...  3.86 us
    ppermute x12, starting transfers between devices, swapped(): return lax.ppermute(value, AXES, everyone(lambda d, s: (d ^ 1, s)))  2.07 us
  transfers between devices with their start and end apart: 33, of which 23 were waited for; matrix products, arithmetic and copies ran while one was open for 0% of the time, Pallas kernels for 14%

profile of v5, /device:TPU:0, one launch (start us, length us, event | category | flops | bytes accessed | tf_op | source)
XLA Modules:
  0.0 82.3 jit_solution(10665686414623537415)
XLA Ops:
  1.2 3.9 %shard_map.70 = (bf16[512,1024]{1,0:T(8,128)(2,1)}, bf16[512,512]{1,0:T(8,128)(2,1)}, bf16[128,1024]{1,0:T(8,128)(2,1)}, bf16[128,1024]{1,0:T(8,128)(2,1)}, bf16...) custom-call(s32[4,16]{1,0:T(4,128)} %bitcast.10, bf16[4,16,128,128]{3,2,1,0:T(8,128)(2,1)} %bitcast.8), custom_call_target="tpu_custom_call" | custom-call | bytes 14400000 | tf_op jit(solution)/shard_map/pallas_call | solution.py:128
  6.4 4.8 %collective-permute-start.5 = (bf16[512,128]{1,0:T(8,128)(2,1)S(1)}, bf16[512,128]{1,0:T(8,128)(2,1)S(1)}, u32[]{:S(2)}, u32[]{:S(2)}) collective-permute-start(bf16[512,128]{1,0:T(8,128)(2,1)S(1)} %shard_map.69.now_ref.rest_3_.refs_0_), channel_id=1, source_target_pairs={{0,6},{1,7},{2,1},{3,2},{4,3},{5,4},{6,5},{7,0},{8,15},{9,10},{10,... | collective-permute-start | bytes 393224 | tf_op jit(solution)/shard_map/ppermute | solution.py:301
  11.2 1.6 %collective-permute-start.7 = (bf16[512,128]{1,0:T(8,128)(2,1)S(1)}, bf16[512,128]{1,0:T(8,128)(2,1)S(1)}, u32[]{:S(2)}, u32[]{:S(2)}) collective-permute-start(bf16[512,128]{1,0:T(8,128)(2,1)S(1)} %shard_map.69.now_ref.rest_3_.refs_0_), channel_id=1, source_target_pairs={{0,16},{1,17},{2,18},{3,19},{4,20},{5,21},{6,22},{7,23},{8,24},{9,... | collective-permute-start | bytes 393224 | tf_op jit(solution)/shard_map/ppermute | solution.py:295
  13.3 3.1 %collective-permute-done.5.first_ref.rest_1_ = bf16[512,128]{1,0:T(8,128)(2,1)S(1)} collective-permute-done((bf16[512,128]{1,0:T(8,128)(2,1)S(1)}, bf16[512,128]{1,0:T(8,128)(2,1)S(1)}, u32[]{:S(2)}, u32[]{:S(2)}) %collective-permute-start.5) | collective-permute-done | bytes 131104 | tf_op jit(solution)/shard_map/ppermute | solution.py:301
  18.2 1.2 %collective-permute-done.8.other_ref = bf16[512,128]{1,0:T(8,128)(2,1)S(1)} collective-permute-done((bf16[512,128]{1,0:T(8,128)(2,1)S(1)}, bf16[512,128]{1,0:T(8,128)(2,1)S(1)}, u32[]{:S(2)}, u32[]{:S(2)}) %collective-permute-start.8) | collective-permute-done | bytes 131104 | tf_op jit(solution)/shard_map/ppermute | solution.py:292
  19.7 1.5 %collective-permute-start.10 = (bf16[512,128]{1,0:T(8,128)(2,1)S(1)}, bf16[512,128]{1,0:T(8,128)(2,1)S(1)}, u32[]{:S(2)}, u32[]{:S(2)}) collective-permute-start(bf16[512,128]{1,0:T(8,128)(2,1)S(1)} %get-tuple-element.38.now_ref.rest_3_.refs_1_), channel_id=1, source_target_pairs={{0,2},{1,0},{2,4},{3,1},{4,6},{5,3},{6,7},{7,5},{8,9},{9,11},{10,8... | collective-permute-start | bytes 393224 | tf_op jit(solution)/shard_map/ppermute | solution.py:301
  21.1 1.5 %collective-permute-start.11 = (bf16[512,128]{1,0:T(8,128)(2,1)S(1)}, bf16[512,128]{1,0:T(8,128)(2,1)S(1)}, u32[]{:S(2)}, u32[]{:S(2)}) collective-permute-start(bf16[512,128]{1,0:T(8,128)(2,1)S(1)} %get-tuple-element.40), channel_id=1, source_target_pairs={{0,16},{1,17},{2,18},{3,19},{4,20},{5,21},{6,22},{7,23},{8,24},{9,... | collective-permute-start | bytes 393224 | tf_op jit(solution)/shard_map/ppermute | solution.py:295
  22.6 1.7 %collective-permute-start.9 = (bf16[512,128]{1,0:T(8,128)(2,1)S(1)}, bf16[512,128]{1,0:T(8,128)(2,1)S(1)}, u32[]{:S(2)}, u32[]{:S(2)}) collective-permute-start(bf16[512,128]{1,0:T(8,128)(2,1)S(1)} %get-tuple-element.38.now_ref.rest_3_.refs_1_), channel_id=1, source_target_pairs={{0,6},{1,7},{2,1},{3,2},{4,3},{5,4},{6,5},{7,0},{8,15},{9,10},{10,... | collective-permute-start | bytes 393224 | tf_op jit(solution)/shard_map/ppermute | solution.py:301
  24.9 1.2 %collective-permute-done.11.field_ref.came_ref = bf16[512,128]{1,0:T(8,128)(2,1)S(1)} collective-permute-done((bf16[512,128]{1,0:T(8,128)(2,1)S(1)}, bf16[512,128]{1,0:T(8,128)(2,1)S(1)}, u32[]{:S(2)}, u32[]{:S(2)}) %collective-permute-start.11) | collective-permute-done | bytes 131104 | tf_op jit(solution)/shard_map/ppermute | solution.py:295
  26.1 4.2 %collective-permute-done.9.first_ref.rest_1_ = bf16[512,128]{1,0:T(8,128)(2,1)S(1)} collective-permute-done((bf16[512,128]{1,0:T(8,128)(2,1)S(1)}, bf16[512,128]{1,0:T(8,128)(2,1)S(1)}, u32[]{:S(2)}, u32[]{:S(2)}) %collective-permute-start.9) | collective-permute-done | bytes 131104 | tf_op jit(solution)/shard_map/ppermute | solution.py:301
  30.8 1.3 %collective-permute-done.12.other_ref = bf16[512,128]{1,0:T(8,128)(2,1)S(1)} collective-permute-done((bf16[512,128]{1,0:T(8,128)(2,1)S(1)}, bf16[512,128]{1,0:T(8,128)(2,1)S(1)}, u32[]{:S(2)}, u32[]{:S(2)}) %collective-permute-start.12) | collective-permute-done | bytes 131104 | tf_op jit(solution)/shard_map/ppermute | solution.py:292
  32.4 2.0 %collective-permute-start.13 = (bf16[512,128]{1,0:T(8,128)(2,1)S(1)}, bf16[512,128]{1,0:T(8,128)(2,1)S(1)}, u32[]{:S(2)}, u32[]{:S(2)}) collective-permute-start(bf16[512,128]{1,0:T(8,128)(2,1)S(1)} %get-tuple-element.41.now_ref.rest_3_.refs_2_), channel_id=1, source_target_pairs={{0,6},{1,7},{2,1},{3,2},{4,3},{5,4},{6,5},{7,0},{8,15},{9,10},{10,... | collective-permute-start | bytes 393224 | tf_op jit(solution)/shard_map/ppermute | solution.py:301
  35.5 4.8 %collective-permute-done.13.first_ref.rest_1_ = bf16[512,128]{1,0:T(8,128)(2,1)S(1)} collective-permute-done((bf16[512,128]{1,0:T(8,128)(2,1)S(1)}, bf16[512,128]{1,0:T(8,128)(2,1)S(1)}, u32[]{:S(2)}, u32[]{:S(2)}) %collective-permute-start.13) | collective-permute-done | bytes 131104 | tf_op jit(solution)/shard_map/ppermute | solution.py:301
  41.3 1.3 %collective-permute-done.16.other_ref = bf16[512,128]{1,0:T(8,128)(2,1)S(1)} collective-permute-done((bf16[512,128]{1,0:T(8,128)(2,1)S(1)}, bf16[512,128]{1,0:T(8,128)(2,1)S(1)}, u32[]{:S(2)}, u32[]{:S(2)}) %collective-permute-start.16) | collective-permute-done | bytes 131104 | tf_op jit(solution)/shard_map/ppermute | solution.py:292
  42.8 2.0 %collective-permute-start.17 = (bf16[512,128]{1,0:T(8,128)(2,1)S(1)}, bf16[512,128]{1,0:T(8,128)(2,1)S(1)}, u32[]{:S(2)}, u32[]{:S(2)}) collective-permute-start(bf16[512,128]{1,0:T(8,128)(2,1)S(1)} %get-tuple-element.43.now_ref.rest_3_.refs_3_), channel_id=1, source_target_pairs={{0,6},{1,7},{2,1},{3,2},{4,3},{5,4},{6,5},{7,0},{8,15},{9,10},{10,... | collective-permute-start | bytes 393224 | tf_op jit(solution)/shard_map/ppermute | solution.py:301
  46.1 4.6 %collective-permute-done.17.first_ref.rest_1_ = bf16[512,128]{1,0:T(8,128)(2,1)S(1)} collective-permute-done((bf16[512,128]{1,0:T(8,128)(2,1)S(1)}, bf16[512,128]{1,0:T(8,128)(2,1)S(1)}, u32[]{:S(2)}, u32[]{:S(2)}) %collective-permute-start.17) | collective-permute-done | bytes 131104 | tf_op jit(solution)/shard_map/ppermute | solution.py:301
  51.7 1.3 %collective-permute-done.20.other_ref = bf16[512,128]{1,0:T(8,128)(2,1)S(1)} collective-permute-done((bf16[512,128]{1,0:T(8,128)(2,1)S(1)}, bf16[512,128]{1,0:T(8,128)(2,1)S(1)}, u32[]{:S(2)}, u32[]{:S(2)}) %collective-permute-start.20) | collective-permute-done | bytes 131104 | tf_op jit(solution)/shard_map/ppermute | solution.py:292
  53.2 2.3 %collective-permute-start.21 = (bf16[512,128]{1,0:T(8,128)(2,1)S(1)}, bf16[512,128]{1,0:T(8,128)(2,1)S(1)}, u32[]{:S(2)}, u32[]{:S(2)}) collective-permute-start(bf16[512,128]{1,0:T(8,128)(2,1)S(1)} %get-tuple-element.45.now_ref.refs_4_.rest_3_), channel_id=1, source_target_pairs={{0,6},{1,7},{2,1},{3,2},{4,3},{5,4},{6,5},{7,0},{8,15},{9,10},{10,... | collective-permute-start | bytes 393224 | tf_op jit(solution)/shard_map/ppermute | solution.py:301
  57.1 4.5 %collective-permute-done.21.first_ref.rest_1_ = bf16[512,128]{1,0:T(8,128)(2,1)S(1)} collective-permute-done((bf16[512,128]{1,0:T(8,128)(2,1)S(1)}, bf16[512,128]{1,0:T(8,128)(2,1)S(1)}, u32[]{:S(2)}, u32[]{:S(2)}) %collective-permute-start.21) | collective-permute-done | bytes 131104 | tf_op jit(solution)/shard_map/ppermute | solution.py:301
  62.4 1.3 %collective-permute-done.24.other_ref = bf16[512,128]{1,0:T(8,128)(2,1)S(1)} collective-permute-done((bf16[512,128]{1,0:T(8,128)(2,1)S(1)}, bf16[512,128]{1,0:T(8,128)(2,1)S(1)}, u32[]{:S(2)}, u32[]{:S(2)}) %collective-permute-start.24) | collective-permute-done | bytes 131104 | tf_op jit(solution)/shard_map/ppermute | solution.py:292
  64.6 1.9 %collective-permute-start.28 = (bf16[512,128]{1,0:T(8,128)(2,1)S(1)}, bf16[512,128]{1,0:T(8,128)(2,1)S(1)}, u32[]{:S(2)}, u32[]{:S(2)}) collective-permute-start(bf16[512,128]{1,0:T(8,128)(2,1)S(1)} %get-tuple-element.47.refs_5_.rest_3_.now_ref), channel_id=1, source_target_pairs={{0,6},{1,7},{2,1},{3,2},{4,3},{5,4},{6,5},{7,0},{8,15},{9,10},{10,... | collective-permute-start | bytes 393224 | tf_op jit(solution)/shard_map/ppermute | solution.py:301
  66.5 0.9 %collective-permute-start.29 = (bf16[512,128]{1,0:T(8,128)(2,1)S(1)}, bf16[512,128]{1,0:T(8,128)(2,1)S(1)}, u32[]{:S(2)}, u32[]{:S(2)}) collective-permute-start(bf16[512,128]{1,0:T(8,128)(2,1)S(1)} %get-tuple-element.47.refs_5_.rest_3_.now_ref), channel_id=1, source_target_pairs={{0,2},{1,0},{2,4},{3,1},{4,6},{5,3},{6,7},{7,5},{8,9},{9,11},{10,8... | collective-permute-start | bytes 393224 | tf_op jit(solution)/shard_map/ppermute | solution.py:301
  68.0 1.6 %collective-permute-done.25.refs_6_.now_ref.field_ref = bf16[512,128]{1,0:T(8,128)(2,1)S(1)} collective-permute-done((bf16[512,128]{1,0:T(8,128)(2,1)S(1)}, bf16[512,128]{1,0:T(8,128)(2,1)S(1)}, u32[]{:S(2)}, u32[]{:S(2)}) %collective-permute-start.25) | collective-permute-done | bytes 131104 | tf_op jit(solution)/shard_map/ppermute | solution.py:295
  69.6 2.0 %collective-permute-start.26 = (bf16[512,128]{1,0:T(8,128)(2,1)S(1)}, bf16[512,128]{1,0:T(8,128)(2,1)S(1)}, u32[]{:S(2)}, u32[]{:S(2)}) collective-permute-start(bf16[512,128]{1,0:T(8,128)(2,1)S(1)} %collective-permute-done.25.refs_6_.now_ref.field_ref), channel_id=1, source_target_pairs={{0,6},{1,7},{2,1},{3,2},{4,3},{5,4},{6,5},{7,0},{8,15},{9,10},{10,... | collective-permute-start | bytes 393224 | tf_op jit(solution)/shard_map/ppermute | solution.py:301
  71.5 0.9 %collective-permute-start.27 = (bf16[512,128]{1,0:T(8,128)(2,1)S(1)}, bf16[512,128]{1,0:T(8,128)(2,1)S(1)}, u32[]{:S(2)}, u32[]{:S(2)}) collective-permute-start(bf16[512,128]{1,0:T(8,128)(2,1)S(1)} %collective-permute-done.25.refs_6_.now_ref.field_ref), channel_id=1, source_target_pairs={{0,2},{1,0},{2,4},{3,1},{4,6},{5,3},{6,7},{7,5},{8,9},{9,11},{10,8... | collective-permute-start | bytes 393224 | tf_op jit(solution)/shard_map/ppermute | solution.py:301
  72.9 0.9 %shard_map.91 = (f32[512,128]{1,0:T(8,128)S(1)}, f32[512,128]{1,0:T(8,128)S(1)}) custom-call(bf16[512,1024]{1,0:T(8,128)(2,1)S(1)} %get-tuple-element.36.near_ref.refs_0_, bf16[512,128]{1,0:T(8,128)(2,1)S(1)} %collective-permute-done.28.rest_1_.first_ref, bf16[512,128]{1,0:T(8,128)(2,1)S(1)} %collective-permute-done.29.rest_2_.second_ref, ...), custom_call_target="tpu_custom_call" | custom-call | bytes 1800000 | tf_op jit(solution)/shard_map/pallas_call | solution.py:37
  73.9 1.6 %collective-permute-start.30 = (bf16[512,128]{1,0:T(8,128)(2,1)S(1)}, bf16[512,128]{1,0:T(8,128)(2,1)S(1)}, u32[]{:S(2)}, u32[]{:S(2)}) collective-permute-start(bf16[512,128]{1,0:T(8,128)(2,1)S(1)} %get-tuple-element.55), channel_id=1, source_target_pairs={{0,16},{1,17},{2,18},{3,19},{4,20},{5,21},{6,22},{7,23},{8,24},{9,... | collective-permute-start | bytes 393224 | tf_op jit(solution)/shard_map/ppermute | solution.py:295
  76.0 1.0 %shard_map.87 = (bf16[6,512,128]{2,1,0:T(8,128)(2,1)}, f32[8,128]{1,0:T(8,128)S(1)}) custom-call(bf16[512,128]{1,0:T(8,128)(2,1)S(1)} %shard_map.69.now_ref.rest_3_.refs_0_, bf16[512,128]{1,0:T(8,128)(2,1)S(1)} %get-tuple-element.38.now_ref.rest_3_.refs_1_, bf16[512,128]{1,0:T(8,128)(2,1)S(1)} %get-tuple-element.41.now_ref.rest_3_.refs_2_, ...), custom_call_target="tpu_custom_call" | custom-call | bytes 1800000 | tf_op jit(solution)/shard_map/pallas_call | solution.py:37
  77.9 0.9 %shard_map.89 = (f32[512,128]{1,0:T(8,128)S(1)}, f32[512,128]{1,0:T(8,128)S(1)}) custom-call(f32[8,128]{1,0:T(8,128)S(1)} %get-tuple-element.50._, bf16[512,1024]{1,0:T(8,128)(2,1)S(1)} %get-tuple-element.36.near_ref.refs_0_, bf16[512,128]{1,0:T(8,128)(2,1)S(1)} %collective-permute-done.26.refs_1_, bf16[512,128]{1,0:T(8,128)(2,1)S(1)} %collective-permute-done.27.refs_2_, ...), custom_call_target="tpu_custom_call" | custom-call | bytes 72000000 | tf_op jit(solution)/shard_map/pallas_call | solution.py:37
  79.5 0.7 shard_map.93
  80.2 1.3 %collective-permute-done.31.other_ref = bf16[512,128]{1,0:T(8,128)(2,1)S(1)} collective-permute-done((bf16[512,128]{1,0:T(8,128)(2,1)S(1)}, bf16[512,128]{1,0:T(8,128)(2,1)S(1)}, u32[]{:S(2)}, u32[]{:S(2)}) %collective-permute-start.31) | collective-permute-done | bytes 131104 | tf_op jit(solution)/shard_map/ppermute | solution.py:292
  81.5 0.8 shard_map.95
  (72 shorter events, 16.9 us)
Async XLA Ops:
  0.7 5.5 %collective-permute-start = (f32[512,128]{1,0:T(8,128)}, f32[512,128]{1,0:T(8,128)S(1)}, u32[]{:S(2)}, u32[]{:S(2)}) collective-permute-start(f32[512,128]{1,0:T(8,128)} %bitcast.4), channel_id=1, source_target_pairs={{0,8},{1,9},{2,10},{3,11},{4,12},{5,13},{6,14},{7,15},{8,0},{9,1},... | collective-permute-start | bytes 786440 | tf_op jit(solution)/shard_map/ppermute | solution.py:292
  5.1 6.1 %collective-permute-start.1 = (bf16[128,1024]{1,0:T(8,128)(2,1)}, bf16[128,1024]{1,0:T(8,128)(2,1)S(1)}, u32[]{:S(2)}, u32[]{:S(2)}) collective-permute-start(bf16[128,1024]{1,0:T(8,128)(2,1)} %get-tuple-element.32), channel_id=1, source_target_pairs={{0,8},{1,9},{2,10},{3,11},{4,12},{5,13},{6,14},{7,15},{8,0},{9,1},... | collective-permute-start | bytes 786440 | tf_op jit(solution)/shard_map/ppermute | solution.py:292
  5.3 5.9 %collective-permute-start.2 = (bf16[128,1024]{1,0:T(8,128)(2,1)}, bf16[128,1024]{1,0:T(8,128)(2,1)S(1)}, u32[]{:S(2)}, u32[]{:S(2)}) collective-permute-start(bf16[128,1024]{1,0:T(8,128)(2,1)} %get-tuple-element.33), channel_id=1, source_target_pairs={{0,8},{1,9},{2,10},{3,11},{4,12},{5,13},{6,14},{7,15},{8,0},{9,1},... | collective-permute-start | bytes 786440 | tf_op jit(solution)/shard_map/ppermute | solution.py:292
  5.6 7.4 %collective-permute-start.3 = (bf16[128,1024]{1,0:T(8,128)(2,1)}, bf16[128,1024]{1,0:T(8,128)(2,1)S(1)}, u32[]{:S(2)}, u32[]{:S(2)}) collective-permute-start(bf16[128,1024]{1,0:T(8,128)(2,1)} %get-tuple-element.34), channel_id=1, source_target_pairs={{0,8},{1,9},{2,10},{3,11},{4,12},{5,13},{6,14},{7,15},{8,0},{9,1},... | collective-permute-start | bytes 786440 | tf_op jit(solution)/shard_map/ppermute | solution.py:292
  5.8 7.3 %collective-permute-start.4 = (bf16[128,1024]{1,0:T(8,128)(2,1)}, bf16[128,1024]{1,0:T(8,128)(2,1)S(1)}, u32[]{:S(2)}, u32[]{:S(2)}) collective-permute-start(bf16[128,1024]{1,0:T(8,128)(2,1)} %get-tuple-element.35), channel_id=1, source_target_pairs={{0,8},{1,9},{2,10},{3,11},{4,12},{5,13},{6,14},{7,15},{8,0},{9,1},... | collective-permute-start | bytes 786440 | tf_op jit(solution)/shard_map/ppermute | solution.py:292
  6.4 10.0 %collective-permute-start.5 = (bf16[512,128]{1,0:T(8,128)(2,1)S(1)}, bf16[512,128]{1,0:T(8,128)(2,1)S(1)}, u32[]{:S(2)}, u32[]{:S(2)}) collective-permute-start(bf16[512,128]{1,0:T(8,128)(2,1)S(1)} %shard_map.69.now_ref.rest_3_.refs_0_), channel_id=1, source_target_pairs={{0,6},{1,7},{2,1},{3,2},{4,3},{5,4},{6,5},{7,0},{8,15},{9,10},{10,... | collective-permute-start | bytes 393224 | tf_op jit(solution)/shard_map/ppermute | solution.py:301
  11.2 5.9 %collective-permute-start.6 = (bf16[512,128]{1,0:T(8,128)(2,1)S(1)}, bf16[512,128]{1,0:T(8,128)(2,1)S(1)}, u32[]{:S(2)}, u32[]{:S(2)}) collective-permute-start(bf16[512,128]{1,0:T(8,128)(2,1)S(1)} %shard_map.69.now_ref.rest_3_.refs_0_), channel_id=1, source_target_pairs={{0,2},{1,0},{2,4},{3,1},{4,6},{5,3},{6,7},{7,5},{8,9},{9,11},{10,8... | collective-permute-start | bytes 393224 | tf_op jit(solution)/shard_map/ppermute | solution.py:301
  11.2 6.4 %collective-permute-start.7 = (bf16[512,128]{1,0:T(8,128)(2,1)S(1)}, bf16[512,128]{1,0:T(8,128)(2,1)S(1)}, u32[]{:S(2)}, u32[]{:S(2)}) collective-permute-start(bf16[512,128]{1,0:T(8,128)(2,1)S(1)} %shard_map.69.now_ref.rest_3_.refs_0_), channel_id=1, source_target_pairs={{0,16},{1,17},{2,18},{3,19},{4,20},{5,21},{6,22},{7,23},{8,24},{9,... | collective-permute-start | bytes 393224 | tf_op jit(solution)/shard_map/ppermute | solution.py:295
  18.0 1.4 %collective-permute-start.8 = (bf16[512,128]{1,0:T(8,128)(2,1)S(1)}, bf16[512,128]{1,0:T(8,128)(2,1)S(1)}, u32[]{:S(2)}, u32[]{:S(2)}) collective-permute-start(bf16[512,128]{1,0:T(8,128)(2,1)S(1)} %shard_map.73.mine_ref), channel_id=1, source_target_pairs={{0,8},{1,9},{2,10},{3,11},{4,12},{5,13},{6,14},{7,15},{8,0},{9,1},... | collective-permute-start | bytes 393224 | tf_op jit(solution)/shard_map/ppermute | solution.py:292
  19.7 5.2 %collective-permute-start.10 = (bf16[512,128]{1,0:T(8,128)(2,1)S(1)}, bf16[512,128]{1,0:T(8,128)(2,1)S(1)}, u32[]{:S(2)}, u32[]{:S(2)}) collective-permute-start(bf16[512,128]{1,0:T(8,128)(2,1)S(1)} %get-tuple-element.38.now_ref.rest_3_.refs_1_), channel_id=1, source_target_pairs={{0,2},{1,0},{2,4},{3,1},{4,6},{5,3},{6,7},{7,5},{8,9},{9,11},{10,8... | collective-permute-start | bytes 393224 | tf_op jit(solution)/shard_map/ppermute | solution.py:301
  21.1 5.0 %collective-permute-start.11 = (bf16[512,128]{1,0:T(8,128)(2,1)S(1)}, bf16[512,128]{1,0:T(8,128)(2,1)S(1)}, u32[]{:S(2)}, u32[]{:S(2)}) collective-permute-start(bf16[512,128]{1,0:T(8,128)(2,1)S(1)} %get-tuple-element.40), channel_id=1, source_target_pairs={{0,16},{1,17},{2,18},{3,19},{4,20},{5,21},{6,22},{7,23},{8,24},{9,... | collective-permute-start | bytes 393224 | tf_op jit(solution)/shard_map/ppermute | solution.py:295
  22.6 7.7 %collective-permute-start.9 = (bf16[512,128]{1,0:T(8,128)(2,1)S(1)}, bf16[512,128]{1,0:T(8,128)(2,1)S(1)}, u32[]{:S(2)}, u32[]{:S(2)}) collective-permute-start(bf16[512,128]{1,0:T(8,128)(2,1)S(1)} %get-tuple-element.38.now_ref.rest_3_.refs_1_), channel_id=1, source_target_pairs={{0,6},{1,7},{2,1},{3,2},{4,3},{5,4},{6,5},{7,0},{8,15},{9,10},{10,... | collective-permute-start | bytes 393224 | tf_op jit(solution)/shard_map/ppermute | solution.py:301
  30.8 1.4 %collective-permute-start.12 = (bf16[512,128]{1,0:T(8,128)(2,1)S(1)}, bf16[512,128]{1,0:T(8,128)(2,1)S(1)}, u32[]{:S(2)}, u32[]{:S(2)}) collective-permute-start(bf16[512,128]{1,0:T(8,128)(2,1)S(1)} %shard_map.76.mine_ref), channel_id=1, source_target_pairs={{0,8},{1,9},{2,10},{3,11},{4,12},{5,13},{6,14},{7,15},{8,0},{9,1},... | collective-permute-start | bytes 393224 | tf_op jit(solution)/shard_map/ppermute | solution.py:292
  32.4 7.9 %collective-permute-start.13 = (bf16[512,128]{1,0:T(8,128)(2,1)S(1)}, bf16[512,128]{1,0:T(8,128)(2,1)S(1)}, u32[]{:S(2)}, u32[]{:S(2)}) collective-permute-start(bf16[512,128]{1,0:T(8,128)(2,1)S(1)} %get-tuple-element.41.now_ref.rest_3_.refs_2_), channel_id=1, source_target_pairs={{0,6},{1,7},{2,1},{3,2},{4,3},{5,4},{6,5},{7,0},{8,15},{9,10},{10,... | collective-permute-start | bytes 393224 | tf_op jit(solution)/shard_map/ppermute | solution.py:301
  34.4 6.4 %collective-permute-start.14 = (bf16[512,128]{1,0:T(8,128)(2,1)S(1)}, bf16[512,128]{1,0:T(8,128)(2,1)S(1)}, u32[]{:S(2)}, u32[]{:S(2)}) collective-permute-start(bf16[512,128]{1,0:T(8,128)(2,1)S(1)} %get-tuple-element.41.now_ref.rest_3_.refs_2_), channel_id=1, source_target_pairs={{0,2},{1,0},{2,4},{3,1},{4,6},{5,3},{6,7},{7,5},{8,9},{9,11},{10,8... | collective-permute-start | bytes 393224 | tf_op jit(solution)/shard_map/ppermute | solution.py:301
  34.4 6.4 %collective-permute-start.15 = (bf16[512,128]{1,0:T(8,128)(2,1)S(1)}, bf16[512,128]{1,0:T(8,128)(2,1)S(1)}, u32[]{:S(2)}, u32[]{:S(2)}) collective-permute-start(bf16[512,128]{1,0:T(8,128)(2,1)S(1)} %get-tuple-element.42), channel_id=1, source_target_pairs={{0,16},{1,17},{2,18},{3,19},{4,20},{5,21},{6,22},{7,23},{8,24},{9,... | collective-permute-start | bytes 393224 | tf_op jit(solution)/shard_map/ppermute | solution.py:295
  41.2 1.4 %collective-permute-start.16 = (bf16[512,128]{1,0:T(8,128)(2,1)S(1)}, bf16[512,128]{1,0:T(8,128)(2,1)S(1)}, u32[]{:S(2)}, u32[]{:S(2)}) collective-permute-start(bf16[512,128]{1,0:T(8,128)(2,1)S(1)} %shard_map.79.mine_ref), channel_id=1, source_target_pairs={{0,8},{1,9},{2,10},{3,11},{4,12},{5,13},{6,14},{7,15},{8,0},{9,1},... | collective-permute-start | bytes 393224 | tf_op jit(solution)/shard_map/ppermute | solution.py:292
  42.8 7.9 %collective-permute-start.17 = (bf16[512,128]{1,0:T(8,128)(2,1)S(1)}, bf16[512,128]{1,0:T(8,128)(2,1)S(1)}, u32[]{:S(2)}, u32[]{:S(2)}) collective-permute-start(bf16[512,128]{1,0:T(8,128)(2,1)S(1)} %get-tuple-element.43.now_ref.rest_3_.refs_3_), channel_id=1, source_target_pairs={{0,6},{1,7},{2,1},{3,2},{4,3},{5,4},{6,5},{7,0},{8,15},{9,10},{10,... | collective-permute-start | bytes 393224 | tf_op jit(solution)/shard_map/ppermute | solution.py:301
  44.8 6.4 %collective-permute-start.18 = (bf16[512,128]{1,0:T(8,128)(2,1)S(1)}, bf16[512,128]{1,0:T(8,128)(2,1)S(1)}, u32[]{:S(2)}, u32[]{:S(2)}) collective-permute-start(bf16[512,128]{1,0:T(8,128)(2,1)S(1)} %get-tuple-element.43.now_ref.rest_3_.refs_3_), channel_id=1, source_target_pairs={{0,2},{1,0},{2,4},{3,1},{4,6},{5,3},{6,7},{7,5},{8,9},{9,11},{10,8... | collective-permute-start | bytes 393224 | tf_op jit(solution)/shard_map/ppermute | solution.py:301
  45.0 6.1 %collective-permute-start.19 = (bf16[512,128]{1,0:T(8,128)(2,1)S(1)}, bf16[512,128]{1,0:T(8,128)(2,1)S(1)}, u32[]{:S(2)}, u32[]{:S(2)}) collective-permute-start(bf16[512,128]{1,0:T(8,128)(2,1)S(1)} %get-tuple-element.44), channel_id=1, source_target_pairs={{0,16},{1,17},{2,18},{3,19},{4,20},{5,21},{6,22},{7,23},{8,24},{9,... | collective-permute-start | bytes 393224 | tf_op jit(solution)/shard_map/ppermute | solution.py:295
  51.6 1.4 %collective-permute-start.20 = (bf16[512,128]{1,0:T(8,128)(2,1)S(1)}, bf16[512,128]{1,0:T(8,128)(2,1)S(1)}, u32[]{:S(2)}, u32[]{:S(2)}) collective-permute-start(bf16[512,128]{1,0:T(8,128)(2,1)S(1)} %shard_map.82.mine_ref), channel_id=1, source_target_pairs={{0,8},{1,9},{2,10},{3,11},{4,12},{5,13},{6,14},{7,15},{8,0},{9,1},... | collective-permute-start | bytes 393224 | tf_op jit(solution)/shard_map/ppermute | solution.py:292
  53.2 8.3 %collective-permute-start.21 = (bf16[512,128]{1,0:T(8,128)(2,1)S(1)}, bf16[512,128]{1,0:T(8,128)(2,1)S(1)}, u32[]{:S(2)}, u32[]{:S(2)}) collective-permute-start(bf16[512,128]{1,0:T(8,128)(2,1)S(1)} %get-tuple-element.45.now_ref.refs_4_.rest_3_), channel_id=1, source_target_pairs={{0,6},{1,7},{2,1},{3,2},{4,3},{5,4},{6,5},{7,0},{8,15},{9,10},{10,... | collective-permute-start | bytes 393224 | tf_op jit(solution)/shard_map/ppermute | solution.py:301
  55.5 6.4 %collective-permute-start.22 = (bf16[512,128]{1,0:T(8,128)(2,1)S(1)}, bf16[512,128]{1,0:T(8,128)(2,1)S(1)}, u32[]{:S(2)}, u32[]{:S(2)}) collective-permute-start(bf16[512,128]{1,0:T(8,128)(2,1)S(1)} %get-tuple-element.45.now_ref.refs_4_.rest_3_), channel_id=1, source_target_pairs={{0,2},{1,0},{2,4},{3,1},{4,6},{5,3},{6,7},{7,5},{8,9},{9,11},{10,8... | collective-permute-start | bytes 393224 | tf_op jit(solution)/shard_map/ppermute | solution.py:301
  55.9 6.0 %collective-permute-start.23 = (bf16[512,128]{1,0:T(8,128)(2,1)S(1)}, bf16[512,128]{1,0:T(8,128)(2,1)S(1)}, u32[]{:S(2)}, u32[]{:S(2)}) collective-permute-start(bf16[512,128]{1,0:T(8,128)(2,1)S(1)} %get-tuple-element.46), channel_id=1, source_target_pairs={{0,16},{1,17},{2,18},{3,19},{4,20},{5,21},{6,22},{7,23},{8,24},{9,... | collective-permute-start | bytes 393224 | tf_op jit(solution)/shard_map/ppermute | solution.py:295
  62.4 1.4 %collective-permute-start.24 = (bf16[512,128]{1,0:T(8,128)(2,1)S(1)}, bf16[512,128]{1,0:T(8,128)(2,1)S(1)}, u32[]{:S(2)}, u32[]{:S(2)}) collective-permute-start(bf16[512,128]{1,0:T(8,128)(2,1)S(1)} %shard_map.85.mine_ref), channel_id=1, source_target_pairs={{0,8},{1,9},{2,10},{3,11},{4,12},{5,13},{6,14},{7,15},{8,0},{9,1},... | collective-permute-start | bytes 393224 | tf_op jit(solution)/shard_map/ppermute | solution.py:292
  64.0 5.6 %collective-permute-start.25 = (bf16[512,128]{1,0:T(8,128)(2,1)S(1)}, bf16[512,128]{1,0:T(8,128)(2,1)S(1)}, u32[]{:S(2)}, u32[]{:S(2)}) collective-permute-start(bf16[512,128]{1,0:T(8,128)(2,1)S(1)} %get-tuple-element.48), channel_id=1, source_target_pairs={{0,16},{1,17},{2,18},{3,19},{4,20},{5,21},{6,22},{7,23},{8,24},{9,... | collective-permute-start | bytes 393224 | tf_op jit(solution)/shard_map/ppermute | solution.py:295
  64.6 8.1 %collective-permute-start.28 = (bf16[512,128]{1,0:T(8,128)(2,1)S(1)}, bf16[512,128]{1,0:T(8,128)(2,1)S(1)}, u32[]{:S(2)}, u32[]{:S(2)}) collective-permute-start(bf16[512,128]{1,0:T(8,128)(2,1)S(1)} %get-tuple-element.47.refs_5_.rest_3_.now_ref), channel_id=1, source_target_pairs={{0,6},{1,7},{2,1},{3,2},{4,3},{5,4},{6,5},{7,0},{8,15},{9,10},{10,... | collective-permute-start | bytes 393224 | tf_op jit(solution)/shard_map/ppermute | solution.py:301
  66.5 6.4 %collective-permute-start.29 = (bf16[512,128]{1,0:T(8,128)(2,1)S(1)}, bf16[512,128]{1,0:T(8,128)(2,1)S(1)}, u32[]{:S(2)}, u32[]{:S(2)}) collective-permute-start(bf16[512,128]{1,0:T(8,128)(2,1)S(1)} %get-tuple-element.47.refs_5_.rest_3_.now_ref), channel_id=1, source_target_pairs={{0,2},{1,0},{2,4},{3,1},{4,6},{5,3},{6,7},{7,5},{8,9},{9,11},{10,8... | collective-permute-start | bytes 393224 | tf_op jit(solution)/shard_map/ppermute | solution.py:301
  69.6 7.8 %collective-permute-start.26 = (bf16[512,128]{1,0:T(8,128)(2,1)S(1)}, bf16[512,128]{1,0:T(8,128)(2,1)S(1)}, u32[]{:S(2)}, u32[]{:S(2)}) collective-permute-start(bf16[512,128]{1,0:T(8,128)(2,1)S(1)} %collective-permute-done.25.refs_6_.now_ref.field_ref), channel_id=1, source_target_pairs={{0,6},{1,7},{2,1},{3,2},{4,3},{5,4},{6,5},{7,0},{8,15},{9,10},{10,... | collective-permute-start | bytes 393224 | tf_op jit(solution)/shard_map/ppermute | solution.py:301
  71.5 6.4 %collective-permute-start.27 = (bf16[512,128]{1,0:T(8,128)(2,1)S(1)}, bf16[512,128]{1,0:T(8,128)(2,1)S(1)}, u32[]{:S(2)}, u32[]{:S(2)}) collective-permute-start(bf16[512,128]{1,0:T(8,128)(2,1)S(1)} %collective-permute-done.25.refs_6_.now_ref.field_ref), channel_id=1, source_target_pairs={{0,2},{1,0},{2,4},{3,1},{4,6},{5,3},{6,7},{7,5},{8,9},{9,11},{10,8... | collective-permute-start | bytes 393224 | tf_op jit(solution)/shard_map/ppermute | solution.py:301
  73.9 5.6 %collective-permute-start.30 = (bf16[512,128]{1,0:T(8,128)(2,1)S(1)}, bf16[512,128]{1,0:T(8,128)(2,1)S(1)}, u32[]{:S(2)}, u32[]{:S(2)}) collective-permute-start(bf16[512,128]{1,0:T(8,128)(2,1)S(1)} %get-tuple-element.55), channel_id=1, source_target_pairs={{0,16},{1,17},{2,18},{3,19},{4,20},{5,21},{6,22},{7,23},{8,24},{9,... | collective-permute-start | bytes 393224 | tf_op jit(solution)/shard_map/ppermute | solution.py:295
  75.4 4.7 %collective-permute-start.32 = (bf16[512,128]{1,0:T(8,128)(2,1)S(1)}, bf16[512,128]{1,0:T(8,128)(2,1)S(1)}, u32[]{:S(2)}, u32[]{:S(2)}) collective-permute-start(bf16[512,128]{1,0:T(8,128)(2,1)S(1)} %get-tuple-element.59), channel_id=1, source_target_pairs={{0,8},{1,9},{2,10},{3,11},{4,12},{5,13},{6,14},{7,15},{8,0},{9,1},... | collective-permute-start | bytes 393224 | tf_op jit(solution)/shard_map/ppermute | solution.py:292
  (6 other events, 33.8 us)

commit v6 on v5

--- a/solution.py
+++ b/solution.py
@@ -29,8 +29,11 @@
     return pl.CostEstimate(flops=0, bytes_accessed=moved, transcendentals=0)
 
 
-def call(body, outs, args, after=None, microseconds=0.5):
+def call(body, outs, args, after=None, field_last=False, microseconds=0.5):
     specs = [VMEM] * len(args)
+    if field_last:
+        args = args[1:] + args[:1]
+        body = functools.partial(field_to_front, body, len(args))
     if after is not None:
         args, specs = [after] + args, [pl.BlockSpec(memory_space=pl.ANY)] + specs
         body = functools.partial(skip_first, body)
@@ -44,78 +47,48 @@
     )(*args)
 
 
+def field_to_front(body, count, *refs):
+    body(refs[count - 1], *refs[: count - 1], *refs[count:])
+
+
 def skip_first(body, _, *refs):
     body(*refs)
 
 
-def choose(*cases):
-    *pairs, value = cases
-    for when, other in reversed(pairs):
-        value = jnp.where(when, other, value)
-    return value
-
-
-def far_next(s, count):
-    return choose((s == 0, count - 2), (s == 1, count - 1), (s == count - 1, 0), s - 1)
-
-
-def far_last(s, count):
-    return choose((s == 0, count - 1), (s == count - 2, 0), (s == count - 1, 1), s + 1)
-
-
-def close_next(s, count):
-    even = lax.rem(s, 2) == 0
-    return choose((s == 1, 0), (s == count - 2, count - 1), (even, s + 2), s - 2)
-
-
-def close_last(s, count):
-    even = lax.rem(s, 2) == 0
-    return choose((s == 0, 1), (s == count - 1, count - 2), (even, s - 2), s + 2)
-
-
-def tour(far, count):
-    if far:
-        return [0] + list(range(count - 2, 0, -1)) + [count - 1]
-    return list(range(0, count, 2)) + list(range(count - 1, 0, -2))
-
-
 def spread_body(groups, pattern_ref, entries_ref, keep_ref, own_ref, *rest):
-    *send_refs, here_ref, all_ref, sems = rest
+    *send_refs, here_ref, all_ref, slots_ref, sems, slots_sem = rest
     core, _ = place()
     blocks, slots, size, _ = entries_ref.shape
+    slots_copy = pltpu.make_async_copy(pattern_ref, slots_ref, slots_sem)
+    slots_copy.start()
     copies = [
         pltpu.make_async_copy(entries_ref.at[row], here_ref.at[row], sems.at[row])
         for row in range(blocks)
     ]
     for copy in copies:
         copy.start()
-    here = lax.axis_index("surface")
-    brought = (
-        (far_last(here, groups), 0),
-        (close_last(here, groups), 1),
-        (far_next(here, groups), 2),
-        (close_next(here, groups), 3),
-    )
-    mine = 2 * blocks * core
+    base = (lax.axis_index("surface") - 2) * blocks
+    total = groups * blocks
     all_ref[...] = jnp.zeros_like(all_ref)
+    slots_copy.wait()
+    width = 2 * blocks * size
+    mine = pl.ds(pl.multiple_of(core * width, width), width)
+    other = pl.ds(pl.multiple_of((1 - core) * width, width), width)
     for row in range(blocks):
         copies[row].wait()
         rows = slice(row * size, (row + 1) * size)
         for slot in range(slots):
-            block = pattern_ref[row, slot]
-            group = lax.div(block, blocks)
-            part = 4
-            for source, number in brought:
-                part = jnp.where(group == source, number, part)
-            column = part * blocks + block - group * blocks
+            j = lax.rem(slots_ref[row, slot] - base + total, total)
+            column = jnp.where(
+                j < 2 * blocks,
+                jnp.where(j < blocks, j + blocks, j - blocks),
+                jnp.where(j < 3 * blocks, j + 2 * blocks, j - blocks),
+            )
             columns = pl.ds(pl.multiple_of(column * size, size), size)
             all_ref[rows, columns] = here_ref[row, slot]
-        width = 2 * blocks * size
-        first = pl.ds(pl.multiple_of(core * width, width), width)
-        second = pl.ds(pl.multiple_of((1 - core) * width, width), width)
-        keep_ref[rows, :] = all_ref[rows, first]
-        send_refs[row][...] = all_ref[rows, second]
+        keep_ref[rows, :] = all_ref[rows, mine]
         own_ref[rows, :] = all_ref[rows, 2 * width :]
+        send_refs[row][...] = all_ref[rows, other]
 
 
 def spread(entries, pattern, groups):
@@ -128,18 +101,17 @@
     return pl.pallas_call(
         functools.partial(spread_body, groups),
         out_shape=(matrix(side, 2 * side), matrix(side, side), *[matrix(size, 2 * side)] * blocks),
-        in_specs=[
-            pl.BlockSpec(memory_space=pltpu.SMEM),
-            pl.BlockSpec(memory_space=pltpu.HBM),
-        ],
+        in_specs=[pl.BlockSpec(memory_space=pl.ANY)] * 2,
         out_specs=(VMEM,) * (blocks + 2),
         scratch_shapes=[
             pltpu.VMEM(entries.shape, entries.dtype),
             pltpu.VMEM((side, 5 * side), entries.dtype),
+            pltpu.SMEM(pattern.shape, pattern.dtype),
             pltpu.SemaphoreType.DMA((blocks,)),
+            pltpu.SemaphoreType.DMA,
         ],
         cost_estimate=cost(4),
-        compiler_params=pltpu.CompilerParams(vmem_limit_bytes=54 * MIB),
+        compiler_params=pltpu.CompilerParams(vmem_limit_bytes=51 * MIB),
     )(pattern, entries)
 
 
@@ -190,7 +162,7 @@
     return value
 
 
-def late_body(step, pairs, near_ref, first_ref, second_ref, early_ref, field_ref, *rest):
+def late_body(step, pairs, field_ref, near_ref, first_ref, second_ref, early_ref, *rest):
     *history, out_ref = rest
     total = early_ref[...] + window(near_ref, first_ref, second_ref)
     out_ref[...] = (total + came(step, pairs, field_ref, history)).astype(BF16)
@@ -204,7 +176,8 @@
 
 
 def share_body(step, steps, pairs, even_ref, odd_ref, field_ref, *rest):
-    *history, keep_ref, send_ref, field_out_ref = rest
+    *rest, keep_ref, send_ref = rest
+    history, field_out_ref = (rest[:-1], rest[-1]) if step < steps + pairs - 2 else (rest, None)
     core, pair = place()
     even = even_ref[...] + came(step, pairs, field_ref, history)
     odd = odd_ref[...]
@@ -212,7 +185,8 @@
     late = field_ref[...].astype(F32)
     keep_ref[...] = jnp.where(ended, late, jnp.where(core == 1, odd, even))
     send_ref[...] = jnp.where(ended, late, jnp.where(core == 0, odd, even)).astype(BF16)
-    field_out_ref[...] = even.astype(BF16)
+    if field_out_ref is not None:
+        field_out_ref[...] = even.astype(BF16)
 
 
 def finish_body(step, steps, mine_ref, other_ref, *rest):
@@ -294,14 +268,9 @@
     def pair_moved(value, hop):
         return lax.ppermute(value, AXES, everyone(lambda d, s: ((d + 2 * hop) % lags, s)))
 
-    def halo(value, far):
-        order = tour(far, groups)
-        following = dict(zip(order, order[1:] + order[:1]))
-        preceding = {t: s for s, t in following.items()}
+    def halo(value, hop):
         return lax.ppermute(
-            value,
-            AXES,
-            everyone(lambda d, s: (d, following[s] if d % 2 == 0 else preceding[s])),
+            value, AXES, everyone(lambda d, s: (d, (s + (hop if d % 2 == 0 else -hop)) % groups))
         )
 
     other_history = swapped(history[0])
@@ -314,7 +283,7 @@
         [current_shape],
         [diagonal_block_inverses, excitation, first_history],
     )
-    matrix_shape = jax.ShapeDtypeStruct(kept.shape, kept.dtype)
+    matrix_shape = jax.ShapeDtypeStruct((rows, 2 * rows), kept.dtype)
     near, far = call(arrange_body, [matrix_shape, matrix_shape], [kept] + [swapped(part) for part in sent])
 
     going = field = current
@@ -332,7 +301,7 @@
                 [jax.ShapeDtypeStruct(excitation.shape, BF16), TOKEN],
                 seen,
             )
-        first, second = windows or (halo(current, True), halo(current, False))
+        first, second = windows or (halo(current, 1), halo(current, 2))
         if pairs == 2:
             current_in = field_in = pair_moved(going, 1)
         else:
@@ -344,7 +313,10 @@
         previous = [first, second, current]
         if step < steps - 1:
             (field,) = call(
-                functools.partial(late_body, step, pairs), [current_shape], received + [field_in] + past
+                functools.partial(late_body, step, pairs),
+                [current_shape],
+                [field_in] + received + past,
+                field_last=step != 1,
             )
             current, going = call(
                 functools.partial(next_body, step),
@@ -353,7 +325,7 @@
             )
         else:
             if step < rounds - 1:
-                windows = halo(current_in, True), halo(current_in, False)
+                windows = halo(current_in, 1), halo(current_in, 2)
             even, odd = call(
                 last_body,
                 [field_shape, field_shape],
@@ -361,11 +333,12 @@
                 after=collected,
                 microseconds=0.5 if step < rounds - 1 else 20,
             )
-            mine, send, field = call(
+            *fields, mine, send = call(
                 functools.partial(share_body, step, steps, pairs),
-                [field_shape, current_shape, current_shape],
+                [current_shape] * (step < rounds - 1) + [field_shape, current_shape],
                 [even, odd, field_in] + past,
             )
+            field = fields[0] if fields else None
             (result,) = call(
                 functools.partial(finish_body, step, steps),
                 [field_shape],

time: 82.4 us -> 79.2 us (0.961)
  starting transfers between devices: 29.4 us -> 25.2 us
  waiting for transfers between devices: 36.4 us -> 39.4 us
  Pallas kernels: 15.5 us -> 12.8 us
    ppermute x14, starting transfers between devices: 20.5 us -> 13.9 us  [halo(): lax.ppermute(value, AXES, everyone(lambda d, s: (d, (s + (hop if d % 2 ==...]
    ppermute x14, waiting for transfers between devices: 24.5 us -> 27.4 us  [halo(): lax.ppermute(value, AXES, everyone(lambda d, s: (d, (s + (hop if d % 2 ==...]
    ppermute x7, starting transfers between devices: 6.81 us -> 9.09 us  [pair_moved(): lax.ppermute(value, AXES, everyone(lambda d, s: ((d + 2 * hop) % lags, s)))]
    pallas_call x1, Pallas kernels: 3.86 us -> 1.74 us  [spread(): pl.pallas_call(functools.partial(spread_body, groups), out_shape=(matrix(...]
  transfers between devices with their start and end apart: 33 -> 33, of which waited for: 23 -> 22; matrix products, arithmetic and copies ran while one was open for 0% -> 0% of each run, Pallas kernels for 14% -> 11%
where the time goes in v6:
time: 79.2 us; the launch traced here: 79 us
  waiting for transfers between devices  39.4 us (50%)
  starting transfers between devices  25.2 us (32%)
  Pallas kernels  12.8 us (16%)
  between operations  0.95 us (1%)
    ppermute x14, waiting for transfers between devices, halo(): lax.ppermute(value, AXES, everyone(lambda d, s: (d, (s + (hop if d % 2 ==...  27.4 us
    ppermute x14, starting transfers between devices, halo(): lax.ppermute(value, AXES, everyone(lambda d, s: (d, (s + (hop if d % 2 ==...  13.9 us
    pallas_call x27, Pallas kernels, call(): pl.pallas_call(body, out_shape=tuple(outs), in_specs=specs, out_specs=tup...  11.1 us
    ppermute x7, starting transfers between devices, pair_moved(): lax.ppermute(value, AXES, everyone(lambda d, s: ((d + 2 * hop) % lags, s)))  9.09 us
    ppermute x12, waiting for transfers between devices, swapped(): return lax.ppermute(value, AXES, everyone(lambda d, s: (d ^ 1, s)))  7.88 us
    ppermute x7, waiting for transfers between devices, pair_moved(): lax.ppermute(value, AXES, everyone(lambda d, s: ((d + 2 * hop) % lags, s)))  4.13 us
    ppermute x12, starting transfers between devices, swapped(): return lax.ppermute(value, AXES, everyone(lambda d, s: (d ^ 1, s)))  2.21 us
    pallas_call x1, Pallas kernels, spread(): pl.pallas_call(functools.partial(spread_body, groups), out_shape=(matrix(...  1.74 us
  transfers between devices with their start and end apart: 33, of which 22 were waited for; matrix products, arithmetic and copies ran while one was open for 0% of the time, Pallas kernels for 11%

profile of v6, /device:TPU:0, one launch (start us, length us, event | category | flops | bytes accessed | tf_op | source)
XLA Modules:
  0.0 79.0 jit_solution(11305680757678807849)
XLA Ops:
  1.9 1.7 %shard_map.70 = (bf16[512,1024]{1,0:T(8,128)(2,1)S(1)}, bf16[512,512]{1,0:T(8,128)(2,1)S(1)}, bf16[128,1024]{1,0:T(8,128)(2,1)S(1)}, bf16[128,1024]{1,0:T(8,128)...) custom-call(s32[4,16]{1,0:T(4,128)S(1)} %bitcast.8, bf16[4,16,128,128]{3,2,1,0:T(8,128)(2,1)} %bitcast.9), custom_call_target="tpu_custom_call" | custom-call | bytes 14400000 | tf_op jit(solution)/shard_map/pallas_call | solution.py:101
  4.9 2.7 %collective-permute-start.5 = (bf16[512,128]{1,0:T(8,128)(2,1)S(1)}, bf16[512,128]{1,0:T(8,128)(2,1)S(1)}, u32[]{:S(2)}, u32[]{:S(2)}) collective-permute-start(bf16[512,128]{1,0:T(8,128)(2,1)S(1)} %shard_map.69.now_ref.rest_3_.refs_0_), channel_id=1, source_target_pairs={{0,1},{1,2},{2,3},{3,4},{4,5},{5,6},{6,7},{7,0},{8,15},{9,8},{10,9... | collective-permute-start | bytes 393224 | tf_op jit(solution)/shard_map/ppermute | solution.py:272
  7.6 1.6 %collective-permute-start.6 = (bf16[512,128]{1,0:T(8,128)(2,1)S(1)}, bf16[512,128]{1,0:T(8,128)(2,1)S(1)}, u32[]{:S(2)}, u32[]{:S(2)}) collective-permute-start(bf16[512,128]{1,0:T(8,128)(2,1)S(1)} %shard_map.69.now_ref.rest_3_.refs_0_), channel_id=1, source_target_pairs={{0,2},{1,3},{2,4},{3,5},{4,6},{5,7},{6,0},{7,1},{8,14},{9,15},{10,... | collective-permute-start | bytes 393224 | tf_op jit(solution)/shard_map/ppermute | solution.py:272
  9.2 1.5 %collective-permute-start.7 = (bf16[512,128]{1,0:T(8,128)(2,1)S(1)}, bf16[512,128]{1,0:T(8,128)(2,1)S(1)}, u32[]{:S(2)}, u32[]{:S(2)}) collective-permute-start(bf16[512,128]{1,0:T(8,128)(2,1)S(1)} %shard_map.69.now_ref.rest_3_.refs_0_), channel_id=1, source_target_pairs={{0,16},{1,17},{2,18},{3,19},{4,20},{5,21},{6,22},{7,23},{8,24},{9,... | collective-permute-start | bytes 393224 | tf_op jit(solution)/shard_map/ppermute | solution.py:269
  11.2 3.7 %collective-permute-done.5.refs_1_.rest_1_ = bf16[512,128]{1,0:T(8,128)(2,1)S(1)} collective-permute-done((bf16[512,128]{1,0:T(8,128)(2,1)S(1)}, bf16[512,128]{1,0:T(8,128)(2,1)S(1)}, u32[]{:S(2)}, u32[]{:S(2)}) %collective-permute-start.5) | collective-permute-done | bytes 131104 | tf_op jit(solution)/shard_map/ppermute | solution.py:272
  14.9 0.9 %collective-permute-done.6.refs_2_.rest_2_ = bf16[512,128]{1,0:T(8,128)(2,1)S(1)} collective-permute-done((bf16[512,128]{1,0:T(8,128)(2,1)S(1)}, bf16[512,128]{1,0:T(8,128)(2,1)S(1)}, u32[]{:S(2)}, u32[]{:S(2)}) %collective-permute-start.6) | collective-permute-done | bytes 131104 | tf_op jit(solution)/shard_map/ppermute | solution.py:272
  16.4 1.2 %collective-permute-done.8.other_ref = bf16[512,128]{1,0:T(8,128)(2,1)S(1)} collective-permute-done((bf16[512,128]{1,0:T(8,128)(2,1)S(1)}, bf16[512,128]{1,0:T(8,128)(2,1)S(1)}, u32[]{:S(2)}, u32[]{:S(2)}) %collective-permute-start.8) | collective-permute-done | bytes 131104 | tf_op jit(solution)/shard_map/ppermute | solution.py:266
  17.8 1.3 %collective-permute-start.10 = (bf16[512,128]{1,0:T(8,128)(2,1)S(1)}, bf16[512,128]{1,0:T(8,128)(2,1)S(1)}, u32[]{:S(2)}, u32[]{:S(2)}) collective-permute-start(bf16[512,128]{1,0:T(8,128)(2,1)S(1)} %get-tuple-element.38.now_ref.rest_3_.refs_1_), channel_id=1, source_target_pairs={{0,1},{1,2},{2,3},{3,4},{4,5},{5,6},{6,7},{7,0},{8,15},{9,8},{10,9... | collective-permute-start | bytes 393224 | tf_op jit(solution)/shard_map/ppermute | solution.py:272
  19.4 1.5 %collective-permute-start.9 = (bf16[512,128]{1,0:T(8,128)(2,1)S(1)}, bf16[512,128]{1,0:T(8,128)(2,1)S(1)}, u32[]{:S(2)}, u32[]{:S(2)}) collective-permute-start(bf16[512,128]{1,0:T(8,128)(2,1)S(1)} %get-tuple-element.39), channel_id=1, source_target_pairs={{0,16},{1,17},{2,18},{3,19},{4,20},{5,21},{6,22},{7,23},{8,24},{9,... | collective-permute-start | bytes 393224 | tf_op jit(solution)/shard_map/ppermute | solution.py:269
  21.5 4.8 %collective-permute-done.10.first_ref.rest_1_ = bf16[512,128]{1,0:T(8,128)(2,1)S(1)} collective-permute-done((bf16[512,128]{1,0:T(8,128)(2,1)S(1)}, bf16[512,128]{1,0:T(8,128)(2,1)S(1)}, u32[]{:S(2)}, u32[]{:S(2)}) %collective-permute-start.10) | collective-permute-done | bytes 131104 | tf_op jit(solution)/shard_map/ppermute | solution.py:272
  26.9 1.3 %collective-permute-done.12.other_ref = bf16[512,128]{1,0:T(8,128)(2,1)S(1)} collective-permute-done((bf16[512,128]{1,0:T(8,128)(2,1)S(1)}, bf16[512,128]{1,0:T(8,128)(2,1)S(1)}, u32[]{:S(2)}, u32[]{:S(2)}) %collective-permute-start.12) | collective-permute-done | bytes 131104 | tf_op jit(solution)/shard_map/ppermute | solution.py:266
  28.5 1.9 %collective-permute-start.13 = (bf16[512,128]{1,0:T(8,128)(2,1)S(1)}, bf16[512,128]{1,0:T(8,128)(2,1)S(1)}, u32[]{:S(2)}, u32[]{:S(2)}) collective-permute-start(bf16[512,128]{1,0:T(8,128)(2,1)S(1)} %get-tuple-element.41.now_ref.rest_3_.refs_2_), channel_id=1, source_target_pairs={{0,1},{1,2},{2,3},{3,4},{4,5},{5,6},{6,7},{7,0},{8,15},{9,8},{10,9... | collective-permute-start | bytes 393224 | tf_op jit(solution)/shard_map/ppermute | solution.py:272
  30.8 1.5 %collective-permute-start.15 = (bf16[512,128]{1,0:T(8,128)(2,1)S(1)}, bf16[512,128]{1,0:T(8,128)(2,1)S(1)}, u32[]{:S(2)}, u32[]{:S(2)}) collective-permute-start(bf16[512,128]{1,0:T(8,128)(2,1)S(1)} %get-tuple-element.42), channel_id=1, source_target_pairs={{0,16},{1,17},{2,18},{3,19},{4,20},{5,21},{6,22},{7,23},{8,24},{9,... | collective-permute-start | bytes 393224 | tf_op jit(solution)/shard_map/ppermute | solution.py:269
  32.9 3.3 %collective-permute-done.13.refs_1_.rest_1_ = bf16[512,128]{1,0:T(8,128)(2,1)S(1)} collective-permute-done((bf16[512,128]{1,0:T(8,128)(2,1)S(1)}, bf16[512,128]{1,0:T(8,128)(2,1)S(1)}, u32[]{:S(2)}, u32[]{:S(2)}) %collective-permute-start.13) | collective-permute-done | bytes 131104 | tf_op jit(solution)/shard_map/ppermute | solution.py:272
  36.2 1.2 %collective-permute-done.14.refs_2_.rest_2_ = bf16[512,128]{1,0:T(8,128)(2,1)S(1)} collective-permute-done((bf16[512,128]{1,0:T(8,128)(2,1)S(1)}, bf16[512,128]{1,0:T(8,128)(2,1)S(1)}, u32[]{:S(2)}, u32[]{:S(2)}) %collective-permute-start.14) | collective-permute-done | bytes 131104 | tf_op jit(solution)/shard_map/ppermute | solution.py:272
  37.9 1.3 %collective-permute-done.16.other_ref = bf16[512,128]{1,0:T(8,128)(2,1)S(1)} collective-permute-done((bf16[512,128]{1,0:T(8,128)(2,1)S(1)}, bf16[512,128]{1,0:T(8,128)(2,1)S(1)}, u32[]{:S(2)}, u32[]{:S(2)}) %collective-permute-start.16) | collective-permute-done | bytes 131104 | tf_op jit(solution)/shard_map/ppermute | solution.py:266
  40.5 1.5 %collective-permute-start.19 = (bf16[512,128]{1,0:T(8,128)(2,1)S(1)}, bf16[512,128]{1,0:T(8,128)(2,1)S(1)}, u32[]{:S(2)}, u32[]{:S(2)}) collective-permute-start(bf16[512,128]{1,0:T(8,128)(2,1)S(1)} %get-tuple-element.44), channel_id=1, source_target_pairs={{0,16},{1,17},{2,18},{3,19},{4,20},{5,21},{6,22},{7,23},{8,24},{9,... | collective-permute-start | bytes 393224 | tf_op jit(solution)/shard_map/ppermute | solution.py:269
  42.5 4.6 %collective-permute-done.17.refs_1_.rest_1_ = bf16[512,128]{1,0:T(8,128)(2,1)S(1)} collective-permute-done((bf16[512,128]{1,0:T(8,128)(2,1)S(1)}, bf16[512,128]{1,0:T(8,128)(2,1)S(1)}, u32[]{:S(2)}, u32[]{:S(2)}) %collective-permute-start.17) | collective-permute-done | bytes 131104 | tf_op jit(solution)/shard_map/ppermute | solution.py:272
  48.0 1.3 %collective-permute-done.20.other_ref = bf16[512,128]{1,0:T(8,128)(2,1)S(1)} collective-permute-done((bf16[512,128]{1,0:T(8,128)(2,1)S(1)}, bf16[512,128]{1,0:T(8,128)(2,1)S(1)}, u32[]{:S(2)}, u32[]{:S(2)}) %collective-permute-start.20) | collective-permute-done | bytes 131104 | tf_op jit(solution)/shard_map/ppermute | solution.py:266
  49.5 1.7 %collective-permute-start.21 = (bf16[512,128]{1,0:T(8,128)(2,1)S(1)}, bf16[512,128]{1,0:T(8,128)(2,1)S(1)}, u32[]{:S(2)}, u32[]{:S(2)}) collective-permute-start(bf16[512,128]{1,0:T(8,128)(2,1)S(1)} %get-tuple-element.45.now_ref.refs_4_.rest_3_), channel_id=1, source_target_pairs={{0,1},{1,2},{2,3},{3,4},{4,5},{5,6},{6,7},{7,0},{8,15},{9,8},{10,9... | collective-permute-start | bytes 393224 | tf_op jit(solution)/shard_map/ppermute | solution.py:272
  51.6 1.5 %collective-permute-start.23 = (bf16[512,128]{1,0:T(8,128)(2,1)S(1)}, bf16[512,128]{1,0:T(8,128)(2,1)S(1)}, u32[]{:S(2)}, u32[]{:S(2)}) collective-permute-start(bf16[512,128]{1,0:T(8,128)(2,1)S(1)} %get-tuple-element.46), channel_id=1, source_target_pairs={{0,16},{1,17},{2,18},{3,19},{4,20},{5,21},{6,22},{7,23},{8,24},{9,... | collective-permute-start | bytes 393224 | tf_op jit(solution)/shard_map/ppermute | solution.py:269
  53.7 3.8 %collective-permute-done.21.refs_1_.rest_1_ = bf16[512,128]{1,0:T(8,128)(2,1)S(1)} collective-permute-done((bf16[512,128]{1,0:T(8,128)(2,1)S(1)}, bf16[512,128]{1,0:T(8,128)(2,1)S(1)}, u32[]{:S(2)}, u32[]{:S(2)}) %collective-permute-start.21) | collective-permute-done | bytes 131104 | tf_op jit(solution)/shard_map/ppermute | solution.py:272
  58.9 1.3 %collective-permute-done.24.other_ref = bf16[512,128]{1,0:T(8,128)(2,1)S(1)} collective-permute-done((bf16[512,128]{1,0:T(8,128)(2,1)S(1)}, bf16[512,128]{1,0:T(8,128)(2,1)S(1)}, u32[]{:S(2)}, u32[]{:S(2)}) %collective-permute-start.24) | collective-permute-done | bytes 131104 | tf_op jit(solution)/shard_map/ppermute | solution.py:266
  60.4 1.6 %collective-permute-start.25 = (bf16[512,128]{1,0:T(8,128)(2,1)S(1)}, bf16[512,128]{1,0:T(8,128)(2,1)S(1)}, u32[]{:S(2)}, u32[]{:S(2)}) collective-permute-start(bf16[512,128]{1,0:T(8,128)(2,1)S(1)} %get-tuple-element.48), channel_id=1, source_target_pairs={{0,16},{1,17},{2,18},{3,19},{4,20},{5,21},{6,22},{7,23},{8,24},{9,... | collective-permute-start | bytes 393224 | tf_op jit(solution)/shard_map/ppermute | solution.py:269
  62.0 1.1 %collective-permute-start.28 = (bf16[512,128]{1,0:T(8,128)(2,1)S(1)}, bf16[512,128]{1,0:T(8,128)(2,1)S(1)}, u32[]{:S(2)}, u32[]{:S(2)}) collective-permute-start(bf16[512,128]{1,0:T(8,128)(2,1)S(1)} %get-tuple-element.47.refs_5_.rest_3_.now_ref), channel_id=1, source_target_pairs={{0,1},{1,2},{2,3},{3,4},{4,5},{5,6},{6,7},{7,0},{8,15},{9,8},{10,9... | collective-permute-start | bytes 393224 | tf_op jit(solution)/shard_map/ppermute | solution.py:272
  63.7 2.3 %collective-permute-done.25.refs_6_.now_ref.field_ref = bf16[512,128]{1,0:T(8,128)(2,1)S(1)} collective-permute-done((bf16[512,128]{1,0:T(8,128)(2,1)S(1)}, bf16[512,128]{1,0:T(8,128)(2,1)S(1)}, u32[]{:S(2)}, u32[]{:S(2)}) %collective-permute-start.25) | collective-permute-done | bytes 131104 | tf_op jit(solution)/shard_map/ppermute | solution.py:269
  66.0 1.1 %collective-permute-start.26 = (bf16[512,128]{1,0:T(8,128)(2,1)S(1)}, bf16[512,128]{1,0:T(8,128)(2,1)S(1)}, u32[]{:S(2)}, u32[]{:S(2)}) collective-permute-start(bf16[512,128]{1,0:T(8,128)(2,1)S(1)} %collective-permute-done.25.refs_6_.now_ref.field_ref), channel_id=1, source_target_pairs={{0,1},{1,2},{2,3},{3,4},{4,5},{5,6},{6,7},{7,0},{8,15},{9,8},{10,9... | collective-permute-start | bytes 393224 | tf_op jit(solution)/shard_map/ppermute | solution.py:272
  67.6 2.2 %collective-permute-done.28.rest_1_.first_ref = bf16[512,128]{1,0:T(8,128)(2,1)S(1)} collective-permute-done((bf16[512,128]{1,0:T(8,128)(2,1)S(1)}, bf16[512,128]{1,0:T(8,128)(2,1)S(1)}, u32[]{:S(2)}, u32[]{:S(2)}) %collective-permute-start.28) | collective-permute-done | bytes 131104 | tf_op jit(solution)/shard_map/ppermute | solution.py:272
  69.8 1.0 %collective-permute-done.29.rest_2_.second_ref = bf16[512,128]{1,0:T(8,128)(2,1)S(1)} collective-permute-done((bf16[512,128]{1,0:T(8,128)(2,1)S(1)}, bf16[512,128]{1,0:T(8,128)(2,1)S(1)}, u32[]{:S(2)}, u32[]{:S(2)}) %collective-permute-start.29) | collective-permute-done | bytes 131104 | tf_op jit(solution)/shard_map/ppermute | solution.py:272
  72.5 1.0 %shard_map.87 = (bf16[6,512,128]{2,1,0:T(8,128)(2,1)}, f32[8,128]{1,0:T(8,128)S(1)}) custom-call(bf16[512,128]{1,0:T(8,128)(2,1)S(1)} %shard_map.69.now_ref.rest_3_.refs_0_, bf16[512,128]{1,0:T(8,128)(2,1)S(1)} %get-tuple-element.38.now_ref.rest_3_.refs_1_, bf16[512,128]{1,0:T(8,128)(2,1)S(1)} %get-tuple-element.41.now_ref.rest_3_.refs_2_, ...), custom_call_target="tpu_custom_call" | custom-call | bytes 1800000 | tf_op jit(solution)/shard_map/pallas_call | solution.py:40
  75.0 1.8 %collective-permute-done.30.field_ref = bf16[512,128]{1,0:T(8,128)(2,1)S(1)} collective-permute-done((bf16[512,128]{1,0:T(8,128)(2,1)S(1)}, bf16[512,128]{1,0:T(8,128)(2,1)S(1)}, u32[]{:S(2)}, u32[]{:S(2)}) %collective-permute-start.30) | collective-permute-done | bytes 131104 | tf_op jit(solution)/shard_map/ppermute | solution.py:269
  77.0 1.3 %collective-permute-done.31.other_ref = bf16[512,128]{1,0:T(8,128)(2,1)S(1)} collective-permute-done((bf16[512,128]{1,0:T(8,128)(2,1)S(1)}, bf16[512,128]{1,0:T(8,128)(2,1)S(1)}, u32[]{:S(2)}, u32[]{:S(2)}) %collective-permute-start.31) | collective-permute-done | bytes 131104 | tf_op jit(solution)/shard_map/ppermute | solution.py:266
  (70 shorter events, 17.3 us)
Async XLA Ops:
  0.7 4.0 %collective-permute-start = (f32[512,128]{1,0:T(8,128)}, f32[512,128]{1,0:T(8,128)S(1)}, u32[]{:S(2)}, u32[]{:S(2)}) collective-permute-start(f32[512,128]{1,0:T(8,128)} %bitcast.4), channel_id=1, source_target_pairs={{0,8},{1,9},{2,10},{3,11},{4,12},{5,13},{6,14},{7,15},{8,0},{9,1},... | collective-permute-start | bytes 786440 | tf_op jit(solution)/shard_map/ppermute | solution.py:266
  3.6 4.0 %collective-permute-start.1 = (bf16[128,1024]{1,0:T(8,128)(2,1)S(1)}, bf16[128,1024]{1,0:T(8,128)(2,1)S(1)}, u32[]{:S(2)}, u32[]{:S(2)}) collective-permute-start(bf16[128,1024]{1,0:T(8,128)(2,1)S(1)} %get-tuple-element.32), channel_id=1, source_target_pairs={{0,8},{1,9},{2,10},{3,11},{4,12},{5,13},{6,14},{7,15},{8,0},{9,1},... | collective-permute-start | bytes 786440 | tf_op jit(solution)/shard_map/ppermute | solution.py:266
  3.8 5.4 %collective-permute-start.2 = (bf16[128,1024]{1,0:T(8,128)(2,1)S(1)}, bf16[128,1024]{1,0:T(8,128)(2,1)S(1)}, u32[]{:S(2)}, u32[]{:S(2)}) collective-permute-start(bf16[128,1024]{1,0:T(8,128)(2,1)S(1)} %get-tuple-element.33), channel_id=1, source_target_pairs={{0,8},{1,9},{2,10},{3,11},{4,12},{5,13},{6,14},{7,15},{8,0},{9,1},... | collective-permute-start | bytes 786440 | tf_op jit(solution)/shard_map/ppermute | solution.py:266
  4.2 6.8 %collective-permute-start.3 = (bf16[128,1024]{1,0:T(8,128)(2,1)S(1)}, bf16[128,1024]{1,0:T(8,128)(2,1)S(1)}, u32[]{:S(2)}, u32[]{:S(2)}) collective-permute-start(bf16[128,1024]{1,0:T(8,128)(2,1)S(1)} %get-tuple-element.34), channel_id=1, source_target_pairs={{0,8},{1,9},{2,10},{3,11},{4,12},{5,13},{6,14},{7,15},{8,0},{9,1},... | collective-permute-start | bytes 786440 | tf_op jit(solution)/shard_map/ppermute | solution.py:266
  4.3 6.7 %collective-permute-start.4 = (bf16[128,1024]{1,0:T(8,128)(2,1)S(1)}, bf16[128,1024]{1,0:T(8,128)(2,1)S(1)}, u32[]{:S(2)}, u32[]{:S(2)}) collective-permute-start(bf16[128,1024]{1,0:T(8,128)(2,1)S(1)} %get-tuple-element.35), channel_id=1, source_target_pairs={{0,8},{1,9},{2,10},{3,11},{4,12},{5,13},{6,14},{7,15},{8,0},{9,1},... | collective-permute-start | bytes 786440 | tf_op jit(solution)/shard_map/ppermute | solution.py:266
  4.9 9.9 %collective-permute-start.5 = (bf16[512,128]{1,0:T(8,128)(2,1)S(1)}, bf16[512,128]{1,0:T(8,128)(2,1)S(1)}, u32[]{:S(2)}, u32[]{:S(2)}) collective-permute-start(bf16[512,128]{1,0:T(8,128)(2,1)S(1)} %shard_map.69.now_ref.rest_3_.refs_0_), channel_id=1, source_target_pairs={{0,1},{1,2},{2,3},{3,4},{4,5},{5,6},{6,7},{7,0},{8,15},{9,8},{10,9... | collective-permute-start | bytes 393224 | tf_op jit(solution)/shard_map/ppermute | solution.py:272
  7.6 8.2 %collective-permute-start.6 = (bf16[512,128]{1,0:T(8,128)(2,1)S(1)}, bf16[512,128]{1,0:T(8,128)(2,1)S(1)}, u32[]{:S(2)}, u32[]{:S(2)}) collective-permute-start(bf16[512,128]{1,0:T(8,128)(2,1)S(1)} %shard_map.69.now_ref.rest_3_.refs_0_), channel_id=1, source_target_pairs={{0,2},{1,3},{2,4},{3,5},{4,6},{5,7},{6,0},{7,1},{8,14},{9,15},{10,... | collective-permute-start | bytes 393224 | tf_op jit(solution)/shard_map/ppermute | solution.py:272
  9.2 6.6 %collective-permute-start.7 = (bf16[512,128]{1,0:T(8,128)(2,1)S(1)}, bf16[512,128]{1,0:T(8,128)(2,1)S(1)}, u32[]{:S(2)}, u32[]{:S(2)}) collective-permute-start(bf16[512,128]{1,0:T(8,128)(2,1)S(1)} %shard_map.69.now_ref.rest_3_.refs_0_), channel_id=1, source_target_pairs={{0,16},{1,17},{2,18},{3,19},{4,20},{5,21},{6,22},{7,23},{8,24},{9,... | collective-permute-start | bytes 393224 | tf_op jit(solution)/shard_map/ppermute | solution.py:269
  16.2 1.4 %collective-permute-start.8 = (bf16[512,128]{1,0:T(8,128)(2,1)S(1)}, bf16[512,128]{1,0:T(8,128)(2,1)S(1)}, u32[]{:S(2)}, u32[]{:S(2)}) collective-permute-start(bf16[512,128]{1,0:T(8,128)(2,1)S(1)} %shard_map.73.mine_ref), channel_id=1, source_target_pairs={{0,8},{1,9},{2,10},{3,11},{4,12},{5,13},{6,14},{7,15},{8,0},{9,1},... | collective-permute-start | bytes 393224 | tf_op jit(solution)/shard_map/ppermute | solution.py:266
  17.8 8.4 %collective-permute-start.10 = (bf16[512,128]{1,0:T(8,128)(2,1)S(1)}, bf16[512,128]{1,0:T(8,128)(2,1)S(1)}, u32[]{:S(2)}, u32[]{:S(2)}) collective-permute-start(bf16[512,128]{1,0:T(8,128)(2,1)S(1)} %get-tuple-element.38.now_ref.rest_3_.refs_1_), channel_id=1, source_target_pairs={{0,1},{1,2},{2,3},{3,4},{4,5},{5,6},{6,7},{7,0},{8,15},{9,8},{10,9... | collective-permute-start | bytes 393224 | tf_op jit(solution)/shard_map/ppermute | solution.py:272
  19.1 7.3 %collective-permute-start.11 = (bf16[512,128]{1,0:T(8,128)(2,1)S(1)}, bf16[512,128]{1,0:T(8,128)(2,1)S(1)}, u32[]{:S(2)}, u32[]{:S(2)}) collective-permute-start(bf16[512,128]{1,0:T(8,128)(2,1)S(1)} %get-tuple-element.38.now_ref.rest_3_.refs_1_), channel_id=1, source_target_pairs={{0,2},{1,3},{2,4},{3,5},{4,6},{5,7},{6,0},{7,1},{8,14},{9,15},{10,... | collective-permute-start | bytes 393224 | tf_op jit(solution)/shard_map/ppermute | solution.py:272
  19.4 7.0 %collective-permute-start.9 = (bf16[512,128]{1,0:T(8,128)(2,1)S(1)}, bf16[512,128]{1,0:T(8,128)(2,1)S(1)}, u32[]{:S(2)}, u32[]{:S(2)}) collective-permute-start(bf16[512,128]{1,0:T(8,128)(2,1)S(1)} %get-tuple-element.39), channel_id=1, source_target_pairs={{0,16},{1,17},{2,18},{3,19},{4,20},{5,21},{6,22},{7,23},{8,24},{9,... | collective-permute-start | bytes 393224 | tf_op jit(solution)/shard_map/ppermute | solution.py:269
  26.8 1.4 %collective-permute-start.12 = (bf16[512,128]{1,0:T(8,128)(2,1)S(1)}, bf16[512,128]{1,0:T(8,128)(2,1)S(1)}, u32[]{:S(2)}, u32[]{:S(2)}) collective-permute-start(bf16[512,128]{1,0:T(8,128)(2,1)S(1)} %shard_map.76.mine_ref), channel_id=1, source_target_pairs={{0,8},{1,9},{2,10},{3,11},{4,12},{5,13},{6,14},{7,15},{8,0},{9,1},... | collective-permute-start | bytes 393224 | tf_op jit(solution)/shard_map/ppermute | solution.py:266
  28.5 7.7 %collective-permute-start.13 = (bf16[512,128]{1,0:T(8,128)(2,1)S(1)}, bf16[512,128]{1,0:T(8,128)(2,1)S(1)}, u32[]{:S(2)}, u32[]{:S(2)}) collective-permute-start(bf16[512,128]{1,0:T(8,128)(2,1)S(1)} %get-tuple-element.41.now_ref.rest_3_.refs_2_), channel_id=1, source_target_pairs={{0,1},{1,2},{2,3},{3,4},{4,5},{5,6},{6,7},{7,0},{8,15},{9,8},{10,9... | collective-permute-start | bytes 393224 | tf_op jit(solution)/shard_map/ppermute | solution.py:272
  30.4 7.0 %collective-permute-start.14 = (bf16[512,128]{1,0:T(8,128)(2,1)S(1)}, bf16[512,128]{1,0:T(8,128)(2,1)S(1)}, u32[]{:S(2)}, u32[]{:S(2)}) collective-permute-start(bf16[512,128]{1,0:T(8,128)(2,1)S(1)} %get-tuple-element.41.now_ref.rest_3_.refs_2_), channel_id=1, source_target_pairs={{0,2},{1,3},{2,4},{3,5},{4,6},{5,7},{6,0},{7,1},{8,14},{9,15},{10,... | collective-permute-start | bytes 393224 | tf_op jit(solution)/shard_map/ppermute | solution.py:272
  30.8 6.6 %collective-permute-start.15 = (bf16[512,128]{1,0:T(8,128)(2,1)S(1)}, bf16[512,128]{1,0:T(8,128)(2,1)S(1)}, u32[]{:S(2)}, u32[]{:S(2)}) collective-permute-start(bf16[512,128]{1,0:T(8,128)(2,1)S(1)} %get-tuple-element.42), channel_id=1, source_target_pairs={{0,16},{1,17},{2,18},{3,19},{4,20},{5,21},{6,22},{7,23},{8,24},{9,... | collective-permute-start | bytes 393224 | tf_op jit(solution)/shard_map/ppermute | solution.py:269
  37.8 1.4 %collective-permute-start.16 = (bf16[512,128]{1,0:T(8,128)(2,1)S(1)}, bf16[512,128]{1,0:T(8,128)(2,1)S(1)}, u32[]{:S(2)}, u32[]{:S(2)}) collective-permute-start(bf16[512,128]{1,0:T(8,128)(2,1)S(1)} %shard_map.79.mine_ref), channel_id=1, source_target_pairs={{0,8},{1,9},{2,10},{3,11},{4,12},{5,13},{6,14},{7,15},{8,0},{9,1},... | collective-permute-start | bytes 393224 | tf_op jit(solution)/shard_map/ppermute | solution.py:266
  39.4 7.7 %collective-permute-start.17 = (bf16[512,128]{1,0:T(8,128)(2,1)S(1)}, bf16[512,128]{1,0:T(8,128)(2,1)S(1)}, u32[]{:S(2)}, u32[]{:S(2)}) collective-permute-start(bf16[512,128]{1,0:T(8,128)(2,1)S(1)} %get-tuple-element.43.now_ref.rest_3_.refs_3_), channel_id=1, source_target_pairs={{0,1},{1,2},{2,3},{3,4},{4,5},{5,6},{6,7},{7,0},{8,15},{9,8},{10,9... | collective-permute-start | bytes 393224 | tf_op jit(solution)/shard_map/ppermute | solution.py:272
  40.3 7.2 %collective-permute-start.18 = (bf16[512,128]{1,0:T(8,128)(2,1)S(1)}, bf16[512,128]{1,0:T(8,128)(2,1)S(1)}, u32[]{:S(2)}, u32[]{:S(2)}) collective-permute-start(bf16[512,128]{1,0:T(8,128)(2,1)S(1)} %get-tuple-element.43.now_ref.rest_3_.refs_3_), channel_id=1, source_target_pairs={{0,2},{1,3},{2,4},{3,5},{4,6},{5,7},{6,0},{7,1},{8,14},{9,15},{10,... | collective-permute-start | bytes 393224 | tf_op jit(solution)/shard_map/ppermute | solution.py:272
  40.5 7.0 %collective-permute-start.19 = (bf16[512,128]{1,0:T(8,128)(2,1)S(1)}, bf16[512,128]{1,0:T(8,128)(2,1)S(1)}, u32[]{:S(2)}, u32[]{:S(2)}) collective-permute-start(bf16[512,128]{1,0:T(8,128)(2,1)S(1)} %get-tuple-element.44), channel_id=1, source_target_pairs={{0,16},{1,17},{2,18},{3,19},{4,20},{5,21},{6,22},{7,23},{8,24},{9,... | collective-permute-start | bytes 393224 | tf_op jit(solution)/shard_map/ppermute | solution.py:269
  47.9 1.4 %collective-permute-start.20 = (bf16[512,128]{1,0:T(8,128)(2,1)S(1)}, bf16[512,128]{1,0:T(8,128)(2,1)S(1)}, u32[]{:S(2)}, u32[]{:S(2)}) collective-permute-start(bf16[512,128]{1,0:T(8,128)(2,1)S(1)} %shard_map.82.mine_ref), channel_id=1, source_target_pairs={{0,8},{1,9},{2,10},{3,11},{4,12},{5,13},{6,14},{7,15},{8,0},{9,1},... | collective-permute-start | bytes 393224 | tf_op jit(solution)/shard_map/ppermute | solution.py:266
  49.5 8.0 %collective-permute-start.21 = (bf16[512,128]{1,0:T(8,128)(2,1)S(1)}, bf16[512,128]{1,0:T(8,128)(2,1)S(1)}, u32[]{:S(2)}, u32[]{:S(2)}) collective-permute-start(bf16[512,128]{1,0:T(8,128)(2,1)S(1)} %get-tuple-element.45.now_ref.refs_4_.rest_3_), channel_id=1, source_target_pairs={{0,1},{1,2},{2,3},{3,4},{4,5},{5,6},{6,7},{7,0},{8,15},{9,8},{10,9... | collective-permute-start | bytes 393224 | tf_op jit(solution)/shard_map/ppermute | solution.py:272
  51.3 7.1 %collective-permute-start.22 = (bf16[512,128]{1,0:T(8,128)(2,1)S(1)}, bf16[512,128]{1,0:T(8,128)(2,1)S(1)}, u32[]{:S(2)}, u32[]{:S(2)}) collective-permute-start(bf16[512,128]{1,0:T(8,128)(2,1)S(1)} %get-tuple-element.45.now_ref.refs_4_.rest_3_), channel_id=1, source_target_pairs={{0,2},{1,3},{2,4},{3,5},{4,6},{5,7},{6,0},{7,1},{8,14},{9,15},{10,... | collective-permute-start | bytes 393224 | tf_op jit(solution)/shard_map/ppermute | solution.py:272
  51.6 6.7 %collective-permute-start.23 = (bf16[512,128]{1,0:T(8,128)(2,1)S(1)}, bf16[512,128]{1,0:T(8,128)(2,1)S(1)}, u32[]{:S(2)}, u32[]{:S(2)}) collective-permute-start(bf16[512,128]{1,0:T(8,128)(2,1)S(1)} %get-tuple-element.46), channel_id=1, source_target_pairs={{0,16},{1,17},{2,18},{3,19},{4,20},{5,21},{6,22},{7,23},{8,24},{9,... | collective-permute-start | bytes 393224 | tf_op jit(solution)/shard_map/ppermute | solution.py:269
  58.8 1.4 %collective-permute-start.24 = (bf16[512,128]{1,0:T(8,128)(2,1)S(1)}, bf16[512,128]{1,0:T(8,128)(2,1)S(1)}, u32[]{:S(2)}, u32[]{:S(2)}) collective-permute-start(bf16[512,128]{1,0:T(8,128)(2,1)S(1)} %shard_map.85.mine_ref), channel_id=1, source_target_pairs={{0,8},{1,9},{2,10},{3,11},{4,12},{5,13},{6,14},{7,15},{8,0},{9,1},... | collective-permute-start | bytes 393224 | tf_op jit(solution)/shard_map/ppermute | solution.py:266
  60.4 5.6 %collective-permute-start.25 = (bf16[512,128]{1,0:T(8,128)(2,1)S(1)}, bf16[512,128]{1,0:T(8,128)(2,1)S(1)}, u32[]{:S(2)}, u32[]{:S(2)}) collective-permute-start(bf16[512,128]{1,0:T(8,128)(2,1)S(1)} %get-tuple-element.48), channel_id=1, source_target_pairs={{0,16},{1,17},{2,18},{3,19},{4,20},{5,21},{6,22},{7,23},{8,24},{9,... | collective-permute-start | bytes 393224 | tf_op jit(solution)/shard_map/ppermute | solution.py:269
  62.0 7.8 %collective-permute-start.28 = (bf16[512,128]{1,0:T(8,128)(2,1)S(1)}, bf16[512,128]{1,0:T(8,128)(2,1)S(1)}, u32[]{:S(2)}, u32[]{:S(2)}) collective-permute-start(bf16[512,128]{1,0:T(8,128)(2,1)S(1)} %get-tuple-element.47.refs_5_.rest_3_.now_ref), channel_id=1, source_target_pairs={{0,1},{1,2},{2,3},{3,4},{4,5},{5,6},{6,7},{7,0},{8,15},{9,8},{10,9... | collective-permute-start | bytes 393224 | tf_op jit(solution)/shard_map/ppermute | solution.py:272
  63.1 7.7 %collective-permute-start.29 = (bf16[512,128]{1,0:T(8,128)(2,1)S(1)}, bf16[512,128]{1,0:T(8,128)(2,1)S(1)}, u32[]{:S(2)}, u32[]{:S(2)}) collective-permute-start(bf16[512,128]{1,0:T(8,128)(2,1)S(1)} %get-tuple-element.47.refs_5_.rest_3_.now_ref), channel_id=1, source_target_pairs={{0,2},{1,3},{2,4},{3,5},{4,6},{5,7},{6,0},{7,1},{8,14},{9,15},{10,... | collective-permute-start | bytes 393224 | tf_op jit(solution)/shard_map/ppermute | solution.py:272
  66.0 7.8 %collective-permute-start.26 = (bf16[512,128]{1,0:T(8,128)(2,1)S(1)}, bf16[512,128]{1,0:T(8,128)(2,1)S(1)}, u32[]{:S(2)}, u32[]{:S(2)}) collective-permute-start(bf16[512,128]{1,0:T(8,128)(2,1)S(1)} %collective-permute-done.25.refs_6_.now_ref.field_ref), channel_id=1, source_target_pairs={{0,1},{1,2},{2,3},{3,4},{4,5},{5,6},{6,7},{7,0},{8,15},{9,8},{10,9... | collective-permute-start | bytes 393224 | tf_op jit(solution)/shard_map/ppermute | solution.py:272
  67.2 7.0 %collective-permute-start.27 = (bf16[512,128]{1,0:T(8,128)(2,1)S(1)}, bf16[512,128]{1,0:T(8,128)(2,1)S(1)}, u32[]{:S(2)}, u32[]{:S(2)}) collective-permute-start(bf16[512,128]{1,0:T(8,128)(2,1)S(1)} %collective-permute-done.25.refs_6_.now_ref.field_ref), channel_id=1, source_target_pairs={{0,2},{1,3},{2,4},{3,5},{4,6},{5,7},{6,0},{7,1},{8,14},{9,15},{10,... | collective-permute-start | bytes 393224 | tf_op jit(solution)/shard_map/ppermute | solution.py:272
  71.7 5.0 %collective-permute-start.30 = (bf16[512,128]{1,0:T(8,128)(2,1)S(1)}, bf16[512,128]{1,0:T(8,128)(2,1)S(1)}, u32[]{:S(2)}, u32[]{:S(2)}) collective-permute-start(bf16[512,128]{1,0:T(8,128)(2,1)S(1)} %get-tuple-element.55), channel_id=1, source_target_pairs={{0,16},{1,17},{2,18},{3,19},{4,20},{5,21},{6,22},{7,23},{8,24},{9,... | collective-permute-start | bytes 393224 | tf_op jit(solution)/shard_map/ppermute | solution.py:269
  71.8 5.1 %collective-permute-start.32 = (bf16[512,128]{1,0:T(8,128)(2,1)S(1)}, bf16[512,128]{1,0:T(8,128)(2,1)S(1)}, u32[]{:S(2)}, u32[]{:S(2)}) collective-permute-start(bf16[512,128]{1,0:T(8,128)(2,1)S(1)} %get-tuple-element.59), channel_id=1, source_target_pairs={{0,8},{1,9},{2,10},{3,11},{4,12},{5,13},{6,14},{7,15},{8,0},{9,1},... | collective-permute-start | bytes 393224 | tf_op jit(solution)/shard_map/ppermute | solution.py:266
  (5 other events, 14.4 us)

commit v7 on v6

--- a/solution.py
+++ b/solution.py
@@ -168,38 +168,34 @@
     out_ref[...] = (total + came(step, pairs, field_ref, history)).astype(BF16)
 
 
-def last_body(near_ref, first_ref, second_ref, early_ref, far_ref, own_ref, now_ref, even_ref, odd_ref):
-    core, _ = place()
-    even_ref[...] = early_ref[...] + window(near_ref, first_ref, second_ref)
+def even_body(step, pairs, near_ref, first_ref, second_ref, early_ref, *rest):
+    *field, even_ref, out_ref = rest
+    total = early_ref[...] + window(near_ref, first_ref, second_ref)
+    if field:
+        total += came(step, pairs, field[0], field[1:])
+    even_ref[...] = total
+    out_ref[...] = total.astype(BF16)
+
+
+def odd_body(even_ref, far_ref, first_ref, second_ref, own_ref, now_ref, keep_ref, send_ref):
+    core, _ = place()
     local = jnp.where(core == 1, now_ref[...], jnp.zeros_like(now_ref))
-    odd_ref[...] = window(far_ref, first_ref, second_ref) + dot(own_ref[...], local)
-
-
-def share_body(step, steps, pairs, even_ref, odd_ref, field_ref, *rest):
-    *rest, keep_ref, send_ref = rest
-    history, field_out_ref = (rest[:-1], rest[-1]) if step < steps + pairs - 2 else (rest, None)
-    core, pair = place()
-    even = even_ref[...] + came(step, pairs, field_ref, history)
-    odd = odd_ref[...]
-    ended = pair == step - steps
-    late = field_ref[...].astype(F32)
-    keep_ref[...] = jnp.where(ended, late, jnp.where(core == 1, odd, even))
-    send_ref[...] = jnp.where(ended, late, jnp.where(core == 0, odd, even)).astype(BF16)
-    if field_out_ref is not None:
-        field_out_ref[...] = even.astype(BF16)
-
-
-def finish_body(step, steps, mine_ref, other_ref, *rest):
-    *earlier, result_ref = rest
+    odd = window(far_ref, first_ref, second_ref) + dot(own_ref[...], local)
+    even = even_ref[...]
+    keep_ref[...] = jnp.where(core == 1, odd, even)
+    send_ref[...] = jnp.where(core == 0, odd, even).astype(BF16)
+
+
+def finish_body(step, steps, *refs):
+    *earlier, mine_ref, other_ref, result_ref = refs
     core, pair = place()
     field = mine_ref[...] + other_ref[...].astype(F32)
     if earlier:
-        before = earlier[0][...]
-        ended = pair == step - steps
-        adds = jnp.logical_and(ended, core == 1)
-        field = jnp.where(
-            adds, before + field, jnp.where(pair == step - (steps - 1), field, before)
-        )
+        before_ref, straight_ref, crossed_ref = earlier
+        adds = jnp.logical_and(core == 1, pair == step - steps)
+        rest = straight_ref[...].astype(F32) + crossed_ref[...].astype(F32)
+        before = before_ref[...] + jnp.where(adds, rest, 0.0)
+        field = jnp.where(pair == step - (steps - 1), field, before)
     result_ref[...] = field
 
 
@@ -267,6 +263,9 @@
 
     def pair_moved(value, hop):
         return lax.ppermute(value, AXES, everyone(lambda d, s: ((d + 2 * hop) % lags, s)))
+
+    def crossed(value):
+        return lax.ppermute(value, AXES, everyone(lambda d, s: (((d - 2) % lags) ^ 1, s)))
 
     def halo(value, hop):
         return lax.ppermute(
@@ -326,24 +325,24 @@
         else:
             if step < rounds - 1:
                 windows = halo(current_in, 1), halo(current_in, 2)
-            even, odd = call(
-                last_body,
-                [field_shape, field_shape],
-                received + [far, own, current],
+            even, next_field = call(
+                functools.partial(even_body, step, pairs),
+                [field_shape, current_shape],
+                received + ([field_in] + past if step < rounds - 1 else []),
+            )
+            mine, send = call(
+                odd_body,
+                [field_shape, current_shape],
+                [even, far, first, second, own, current],
                 after=collected,
-                microseconds=0.5 if step < rounds - 1 else 20,
-            )
-            *fields, mine, send = call(
-                functools.partial(share_body, step, steps, pairs),
-                [current_shape] * (step < rounds - 1) + [field_shape, current_shape],
-                [even, odd, field_in] + past,
-            )
-            field = fields[0] if fields else None
+            )
+            earlier = [result, field_in, crossed(field)] if step >= steps else []
             (result,) = call(
                 functools.partial(finish_body, step, steps),
                 [field_shape],
-                [mine, swapped(send)] + ([result] if step >= steps else []),
-            )
+                earlier + [mine, swapped(send)],
+            )
+            field = next_field
             current, going = current_in, field
     return (out, result[None])
 

time: 79.2 us -> 79.7 us (level)
  starting transfers between devices: 25.2 us -> 23.3 us
  waiting for transfers between devices: 39.4 us -> 41 us
  Pallas kernels: 12.8 us -> 13.6 us
    ppermute x7, starting transfers between devices: 9.09 us -> 7.16 us  [pair_moved(): lax.ppermute(value, AXES, everyone(lambda d, s: ((d + 2 * hop) % lags, s)))]
    ppermute x7, waiting for transfers between devices: 4.13 us -> 5.76 us  [pair_moved(): lax.ppermute(value, AXES, everyone(lambda d, s: ((d + 2 * hop) % lags, s)))]
    ppermute x12, waiting for transfers between devices: 7.88 us -> 6.59 us  [swapped(): return lax.ppermute(value, AXES, everyone(lambda d, s: (d ^ 1, s)))]
    ppermute x0 -> x1, waiting for transfers between devices: none -> 1.22 us  [crossed(): lax.ppermute(value, AXES, everyone(lambda d, s: ((d - 2) % lags ^ 1, s)))]
    pallas_call x27, Pallas kernels: 11.1 us -> 11.9 us  [call(): pl.pallas_call(body, out_shape=tuple(outs), in_specs=specs, out_specs=tup...]
  transfers between devices with their start and end apart: 33 -> 34, of which waited for: 22 -> 19; matrix products, arithmetic and copies ran while one was open for 0% -> 0% of each run, Pallas kernels for 11% -> 12%
where the time goes in v7:
time: 79.7 us; the launch traced here: 79.5 us
  waiting for transfers between devices  41 us (51%)
  starting transfers between devices  23.3 us (29%)
  Pallas kernels  13.6 us (17%)
  between operations  0.92 us (1%)
    ppermute x14, waiting for transfers between devices, halo(): lax.ppermute(value, AXES, everyone(lambda d, s: (d, (s + (hop if d % 2 ==...  27.4 us
    ppermute x14, starting transfers between devices, halo(): lax.ppermute(value, AXES, everyone(lambda d, s: (d, (s + (hop if d % 2 ==...  13.4 us
    pallas_call x27, Pallas kernels, call(): pl.pallas_call(body, out_shape=tuple(outs), in_specs=specs, out_specs=tup...  11.9 us
    ppermute x7, starting transfers between devices, pair_moved(): lax.ppermute(value, AXES, everyone(lambda d, s: ((d + 2 * hop) % lags, s)))  7.16 us
    ppermute x12, waiting for transfers between devices, swapped(): return lax.ppermute(value, AXES, everyone(lambda d, s: (d ^ 1, s)))  6.59 us
    ppermute x7, waiting for transfers between devices, pair_moved(): lax.ppermute(value, AXES, everyone(lambda d, s: ((d + 2 * hop) % lags, s)))  5.76 us
    ppermute x12, starting transfers between devices, swapped(): return lax.ppermute(value, AXES, everyone(lambda d, s: (d ^ 1, s)))  2.7 us
    pallas_call x1, Pallas kernels, spread(): pl.pallas_call(functools.partial(spread_body, groups), out_shape=(matrix(...  1.74 us
  transfers between devices with their start and end apart: 34, of which 19 were waited for; matrix products, arithmetic and copies ran while one was open for 0% of the time, Pallas kernels for 12%

profile of v7, /device:TPU:0, one launch (start us, length us, event | category | flops | bytes accessed | tf_op | source)
XLA Modules:
  0.0 79.5 jit_solution(17035716412774259297)
XLA Ops:
  1.2 0.7 copy-done.3
  1.9 1.7 %shard_map.70 = (bf16[512,1024]{1,0:T(8,128)(2,1)S(1)}, bf16[512,512]{1,0:T(8,128)(2,1)S(1)}, bf16[128,1024]{1,0:T(8,128)(2,1)S(1)}, bf16[128,1024]{1,0:T(8,128)...) custom-call(s32[4,16]{1,0:T(4,128)S(1)} %bitcast.8, bf16[4,16,128,128]{3,2,1,0:T(8,128)(2,1)} %bitcast.9), custom_call_target="tpu_custom_call" | custom-call | bytes 14400000 | tf_op jit(solution)/shard_map/pallas_call | solution.py:101
  4.9 2.7 %collective-permute-start.5 = (bf16[512,128]{1,0:T(8,128)(2,1)S(1)}, bf16[512,128]{1,0:T(8,128)(2,1)S(1)}, u32[]{:S(2)}, u32[]{:S(2)}) collective-permute-start(bf16[512,128]{1,0:T(8,128)(2,1)S(1)} %shard_map.69.now_ref.rest_3_.refs_0_), channel_id=1, source_target_pairs={{0,1},{1,2},{2,3},{3,4},{4,5},{5,6},{6,7},{7,0},{8,15},{9,8},{10,9... | collective-permute-start | bytes 393224 | tf_op jit(solution)/shard_map/ppermute | solution.py:271
  7.6 1.6 %collective-permute-start.6 = (bf16[512,128]{1,0:T(8,128)(2,1)S(1)}, bf16[512,128]{1,0:T(8,128)(2,1)S(1)}, u32[]{:S(2)}, u32[]{:S(2)}) collective-permute-start(bf16[512,128]{1,0:T(8,128)(2,1)S(1)} %shard_map.69.now_ref.rest_3_.refs_0_), channel_id=1, source_target_pairs={{0,2},{1,3},{2,4},{3,5},{4,6},{5,7},{6,0},{7,1},{8,14},{9,15},{10,... | collective-permute-start | bytes 393224 | tf_op jit(solution)/shard_map/ppermute | solution.py:271
  9.2 1.5 %collective-permute-start.7 = (bf16[512,128]{1,0:T(8,128)(2,1)S(1)}, bf16[512,128]{1,0:T(8,128)(2,1)S(1)}, u32[]{:S(2)}, u32[]{:S(2)}) collective-permute-start(bf16[512,128]{1,0:T(8,128)(2,1)S(1)} %shard_map.69.now_ref.rest_3_.refs_0_), channel_id=1, source_target_pairs={{0,16},{1,17},{2,18},{3,19},{4,20},{5,21},{6,22},{7,23},{8,24},{9,... | collective-permute-start | bytes 393224 | tf_op jit(solution)/shard_map/ppermute | solution.py:265
  11.2 3.7 %collective-permute-done.5.refs_1_.rest_1_ = bf16[512,128]{1,0:T(8,128)(2,1)S(1)} collective-permute-done((bf16[512,128]{1,0:T(8,128)(2,1)S(1)}, bf16[512,128]{1,0:T(8,128)(2,1)S(1)}, u32[]{:S(2)}, u32[]{:S(2)}) %collective-permute-start.5) | collective-permute-done | bytes 131104 | tf_op jit(solution)/shard_map/ppermute | solution.py:271
  14.9 0.9 %collective-permute-done.6.refs_2_.rest_2_ = bf16[512,128]{1,0:T(8,128)(2,1)S(1)} collective-permute-done((bf16[512,128]{1,0:T(8,128)(2,1)S(1)}, bf16[512,128]{1,0:T(8,128)(2,1)S(1)}, u32[]{:S(2)}, u32[]{:S(2)}) %collective-permute-start.6) | collective-permute-done | bytes 131104 | tf_op jit(solution)/shard_map/ppermute | solution.py:271
  16.4 1.2 %collective-permute-done.8.other_ref = bf16[512,128]{1,0:T(8,128)(2,1)S(1)} collective-permute-done((bf16[512,128]{1,0:T(8,128)(2,1)S(1)}, bf16[512,128]{1,0:T(8,128)(2,1)S(1)}, u32[]{:S(2)}, u32[]{:S(2)}) %collective-permute-start.8) | collective-permute-done | bytes 131104 | tf_op jit(solution)/shard_map/ppermute | solution.py:262
  17.8 1.6 %collective-permute-start.9 = (bf16[512,128]{1,0:T(8,128)(2,1)S(1)}, bf16[512,128]{1,0:T(8,128)(2,1)S(1)}, u32[]{:S(2)}, u32[]{:S(2)}) collective-permute-start(bf16[512,128]{1,0:T(8,128)(2,1)S(1)} %get-tuple-element.37), channel_id=1, source_target_pairs={{0,16},{1,17},{2,18},{3,19},{4,20},{5,21},{6,22},{7,23},{8,24},{9,... | collective-permute-start | bytes 393224 | tf_op jit(solution)/shard_map/ppermute | solution.py:265
  19.4 1.3 %collective-permute-start.10 = (bf16[512,128]{1,0:T(8,128)(2,1)S(1)}, bf16[512,128]{1,0:T(8,128)(2,1)S(1)}, u32[]{:S(2)}, u32[]{:S(2)}) collective-permute-start(bf16[512,128]{1,0:T(8,128)(2,1)S(1)} %get-tuple-element.36.now_ref.rest_3_.refs_1_), channel_id=1, source_target_pairs={{0,1},{1,2},{2,3},{3,4},{4,5},{5,6},{6,7},{7,0},{8,15},{9,8},{10,9... | collective-permute-start | bytes 393224 | tf_op jit(solution)/shard_map/ppermute | solution.py:271
  21.5 2.0 %collective-permute-done.9.field_ref.came_ref = bf16[512,128]{1,0:T(8,128)(2,1)S(1)} collective-permute-done((bf16[512,128]{1,0:T(8,128)(2,1)S(1)}, bf16[512,128]{1,0:T(8,128)(2,1)S(1)}, u32[]{:S(2)}, u32[]{:S(2)}) %collective-permute-start.9) | collective-permute-done | bytes 131104 | tf_op jit(solution)/shard_map/ppermute | solution.py:265
  23.4 4.0 %collective-permute-done.10.first_ref.rest_1_ = bf16[512,128]{1,0:T(8,128)(2,1)S(1)} collective-permute-done((bf16[512,128]{1,0:T(8,128)(2,1)S(1)}, bf16[512,128]{1,0:T(8,128)(2,1)S(1)}, u32[]{:S(2)}, u32[]{:S(2)}) %collective-permute-start.10) | collective-permute-done | bytes 131104 | tf_op jit(solution)/shard_map/ppermute | solution.py:271
  28.1 1.3 %collective-permute-done.12.other_ref = bf16[512,128]{1,0:T(8,128)(2,1)S(1)} collective-permute-done((bf16[512,128]{1,0:T(8,128)(2,1)S(1)}, bf16[512,128]{1,0:T(8,128)(2,1)S(1)}, u32[]{:S(2)}, u32[]{:S(2)}) %collective-permute-start.12) | collective-permute-done | bytes 131104 | tf_op jit(solution)/shard_map/ppermute | solution.py:262
  29.7 1.9 %collective-permute-start.13 = (bf16[512,128]{1,0:T(8,128)(2,1)S(1)}, bf16[512,128]{1,0:T(8,128)(2,1)S(1)}, u32[]{:S(2)}, u32[]{:S(2)}) collective-permute-start(bf16[512,128]{1,0:T(8,128)(2,1)S(1)} %get-tuple-element.39.now_ref.rest_3_.refs_2_), channel_id=1, source_target_pairs={{0,1},{1,2},{2,3},{3,4},{4,5},{5,6},{6,7},{7,0},{8,15},{9,8},{10,9... | collective-permute-start | bytes 393224 | tf_op jit(solution)/shard_map/ppermute | solution.py:271
  32.9 4.6 %collective-permute-done.13.refs_1_.rest_1_ = bf16[512,128]{1,0:T(8,128)(2,1)S(1)} collective-permute-done((bf16[512,128]{1,0:T(8,128)(2,1)S(1)}, bf16[512,128]{1,0:T(8,128)(2,1)S(1)}, u32[]{:S(2)}, u32[]{:S(2)}) %collective-permute-start.13) | collective-permute-done | bytes 131104 | tf_op jit(solution)/shard_map/ppermute | solution.py:271
  37.5 1.4 %collective-permute-done.14.refs_2_.rest_2_ = bf16[512,128]{1,0:T(8,128)(2,1)S(1)} collective-permute-done((bf16[512,128]{1,0:T(8,128)(2,1)S(1)}, bf16[512,128]{1,0:T(8,128)(2,1)S(1)}, u32[]{:S(2)}, u32[]{:S(2)}) %collective-permute-start.14) | collective-permute-done | bytes 131104 | tf_op jit(solution)/shard_map/ppermute | solution.py:271
  39.4 1.3 %collective-permute-done.16.other_ref = bf16[512,128]{1,0:T(8,128)(2,1)S(1)} collective-permute-done((bf16[512,128]{1,0:T(8,128)(2,1)S(1)}, bf16[512,128]{1,0:T(8,128)(2,1)S(1)}, u32[]{:S(2)}, u32[]{:S(2)}) %collective-permute-start.16) | collective-permute-done | bytes 131104 | tf_op jit(solution)/shard_map/ppermute | solution.py:262
  42.7 6.3 %collective-permute-done.17.refs_1_.rest_1_ = bf16[512,128]{1,0:T(8,128)(2,1)S(1)} collective-permute-done((bf16[512,128]{1,0:T(8,128)(2,1)S(1)}, bf16[512,128]{1,0:T(8,128)(2,1)S(1)}, u32[]{:S(2)}, u32[]{:S(2)}) %collective-permute-start.17) | collective-permute-done | bytes 131104 | tf_op jit(solution)/shard_map/ppermute | solution.py:271
  49.7 1.3 %collective-permute-done.20.other_ref = bf16[512,128]{1,0:T(8,128)(2,1)S(1)} collective-permute-done((bf16[512,128]{1,0:T(8,128)(2,1)S(1)}, bf16[512,128]{1,0:T(8,128)(2,1)S(1)}, u32[]{:S(2)}, u32[]{:S(2)}) %collective-permute-start.20) | collective-permute-done | bytes 131104 | tf_op jit(solution)/shard_map/ppermute | solution.py:262
  51.2 1.9 %collective-permute-start.21 = (bf16[512,128]{1,0:T(8,128)(2,1)S(1)}, bf16[512,128]{1,0:T(8,128)(2,1)S(1)}, u32[]{:S(2)}, u32[]{:S(2)}) collective-permute-start(bf16[512,128]{1,0:T(8,128)(2,1)S(1)} %get-tuple-element.43.now_ref.refs_4_.rest_3_), channel_id=1, source_target_pairs={{0,1},{1,2},{2,3},{3,4},{4,5},{5,6},{6,7},{7,0},{8,15},{9,8},{10,9... | collective-permute-start | bytes 393224 | tf_op jit(solution)/shard_map/ppermute | solution.py:271
  54.7 4.3 %collective-permute-done.21.refs_1_.rest_1_ = bf16[512,128]{1,0:T(8,128)(2,1)S(1)} collective-permute-done((bf16[512,128]{1,0:T(8,128)(2,1)S(1)}, bf16[512,128]{1,0:T(8,128)(2,1)S(1)}, u32[]{:S(2)}, u32[]{:S(2)}) %collective-permute-start.21) | collective-permute-done | bytes 131104 | tf_op jit(solution)/shard_map/ppermute | solution.py:271
  59.0 1.1 %collective-permute-done.22.refs_2_.rest_2_ = bf16[512,128]{1,0:T(8,128)(2,1)S(1)} collective-permute-done((bf16[512,128]{1,0:T(8,128)(2,1)S(1)}, bf16[512,128]{1,0:T(8,128)(2,1)S(1)}, u32[]{:S(2)}, u32[]{:S(2)}) %collective-permute-start.22) | collective-permute-done | bytes 131104 | tf_op jit(solution)/shard_map/ppermute | solution.py:271
  60.6 1.3 %collective-permute-done.24.other_ref = bf16[512,128]{1,0:T(8,128)(2,1)S(1)} collective-permute-done((bf16[512,128]{1,0:T(8,128)(2,1)S(1)}, bf16[512,128]{1,0:T(8,128)(2,1)S(1)}, u32[]{:S(2)}, u32[]{:S(2)}) %collective-permute-start.24) | collective-permute-done | bytes 131104 | tf_op jit(solution)/shard_map/ppermute | solution.py:262
  62.8 0.8 %collective-permute-start.26 = (bf16[512,128]{1,0:T(8,128)(2,1)S(1)}, bf16[512,128]{1,0:T(8,128)(2,1)S(1)}, u32[]{:S(2)}, u32[]{:S(2)}) collective-permute-start(bf16[512,128]{1,0:T(8,128)(2,1)S(1)} %get-tuple-element.45.refs_5_.now_ref.rest_3_), channel_id=1, source_target_pairs={{0,1},{1,2},{2,3},{3,4},{4,5},{5,6},{6,7},{7,0},{8,15},{9,8},{10,9... | collective-permute-start | bytes 393224 | tf_op jit(solution)/shard_map/ppermute | solution.py:271
  64.1 3.8 %collective-permute-done.25.refs_6_.rest_0_.now_ref.refs_5_ = bf16[512,128]{1,0:T(8,128)(2,1)S(1)} collective-permute-done((bf16[512,128]{1,0:T(8,128)(2,1)S(1)}, bf16[512,128]{1,0:T(8,128)(2,1)S(1)}, u32[]{:S(2)}, u32[]{:S(2)}) %collective-permute-start.25) | collective-permute-done | bytes 131104 | tf_op jit(solution)/shard_map/ppermute | solution.py:265
  67.8 0.8 %collective-permute-start.31 = (bf16[512,128]{1,0:T(8,128)(2,1)S(1)}, bf16[512,128]{1,0:T(8,128)(2,1)S(1)}, u32[]{:S(2)}, u32[]{:S(2)}) collective-permute-start(bf16[512,128]{1,0:T(8,128)(2,1)S(1)} %collective-permute-done.25.refs_6_.rest_0_.now_ref.refs_5_), channel_id=1, source_target_pairs={{0,1},{1,2},{2,3},{3,4},{4,5},{5,6},{6,7},{7,0},{8,15},{9,8},{10,9... | collective-permute-start | bytes 393224 | tf_op jit(solution)/shard_map/ppermute | solution.py:271
  69.7 0.9 %collective-permute-done.26.first_ref.rest_1_ = bf16[512,128]{1,0:T(8,128)(2,1)S(1)} collective-permute-done((bf16[512,128]{1,0:T(8,128)(2,1)S(1)}, bf16[512,128]{1,0:T(8,128)(2,1)S(1)}, u32[]{:S(2)}, u32[]{:S(2)}) %collective-permute-start.26) | collective-permute-done | bytes 131104 | tf_op jit(solution)/shard_map/ppermute | solution.py:271
  71.0 1.9 %collective-permute-start.29 = (bf16[512,128]{1,0:T(8,128)(2,1)S(1)}, bf16[512,128]{1,0:T(8,128)(2,1)S(1)}, u32[]{:S(2)}, u32[]{:S(2)}) collective-permute-start(bf16[512,128]{1,0:T(8,128)(2,1)S(1)} %get-tuple-element.51), channel_id=1, source_target_pairs={{0,16},{1,17},{2,18},{3,19},{4,20},{5,21},{6,22},{7,23},{8,24},{9,... | collective-permute-start | bytes 393224 | tf_op jit(solution)/shard_map/ppermute | solution.py:265
  73.8 1.0 %shard_map.87 = (bf16[6,512,128]{2,1,0:T(8,128)(2,1)}, f32[8,128]{1,0:T(8,128)S(1)}) custom-call(bf16[512,128]{1,0:T(8,128)(2,1)S(1)} %shard_map.69.now_ref.rest_3_.refs_0_, bf16[512,128]{1,0:T(8,128)(2,1)S(1)} %get-tuple-element.36.now_ref.rest_3_.refs_1_, bf16[512,128]{1,0:T(8,128)(2,1)S(1)} %get-tuple-element.39.now_ref.rest_3_.refs_2_, ...), custom_call_target="tpu_custom_call" | custom-call | bytes 1800000 | tf_op jit(solution)/shard_map/pallas_call | solution.py:40
  75.5 1.1 %shard_map.93 = (f32[512,128]{1,0:T(8,128)S(1)}, bf16[512,128]{1,0:T(8,128)(2,1)}) custom-call(bf16[512,1024]{1,0:T(8,128)(2,1)S(1)} %get-tuple-element.34.refs_0_.near_ref, bf16[512,128]{1,0:T(8,128)(2,1)S(1)} %collective-permute-done.31.first_ref.refs_2_, bf16[512,128]{1,0:T(8,128)(2,1)S(1)} %collective-permute-done.32.second_ref.refs_3_, ...), custom_call_target="tpu_custom_call" | custom-call | bytes 1800000 | tf_op jit(solution)/shard_map/pallas_call | solution.py:40
  77.5 1.2 %collective-permute-done.30.refs_2_ = bf16[512,128]{1,0:T(8,128)(2,1)S(1)} collective-permute-done((bf16[512,128]{1,0:T(8,128)(2,1)S(1)}, bf16[512,128]{1,0:T(8,128)(2,1)S(1)}, u32[]{:S(2)}, u32[]{:S(2)}) %collective-permute-start.30) | collective-permute-done | bytes 131104 | tf_op jit(solution)/shard_map/ppermute | solution.py:268
  78.7 0.8 shard_map.95
  (72 shorter events, 16.4 us)
Async XLA Ops:
  0.7 4.0 %collective-permute-start = (f32[512,128]{1,0:T(8,128)}, f32[512,128]{1,0:T(8,128)S(1)}, u32[]{:S(2)}, u32[]{:S(2)}) collective-permute-start(f32[512,128]{1,0:T(8,128)} %bitcast.4), channel_id=1, source_target_pairs={{0,8},{1,9},{2,10},{3,11},{4,12},{5,13},{6,14},{7,15},{8,0},{9,1},... | collective-permute-start | bytes 786440 | tf_op jit(solution)/shard_map/ppermute | solution.py:262
  3.6 4.0 %collective-permute-start.1 = (bf16[128,1024]{1,0:T(8,128)(2,1)S(1)}, bf16[128,1024]{1,0:T(8,128)(2,1)S(1)}, u32[]{:S(2)}, u32[]{:S(2)}) collective-permute-start(bf16[128,1024]{1,0:T(8,128)(2,1)S(1)} %get-tuple-element.30), channel_id=1, source_target_pairs={{0,8},{1,9},{2,10},{3,11},{4,12},{5,13},{6,14},{7,15},{8,0},{9,1},... | collective-permute-start | bytes 786440 | tf_op jit(solution)/shard_map/ppermute | solution.py:262
  3.8 5.4 %collective-permute-start.2 = (bf16[128,1024]{1,0:T(8,128)(2,1)S(1)}, bf16[128,1024]{1,0:T(8,128)(2,1)S(1)}, u32[]{:S(2)}, u32[]{:S(2)}) collective-permute-start(bf16[128,1024]{1,0:T(8,128)(2,1)S(1)} %get-tuple-element.31), channel_id=1, source_target_pairs={{0,8},{1,9},{2,10},{3,11},{4,12},{5,13},{6,14},{7,15},{8,0},{9,1},... | collective-permute-start | bytes 786440 | tf_op jit(solution)/shard_map/ppermute | solution.py:262
  4.2 6.8 %collective-permute-start.3 = (bf16[128,1024]{1,0:T(8,128)(2,1)S(1)}, bf16[128,1024]{1,0:T(8,128)(2,1)S(1)}, u32[]{:S(2)}, u32[]{:S(2)}) collective-permute-start(bf16[128,1024]{1,0:T(8,128)(2,1)S(1)} %get-tuple-element.32), channel_id=1, source_target_pairs={{0,8},{1,9},{2,10},{3,11},{4,12},{5,13},{6,14},{7,15},{8,0},{9,1},... | collective-permute-start | bytes 786440 | tf_op jit(solution)/shard_map/ppermute | solution.py:262
  4.3 6.7 %collective-permute-start.4 = (bf16[128,1024]{1,0:T(8,128)(2,1)S(1)}, bf16[128,1024]{1,0:T(8,128)(2,1)S(1)}, u32[]{:S(2)}, u32[]{:S(2)}) collective-permute-start(bf16[128,1024]{1,0:T(8,128)(2,1)S(1)} %get-tuple-element.33), channel_id=1, source_target_pairs={{0,8},{1,9},{2,10},{3,11},{4,12},{5,13},{6,14},{7,15},{8,0},{9,1},... | collective-permute-start | bytes 786440 | tf_op jit(solution)/shard_map/ppermute | solution.py:262
  4.9 9.9 %collective-permute-start.5 = (bf16[512,128]{1,0:T(8,128)(2,1)S(1)}, bf16[512,128]{1,0:T(8,128)(2,1)S(1)}, u32[]{:S(2)}, u32[]{:S(2)}) collective-permute-start(bf16[512,128]{1,0:T(8,128)(2,1)S(1)} %shard_map.69.now_ref.rest_3_.refs_0_), channel_id=1, source_target_pairs={{0,1},{1,2},{2,3},{3,4},{4,5},{5,6},{6,7},{7,0},{8,15},{9,8},{10,9... | collective-permute-start | bytes 393224 | tf_op jit(solution)/shard_map/ppermute | solution.py:271
  7.6 8.2 %collective-permute-start.6 = (bf16[512,128]{1,0:T(8,128)(2,1)S(1)}, bf16[512,128]{1,0:T(8,128)(2,1)S(1)}, u32[]{:S(2)}, u32[]{:S(2)}) collective-permute-start(bf16[512,128]{1,0:T(8,128)(2,1)S(1)} %shard_map.69.now_ref.rest_3_.refs_0_), channel_id=1, source_target_pairs={{0,2},{1,3},{2,4},{3,5},{4,6},{5,7},{6,0},{7,1},{8,14},{9,15},{10,... | collective-permute-start | bytes 393224 | tf_op jit(solution)/shard_map/ppermute | solution.py:271
  9.2 6.6 %collective-permute-start.7 = (bf16[512,128]{1,0:T(8,128)(2,1)S(1)}, bf16[512,128]{1,0:T(8,128)(2,1)S(1)}, u32[]{:S(2)}, u32[]{:S(2)}) collective-permute-start(bf16[512,128]{1,0:T(8,128)(2,1)S(1)} %shard_map.69.now_ref.rest_3_.refs_0_), channel_id=1, source_target_pairs={{0,16},{1,17},{2,18},{3,19},{4,20},{5,21},{6,22},{7,23},{8,24},{9,... | collective-permute-start | bytes 393224 | tf_op jit(solution)/shard_map/ppermute | solution.py:265
  16.2 1.4 %collective-permute-start.8 = (bf16[512,128]{1,0:T(8,128)(2,1)S(1)}, bf16[512,128]{1,0:T(8,128)(2,1)S(1)}, u32[]{:S(2)}, u32[]{:S(2)}) collective-permute-start(bf16[512,128]{1,0:T(8,128)(2,1)S(1)} %shard_map.73.mine_ref), channel_id=1, source_target_pairs={{0,8},{1,9},{2,10},{3,11},{4,12},{5,13},{6,14},{7,15},{8,0},{9,1},... | collective-permute-start | bytes 393224 | tf_op jit(solution)/shard_map/ppermute | solution.py:262
  17.8 5.6 %collective-permute-start.9 = (bf16[512,128]{1,0:T(8,128)(2,1)S(1)}, bf16[512,128]{1,0:T(8,128)(2,1)S(1)}, u32[]{:S(2)}, u32[]{:S(2)}) collective-permute-start(bf16[512,128]{1,0:T(8,128)(2,1)S(1)} %get-tuple-element.37), channel_id=1, source_target_pairs={{0,16},{1,17},{2,18},{3,19},{4,20},{5,21},{6,22},{7,23},{8,24},{9,... | collective-permute-start | bytes 393224 | tf_op jit(solution)/shard_map/ppermute | solution.py:265
  19.4 8.1 %collective-permute-start.10 = (bf16[512,128]{1,0:T(8,128)(2,1)S(1)}, bf16[512,128]{1,0:T(8,128)(2,1)S(1)}, u32[]{:S(2)}, u32[]{:S(2)}) collective-permute-start(bf16[512,128]{1,0:T(8,128)(2,1)S(1)} %get-tuple-element.36.now_ref.rest_3_.refs_1_), channel_id=1, source_target_pairs={{0,1},{1,2},{2,3},{3,4},{4,5},{5,6},{6,7},{7,0},{8,15},{9,8},{10,9... | collective-permute-start | bytes 393224 | tf_op jit(solution)/shard_map/ppermute | solution.py:271
  20.7 6.9 %collective-permute-start.11 = (bf16[512,128]{1,0:T(8,128)(2,1)S(1)}, bf16[512,128]{1,0:T(8,128)(2,1)S(1)}, u32[]{:S(2)}, u32[]{:S(2)}) collective-permute-start(bf16[512,128]{1,0:T(8,128)(2,1)S(1)} %get-tuple-element.36.now_ref.rest_3_.refs_1_), channel_id=1, source_target_pairs={{0,2},{1,3},{2,4},{3,5},{4,6},{5,7},{6,0},{7,1},{8,14},{9,15},{10,... | collective-permute-start | bytes 393224 | tf_op jit(solution)/shard_map/ppermute | solution.py:271
  28.0 1.4 %collective-permute-start.12 = (bf16[512,128]{1,0:T(8,128)(2,1)S(1)}, bf16[512,128]{1,0:T(8,128)(2,1)S(1)}, u32[]{:S(2)}, u32[]{:S(2)}) collective-permute-start(bf16[512,128]{1,0:T(8,128)(2,1)S(1)} %shard_map.76.mine_ref), channel_id=1, source_target_pairs={{0,8},{1,9},{2,10},{3,11},{4,12},{5,13},{6,14},{7,15},{8,0},{9,1},... | collective-permute-start | bytes 393224 | tf_op jit(solution)/shard_map/ppermute | solution.py:262
  29.7 7.8 %collective-permute-start.13 = (bf16[512,128]{1,0:T(8,128)(2,1)S(1)}, bf16[512,128]{1,0:T(8,128)(2,1)S(1)}, u32[]{:S(2)}, u32[]{:S(2)}) collective-permute-start(bf16[512,128]{1,0:T(8,128)(2,1)S(1)} %get-tuple-element.39.now_ref.rest_3_.refs_2_), channel_id=1, source_target_pairs={{0,1},{1,2},{2,3},{3,4},{4,5},{5,6},{6,7},{7,0},{8,15},{9,8},{10,9... | collective-permute-start | bytes 393224 | tf_op jit(solution)/shard_map/ppermute | solution.py:271
  31.6 7.3 %collective-permute-start.14 = (bf16[512,128]{1,0:T(8,128)(2,1)S(1)}, bf16[512,128]{1,0:T(8,128)(2,1)S(1)}, u32[]{:S(2)}, u32[]{:S(2)}) collective-permute-start(bf16[512,128]{1,0:T(8,128)(2,1)S(1)} %get-tuple-element.39.now_ref.rest_3_.refs_2_), channel_id=1, source_target_pairs={{0,2},{1,3},{2,4},{3,5},{4,6},{5,7},{6,0},{7,1},{8,14},{9,15},{10,... | collective-permute-start | bytes 393224 | tf_op jit(solution)/shard_map/ppermute | solution.py:271
  31.8 7.1 %collective-permute-start.15 = (bf16[512,128]{1,0:T(8,128)(2,1)S(1)}, bf16[512,128]{1,0:T(8,128)(2,1)S(1)}, u32[]{:S(2)}, u32[]{:S(2)}) collective-permute-start(bf16[512,128]{1,0:T(8,128)(2,1)S(1)} %get-tuple-element.40), channel_id=1, source_target_pairs={{0,16},{1,17},{2,18},{3,19},{4,20},{5,21},{6,22},{7,23},{8,24},{9,... | collective-permute-start | bytes 393224 | tf_op jit(solution)/shard_map/ppermute | solution.py:265
  39.3 1.4 %collective-permute-start.16 = (bf16[512,128]{1,0:T(8,128)(2,1)S(1)}, bf16[512,128]{1,0:T(8,128)(2,1)S(1)}, u32[]{:S(2)}, u32[]{:S(2)}) collective-permute-start(bf16[512,128]{1,0:T(8,128)(2,1)S(1)} %shard_map.79.mine_ref), channel_id=1, source_target_pairs={{0,8},{1,9},{2,10},{3,11},{4,12},{5,13},{6,14},{7,15},{8,0},{9,1},... | collective-permute-start | bytes 393224 | tf_op jit(solution)/shard_map/ppermute | solution.py:262
  40.9 8.1 %collective-permute-start.17 = (bf16[512,128]{1,0:T(8,128)(2,1)S(1)}, bf16[512,128]{1,0:T(8,128)(2,1)S(1)}, u32[]{:S(2)}, u32[]{:S(2)}) collective-permute-start(bf16[512,128]{1,0:T(8,128)(2,1)S(1)} %get-tuple-element.41.now_ref.rest_3_.refs_3_), channel_id=1, source_target_pairs={{0,1},{1,2},{2,3},{3,4},{4,5},{5,6},{6,7},{7,0},{8,15},{9,8},{10,9... | collective-permute-start | bytes 393224 | tf_op jit(solution)/shard_map/ppermute | solution.py:271
  41.5 7.6 %collective-permute-start.18 = (bf16[512,128]{1,0:T(8,128)(2,1)S(1)}, bf16[512,128]{1,0:T(8,128)(2,1)S(1)}, u32[]{:S(2)}, u32[]{:S(2)}) collective-permute-start(bf16[512,128]{1,0:T(8,128)(2,1)S(1)} %get-tuple-element.41.now_ref.rest_3_.refs_3_), channel_id=1, source_target_pairs={{0,2},{1,3},{2,4},{3,5},{4,6},{5,7},{6,0},{7,1},{8,14},{9,15},{10,... | collective-permute-start | bytes 393224 | tf_op jit(solution)/shard_map/ppermute | solution.py:271
  41.6 7.5 %collective-permute-start.19 = (bf16[512,128]{1,0:T(8,128)(2,1)S(1)}, bf16[512,128]{1,0:T(8,128)(2,1)S(1)}, u32[]{:S(2)}, u32[]{:S(2)}) collective-permute-start(bf16[512,128]{1,0:T(8,128)(2,1)S(1)} %get-tuple-element.42), channel_id=1, source_target_pairs={{0,16},{1,17},{2,18},{3,19},{4,20},{5,21},{6,22},{7,23},{8,24},{9,... | collective-permute-start | bytes 393224 | tf_op jit(solution)/shard_map/ppermute | solution.py:265
  51.2 7.8 %collective-permute-start.21 = (bf16[512,128]{1,0:T(8,128)(2,1)S(1)}, bf16[512,128]{1,0:T(8,128)(2,1)S(1)}, u32[]{:S(2)}, u32[]{:S(2)}) collective-permute-start(bf16[512,128]{1,0:T(8,128)(2,1)S(1)} %get-tuple-element.43.now_ref.refs_4_.rest_3_), channel_id=1, source_target_pairs={{0,1},{1,2},{2,3},{3,4},{4,5},{5,6},{6,7},{7,0},{8,15},{9,8},{10,9... | collective-permute-start | bytes 393224 | tf_op jit(solution)/shard_map/ppermute | solution.py:271
  53.1 7.0 %collective-permute-start.22 = (bf16[512,128]{1,0:T(8,128)(2,1)S(1)}, bf16[512,128]{1,0:T(8,128)(2,1)S(1)}, u32[]{:S(2)}, u32[]{:S(2)}) collective-permute-start(bf16[512,128]{1,0:T(8,128)(2,1)S(1)} %get-tuple-element.43.now_ref.refs_4_.rest_3_), channel_id=1, source_target_pairs={{0,2},{1,3},{2,4},{3,5},{4,6},{5,7},{6,0},{7,1},{8,14},{9,15},{10,... | collective-permute-start | bytes 393224 | tf_op jit(solution)/shard_map/ppermute | solution.py:271
  53.6 6.6 %collective-permute-start.23 = (bf16[512,128]{1,0:T(8,128)(2,1)S(1)}, bf16[512,128]{1,0:T(8,128)(2,1)S(1)}, u32[]{:S(2)}, u32[]{:S(2)}) collective-permute-start(bf16[512,128]{1,0:T(8,128)(2,1)S(1)} %get-tuple-element.44), channel_id=1, source_target_pairs={{0,16},{1,17},{2,18},{3,19},{4,20},{5,21},{6,22},{7,23},{8,24},{9,... | collective-permute-start | bytes 393224 | tf_op jit(solution)/shard_map/ppermute | solution.py:265
  62.2 5.6 %collective-permute-start.25 = (bf16[512,128]{1,0:T(8,128)(2,1)S(1)}, bf16[512,128]{1,0:T(8,128)(2,1)S(1)}, u32[]{:S(2)}, u32[]{:S(2)}) collective-permute-start(bf16[512,128]{1,0:T(8,128)(2,1)S(1)} %get-tuple-element.46), channel_id=1, source_target_pairs={{0,16},{1,17},{2,18},{3,19},{4,20},{5,21},{6,22},{7,23},{8,24},{9,... | collective-permute-start | bytes 393224 | tf_op jit(solution)/shard_map/ppermute | solution.py:265
  62.8 7.7 %collective-permute-start.26 = (bf16[512,128]{1,0:T(8,128)(2,1)S(1)}, bf16[512,128]{1,0:T(8,128)(2,1)S(1)}, u32[]{:S(2)}, u32[]{:S(2)}) collective-permute-start(bf16[512,128]{1,0:T(8,128)(2,1)S(1)} %get-tuple-element.45.refs_5_.now_ref.rest_3_), channel_id=1, source_target_pairs={{0,1},{1,2},{2,3},{3,4},{4,5},{5,6},{6,7},{7,0},{8,15},{9,8},{10,9... | collective-permute-start | bytes 393224 | tf_op jit(solution)/shard_map/ppermute | solution.py:271
  63.6 6.9 %collective-permute-start.27 = (bf16[512,128]{1,0:T(8,128)(2,1)S(1)}, bf16[512,128]{1,0:T(8,128)(2,1)S(1)}, u32[]{:S(2)}, u32[]{:S(2)}) collective-permute-start(bf16[512,128]{1,0:T(8,128)(2,1)S(1)} %get-tuple-element.45.refs_5_.now_ref.rest_3_), channel_id=1, source_target_pairs={{0,2},{1,3},{2,4},{3,5},{4,6},{5,7},{6,0},{7,1},{8,14},{9,15},{10,... | collective-permute-start | bytes 393224 | tf_op jit(solution)/shard_map/ppermute | solution.py:271
  67.8 7.7 %collective-permute-start.31 = (bf16[512,128]{1,0:T(8,128)(2,1)S(1)}, bf16[512,128]{1,0:T(8,128)(2,1)S(1)}, u32[]{:S(2)}, u32[]{:S(2)}) collective-permute-start(bf16[512,128]{1,0:T(8,128)(2,1)S(1)} %collective-permute-done.25.refs_6_.rest_0_.now_ref.refs_5_), channel_id=1, source_target_pairs={{0,1},{1,2},{2,3},{3,4},{4,5},{5,6},{6,7},{7,0},{8,15},{9,8},{10,9... | collective-permute-start | bytes 393224 | tf_op jit(solution)/shard_map/ppermute | solution.py:271
  68.7 6.8 %collective-permute-start.32 = (bf16[512,128]{1,0:T(8,128)(2,1)S(1)}, bf16[512,128]{1,0:T(8,128)(2,1)S(1)}, u32[]{:S(2)}, u32[]{:S(2)}) collective-permute-start(bf16[512,128]{1,0:T(8,128)(2,1)S(1)} %collective-permute-done.25.refs_6_.rest_0_.now_ref.refs_5_), channel_id=1, source_target_pairs={{0,2},{1,3},{2,4},{3,5},{4,6},{5,7},{6,0},{7,1},{8,14},{9,15},{10,... | collective-permute-start | bytes 393224 | tf_op jit(solution)/shard_map/ppermute | solution.py:271
  71.0 6.5 %collective-permute-start.29 = (bf16[512,128]{1,0:T(8,128)(2,1)S(1)}, bf16[512,128]{1,0:T(8,128)(2,1)S(1)}, u32[]{:S(2)}, u32[]{:S(2)}) collective-permute-start(bf16[512,128]{1,0:T(8,128)(2,1)S(1)} %get-tuple-element.51), channel_id=1, source_target_pairs={{0,16},{1,17},{2,18},{3,19},{4,20},{5,21},{6,22},{7,23},{8,24},{9,... | collective-permute-start | bytes 393224 | tf_op jit(solution)/shard_map/ppermute | solution.py:265
  72.9 5.8 %collective-permute-start.30 = (bf16[512,128]{1,0:T(8,128)(2,1)S(1)}, bf16[512,128]{1,0:T(8,128)(2,1)S(1)}, u32[]{:S(2)}, u32[]{:S(2)}) collective-permute-start(bf16[512,128]{1,0:T(8,128)(2,1)S(1)} %get-tuple-element.51), channel_id=1, source_target_pairs={{0,24},{1,25},{2,26},{3,27},{4,28},{5,29},{6,30},{7,31},{8,16},{9,... | collective-permute-start | bytes 393224 | tf_op jit(solution)/shard_map/ppermute | solution.py:268
  73.5 4.0 %collective-permute-start.28 = (bf16[512,128]{1,0:T(8,128)(2,1)S(1)}, bf16[512,128]{1,0:T(8,128)(2,1)S(1)}, u32[]{:S(2)}, u32[]{:S(2)}) collective-permute-start(bf16[512,128]{1,0:T(8,128)(2,1)S(1)} %get-tuple-element.50), channel_id=1, source_target_pairs={{0,8},{1,9},{2,10},{3,11},{4,12},{5,13},{6,14},{7,15},{8,0},{9,1},... | collective-permute-start | bytes 393224 | tf_op jit(solution)/shard_map/ppermute | solution.py:262
  77.2 1.6 %collective-permute-start.33 = (bf16[512,128]{1,0:T(8,128)(2,1)S(1)}, bf16[512,128]{1,0:T(8,128)(2,1)S(1)}, u32[]{:S(2)}, u32[]{:S(2)}) collective-permute-start(bf16[512,128]{1,0:T(8,128)(2,1)S(1)} %get-tuple-element.55), channel_id=1, source_target_pairs={{0,8},{1,9},{2,10},{3,11},{4,12},{5,13},{6,14},{7,15},{8,0},{9,1},... | collective-permute-start | bytes 393224 | tf_op jit(solution)/shard_map/ppermute | solution.py:262
  (6 other events, 15.8 us)

commit v8 on v7

--- a/solution.py
+++ b/solution.py
@@ -24,35 +24,33 @@
     return lax.rem(lag, 2), lax.div(lag, 2)
 
 
-def cost(microseconds):
-    moved = int(3.6e6 * microseconds)
-    return pl.CostEstimate(flops=0, bytes_accessed=moved, transcendentals=0)
-
-
-def call(body, outs, args, after=None, field_last=False, microseconds=0.5):
+COST = pl.CostEstimate(flops=0, bytes_accessed=1 << 20, transcendentals=0)
+
+
+def call(body, outs, args, after=None, in_front=None):
     specs = [VMEM] * len(args)
-    if field_last:
-        args = args[1:] + args[:1]
-        body = functools.partial(field_to_front, body, len(args))
+    if in_front is not None:
+        args = args[in_front : in_front + 1] + args[:in_front] + args[in_front + 1 :]
+        body = functools.partial(put_back, body, in_front)
     if after is not None:
-        args, specs = [after] + args, [pl.BlockSpec(memory_space=pl.ANY)] + specs
-        body = functools.partial(skip_first, body)
+        body = functools.partial(skip, body, len(args))
+        args, specs = args + [after], specs + [pl.BlockSpec(memory_space=pl.ANY)]
     return pl.pallas_call(
         body,
         out_shape=tuple(outs),
         in_specs=specs,
         out_specs=tuple(VMEM for _ in outs),
-        cost_estimate=cost(microseconds),
+        cost_estimate=COST,
         compiler_params=pltpu.CompilerParams(vmem_limit_bytes=8 * MIB),
     )(*args)
 
 
-def field_to_front(body, count, *refs):
-    body(refs[count - 1], *refs[: count - 1], *refs[count:])
-
-
-def skip_first(body, _, *refs):
-    body(*refs)
+def put_back(body, in_front, moved, *refs):
+    body(*refs[:in_front], moved, *refs[in_front:])
+
+
+def skip(body, number, *refs):
+    body(*refs[:number], *refs[number + 1 :])
 
 
 def spread_body(groups, pattern_ref, entries_ref, keep_ref, own_ref, *rest):
@@ -110,7 +108,7 @@
             pltpu.SemaphoreType.DMA((blocks,)),
             pltpu.SemaphoreType.DMA,
         ],
-        cost_estimate=cost(4),
+        cost_estimate=COST,
         compiler_params=pltpu.CompilerParams(vmem_limit_bytes=51 * MIB),
     )(pattern, entries)
 
@@ -134,9 +132,13 @@
         put(near_ref, far_ref)
 
 
+def half(matrix_ref, block_ref, which):
+    rows = block_ref.shape[0]
+    return dot(matrix_ref[:, which * rows : (which + 1) * rows], block_ref[...])
+
+
 def window(matrix_ref, first_ref, second_ref):
-    rows = first_ref.shape[0]
-    return dot(matrix_ref[:, :rows], first_ref[...]) + dot(matrix_ref[:, rows:], second_ref[...])
+    return half(matrix_ref, first_ref, 0) + half(matrix_ref, second_ref, 1)
 
 
 def early_body(own_ref, now_ref, *rest):
@@ -162,40 +164,58 @@
     return value
 
 
-def late_body(step, pairs, field_ref, near_ref, first_ref, second_ref, early_ref, *rest):
+def first_body(near_ref, first_ref, early_ref, out_ref):
+    out_ref[...] = early_ref[...] + half(near_ref, first_ref, 0)
+
+
+def late_body(step, pairs, near_ref, second_ref, early_ref, field_ref, *rest):
     *history, out_ref = rest
-    total = early_ref[...] + window(near_ref, first_ref, second_ref)
+    total = early_ref[...] + half(near_ref, second_ref, 1)
     out_ref[...] = (total + came(step, pairs, field_ref, history)).astype(BF16)
 
 
-def even_body(step, pairs, near_ref, first_ref, second_ref, early_ref, *rest):
-    *field, even_ref, out_ref = rest
-    total = early_ref[...] + window(near_ref, first_ref, second_ref)
-    if field:
-        total += came(step, pairs, field[0], field[1:])
+def even_body(step, pairs, near_ref, second_ref, early_ref, *rest):
+    total = early_ref[...] + half(near_ref, second_ref, 1)
+    if len(rest) == 1:
+        rest[0][...] = total
+        return
+    field_ref, *history, even_ref, out_ref = rest
+    total += came(step, pairs, field_ref, history)
     even_ref[...] = total
     out_ref[...] = total.astype(BF16)
 
 
-def odd_body(even_ref, far_ref, first_ref, second_ref, own_ref, now_ref, keep_ref, send_ref):
-    core, _ = place()
-    local = jnp.where(core == 1, now_ref[...], jnp.zeros_like(now_ref))
-    odd = window(far_ref, first_ref, second_ref) + dot(own_ref[...], local)
-    even = even_ref[...]
+def odd_early_body(own_ref, now_ref, out_ref):
+    core, _ = place()
+    out_ref[...] = dot(own_ref[...], jnp.where(core == 1, now_ref[...], jnp.zeros_like(now_ref)))
+
+
+def odd_body(which, far_ref, block_ref, early_ref, out_ref):
+    out_ref[...] = early_ref[...] + half(far_ref, block_ref, which)
+
+
+def share_body(step, steps, even_ref, odd_ref, *rest):
+    *field, keep_ref, send_ref = rest
+    core, pair = place()
+    even, odd = even_ref[...], odd_ref[...]
+    if field:
+        ended = pair == step - steps
+        came_late = field[0][...].astype(F32)
+        even, odd = jnp.where(ended, came_late, even), jnp.where(ended, came_late, odd)
     keep_ref[...] = jnp.where(core == 1, odd, even)
     send_ref[...] = jnp.where(core == 0, odd, even).astype(BF16)
 
 
-def finish_body(step, steps, *refs):
-    *earlier, mine_ref, other_ref, result_ref = refs
+def finish_body(step, steps, mine_ref, other_ref, *rest):
+    *earlier, result_ref = rest
     core, pair = place()
     field = mine_ref[...] + other_ref[...].astype(F32)
     if earlier:
-        before_ref, straight_ref, crossed_ref = earlier
+        before = earlier[0][...]
         adds = jnp.logical_and(core == 1, pair == step - steps)
-        rest = straight_ref[...].astype(F32) + crossed_ref[...].astype(F32)
-        before = before_ref[...] + jnp.where(adds, rest, 0.0)
-        field = jnp.where(pair == step - (steps - 1), field, before)
+        field = jnp.where(
+            adds, before + field, jnp.where(pair == step - (steps - 1), field, before)
+        )
     result_ref[...] = field
 
 
@@ -263,9 +283,6 @@
 
     def pair_moved(value, hop):
         return lax.ppermute(value, AXES, everyone(lambda d, s: ((d + 2 * hop) % lags, s)))
-
-    def crossed(value):
-        return lax.ppermute(value, AXES, everyone(lambda d, s: (((d - 2) % lags) ^ 1, s)))
 
     def halo(value, hop):
         return lax.ppermute(
@@ -288,7 +305,7 @@
     going = field = current
     seen = []
     previous = []
-    result = []
+    result = None
     out = collected = None
     rounds = steps + pairs - 1
     windows = None
@@ -307,15 +324,16 @@
             current_in, field_in = pair_moved(current, 1), pair_moved(field, -1)
         last = [far, *previous] if previous else []
         (early,) = call(early_body, [field_shape], [own, current] + last)
-        received = [near, first, second, early]
+        (partly,) = call(first_body, [field_shape], [near, first, early])
+        received = [near, second, partly]
         past = [history[0], other_history] if step < pairs else []
         previous = [first, second, current]
         if step < steps - 1:
             (field,) = call(
                 functools.partial(late_body, step, pairs),
                 [current_shape],
-                [field_in] + received + past,
-                field_last=step != 1,
+                received + [field_in] + past,
+                in_front=len(received) if step == 1 else None,
             )
             current, going = call(
                 functools.partial(next_body, step),
@@ -325,24 +343,29 @@
         else:
             if step < rounds - 1:
                 windows = halo(current_in, 1), halo(current_in, 2)
-            even, next_field = call(
+            more = step < rounds - 1
+            even, *next_field = call(
                 functools.partial(even_body, step, pairs),
+                [field_shape] + [current_shape] * more,
+                received + ([field_in] + past) * more,
+            )
+            (odd_early,) = call(odd_early_body, [field_shape], [own, current])
+            for which, block in enumerate((first, second)):
+                (odd_early,) = call(
+                    functools.partial(odd_body, which), [field_shape], [far, block, odd_early]
+                )
+            mine, send = call(
+                functools.partial(share_body, step, steps),
                 [field_shape, current_shape],
-                received + ([field_in] + past if step < rounds - 1 else []),
-            )
-            mine, send = call(
-                odd_body,
-                [field_shape, current_shape],
-                [even, far, first, second, own, current],
-                after=collected,
-            )
-            earlier = [result, field_in, crossed(field)] if step >= steps else []
+                [even, odd_early] + [field_in] * (step >= steps),
+            )
             (result,) = call(
                 functools.partial(finish_body, step, steps),
                 [field_shape],
-                earlier + [mine, swapped(send)],
-            )
-            field = next_field
+                [mine, swapped(send)] + [result] * (step >= steps),
+                after=collected,
+            )
+            field = next_field[0] if more else None
             current, going = current_in, field
     return (out, result[None])
 

time: 79.7 us -> 78 us (0.979)
  waiting for transfers between devices: 41 us -> 36.2 us
  starting transfers between devices: 23.3 us -> 25.2 us
  Pallas kernels: 13.6 us -> 14.8 us
    ppermute x7, waiting for transfers between devices: 5.76 us -> 3.37 us  [pair_moved(): lax.ppermute(value, AXES, everyone(lambda d, s: ((d + 2 * hop) % lags, s)))]
    ppermute x7, starting transfers between devices: 7.16 us -> 9.05 us  [pair_moved(): lax.ppermute(value, AXES, everyone(lambda d, s: ((d + 2 * hop) % lags, s)))]
    ppermute x14, waiting for transfers between devices: 27.4 us -> 25.9 us  [halo(): lax.ppermute(value, AXES, everyone(lambda d, s: (d, (s + (hop if d % 2 ==...]
    ppermute x1 -> x0, waiting for transfers between devices: 1.22 us -> none  [crossed(): lax.ppermute(value, AXES, everyone(lambda d, s: ((d - 2) % lags ^ 1, s)))]
    pallas_call x27 -> x40, Pallas kernels: 11.9 us -> 13 us  [call(): pl.pallas_call(body, out_shape=tuple(outs), in_specs=specs, out_specs=tup...]
  transfers between devices with their start and end apart: 34 -> 33, of which waited for: 19 -> 20; matrix products, arithmetic and copies ran while one was open for 0% -> 0% of each run, Pallas kernels for 12% -> 15%
where the time goes in v8:
time: 78 us; the launch traced here: 77.8 us
  waiting for transfers between devices  36.2 us (46%)
  starting transfers between devices  25.2 us (32%)
  Pallas kernels  14.8 us (19%)
  between operations  1.02 us (1%)
    ppermute x14, waiting for transfers between devices, halo(): lax.ppermute(value, AXES, everyone(lambda d, s: (d, (s + (hop if d % 2 ==...  25.9 us
    ppermute x14, starting transfers between devices, halo(): lax.ppermute(value, AXES, everyone(lambda d, s: (d, (s + (hop if d % 2 ==...  13.9 us
    pallas_call x40, Pallas kernels, call(): pl.pallas_call(body, out_shape=tuple(outs), in_specs=specs, out_specs=tup...  13 us
    ppermute x7, starting transfers between devices, pair_moved(): lax.ppermute(value, AXES, everyone(lambda d, s: ((d + 2 * hop) % lags, s)))  9.05 us
    ppermute x12, waiting for transfers between devices, swapped(): return lax.ppermute(value, AXES, everyone(lambda d, s: (d ^ 1, s)))  6.85 us
    ppermute x7, waiting for transfers between devices, pair_moved(): lax.ppermute(value, AXES, everyone(lambda d, s: ((d + 2 * hop) % lags, s)))  3.37 us
    ppermute x12, starting transfers between devices, swapped(): return lax.ppermute(value, AXES, everyone(lambda d, s: (d ^ 1, s)))  2.21 us
    pallas_call x1, Pallas kernels, spread(): pl.pallas_call(functools.partial(spread_body, groups), out_shape=(matrix(...  1.74 us
  transfers between devices with their start and end apart: 33, of which 20 were waited for; matrix products, arithmetic and copies ran while one was open for 0% of the time, Pallas kernels for 15%

profile of v8, /device:TPU:0, one launch (start us, length us, event | category | flops | bytes accessed | tf_op | source)
XLA Modules:
  0.0 77.8 jit_solution(17008733541755710071)
XLA Ops:
  1.9 1.7 %shard_map.70 = (bf16[512,1024]{1,0:T(8,128)(2,1)S(1)}, bf16[512,512]{1,0:T(8,128)(2,1)S(1)}, bf16[128,1024]{1,0:T(8,128)(2,1)S(1)}, bf16[128,1024]{1,0:T(8,128)...) custom-call(s32[4,16]{1,0:T(4,128)S(1)} %bitcast.8, bf16[4,16,128,128]{3,2,1,0:T(8,128)(2,1)} %bitcast.9), custom_call_target="tpu_custom_call" | custom-call | bytes 1048576 | tf_op jit(solution)/shard_map/pallas_call | solution.py:99
  4.9 2.7 %collective-permute-start.6 = (bf16[512,128]{1,0:T(8,128)(2,1)S(1)}, bf16[512,128]{1,0:T(8,128)(2,1)S(1)}, u32[]{:S(2)}, u32[]{:S(2)}) collective-permute-start(bf16[512,128]{1,0:T(8,128)(2,1)S(1)} %shard_map.69.now_ref.rest_3_.refs_0_), channel_id=1, source_target_pairs={{0,1},{1,2},{2,3},{3,4},{4,5},{5,6},{6,7},{7,0},{8,15},{9,8},{10,9... | collective-permute-start | bytes 393224 | tf_op jit(solution)/shard_map/ppermute | solution.py:288
  7.6 1.6 %collective-permute-start.5 = (bf16[512,128]{1,0:T(8,128)(2,1)S(1)}, bf16[512,128]{1,0:T(8,128)(2,1)S(1)}, u32[]{:S(2)}, u32[]{:S(2)}) collective-permute-start(bf16[512,128]{1,0:T(8,128)(2,1)S(1)} %shard_map.69.now_ref.rest_3_.refs_0_), channel_id=1, source_target_pairs={{0,2},{1,3},{2,4},{3,5},{4,6},{5,7},{6,0},{7,1},{8,14},{9,15},{10,... | collective-permute-start | bytes 393224 | tf_op jit(solution)/shard_map/ppermute | solution.py:288
  9.2 1.5 %collective-permute-start.7 = (bf16[512,128]{1,0:T(8,128)(2,1)S(1)}, bf16[512,128]{1,0:T(8,128)(2,1)S(1)}, u32[]{:S(2)}, u32[]{:S(2)}) collective-permute-start(bf16[512,128]{1,0:T(8,128)(2,1)S(1)} %shard_map.69.now_ref.rest_3_.refs_0_), channel_id=1, source_target_pairs={{0,16},{1,17},{2,18},{3,19},{4,20},{5,21},{6,22},{7,23},{8,24},{9,... | collective-permute-start | bytes 393224 | tf_op jit(solution)/shard_map/ppermute | solution.py:285
  11.2 3.7 %collective-permute-done.6.first_ref.rest_1_ = bf16[512,128]{1,0:T(8,128)(2,1)S(1)} collective-permute-done((bf16[512,128]{1,0:T(8,128)(2,1)S(1)}, bf16[512,128]{1,0:T(8,128)(2,1)S(1)}, u32[]{:S(2)}, u32[]{:S(2)}) %collective-permute-start.6) | collective-permute-done | bytes 131104 | tf_op jit(solution)/shard_map/ppermute | solution.py:288
  16.2 1.2 %collective-permute-done.8.other_ref = bf16[512,128]{1,0:T(8,128)(2,1)S(1)} collective-permute-done((bf16[512,128]{1,0:T(8,128)(2,1)S(1)}, bf16[512,128]{1,0:T(8,128)(2,1)S(1)}, u32[]{:S(2)}, u32[]{:S(2)}) %collective-permute-start.8) | collective-permute-done | bytes 131104 | tf_op jit(solution)/shard_map/ppermute | solution.py:282
  17.7 1.3 %collective-permute-start.11 = (bf16[512,128]{1,0:T(8,128)(2,1)S(1)}, bf16[512,128]{1,0:T(8,128)(2,1)S(1)}, u32[]{:S(2)}, u32[]{:S(2)}) collective-permute-start(bf16[512,128]{1,0:T(8,128)(2,1)S(1)} %get-tuple-element.35.now_ref.rest_3_.refs_1_), channel_id=1, source_target_pairs={{0,1},{1,2},{2,3},{3,4},{4,5},{5,6},{6,7},{7,0},{8,15},{9,8},{10,9... | collective-permute-start | bytes 393224 | tf_op jit(solution)/shard_map/ppermute | solution.py:288
  19.2 1.5 %collective-permute-start.9 = (bf16[512,128]{1,0:T(8,128)(2,1)S(1)}, bf16[512,128]{1,0:T(8,128)(2,1)S(1)}, u32[]{:S(2)}, u32[]{:S(2)}) collective-permute-start(bf16[512,128]{1,0:T(8,128)(2,1)S(1)} %get-tuple-element.36), channel_id=1, source_target_pairs={{0,16},{1,17},{2,18},{3,19},{4,20},{5,21},{6,22},{7,23},{8,24},{9,... | collective-permute-start | bytes 393224 | tf_op jit(solution)/shard_map/ppermute | solution.py:285
  21.3 4.8 %collective-permute-done.11.first_ref.rest_1_ = bf16[512,128]{1,0:T(8,128)(2,1)S(1)} collective-permute-done((bf16[512,128]{1,0:T(8,128)(2,1)S(1)}, bf16[512,128]{1,0:T(8,128)(2,1)S(1)}, u32[]{:S(2)}, u32[]{:S(2)}) %collective-permute-start.11) | collective-permute-done | bytes 131104 | tf_op jit(solution)/shard_map/ppermute | solution.py:288
  26.8 1.3 %collective-permute-done.12.other_ref = bf16[512,128]{1,0:T(8,128)(2,1)S(1)} collective-permute-done((bf16[512,128]{1,0:T(8,128)(2,1)S(1)}, bf16[512,128]{1,0:T(8,128)(2,1)S(1)}, u32[]{:S(2)}, u32[]{:S(2)}) %collective-permute-start.12) | collective-permute-done | bytes 131104 | tf_op jit(solution)/shard_map/ppermute | solution.py:282
  28.4 1.7 %collective-permute-start.14 = (bf16[512,128]{1,0:T(8,128)(2,1)S(1)}, bf16[512,128]{1,0:T(8,128)(2,1)S(1)}, u32[]{:S(2)}, u32[]{:S(2)}) collective-permute-start(bf16[512,128]{1,0:T(8,128)(2,1)S(1)} %get-tuple-element.38.now_ref.rest_3_.refs_2_), channel_id=1, source_target_pairs={{0,1},{1,2},{2,3},{3,4},{4,5},{5,6},{6,7},{7,0},{8,15},{9,8},{10,9... | collective-permute-start | bytes 393224 | tf_op jit(solution)/shard_map/ppermute | solution.py:288
  30.5 1.5 %collective-permute-start.15 = (bf16[512,128]{1,0:T(8,128)(2,1)S(1)}, bf16[512,128]{1,0:T(8,128)(2,1)S(1)}, u32[]{:S(2)}, u32[]{:S(2)}) collective-permute-start(bf16[512,128]{1,0:T(8,128)(2,1)S(1)} %get-tuple-element.39), channel_id=1, source_target_pairs={{0,16},{1,17},{2,18},{3,19},{4,20},{5,21},{6,22},{7,23},{8,24},{9,... | collective-permute-start | bytes 393224 | tf_op jit(solution)/shard_map/ppermute | solution.py:285
  32.6 3.5 %collective-permute-done.14.first_ref.rest_1_ = bf16[512,128]{1,0:T(8,128)(2,1)S(1)} collective-permute-done((bf16[512,128]{1,0:T(8,128)(2,1)S(1)}, bf16[512,128]{1,0:T(8,128)(2,1)S(1)}, u32[]{:S(2)}, u32[]{:S(2)}) %collective-permute-start.14) | collective-permute-done | bytes 131104 | tf_op jit(solution)/shard_map/ppermute | solution.py:288
  36.4 0.7 collective-permute-done.13.second_ref.rest_2_
  37.5 1.3 %collective-permute-done.16.other_ref = bf16[512,128]{1,0:T(8,128)(2,1)S(1)} collective-permute-done((bf16[512,128]{1,0:T(8,128)(2,1)S(1)}, bf16[512,128]{1,0:T(8,128)(2,1)S(1)}, u32[]{:S(2)}, u32[]{:S(2)}) %collective-permute-start.16) | collective-permute-done | bytes 131104 | tf_op jit(solution)/shard_map/ppermute | solution.py:282
  39.0 1.0 %collective-permute-start.18 = (bf16[512,128]{1,0:T(8,128)(2,1)S(1)}, bf16[512,128]{1,0:T(8,128)(2,1)S(1)}, u32[]{:S(2)}, u32[]{:S(2)}) collective-permute-start(bf16[512,128]{1,0:T(8,128)(2,1)S(1)} %get-tuple-element.40.now_ref.rest_3_.refs_3_), channel_id=1, source_target_pairs={{0,1},{1,2},{2,3},{3,4},{4,5},{5,6},{6,7},{7,0},{8,15},{9,8},{10,9... | collective-permute-start | bytes 393224 | tf_op jit(solution)/shard_map/ppermute | solution.py:288
  40.0 1.5 %collective-permute-start.19 = (bf16[512,128]{1,0:T(8,128)(2,1)S(1)}, bf16[512,128]{1,0:T(8,128)(2,1)S(1)}, u32[]{:S(2)}, u32[]{:S(2)}) collective-permute-start(bf16[512,128]{1,0:T(8,128)(2,1)S(1)} %get-tuple-element.41), channel_id=1, source_target_pairs={{0,16},{1,17},{2,18},{3,19},{4,20},{5,21},{6,22},{7,23},{8,24},{9,... | collective-permute-start | bytes 393224 | tf_op jit(solution)/shard_map/ppermute | solution.py:285
  42.1 4.6 %collective-permute-done.18.first_ref.rest_1_ = bf16[512,128]{1,0:T(8,128)(2,1)S(1)} collective-permute-done((bf16[512,128]{1,0:T(8,128)(2,1)S(1)}, bf16[512,128]{1,0:T(8,128)(2,1)S(1)}, u32[]{:S(2)}, u32[]{:S(2)}) %collective-permute-start.18) | collective-permute-done | bytes 131104 | tf_op jit(solution)/shard_map/ppermute | solution.py:288
  47.5 1.3 %collective-permute-done.20.other_ref = bf16[512,128]{1,0:T(8,128)(2,1)S(1)} collective-permute-done((bf16[512,128]{1,0:T(8,128)(2,1)S(1)}, bf16[512,128]{1,0:T(8,128)(2,1)S(1)}, u32[]{:S(2)}, u32[]{:S(2)}) %collective-permute-start.20) | collective-permute-done | bytes 131104 | tf_op jit(solution)/shard_map/ppermute | solution.py:282
  49.0 1.7 %collective-permute-start.22 = (bf16[512,128]{1,0:T(8,128)(2,1)S(1)}, bf16[512,128]{1,0:T(8,128)(2,1)S(1)}, u32[]{:S(2)}, u32[]{:S(2)}) collective-permute-start(bf16[512,128]{1,0:T(8,128)(2,1)S(1)} %get-tuple-element.42.now_ref.refs_4_.rest_3_), channel_id=1, source_target_pairs={{0,1},{1,2},{2,3},{3,4},{4,5},{5,6},{6,7},{7,0},{8,15},{9,8},{10,9... | collective-permute-start | bytes 393224 | tf_op jit(solution)/shard_map/ppermute | solution.py:288
  51.1 1.5 %collective-permute-start.23 = (bf16[512,128]{1,0:T(8,128)(2,1)S(1)}, bf16[512,128]{1,0:T(8,128)(2,1)S(1)}, u32[]{:S(2)}, u32[]{:S(2)}) collective-permute-start(bf16[512,128]{1,0:T(8,128)(2,1)S(1)} %get-tuple-element.43), channel_id=1, source_target_pairs={{0,16},{1,17},{2,18},{3,19},{4,20},{5,21},{6,22},{7,23},{8,24},{9,... | collective-permute-start | bytes 393224 | tf_op jit(solution)/shard_map/ppermute | solution.py:285
  53.1 4.0 %collective-permute-done.22.first_ref.rest_1_ = bf16[512,128]{1,0:T(8,128)(2,1)S(1)} collective-permute-done((bf16[512,128]{1,0:T(8,128)(2,1)S(1)}, bf16[512,128]{1,0:T(8,128)(2,1)S(1)}, u32[]{:S(2)}, u32[]{:S(2)}) %collective-permute-start.22) | collective-permute-done | bytes 131104 | tf_op jit(solution)/shard_map/ppermute | solution.py:288
  58.1 1.3 %collective-permute-done.24.other_ref = bf16[512,128]{1,0:T(8,128)(2,1)S(1)} collective-permute-done((bf16[512,128]{1,0:T(8,128)(2,1)S(1)}, bf16[512,128]{1,0:T(8,128)(2,1)S(1)}, u32[]{:S(2)}, u32[]{:S(2)}) %collective-permute-start.24) | collective-permute-done | bytes 131104 | tf_op jit(solution)/shard_map/ppermute | solution.py:282
  59.6 1.6 %collective-permute-start.25 = (bf16[512,128]{1,0:T(8,128)(2,1)S(1)}, bf16[512,128]{1,0:T(8,128)(2,1)S(1)}, u32[]{:S(2)}, u32[]{:S(2)}) collective-permute-start(bf16[512,128]{1,0:T(8,128)(2,1)S(1)} %get-tuple-element.45), channel_id=1, source_target_pairs={{0,16},{1,17},{2,18},{3,19},{4,20},{5,21},{6,22},{7,23},{8,24},{9,... | collective-permute-start | bytes 393224 | tf_op jit(solution)/shard_map/ppermute | solution.py:285
  61.2 1.4 %collective-permute-start.28 = (bf16[512,128]{1,0:T(8,128)(2,1)S(1)}, bf16[512,128]{1,0:T(8,128)(2,1)S(1)}, u32[]{:S(2)}, u32[]{:S(2)}) collective-permute-start(bf16[512,128]{1,0:T(8,128)(2,1)S(1)} %get-tuple-element.44.refs_5_.rest_3_.now_ref), channel_id=1, source_target_pairs={{0,1},{1,2},{2,3},{3,4},{4,5},{5,6},{6,7},{7,0},{8,15},{9,8},{10,9... | collective-permute-start | bytes 393224 | tf_op jit(solution)/shard_map/ppermute | solution.py:288
  63.2 2.1 %collective-permute-done.25.refs_6_.now_ref.rest_0_ = bf16[512,128]{1,0:T(8,128)(2,1)S(1)} collective-permute-done((bf16[512,128]{1,0:T(8,128)(2,1)S(1)}, bf16[512,128]{1,0:T(8,128)(2,1)S(1)}, u32[]{:S(2)}, u32[]{:S(2)}) %collective-permute-start.25) | collective-permute-done | bytes 131104 | tf_op jit(solution)/shard_map/ppermute | solution.py:285
  65.3 1.4 %collective-permute-start.27 = (bf16[512,128]{1,0:T(8,128)(2,1)S(1)}, bf16[512,128]{1,0:T(8,128)(2,1)S(1)}, u32[]{:S(2)}, u32[]{:S(2)}) collective-permute-start(bf16[512,128]{1,0:T(8,128)(2,1)S(1)} %collective-permute-done.25.refs_6_.now_ref.rest_0_), channel_id=1, source_target_pairs={{0,1},{1,2},{2,3},{3,4},{4,5},{5,6},{6,7},{7,0},{8,15},{9,8},{10,9... | collective-permute-start | bytes 393224 | tf_op jit(solution)/shard_map/ppermute | solution.py:288
  66.8 2.2 %collective-permute-done.28.rest_1_.first_ref.block_ref = bf16[512,128]{1,0:T(8,128)(2,1)S(1)} collective-permute-done((bf16[512,128]{1,0:T(8,128)(2,1)S(1)}, bf16[512,128]{1,0:T(8,128)(2,1)S(1)}, u32[]{:S(2)}, u32[]{:S(2)}) %collective-permute-start.28) | collective-permute-done | bytes 131104 | tf_op jit(solution)/shard_map/ppermute | solution.py:288
  69.3 0.9 %collective-permute-done.29.rest_2_.second_ref.block_ref = bf16[512,128]{1,0:T(8,128)(2,1)S(1)} collective-permute-done((bf16[512,128]{1,0:T(8,128)(2,1)S(1)}, bf16[512,128]{1,0:T(8,128)(2,1)S(1)}, u32[]{:S(2)}, u32[]{:S(2)}) %collective-permute-start.29) | collective-permute-done | bytes 131104 | tf_op jit(solution)/shard_map/ppermute | solution.py:288
  74.3 1.3 %collective-permute-done.30.rest_0_ = bf16[512,128]{1,0:T(8,128)(2,1)S(1)} collective-permute-done((bf16[512,128]{1,0:T(8,128)(2,1)S(1)}, bf16[512,128]{1,0:T(8,128)(2,1)S(1)}, u32[]{:S(2)}, u32[]{:S(2)}) %collective-permute-start.30) | collective-permute-done | bytes 131104 | tf_op jit(solution)/shard_map/ppermute | solution.py:285
  75.7 1.0 %shard_map.92 = (bf16[6,512,128]{2,1,0:T(8,128)(2,1)}, f32[8,128]{1,0:T(8,128)S(1)}) custom-call(bf16[512,128]{1,0:T(8,128)(2,1)S(1)} %shard_map.69.now_ref.rest_3_.refs_0_, bf16[512,128]{1,0:T(8,128)(2,1)S(1)} %get-tuple-element.35.now_ref.rest_3_.refs_1_, bf16[512,128]{1,0:T(8,128)(2,1)S(1)} %get-tuple-element.38.now_ref.rest_3_.refs_2_, ...), custom_call_target="tpu_custom_call" | custom-call | bytes 1048576 | tf_op jit(solution)/shard_map/pallas_call | solution.py:38
  77.1 0.8 shard_map.108
  (83 shorter events, 17.2 us)
Async XLA Ops:
  0.7 4.0 %collective-permute-start = (f32[512,128]{1,0:T(8,128)}, f32[512,128]{1,0:T(8,128)S(1)}, u32[]{:S(2)}, u32[]{:S(2)}) collective-permute-start(f32[512,128]{1,0:T(8,128)} %bitcast.4), channel_id=1, source_target_pairs={{0,8},{1,9},{2,10},{3,11},{4,12},{5,13},{6,14},{7,15},{8,0},{9,1},... | collective-permute-start | bytes 786440 | tf_op jit(solution)/shard_map/ppermute | solution.py:282
  3.6 4.0 %collective-permute-start.1 = (bf16[128,1024]{1,0:T(8,128)(2,1)S(1)}, bf16[128,1024]{1,0:T(8,128)(2,1)S(1)}, u32[]{:S(2)}, u32[]{:S(2)}) collective-permute-start(bf16[128,1024]{1,0:T(8,128)(2,1)S(1)} %get-tuple-element.29), channel_id=1, source_target_pairs={{0,8},{1,9},{2,10},{3,11},{4,12},{5,13},{6,14},{7,15},{8,0},{9,1},... | collective-permute-start | bytes 786440 | tf_op jit(solution)/shard_map/ppermute | solution.py:282
  3.8 5.4 %collective-permute-start.2 = (bf16[128,1024]{1,0:T(8,128)(2,1)S(1)}, bf16[128,1024]{1,0:T(8,128)(2,1)S(1)}, u32[]{:S(2)}, u32[]{:S(2)}) collective-permute-start(bf16[128,1024]{1,0:T(8,128)(2,1)S(1)} %get-tuple-element.30), channel_id=1, source_target_pairs={{0,8},{1,9},{2,10},{3,11},{4,12},{5,13},{6,14},{7,15},{8,0},{9,1},... | collective-permute-start | bytes 786440 | tf_op jit(solution)/shard_map/ppermute | solution.py:282
  4.2 6.8 %collective-permute-start.3 = (bf16[128,1024]{1,0:T(8,128)(2,1)S(1)}, bf16[128,1024]{1,0:T(8,128)(2,1)S(1)}, u32[]{:S(2)}, u32[]{:S(2)}) collective-permute-start(bf16[128,1024]{1,0:T(8,128)(2,1)S(1)} %get-tuple-element.31), channel_id=1, source_target_pairs={{0,8},{1,9},{2,10},{3,11},{4,12},{5,13},{6,14},{7,15},{8,0},{9,1},... | collective-permute-start | bytes 786440 | tf_op jit(solution)/shard_map/ppermute | solution.py:282
  4.3 6.7 %collective-permute-start.4 = (bf16[128,1024]{1,0:T(8,128)(2,1)S(1)}, bf16[128,1024]{1,0:T(8,128)(2,1)S(1)}, u32[]{:S(2)}, u32[]{:S(2)}) collective-permute-start(bf16[128,1024]{1,0:T(8,128)(2,1)S(1)} %get-tuple-element.32), channel_id=1, source_target_pairs={{0,8},{1,9},{2,10},{3,11},{4,12},{5,13},{6,14},{7,15},{8,0},{9,1},... | collective-permute-start | bytes 786440 | tf_op jit(solution)/shard_map/ppermute | solution.py:282
  4.9 9.9 %collective-permute-start.6 = (bf16[512,128]{1,0:T(8,128)(2,1)S(1)}, bf16[512,128]{1,0:T(8,128)(2,1)S(1)}, u32[]{:S(2)}, u32[]{:S(2)}) collective-permute-start(bf16[512,128]{1,0:T(8,128)(2,1)S(1)} %shard_map.69.now_ref.rest_3_.refs_0_), channel_id=1, source_target_pairs={{0,1},{1,2},{2,3},{3,4},{4,5},{5,6},{6,7},{7,0},{8,15},{9,8},{10,9... | collective-permute-start | bytes 393224 | tf_op jit(solution)/shard_map/ppermute | solution.py:288
  7.6 8.2 %collective-permute-start.5 = (bf16[512,128]{1,0:T(8,128)(2,1)S(1)}, bf16[512,128]{1,0:T(8,128)(2,1)S(1)}, u32[]{:S(2)}, u32[]{:S(2)}) collective-permute-start(bf16[512,128]{1,0:T(8,128)(2,1)S(1)} %shard_map.69.now_ref.rest_3_.refs_0_), channel_id=1, source_target_pairs={{0,2},{1,3},{2,4},{3,5},{4,6},{5,7},{6,0},{7,1},{8,14},{9,15},{10,... | collective-permute-start | bytes 393224 | tf_op jit(solution)/shard_map/ppermute | solution.py:288
  9.2 6.6 %collective-permute-start.7 = (bf16[512,128]{1,0:T(8,128)(2,1)S(1)}, bf16[512,128]{1,0:T(8,128)(2,1)S(1)}, u32[]{:S(2)}, u32[]{:S(2)}) collective-permute-start(bf16[512,128]{1,0:T(8,128)(2,1)S(1)} %shard_map.69.now_ref.rest_3_.refs_0_), channel_id=1, source_target_pairs={{0,16},{1,17},{2,18},{3,19},{4,20},{5,21},{6,22},{7,23},{8,24},{9,... | collective-permute-start | bytes 393224 | tf_op jit(solution)/shard_map/ppermute | solution.py:285
  16.1 1.4 %collective-permute-start.8 = (bf16[512,128]{1,0:T(8,128)(2,1)S(1)}, bf16[512,128]{1,0:T(8,128)(2,1)S(1)}, u32[]{:S(2)}, u32[]{:S(2)}) collective-permute-start(bf16[512,128]{1,0:T(8,128)(2,1)S(1)} %shard_map.74.mine_ref), channel_id=1, source_target_pairs={{0,8},{1,9},{2,10},{3,11},{4,12},{5,13},{6,14},{7,15},{8,0},{9,1},... | collective-permute-start | bytes 393224 | tf_op jit(solution)/shard_map/ppermute | solution.py:282
  17.7 8.4 %collective-permute-start.11 = (bf16[512,128]{1,0:T(8,128)(2,1)S(1)}, bf16[512,128]{1,0:T(8,128)(2,1)S(1)}, u32[]{:S(2)}, u32[]{:S(2)}) collective-permute-start(bf16[512,128]{1,0:T(8,128)(2,1)S(1)} %get-tuple-element.35.now_ref.rest_3_.refs_1_), channel_id=1, source_target_pairs={{0,1},{1,2},{2,3},{3,4},{4,5},{5,6},{6,7},{7,0},{8,15},{9,8},{10,9... | collective-permute-start | bytes 393224 | tf_op jit(solution)/shard_map/ppermute | solution.py:288
  19.0 7.5 %collective-permute-start.10 = (bf16[512,128]{1,0:T(8,128)(2,1)S(1)}, bf16[512,128]{1,0:T(8,128)(2,1)S(1)}, u32[]{:S(2)}, u32[]{:S(2)}) collective-permute-start(bf16[512,128]{1,0:T(8,128)(2,1)S(1)} %get-tuple-element.35.now_ref.rest_3_.refs_1_), channel_id=1, source_target_pairs={{0,2},{1,3},{2,4},{3,5},{4,6},{5,7},{6,0},{7,1},{8,14},{9,15},{10,... | collective-permute-start | bytes 393224 | tf_op jit(solution)/shard_map/ppermute | solution.py:288
  19.2 7.2 %collective-permute-start.9 = (bf16[512,128]{1,0:T(8,128)(2,1)S(1)}, bf16[512,128]{1,0:T(8,128)(2,1)S(1)}, u32[]{:S(2)}, u32[]{:S(2)}) collective-permute-start(bf16[512,128]{1,0:T(8,128)(2,1)S(1)} %get-tuple-element.36), channel_id=1, source_target_pairs={{0,16},{1,17},{2,18},{3,19},{4,20},{5,21},{6,22},{7,23},{8,24},{9,... | collective-permute-start | bytes 393224 | tf_op jit(solution)/shard_map/ppermute | solution.py:285
  26.8 1.4 %collective-permute-start.12 = (bf16[512,128]{1,0:T(8,128)(2,1)S(1)}, bf16[512,128]{1,0:T(8,128)(2,1)S(1)}, u32[]{:S(2)}, u32[]{:S(2)}) collective-permute-start(bf16[512,128]{1,0:T(8,128)(2,1)S(1)} %shard_map.78.mine_ref), channel_id=1, source_target_pairs={{0,8},{1,9},{2,10},{3,11},{4,12},{5,13},{6,14},{7,15},{8,0},{9,1},... | collective-permute-start | bytes 393224 | tf_op jit(solution)/shard_map/ppermute | solution.py:282
  28.4 7.7 %collective-permute-start.14 = (bf16[512,128]{1,0:T(8,128)(2,1)S(1)}, bf16[512,128]{1,0:T(8,128)(2,1)S(1)}, u32[]{:S(2)}, u32[]{:S(2)}) collective-permute-start(bf16[512,128]{1,0:T(8,128)(2,1)S(1)} %get-tuple-element.38.now_ref.rest_3_.refs_2_), channel_id=1, source_target_pairs={{0,1},{1,2},{2,3},{3,4},{4,5},{5,6},{6,7},{7,0},{8,15},{9,8},{10,9... | collective-permute-start | bytes 393224 | tf_op jit(solution)/shard_map/ppermute | solution.py:288
  30.1 7.0 %collective-permute-start.13 = (bf16[512,128]{1,0:T(8,128)(2,1)S(1)}, bf16[512,128]{1,0:T(8,128)(2,1)S(1)}, u32[]{:S(2)}, u32[]{:S(2)}) collective-permute-start(bf16[512,128]{1,0:T(8,128)(2,1)S(1)} %get-tuple-element.38.now_ref.rest_3_.refs_2_), channel_id=1, source_target_pairs={{0,2},{1,3},{2,4},{3,5},{4,6},{5,7},{6,0},{7,1},{8,14},{9,15},{10,... | collective-permute-start | bytes 393224 | tf_op jit(solution)/shard_map/ppermute | solution.py:288
  30.5 6.6 %collective-permute-start.15 = (bf16[512,128]{1,0:T(8,128)(2,1)S(1)}, bf16[512,128]{1,0:T(8,128)(2,1)S(1)}, u32[]{:S(2)}, u32[]{:S(2)}) collective-permute-start(bf16[512,128]{1,0:T(8,128)(2,1)S(1)} %get-tuple-element.39), channel_id=1, source_target_pairs={{0,16},{1,17},{2,18},{3,19},{4,20},{5,21},{6,22},{7,23},{8,24},{9,... | collective-permute-start | bytes 393224 | tf_op jit(solution)/shard_map/ppermute | solution.py:285
  37.4 1.4 %collective-permute-start.16 = (bf16[512,128]{1,0:T(8,128)(2,1)S(1)}, bf16[512,128]{1,0:T(8,128)(2,1)S(1)}, u32[]{:S(2)}, u32[]{:S(2)}) collective-permute-start(bf16[512,128]{1,0:T(8,128)(2,1)S(1)} %shard_map.82.mine_ref), channel_id=1, source_target_pairs={{0,8},{1,9},{2,10},{3,11},{4,12},{5,13},{6,14},{7,15},{8,0},{9,1},... | collective-permute-start | bytes 393224 | tf_op jit(solution)/shard_map/ppermute | solution.py:282
  39.0 7.7 %collective-permute-start.18 = (bf16[512,128]{1,0:T(8,128)(2,1)S(1)}, bf16[512,128]{1,0:T(8,128)(2,1)S(1)}, u32[]{:S(2)}, u32[]{:S(2)}) collective-permute-start(bf16[512,128]{1,0:T(8,128)(2,1)S(1)} %get-tuple-element.40.now_ref.rest_3_.refs_3_), channel_id=1, source_target_pairs={{0,1},{1,2},{2,3},{3,4},{4,5},{5,6},{6,7},{7,0},{8,15},{9,8},{10,9... | collective-permute-start | bytes 393224 | tf_op jit(solution)/shard_map/ppermute | solution.py:288
  40.0 7.1 %collective-permute-start.17 = (bf16[512,128]{1,0:T(8,128)(2,1)S(1)}, bf16[512,128]{1,0:T(8,128)(2,1)S(1)}, u32[]{:S(2)}, u32[]{:S(2)}) collective-permute-start(bf16[512,128]{1,0:T(8,128)(2,1)S(1)} %get-tuple-element.40.now_ref.rest_3_.refs_3_), channel_id=1, source_target_pairs={{0,2},{1,3},{2,4},{3,5},{4,6},{5,7},{6,0},{7,1},{8,14},{9,15},{10,... | collective-permute-start | bytes 393224 | tf_op jit(solution)/shard_map/ppermute | solution.py:288
  40.0 7.1 %collective-permute-start.19 = (bf16[512,128]{1,0:T(8,128)(2,1)S(1)}, bf16[512,128]{1,0:T(8,128)(2,1)S(1)}, u32[]{:S(2)}, u32[]{:S(2)}) collective-permute-start(bf16[512,128]{1,0:T(8,128)(2,1)S(1)} %get-tuple-element.41), channel_id=1, source_target_pairs={{0,16},{1,17},{2,18},{3,19},{4,20},{5,21},{6,22},{7,23},{8,24},{9,... | collective-permute-start | bytes 393224 | tf_op jit(solution)/shard_map/ppermute | solution.py:285
  47.4 1.4 %collective-permute-start.20 = (bf16[512,128]{1,0:T(8,128)(2,1)S(1)}, bf16[512,128]{1,0:T(8,128)(2,1)S(1)}, u32[]{:S(2)}, u32[]{:S(2)}) collective-permute-start(bf16[512,128]{1,0:T(8,128)(2,1)S(1)} %shard_map.86.mine_ref), channel_id=1, source_target_pairs={{0,8},{1,9},{2,10},{3,11},{4,12},{5,13},{6,14},{7,15},{8,0},{9,1},... | collective-permute-start | bytes 393224 | tf_op jit(solution)/shard_map/ppermute | solution.py:282
  49.0 8.1 %collective-permute-start.22 = (bf16[512,128]{1,0:T(8,128)(2,1)S(1)}, bf16[512,128]{1,0:T(8,128)(2,1)S(1)}, u32[]{:S(2)}, u32[]{:S(2)}) collective-permute-start(bf16[512,128]{1,0:T(8,128)(2,1)S(1)} %get-tuple-element.42.now_ref.refs_4_.rest_3_), channel_id=1, source_target_pairs={{0,1},{1,2},{2,3},{3,4},{4,5},{5,6},{6,7},{7,0},{8,15},{9,8},{10,9... | collective-permute-start | bytes 393224 | tf_op jit(solution)/shard_map/ppermute | solution.py:288
  50.7 7.0 %collective-permute-start.21 = (bf16[512,128]{1,0:T(8,128)(2,1)S(1)}, bf16[512,128]{1,0:T(8,128)(2,1)S(1)}, u32[]{:S(2)}, u32[]{:S(2)}) collective-permute-start(bf16[512,128]{1,0:T(8,128)(2,1)S(1)} %get-tuple-element.42.now_ref.refs_4_.rest_3_), channel_id=1, source_target_pairs={{0,2},{1,3},{2,4},{3,5},{4,6},{5,7},{6,0},{7,1},{8,14},{9,15},{10,... | collective-permute-start | bytes 393224 | tf_op jit(solution)/shard_map/ppermute | solution.py:288
  51.1 6.7 %collective-permute-start.23 = (bf16[512,128]{1,0:T(8,128)(2,1)S(1)}, bf16[512,128]{1,0:T(8,128)(2,1)S(1)}, u32[]{:S(2)}, u32[]{:S(2)}) collective-permute-start(bf16[512,128]{1,0:T(8,128)(2,1)S(1)} %get-tuple-element.43), channel_id=1, source_target_pairs={{0,16},{1,17},{2,18},{3,19},{4,20},{5,21},{6,22},{7,23},{8,24},{9,... | collective-permute-start | bytes 393224 | tf_op jit(solution)/shard_map/ppermute | solution.py:285
  58.0 1.4 %collective-permute-start.24 = (bf16[512,128]{1,0:T(8,128)(2,1)S(1)}, bf16[512,128]{1,0:T(8,128)(2,1)S(1)}, u32[]{:S(2)}, u32[]{:S(2)}) collective-permute-start(bf16[512,128]{1,0:T(8,128)(2,1)S(1)} %shard_map.90.mine_ref), channel_id=1, source_target_pairs={{0,8},{1,9},{2,10},{3,11},{4,12},{5,13},{6,14},{7,15},{8,0},{9,1},... | collective-permute-start | bytes 393224 | tf_op jit(solution)/shard_map/ppermute | solution.py:282
  59.6 5.6 %collective-permute-start.25 = (bf16[512,128]{1,0:T(8,128)(2,1)S(1)}, bf16[512,128]{1,0:T(8,128)(2,1)S(1)}, u32[]{:S(2)}, u32[]{:S(2)}) collective-permute-start(bf16[512,128]{1,0:T(8,128)(2,1)S(1)} %get-tuple-element.45), channel_id=1, source_target_pairs={{0,16},{1,17},{2,18},{3,19},{4,20},{5,21},{6,22},{7,23},{8,24},{9,... | collective-permute-start | bytes 393224 | tf_op jit(solution)/shard_map/ppermute | solution.py:285
  61.2 7.8 %collective-permute-start.28 = (bf16[512,128]{1,0:T(8,128)(2,1)S(1)}, bf16[512,128]{1,0:T(8,128)(2,1)S(1)}, u32[]{:S(2)}, u32[]{:S(2)}) collective-permute-start(bf16[512,128]{1,0:T(8,128)(2,1)S(1)} %get-tuple-element.44.refs_5_.rest_3_.now_ref), channel_id=1, source_target_pairs={{0,1},{1,2},{2,3},{3,4},{4,5},{5,6},{6,7},{7,0},{8,15},{9,8},{10,9... | collective-permute-start | bytes 393224 | tf_op jit(solution)/shard_map/ppermute | solution.py:288
  62.6 7.6 %collective-permute-start.29 = (bf16[512,128]{1,0:T(8,128)(2,1)S(1)}, bf16[512,128]{1,0:T(8,128)(2,1)S(1)}, u32[]{:S(2)}, u32[]{:S(2)}) collective-permute-start(bf16[512,128]{1,0:T(8,128)(2,1)S(1)} %get-tuple-element.44.refs_5_.rest_3_.now_ref), channel_id=1, source_target_pairs={{0,2},{1,3},{2,4},{3,5},{4,6},{5,7},{6,0},{7,1},{8,14},{9,15},{10,... | collective-permute-start | bytes 393224 | tf_op jit(solution)/shard_map/ppermute | solution.py:288
  65.3 7.8 %collective-permute-start.27 = (bf16[512,128]{1,0:T(8,128)(2,1)S(1)}, bf16[512,128]{1,0:T(8,128)(2,1)S(1)}, u32[]{:S(2)}, u32[]{:S(2)}) collective-permute-start(bf16[512,128]{1,0:T(8,128)(2,1)S(1)} %collective-permute-done.25.refs_6_.now_ref.rest_0_), channel_id=1, source_target_pairs={{0,1},{1,2},{2,3},{3,4},{4,5},{5,6},{6,7},{7,0},{8,15},{9,8},{10,9... | collective-permute-start | bytes 393224 | tf_op jit(solution)/shard_map/ppermute | solution.py:288
  66.7 7.0 %collective-permute-start.26 = (bf16[512,128]{1,0:T(8,128)(2,1)S(1)}, bf16[512,128]{1,0:T(8,128)(2,1)S(1)}, u32[]{:S(2)}, u32[]{:S(2)}) collective-permute-start(bf16[512,128]{1,0:T(8,128)(2,1)S(1)} %collective-permute-done.25.refs_6_.now_ref.rest_0_), channel_id=1, source_target_pairs={{0,2},{1,3},{2,4},{3,5},{4,6},{5,7},{6,0},{7,1},{8,14},{9,15},{10,... | collective-permute-start | bytes 393224 | tf_op jit(solution)/shard_map/ppermute | solution.py:288
  70.5 5.0 %collective-permute-start.30 = (bf16[512,128]{1,0:T(8,128)(2,1)S(1)}, bf16[512,128]{1,0:T(8,128)(2,1)S(1)}, u32[]{:S(2)}, u32[]{:S(2)}) collective-permute-start(bf16[512,128]{1,0:T(8,128)(2,1)S(1)} %get-tuple-element.47), channel_id=1, source_target_pairs={{0,16},{1,17},{2,18},{3,19},{4,20},{5,21},{6,22},{7,23},{8,24},{9,... | collective-permute-start | bytes 393224 | tf_op jit(solution)/shard_map/ppermute | solution.py:285
  71.6 5.2 %collective-permute-start.32 = (bf16[512,128]{1,0:T(8,128)(2,1)S(1)}, bf16[512,128]{1,0:T(8,128)(2,1)S(1)}, u32[]{:S(2)}, u32[]{:S(2)}) collective-permute-start(bf16[512,128]{1,0:T(8,128)(2,1)S(1)} %get-tuple-element.52), channel_id=1, source_target_pairs={{0,8},{1,9},{2,10},{3,11},{4,12},{5,13},{6,14},{7,15},{8,0},{9,1},... | collective-permute-start | bytes 393224 | tf_op jit(solution)/shard_map/ppermute | solution.py:282
  (5 other events, 14.4 us)

commit v9 on v8

--- a/solution.py
+++ b/solution.py
@@ -284,10 +284,13 @@
     def pair_moved(value, hop):
         return lax.ppermute(value, AXES, everyone(lambda d, s: ((d + 2 * hop) % lags, s)))
 
-    def halo(value, hop):
-        return lax.ppermute(
-            value, AXES, everyone(lambda d, s: (d, (s + (hop if d % 2 == 0 else -hop)) % groups))
-        )
+    def halo(value, hop, since=0, until=pairs):
+        def move(d, s):
+            if not since <= d // 2 <= until:
+                return d ^ 1, s
+            return d, (s + (hop if d % 2 == 0 else -hop)) % groups
+
+        return lax.ppermute(value, AXES, everyone(move))
 
     other_history = swapped(history[0])
     field_shape = jax.ShapeDtypeStruct((rows, columns), F32)
@@ -317,7 +320,7 @@
                 [jax.ShapeDtypeStruct(excitation.shape, BF16), TOKEN],
                 seen,
             )
-        first, second = windows or (halo(current, 1), halo(current, 2))
+        first, second = windows or (halo(current, 1, 0, step), halo(current, 2, 0, step))
         if pairs == 2:
             current_in = field_in = pair_moved(going, 1)
         else:
@@ -342,7 +345,8 @@
             )
         else:
             if step < rounds - 1:
-                windows = halo(current_in, 1), halo(current_in, 2)
+                done = step + 2 - steps
+                windows = halo(current_in, 1, done), halo(current_in, 2, done)
             more = step < rounds - 1
             even, *next_field = call(
                 functools.partial(even_body, step, pairs),

time: 78 us -> 76.9 us (0.986)
  starting transfers between devices: 25.2 us -> 18.3 us
  waiting for transfers between devices: 36.2 us -> 41.9 us
    ppermute x7, starting transfers between devices: 9.05 us -> 2.71 us  [pair_moved(): lax.ppermute(value, AXES, everyone(lambda d, s: ((d + 2 * hop) % lags, s)))]
    ppermute x14, waiting for transfers between devices: 25.9 us -> 31.8 us  [halo(): return lax.ppermute(value, AXES, everyone(move))]
    ppermute x14, starting transfers between devices: 13.9 us -> 12.9 us  [halo(): return lax.ppermute(value, AXES, everyone(move))]
  transfers between devices with their start and end apart: 33 -> 33, of which waited for: 20 -> 17; matrix products, arithmetic and copies ran while one was open for 0% -> 0% of each run, Pallas kernels for 15% -> 15%
where the time goes in v9:
time: 76.9 us; the launch traced here: 76.7 us
  waiting for transfers between devices  41.9 us (54%)
  starting transfers between devices  18.3 us (24%)
  Pallas kernels  14.8 us (19%)
  between operations  1.04 us (1%)
    ppermute x14, waiting for transfers between devices, halo(): return lax.ppermute(value, AXES, everyone(move))  31.8 us
    pallas_call x40, Pallas kernels, call(): pl.pallas_call(body, out_shape=tuple(outs), in_specs=specs, out_specs=tup...  13 us
    ppermute x14, starting transfers between devices, halo(): return lax.ppermute(value, AXES, everyone(move))  12.9 us
    ppermute x12, waiting for transfers between devices, swapped(): return lax.ppermute(value, AXES, everyone(lambda d, s: (d ^ 1, s)))  6.59 us
    ppermute x7, waiting for transfers between devices, pair_moved(): lax.ppermute(value, AXES, everyone(lambda d, s: ((d + 2 * hop) % lags, s)))  3.52 us
    ppermute x7, starting transfers between devices, pair_moved(): lax.ppermute(value, AXES, everyone(lambda d, s: ((d + 2 * hop) % lags, s)))  2.71 us
    ppermute x12, starting transfers between devices, swapped(): return lax.ppermute(value, AXES, everyone(lambda d, s: (d ^ 1, s)))  2.68 us
    pallas_call x1, Pallas kernels, spread(): pl.pallas_call(functools.partial(spread_body, groups), out_shape=(matrix(...  1.74 us
  transfers between devices with their start and end apart: 33, of which 17 were waited for; matrix products, arithmetic and copies ran while one was open for 0% of the time, Pallas kernels for 15%

profile of v9, /device:TPU:0, one launch (start us, length us, event | category | flops | bytes accessed | tf_op | source)
XLA Modules:
  0.0 76.7 jit_solution(5947425551103488416)
XLA Ops:
  1.2 0.7 copy-done.3
  1.9 1.7 %shard_map.70 = (bf16[512,1024]{1,0:T(8,128)(2,1)S(1)}, bf16[512,512]{1,0:T(8,128)(2,1)S(1)}, bf16[128,1024]{1,0:T(8,128)(2,1)S(1)}, bf16[128,1024]{1,0:T(8,128)...) custom-call(s32[4,16]{1,0:T(4,128)S(1)} %bitcast.8, bf16[4,16,128,128]{3,2,1,0:T(8,128)(2,1)} %bitcast.9), custom_call_target="tpu_custom_call" | custom-call | bytes 1048576 | tf_op jit(solution)/shard_map/pallas_call | solution.py:99
  4.9 2.7 %collective-permute-start.6 = (bf16[512,128]{1,0:T(8,128)(2,1)S(1)}, bf16[512,128]{1,0:T(8,128)(2,1)S(1)}, u32[]{:S(2)}, u32[]{:S(2)}) collective-permute-start(bf16[512,128]{1,0:T(8,128)(2,1)S(1)} %shard_map.69.now_ref.rest_3_.refs_0_), channel_id=1, source_target_pairs={{0,1},{1,2},{2,3},{3,4},{4,5},{5,6},{6,7},{7,0},{8,15},{9,8},{10,9... | collective-permute-start | bytes 393224 | tf_op jit(solution)/shard_map/ppermute | solution.py:293
  7.6 1.6 %collective-permute-start.5 = (bf16[512,128]{1,0:T(8,128)(2,1)S(1)}, bf16[512,128]{1,0:T(8,128)(2,1)S(1)}, u32[]{:S(2)}, u32[]{:S(2)}) collective-permute-start(bf16[512,128]{1,0:T(8,128)(2,1)S(1)} %shard_map.69.now_ref.rest_3_.refs_0_), channel_id=1, source_target_pairs={{0,2},{1,3},{2,4},{3,5},{4,6},{5,7},{6,0},{7,1},{8,14},{9,15},{10,... | collective-permute-start | bytes 393224 | tf_op jit(solution)/shard_map/ppermute | solution.py:293
  9.7 5.2 %collective-permute-done.6.first_ref.rest_1_ = bf16[512,128]{1,0:T(8,128)(2,1)S(1)} collective-permute-done((bf16[512,128]{1,0:T(8,128)(2,1)S(1)}, bf16[512,128]{1,0:T(8,128)(2,1)S(1)}, u32[]{:S(2)}, u32[]{:S(2)}) %collective-permute-start.6) | collective-permute-done | bytes 131104 | tf_op jit(solution)/shard_map/ppermute | solution.py:293
  15.2 0.6 collective-permute-done.5.second_ref.rest_2_
  16.2 1.2 %collective-permute-done.8.other_ref = bf16[512,128]{1,0:T(8,128)(2,1)S(1)} collective-permute-done((bf16[512,128]{1,0:T(8,128)(2,1)S(1)}, bf16[512,128]{1,0:T(8,128)(2,1)S(1)}, u32[]{:S(2)}, u32[]{:S(2)}) %collective-permute-start.8) | collective-permute-done | bytes 131104 | tf_op jit(solution)/shard_map/ppermute | solution.py:282
  17.7 1.3 %collective-permute-start.11 = (bf16[512,128]{1,0:T(8,128)(2,1)S(1)}, bf16[512,128]{1,0:T(8,128)(2,1)S(1)}, u32[]{:S(2)}, u32[]{:S(2)}) collective-permute-start(bf16[512,128]{1,0:T(8,128)(2,1)S(1)} %get-tuple-element.35.now_ref.rest_3_.refs_1_), channel_id=1, source_target_pairs={{0,1},{1,2},{2,3},{3,4},{4,5},{5,6},{6,7},{7,0},{8,15},{9,8},{10,9... | collective-permute-start | bytes 393224 | tf_op jit(solution)/shard_map/ppermute | solution.py:293
  19.2 0.6 shard_map.76.early_ref
  19.8 6.3 %collective-permute-done.11.first_ref.rest_1_ = bf16[512,128]{1,0:T(8,128)(2,1)S(1)} collective-permute-done((bf16[512,128]{1,0:T(8,128)(2,1)S(1)}, bf16[512,128]{1,0:T(8,128)(2,1)S(1)}, u32[]{:S(2)}, u32[]{:S(2)}) %collective-permute-start.11) | collective-permute-done | bytes 131104 | tf_op jit(solution)/shard_map/ppermute | solution.py:293
  26.8 1.3 %collective-permute-done.12.other_ref = bf16[512,128]{1,0:T(8,128)(2,1)S(1)} collective-permute-done((bf16[512,128]{1,0:T(8,128)(2,1)S(1)}, bf16[512,128]{1,0:T(8,128)(2,1)S(1)}, u32[]{:S(2)}, u32[]{:S(2)}) %collective-permute-start.12) | collective-permute-done | bytes 131104 | tf_op jit(solution)/shard_map/ppermute | solution.py:282
  28.4 1.7 %collective-permute-start.14 = (bf16[512,128]{1,0:T(8,128)(2,1)S(1)}, bf16[512,128]{1,0:T(8,128)(2,1)S(1)}, u32[]{:S(2)}, u32[]{:S(2)}) collective-permute-start(bf16[512,128]{1,0:T(8,128)(2,1)S(1)} %get-tuple-element.38.now_ref.rest_3_.refs_2_), channel_id=1, source_target_pairs={{0,1},{1,2},{2,3},{3,4},{4,5},{5,6},{6,7},{7,0},{8,15},{9,8},{10,9... | collective-permute-start | bytes 393224 | tf_op jit(solution)/shard_map/ppermute | solution.py:293
  30.5 0.6 shard_map.80.early_ref
  31.1 5.0 %collective-permute-done.14.first_ref.rest_1_ = bf16[512,128]{1,0:T(8,128)(2,1)S(1)} collective-permute-done((bf16[512,128]{1,0:T(8,128)(2,1)S(1)}, bf16[512,128]{1,0:T(8,128)(2,1)S(1)}, u32[]{:S(2)}, u32[]{:S(2)}) %collective-permute-start.14) | collective-permute-done | bytes 131104 | tf_op jit(solution)/shard_map/ppermute | solution.py:293
  36.4 0.7 collective-permute-done.13.second_ref.rest_2_
  37.5 1.3 %collective-permute-done.16.other_ref = bf16[512,128]{1,0:T(8,128)(2,1)S(1)} collective-permute-done((bf16[512,128]{1,0:T(8,128)(2,1)S(1)}, bf16[512,128]{1,0:T(8,128)(2,1)S(1)}, u32[]{:S(2)}, u32[]{:S(2)}) %collective-permute-start.16) | collective-permute-done | bytes 131104 | tf_op jit(solution)/shard_map/ppermute | solution.py:282
  39.0 1.0 %collective-permute-start.18 = (bf16[512,128]{1,0:T(8,128)(2,1)S(1)}, bf16[512,128]{1,0:T(8,128)(2,1)S(1)}, u32[]{:S(2)}, u32[]{:S(2)}) collective-permute-start(bf16[512,128]{1,0:T(8,128)(2,1)S(1)} %get-tuple-element.40.now_ref.rest_3_.refs_3_), channel_id=1, source_target_pairs={{0,1},{1,2},{2,3},{3,4},{4,5},{5,6},{6,7},{7,0},{8,15},{9,8},{10,9... | collective-permute-start | bytes 393224 | tf_op jit(solution)/shard_map/ppermute | solution.py:293
  40.1 0.6 shard_map.84.early_ref
  40.6 6.1 %collective-permute-done.18.first_ref.rest_1_ = bf16[512,128]{1,0:T(8,128)(2,1)S(1)} collective-permute-done((bf16[512,128]{1,0:T(8,128)(2,1)S(1)}, bf16[512,128]{1,0:T(8,128)(2,1)S(1)}, u32[]{:S(2)}, u32[]{:S(2)}) %collective-permute-start.18) | collective-permute-done | bytes 131104 | tf_op jit(solution)/shard_map/ppermute | solution.py:293
  47.5 1.3 %collective-permute-done.20.other_ref = bf16[512,128]{1,0:T(8,128)(2,1)S(1)} collective-permute-done((bf16[512,128]{1,0:T(8,128)(2,1)S(1)}, bf16[512,128]{1,0:T(8,128)(2,1)S(1)}, u32[]{:S(2)}, u32[]{:S(2)}) %collective-permute-start.20) | collective-permute-done | bytes 131104 | tf_op jit(solution)/shard_map/ppermute | solution.py:282
  49.0 1.6 %collective-permute-start.22 = (bf16[512,128]{1,0:T(8,128)(2,1)S(1)}, bf16[512,128]{1,0:T(8,128)(2,1)S(1)}, u32[]{:S(2)}, u32[]{:S(2)}) collective-permute-start(bf16[512,128]{1,0:T(8,128)(2,1)S(1)} %get-tuple-element.42.now_ref.refs_4_.rest_3_), channel_id=1, source_target_pairs={{0,1},{1,2},{2,3},{3,4},{4,5},{5,6},{6,7},{7,0},{8,15},{9,8},{10,9... | collective-permute-start | bytes 393224 | tf_op jit(solution)/shard_map/ppermute | solution.py:293
  51.1 0.6 shard_map.88.early_ref
  51.6 5.5 %collective-permute-done.22.first_ref.rest_1_ = bf16[512,128]{1,0:T(8,128)(2,1)S(1)} collective-permute-done((bf16[512,128]{1,0:T(8,128)(2,1)S(1)}, bf16[512,128]{1,0:T(8,128)(2,1)S(1)}, u32[]{:S(2)}, u32[]{:S(2)}) %collective-permute-start.22) | collective-permute-done | bytes 131104 | tf_op jit(solution)/shard_map/ppermute | solution.py:293
  58.1 1.3 %collective-permute-done.24.other_ref = bf16[512,128]{1,0:T(8,128)(2,1)S(1)} collective-permute-done((bf16[512,128]{1,0:T(8,128)(2,1)S(1)}, bf16[512,128]{1,0:T(8,128)(2,1)S(1)}, u32[]{:S(2)}, u32[]{:S(2)}) %collective-permute-start.24) | collective-permute-done | bytes 131104 | tf_op jit(solution)/shard_map/ppermute | solution.py:282
  59.7 1.4 %collective-permute-start.28 = (bf16[512,128]{1,0:T(8,128)(2,1)S(1)}, bf16[512,128]{1,0:T(8,128)(2,1)S(1)}, u32[]{:S(2)}, u32[]{:S(2)}) collective-permute-start(bf16[512,128]{1,0:T(8,128)(2,1)S(1)} %get-tuple-element.44.refs_5_.rest_3_.now_ref), channel_id=1, source_target_pairs={{0,1},{1,2},{2,3},{3,4},{4,5},{5,6},{6,7},{7,0},{8,15},{9,8},{10,9... | collective-permute-start | bytes 393224 | tf_op jit(solution)/shard_map/ppermute | solution.py:293
  61.2 0.6 shard_map.99.early_ref
  61.8 3.5 %collective-permute-done.25.refs_6_.now_ref.rest_0_ = bf16[512,128]{1,0:T(8,128)(2,1)S(1)} collective-permute-done((bf16[512,128]{1,0:T(8,128)(2,1)S(1)}, bf16[512,128]{1,0:T(8,128)(2,1)S(1)}, u32[]{:S(2)}, u32[]{:S(2)}) %collective-permute-start.25) | collective-permute-done | bytes 131104 | tf_op jit(solution)/shard_map/ppermute | solution.py:285
  65.8 1.7 %collective-permute-done.28.rest_1_.first_ref.block_ref = bf16[512,128]{1,0:T(8,128)(2,1)S(1)} collective-permute-done((bf16[512,128]{1,0:T(8,128)(2,1)S(1)}, bf16[512,128]{1,0:T(8,128)(2,1)S(1)}, u32[]{:S(2)}, u32[]{:S(2)}) %collective-permute-start.28) | collective-permute-done | bytes 131104 | tf_op jit(solution)/shard_map/ppermute | solution.py:293
  68.5 2.6 %collective-permute-start.30 = (bf16[512,128]{1,0:T(8,128)(2,1)S(1)}, bf16[512,128]{1,0:T(8,128)(2,1)S(1)}, u32[]{:S(2)}, u32[]{:S(2)}) collective-permute-start(bf16[512,128]{1,0:T(8,128)(2,1)S(1)} %get-tuple-element.47), channel_id=1, source_target_pairs={{0,16},{1,17},{2,18},{3,19},{4,20},{5,21},{6,22},{7,23},{8,24},{9,... | collective-permute-start | bytes 393224 | tf_op jit(solution)/shard_map/ppermute | solution.py:285
  72.4 0.6 shard_map.93.early_ref
  74.9 1.0 %shard_map.92 = (bf16[6,512,128]{2,1,0:T(8,128)(2,1)}, f32[8,128]{1,0:T(8,128)S(1)}) custom-call(bf16[512,128]{1,0:T(8,128)(2,1)S(1)} %shard_map.69.now_ref.rest_3_.refs_0_, bf16[512,128]{1,0:T(8,128)(2,1)S(1)} %get-tuple-element.35.now_ref.rest_3_.refs_1_, bf16[512,128]{1,0:T(8,128)(2,1)S(1)} %get-tuple-element.38.now_ref.rest_3_.refs_2_, ...), custom_call_target="tpu_custom_call" | custom-call | bytes 1048576 | tf_op jit(solution)/shard_map/pallas_call | solution.py:38
  76.0 0.8 %shard_map.108 = f32[512,128]{1,0:T(8,128)} custom-call(f32[512,128]{1,0:T(8,128)S(1)} %get-tuple-element.48.refs_0_, bf16[512,128]{1,0:T(8,128)(2,1)S(1)} %collective-permute-done.31.refs_1_, f32[512,128]{1,0:T(8,128)S(1)} %shard_map.107.refs_2_, f32[8,128]{1,0:T(8,128)S(1)} %get-tuple-element.53.refs_3_), custom_call_target="tpu_custom_call" | custom-call | bytes 1048576 | tf_op jit(solution)/shard_map/pallas_call | solution.py:38
  (83 shorter events, 12.9 us)
Async XLA Ops:
  0.7 4.0 %collective-permute-start = (f32[512,128]{1,0:T(8,128)}, f32[512,128]{1,0:T(8,128)S(1)}, u32[]{:S(2)}, u32[]{:S(2)}) collective-permute-start(f32[512,128]{1,0:T(8,128)} %bitcast.4), channel_id=1, source_target_pairs={{0,8},{1,9},{2,10},{3,11},{4,12},{5,13},{6,14},{7,15},{8,0},{9,1},... | collective-permute-start | bytes 786440 | tf_op jit(solution)/shard_map/ppermute | solution.py:282
  3.6 4.0 %collective-permute-start.1 = (bf16[128,1024]{1,0:T(8,128)(2,1)S(1)}, bf16[128,1024]{1,0:T(8,128)(2,1)S(1)}, u32[]{:S(2)}, u32[]{:S(2)}) collective-permute-start(bf16[128,1024]{1,0:T(8,128)(2,1)S(1)} %get-tuple-element.29), channel_id=1, source_target_pairs={{0,8},{1,9},{2,10},{3,11},{4,12},{5,13},{6,14},{7,15},{8,0},{9,1},... | collective-permute-start | bytes 786440 | tf_op jit(solution)/shard_map/ppermute | solution.py:282
  3.8 5.4 %collective-permute-start.2 = (bf16[128,1024]{1,0:T(8,128)(2,1)S(1)}, bf16[128,1024]{1,0:T(8,128)(2,1)S(1)}, u32[]{:S(2)}, u32[]{:S(2)}) collective-permute-start(bf16[128,1024]{1,0:T(8,128)(2,1)S(1)} %get-tuple-element.30), channel_id=1, source_target_pairs={{0,8},{1,9},{2,10},{3,11},{4,12},{5,13},{6,14},{7,15},{8,0},{9,1},... | collective-permute-start | bytes 786440 | tf_op jit(solution)/shard_map/ppermute | solution.py:282
  4.2 5.3 %collective-permute-start.3 = (bf16[128,1024]{1,0:T(8,128)(2,1)S(1)}, bf16[128,1024]{1,0:T(8,128)(2,1)S(1)}, u32[]{:S(2)}, u32[]{:S(2)}) collective-permute-start(bf16[128,1024]{1,0:T(8,128)(2,1)S(1)} %get-tuple-element.31), channel_id=1, source_target_pairs={{0,8},{1,9},{2,10},{3,11},{4,12},{5,13},{6,14},{7,15},{8,0},{9,1},... | collective-permute-start | bytes 786440 | tf_op jit(solution)/shard_map/ppermute | solution.py:282
  4.3 5.2 %collective-permute-start.4 = (bf16[128,1024]{1,0:T(8,128)(2,1)S(1)}, bf16[128,1024]{1,0:T(8,128)(2,1)S(1)}, u32[]{:S(2)}, u32[]{:S(2)}) collective-permute-start(bf16[128,1024]{1,0:T(8,128)(2,1)S(1)} %get-tuple-element.32), channel_id=1, source_target_pairs={{0,8},{1,9},{2,10},{3,11},{4,12},{5,13},{6,14},{7,15},{8,0},{9,1},... | collective-permute-start | bytes 786440 | tf_op jit(solution)/shard_map/ppermute | solution.py:282
  4.9 9.9 %collective-permute-start.6 = (bf16[512,128]{1,0:T(8,128)(2,1)S(1)}, bf16[512,128]{1,0:T(8,128)(2,1)S(1)}, u32[]{:S(2)}, u32[]{:S(2)}) collective-permute-start(bf16[512,128]{1,0:T(8,128)(2,1)S(1)} %shard_map.69.now_ref.rest_3_.refs_0_), channel_id=1, source_target_pairs={{0,1},{1,2},{2,3},{3,4},{4,5},{5,6},{6,7},{7,0},{8,15},{9,8},{10,9... | collective-permute-start | bytes 393224 | tf_op jit(solution)/shard_map/ppermute | solution.py:293
  7.6 8.2 %collective-permute-start.5 = (bf16[512,128]{1,0:T(8,128)(2,1)S(1)}, bf16[512,128]{1,0:T(8,128)(2,1)S(1)}, u32[]{:S(2)}, u32[]{:S(2)}) collective-permute-start(bf16[512,128]{1,0:T(8,128)(2,1)S(1)} %shard_map.69.now_ref.rest_3_.refs_0_), channel_id=1, source_target_pairs={{0,2},{1,3},{2,4},{3,5},{4,6},{5,7},{6,0},{7,1},{8,14},{9,15},{10,... | collective-permute-start | bytes 393224 | tf_op jit(solution)/shard_map/ppermute | solution.py:293
  9.2 6.6 %collective-permute-start.7 = (bf16[512,128]{1,0:T(8,128)(2,1)S(1)}, bf16[512,128]{1,0:T(8,128)(2,1)S(1)}, u32[]{:S(2)}, u32[]{:S(2)}) collective-permute-start(bf16[512,128]{1,0:T(8,128)(2,1)S(1)} %shard_map.69.now_ref.rest_3_.refs_0_), channel_id=1, source_target_pairs={{0,16},{1,17},{2,18},{3,19},{4,20},{5,21},{6,22},{7,23},{8,24},{9,... | collective-permute-start | bytes 393224 | tf_op jit(solution)/shard_map/ppermute | solution.py:285
  16.1 1.4 %collective-permute-start.8 = (bf16[512,128]{1,0:T(8,128)(2,1)S(1)}, bf16[512,128]{1,0:T(8,128)(2,1)S(1)}, u32[]{:S(2)}, u32[]{:S(2)}) collective-permute-start(bf16[512,128]{1,0:T(8,128)(2,1)S(1)} %shard_map.74.mine_ref), channel_id=1, source_target_pairs={{0,8},{1,9},{2,10},{3,11},{4,12},{5,13},{6,14},{7,15},{8,0},{9,1},... | collective-permute-start | bytes 393224 | tf_op jit(solution)/shard_map/ppermute | solution.py:282
  17.7 8.4 %collective-permute-start.11 = (bf16[512,128]{1,0:T(8,128)(2,1)S(1)}, bf16[512,128]{1,0:T(8,128)(2,1)S(1)}, u32[]{:S(2)}, u32[]{:S(2)}) collective-permute-start(bf16[512,128]{1,0:T(8,128)(2,1)S(1)} %get-tuple-element.35.now_ref.rest_3_.refs_1_), channel_id=1, source_target_pairs={{0,1},{1,2},{2,3},{3,4},{4,5},{5,6},{6,7},{7,0},{8,15},{9,8},{10,9... | collective-permute-start | bytes 393224 | tf_op jit(solution)/shard_map/ppermute | solution.py:293
  19.0 7.5 %collective-permute-start.10 = (bf16[512,128]{1,0:T(8,128)(2,1)S(1)}, bf16[512,128]{1,0:T(8,128)(2,1)S(1)}, u32[]{:S(2)}, u32[]{:S(2)}) collective-permute-start(bf16[512,128]{1,0:T(8,128)(2,1)S(1)} %get-tuple-element.35.now_ref.rest_3_.refs_1_), channel_id=1, source_target_pairs={{0,2},{1,3},{2,4},{3,5},{4,6},{5,7},{6,0},{7,1},{8,14},{9,15},{10,... | collective-permute-start | bytes 393224 | tf_op jit(solution)/shard_map/ppermute | solution.py:293
  19.2 7.2 %collective-permute-start.9 = (bf16[512,128]{1,0:T(8,128)(2,1)S(1)}, bf16[512,128]{1,0:T(8,128)(2,1)S(1)}, u32[]{:S(2)}, u32[]{:S(2)}) collective-permute-start(bf16[512,128]{1,0:T(8,128)(2,1)S(1)} %get-tuple-element.36), channel_id=1, source_target_pairs={{0,16},{1,17},{2,18},{3,19},{4,20},{5,21},{6,22},{7,23},{8,24},{9,... | collective-permute-start | bytes 393224 | tf_op jit(solution)/shard_map/ppermute | solution.py:285
  26.8 1.4 %collective-permute-start.12 = (bf16[512,128]{1,0:T(8,128)(2,1)S(1)}, bf16[512,128]{1,0:T(8,128)(2,1)S(1)}, u32[]{:S(2)}, u32[]{:S(2)}) collective-permute-start(bf16[512,128]{1,0:T(8,128)(2,1)S(1)} %shard_map.78.mine_ref), channel_id=1, source_target_pairs={{0,8},{1,9},{2,10},{3,11},{4,12},{5,13},{6,14},{7,15},{8,0},{9,1},... | collective-permute-start | bytes 393224 | tf_op jit(solution)/shard_map/ppermute | solution.py:282
  28.4 7.7 %collective-permute-start.14 = (bf16[512,128]{1,0:T(8,128)(2,1)S(1)}, bf16[512,128]{1,0:T(8,128)(2,1)S(1)}, u32[]{:S(2)}, u32[]{:S(2)}) collective-permute-start(bf16[512,128]{1,0:T(8,128)(2,1)S(1)} %get-tuple-element.38.now_ref.rest_3_.refs_2_), channel_id=1, source_target_pairs={{0,1},{1,2},{2,3},{3,4},{4,5},{5,6},{6,7},{7,0},{8,15},{9,8},{10,9... | collective-permute-start | bytes 393224 | tf_op jit(solution)/shard_map/ppermute | solution.py:293
  30.1 7.0 %collective-permute-start.13 = (bf16[512,128]{1,0:T(8,128)(2,1)S(1)}, bf16[512,128]{1,0:T(8,128)(2,1)S(1)}, u32[]{:S(2)}, u32[]{:S(2)}) collective-permute-start(bf16[512,128]{1,0:T(8,128)(2,1)S(1)} %get-tuple-element.38.now_ref.rest_3_.refs_2_), channel_id=1, source_target_pairs={{0,2},{1,3},{2,4},{3,5},{4,6},{5,7},{6,0},{7,1},{8,14},{9,15},{10,... | collective-permute-start | bytes 393224 | tf_op jit(solution)/shard_map/ppermute | solution.py:293
  30.5 6.6 %collective-permute-start.15 = (bf16[512,128]{1,0:T(8,128)(2,1)S(1)}, bf16[512,128]{1,0:T(8,128)(2,1)S(1)}, u32[]{:S(2)}, u32[]{:S(2)}) collective-permute-start(bf16[512,128]{1,0:T(8,128)(2,1)S(1)} %get-tuple-element.39), channel_id=1, source_target_pairs={{0,16},{1,17},{2,18},{3,19},{4,20},{5,21},{6,22},{7,23},{8,24},{9,... | collective-permute-start | bytes 393224 | tf_op jit(solution)/shard_map/ppermute | solution.py:285
  37.4 1.4 %collective-permute-start.16 = (bf16[512,128]{1,0:T(8,128)(2,1)S(1)}, bf16[512,128]{1,0:T(8,128)(2,1)S(1)}, u32[]{:S(2)}, u32[]{:S(2)}) collective-permute-start(bf16[512,128]{1,0:T(8,128)(2,1)S(1)} %shard_map.82.mine_ref), channel_id=1, source_target_pairs={{0,8},{1,9},{2,10},{3,11},{4,12},{5,13},{6,14},{7,15},{8,0},{9,1},... | collective-permute-start | bytes 393224 | tf_op jit(solution)/shard_map/ppermute | solution.py:282
  39.0 7.7 %collective-permute-start.18 = (bf16[512,128]{1,0:T(8,128)(2,1)S(1)}, bf16[512,128]{1,0:T(8,128)(2,1)S(1)}, u32[]{:S(2)}, u32[]{:S(2)}) collective-permute-start(bf16[512,128]{1,0:T(8,128)(2,1)S(1)} %get-tuple-element.40.now_ref.rest_3_.refs_3_), channel_id=1, source_target_pairs={{0,1},{1,2},{2,3},{3,4},{4,5},{5,6},{6,7},{7,0},{8,15},{9,8},{10,9... | collective-permute-start | bytes 393224 | tf_op jit(solution)/shard_map/ppermute | solution.py:293
  40.0 7.1 %collective-permute-start.17 = (bf16[512,128]{1,0:T(8,128)(2,1)S(1)}, bf16[512,128]{1,0:T(8,128)(2,1)S(1)}, u32[]{:S(2)}, u32[]{:S(2)}) collective-permute-start(bf16[512,128]{1,0:T(8,128)(2,1)S(1)} %get-tuple-element.40.now_ref.rest_3_.refs_3_), channel_id=1, source_target_pairs={{0,2},{1,3},{2,4},{3,5},{4,6},{5,7},{6,0},{7,1},{8,14},{9,15},{10,... | collective-permute-start | bytes 393224 | tf_op jit(solution)/shard_map/ppermute | solution.py:293
  40.0 7.1 %collective-permute-start.19 = (bf16[512,128]{1,0:T(8,128)(2,1)S(1)}, bf16[512,128]{1,0:T(8,128)(2,1)S(1)}, u32[]{:S(2)}, u32[]{:S(2)}) collective-permute-start(bf16[512,128]{1,0:T(8,128)(2,1)S(1)} %get-tuple-element.41), channel_id=1, source_target_pairs={{0,16},{1,17},{2,18},{3,19},{4,20},{5,21},{6,22},{7,23},{8,24},{9,... | collective-permute-start | bytes 393224 | tf_op jit(solution)/shard_map/ppermute | solution.py:285
  47.4 1.4 %collective-permute-start.20 = (bf16[512,128]{1,0:T(8,128)(2,1)S(1)}, bf16[512,128]{1,0:T(8,128)(2,1)S(1)}, u32[]{:S(2)}, u32[]{:S(2)}) collective-permute-start(bf16[512,128]{1,0:T(8,128)(2,1)S(1)} %shard_map.86.mine_ref), channel_id=1, source_target_pairs={{0,8},{1,9},{2,10},{3,11},{4,12},{5,13},{6,14},{7,15},{8,0},{9,1},... | collective-permute-start | bytes 393224 | tf_op jit(solution)/shard_map/ppermute | solution.py:282
  49.0 8.1 %collective-permute-start.22 = (bf16[512,128]{1,0:T(8,128)(2,1)S(1)}, bf16[512,128]{1,0:T(8,128)(2,1)S(1)}, u32[]{:S(2)}, u32[]{:S(2)}) collective-permute-start(bf16[512,128]{1,0:T(8,128)(2,1)S(1)} %get-tuple-element.42.now_ref.refs_4_.rest_3_), channel_id=1, source_target_pairs={{0,1},{1,2},{2,3},{3,4},{4,5},{5,6},{6,7},{7,0},{8,15},{9,8},{10,9... | collective-permute-start | bytes 393224 | tf_op jit(solution)/shard_map/ppermute | solution.py:293
  50.7 7.1 %collective-permute-start.21 = (bf16[512,128]{1,0:T(8,128)(2,1)S(1)}, bf16[512,128]{1,0:T(8,128)(2,1)S(1)}, u32[]{:S(2)}, u32[]{:S(2)}) collective-permute-start(bf16[512,128]{1,0:T(8,128)(2,1)S(1)} %get-tuple-element.42.now_ref.refs_4_.rest_3_), channel_id=1, source_target_pairs={{0,2},{1,3},{2,4},{3,5},{4,6},{5,7},{6,0},{7,1},{8,14},{9,15},{10,... | collective-permute-start | bytes 393224 | tf_op jit(solution)/shard_map/ppermute | solution.py:293
  51.0 6.7 %collective-permute-start.23 = (bf16[512,128]{1,0:T(8,128)(2,1)S(1)}, bf16[512,128]{1,0:T(8,128)(2,1)S(1)}, u32[]{:S(2)}, u32[]{:S(2)}) collective-permute-start(bf16[512,128]{1,0:T(8,128)(2,1)S(1)} %get-tuple-element.43), channel_id=1, source_target_pairs={{0,16},{1,17},{2,18},{3,19},{4,20},{5,21},{6,22},{7,23},{8,24},{9,... | collective-permute-start | bytes 393224 | tf_op jit(solution)/shard_map/ppermute | solution.py:285
  59.6 5.6 %collective-permute-start.25 = (bf16[512,128]{1,0:T(8,128)(2,1)S(1)}, bf16[512,128]{1,0:T(8,128)(2,1)S(1)}, u32[]{:S(2)}, u32[]{:S(2)}) collective-permute-start(bf16[512,128]{1,0:T(8,128)(2,1)S(1)} %get-tuple-element.45), channel_id=1, source_target_pairs={{0,16},{1,17},{2,18},{3,19},{4,20},{5,21},{6,22},{7,23},{8,24},{9,... | collective-permute-start | bytes 393224 | tf_op jit(solution)/shard_map/ppermute | solution.py:285
  59.7 7.7 %collective-permute-start.28 = (bf16[512,128]{1,0:T(8,128)(2,1)S(1)}, bf16[512,128]{1,0:T(8,128)(2,1)S(1)}, u32[]{:S(2)}, u32[]{:S(2)}) collective-permute-start(bf16[512,128]{1,0:T(8,128)(2,1)S(1)} %get-tuple-element.44.refs_5_.rest_3_.now_ref), channel_id=1, source_target_pairs={{0,1},{1,2},{2,3},{3,4},{4,5},{5,6},{6,7},{7,0},{8,15},{9,8},{10,9... | collective-permute-start | bytes 393224 | tf_op jit(solution)/shard_map/ppermute | solution.py:293
  61.2 7.0 %collective-permute-start.29 = (bf16[512,128]{1,0:T(8,128)(2,1)S(1)}, bf16[512,128]{1,0:T(8,128)(2,1)S(1)}, u32[]{:S(2)}, u32[]{:S(2)}) collective-permute-start(bf16[512,128]{1,0:T(8,128)(2,1)S(1)} %get-tuple-element.44.refs_5_.rest_3_.now_ref), channel_id=1, source_target_pairs={{0,2},{1,3},{2,4},{3,5},{4,6},{5,7},{6,0},{7,1},{8,14},{9,15},{10,... | collective-permute-start | bytes 393224 | tf_op jit(solution)/shard_map/ppermute | solution.py:293
  65.3 7.7 %collective-permute-start.27 = (bf16[512,128]{1,0:T(8,128)(2,1)S(1)}, bf16[512,128]{1,0:T(8,128)(2,1)S(1)}, u32[]{:S(2)}, u32[]{:S(2)}) collective-permute-start(bf16[512,128]{1,0:T(8,128)(2,1)S(1)} %collective-permute-done.25.refs_6_.now_ref.rest_0_), channel_id=1, source_target_pairs={{0,8},{1,9},{2,10},{3,11},{4,12},{5,13},{6,14},{7,15},{8,0},{9,1},... | collective-permute-start | bytes 393224 | tf_op jit(solution)/shard_map/ppermute | solution.py:293
  65.3 8.3 %collective-permute-start.26 = (bf16[512,128]{1,0:T(8,128)(2,1)S(1)}, bf16[512,128]{1,0:T(8,128)(2,1)S(1)}, u32[]{:S(2)}, u32[]{:S(2)}) collective-permute-start(bf16[512,128]{1,0:T(8,128)(2,1)S(1)} %collective-permute-done.25.refs_6_.now_ref.rest_0_), channel_id=1, source_target_pairs={{0,8},{1,9},{2,10},{3,11},{4,12},{5,13},{6,14},{7,15},{8,0},{9,1},... | collective-permute-start | bytes 393224 | tf_op jit(solution)/shard_map/ppermute | solution.py:293
  68.5 5.8 %collective-permute-start.30 = (bf16[512,128]{1,0:T(8,128)(2,1)S(1)}, bf16[512,128]{1,0:T(8,128)(2,1)S(1)}, u32[]{:S(2)}, u32[]{:S(2)}) collective-permute-start(bf16[512,128]{1,0:T(8,128)(2,1)S(1)} %get-tuple-element.47), channel_id=1, source_target_pairs={{0,16},{1,17},{2,18},{3,19},{4,20},{5,21},{6,22},{7,23},{8,24},{9,... | collective-permute-start | bytes 393224 | tf_op jit(solution)/shard_map/ppermute | solution.py:285
  72.0 3.9 %collective-permute-start.32 = (bf16[512,128]{1,0:T(8,128)(2,1)S(1)}, bf16[512,128]{1,0:T(8,128)(2,1)S(1)}, u32[]{:S(2)}, u32[]{:S(2)}) collective-permute-start(bf16[512,128]{1,0:T(8,128)(2,1)S(1)} %get-tuple-element.52), channel_id=1, source_target_pairs={{0,8},{1,9},{2,10},{3,11},{4,12},{5,13},{6,14},{7,15},{8,0},{9,1},... | collective-permute-start | bytes 393224 | tf_op jit(solution)/shard_map/ppermute | solution.py:282
  74.3 1.6 %collective-permute-start.31 = (bf16[512,128]{1,0:T(8,128)(2,1)S(1)}, bf16[512,128]{1,0:T(8,128)(2,1)S(1)}, u32[]{:S(2)}, u32[]{:S(2)}) collective-permute-start(bf16[512,128]{1,0:T(8,128)(2,1)S(1)} %get-tuple-element.49), channel_id=1, source_target_pairs={{0,8},{1,9},{2,10},{3,11},{4,12},{5,13},{6,14},{7,15},{8,0},{9,1},... | collective-permute-start | bytes 393224 | tf_op jit(solution)/shard_map/ppermute | solution.py:282
  (5 other events, 14.4 us)

commit v10 on v9

--- a/solution.py
+++ b/solution.py
@@ -43,6 +43,20 @@
         cost_estimate=COST,
         compiler_params=pltpu.CompilerParams(vmem_limit_bytes=8 * MIB),
     )(*args)
+
+
+def only(lowest, highest, outs, body, *refs):
+    _, pair = place()
+    wanted = jnp.logical_and(pair >= lowest, pair <= highest)
+
+    @pl.when(wanted)
+    def _():
+        body(*refs)
+
+    @pl.when(jnp.logical_not(wanted))
+    def _():
+        for ref in refs[len(refs) - outs :]:
+            ref[...] = jnp.zeros_like(ref)
 
 
 def put_back(body, in_front, moved, *refs):
@@ -326,8 +340,14 @@
         else:
             current_in, field_in = pair_moved(current, 1), pair_moved(field, -1)
         last = [far, *previous] if previous else []
-        (early,) = call(early_body, [field_shape], [own, current] + last)
-        (partly,) = call(first_body, [field_shape], [near, first, early])
+        ending = max(step - (steps - 1), 0)
+        going_on = functools.partial(only, ending, pairs)
+        (early,) = call(
+            functools.partial(going_on, 1, early_body), [field_shape], [own, current] + last
+        )
+        (partly,) = call(
+            functools.partial(going_on, 1, first_body), [field_shape], [near, first, early]
+        )
         received = [near, second, partly]
         past = [history[0], other_history] if step < pairs else []
         previous = [first, second, current]
@@ -349,14 +369,19 @@
                 windows = halo(current_in, 1, done), halo(current_in, 2, done)
             more = step < rounds - 1
             even, *next_field = call(
-                functools.partial(even_body, step, pairs),
+                functools.partial(going_on, 1 + more, functools.partial(even_body, step, pairs)),
                 [field_shape] + [current_shape] * more,
                 received + ([field_in] + past) * more,
             )
-            (odd_early,) = call(odd_early_body, [field_shape], [own, current])
+            alone = functools.partial(only, ending, ending, 1)
+            (odd_early,) = call(
+                functools.partial(alone, odd_early_body), [field_shape], [own, current]
+            )
             for which, block in enumerate((first, second)):
                 (odd_early,) = call(
-                    functools.partial(odd_body, which), [field_shape], [far, block, odd_early]
+                    functools.partial(alone, functools.partial(odd_body, which)),
+                    [field_shape],
+                    [far, block, odd_early],
                 )
             mine, send = call(
                 functools.partial(share_body, step, steps),

time: 76.9 us -> 76.4 us (level)
  Pallas kernels: 14.8 us -> 12.9 us
  waiting for transfers between devices: 41.9 us -> 43.7 us
    pallas_call x40, Pallas kernels: 13 us -> 11.2 us  [call(): pl.pallas_call(body, out_shape=tuple(outs), in_specs=specs, out_specs=tup...]
    ppermute x7, waiting for transfers between devices: 3.52 us -> 5.09 us  [pair_moved(): lax.ppermute(value, AXES, everyone(lambda d, s: ((d + 2 * hop) % lags, s)))]
  transfers between devices with their start and end apart: 33 -> 33, of which waited for: 17 -> 19; matrix products, arithmetic and copies ran while one was open for 0% -> 0% of each run, Pallas kernels for 15% -> 13%
where the time goes in v10:
time: 76.4 us; the launch traced here: 76.3 us
  waiting for transfers between devices  43.7 us (57%)
  starting transfers between devices  17.8 us (23%)
  Pallas kernels  12.9 us (17%)
  between operations  1.09 us (1%)
    ppermute x14, waiting for transfers between devices, halo(): return lax.ppermute(value, AXES, everyone(move))  31.8 us
    ppermute x14, starting transfers between devices, halo(): return lax.ppermute(value, AXES, everyone(move))  12.9 us
    pallas_call x40, Pallas kernels, call(): pl.pallas_call(body, out_shape=tuple(outs), in_specs=specs, out_specs=tup...  11.2 us
    ppermute x12, waiting for transfers between devices, swapped(): return lax.ppermute(value, AXES, everyone(lambda d, s: (d ^ 1, s)))  6.85 us
    ppermute x7, waiting for transfers between devices, pair_moved(): lax.ppermute(value, AXES, everyone(lambda d, s: ((d + 2 * hop) % lags, s)))  5.09 us
    ppermute x7, starting transfers between devices, pair_moved(): lax.ppermute(value, AXES, everyone(lambda d, s: ((d + 2 * hop) % lags, s)))  2.7 us
    ppermute x12, starting transfers between devices, swapped(): return lax.ppermute(value, AXES, everyone(lambda d, s: (d ^ 1, s)))  2.21 us
    pallas_call x1, Pallas kernels, spread(): pl.pallas_call(functools.partial(spread_body, groups), out_shape=(matrix(...  1.74 us
  transfers between devices with their start and end apart: 33, of which 19 were waited for; matrix products, arithmetic and copies ran while one was open for 0% of the time, Pallas kernels for 13%

profile of v10, /device:TPU:0, one launch (start us, length us, event | category | flops | bytes accessed | tf_op | source)
XLA Modules:
  0.0 76.3 jit_solution(2666920868918821052)
XLA Ops:
  1.2 0.7 copy-done.3
  1.9 1.7 %shard_map.70 = (bf16[512,1024]{1,0:T(8,128)(2,1)S(1)}, bf16[512,512]{1,0:T(8,128)(2,1)S(1)}, bf16[128,1024]{1,0:T(8,128)(2,1)S(1)}, bf16[128,1024]{1,0:T(8,128)...) custom-call(s32[4,16]{1,0:T(4,128)S(1)} %bitcast.8, bf16[4,16,128,128]{3,2,1,0:T(8,128)(2,1)} %bitcast.9), custom_call_target="tpu_custom_call" | custom-call | bytes 1048576 | tf_op jit(solution)/shard_map/pallas_call | solution.py:113
  4.9 2.7 %collective-permute-start.6 = (bf16[512,128]{1,0:T(8,128)(2,1)S(1)}, bf16[512,128]{1,0:T(8,128)(2,1)S(1)}, u32[]{:S(2)}, u32[]{:S(2)}) collective-permute-start(bf16[512,128]{1,0:T(8,128)(2,1)S(1)} %shard_map.69.refs_1_.refs_5_.refs_0_), channel_id=1, source_target_pairs={{0,1},{1,2},{2,3},{3,4},{4,5},{5,6},{6,7},{7,0},{8,15},{9,8},{10,9... | collective-permute-start | bytes 393224 | tf_op jit(solution)/shard_map/ppermute | solution.py:307
  7.6 1.6 %collective-permute-start.5 = (bf16[512,128]{1,0:T(8,128)(2,1)S(1)}, bf16[512,128]{1,0:T(8,128)(2,1)S(1)}, u32[]{:S(2)}, u32[]{:S(2)}) collective-permute-start(bf16[512,128]{1,0:T(8,128)(2,1)S(1)} %shard_map.69.refs_1_.refs_5_.refs_0_), channel_id=1, source_target_pairs={{0,2},{1,3},{2,4},{3,5},{4,6},{5,7},{6,0},{7,1},{8,14},{9,15},{10,... | collective-permute-start | bytes 393224 | tf_op jit(solution)/shard_map/ppermute | solution.py:307
  9.7 5.2 %collective-permute-done.6.refs_1_.refs_3_ = bf16[512,128]{1,0:T(8,128)(2,1)S(1)} collective-permute-done((bf16[512,128]{1,0:T(8,128)(2,1)S(1)}, bf16[512,128]{1,0:T(8,128)(2,1)S(1)}, u32[]{:S(2)}, u32[]{:S(2)}) %collective-permute-start.6) | collective-permute-done | bytes 131104 | tf_op jit(solution)/shard_map/ppermute | solution.py:307
  15.2 0.6 collective-permute-done.5.second_ref.refs_4_
  16.2 1.2 %collective-permute-done.8.other_ref = bf16[512,128]{1,0:T(8,128)(2,1)S(1)} collective-permute-done((bf16[512,128]{1,0:T(8,128)(2,1)S(1)}, bf16[512,128]{1,0:T(8,128)(2,1)S(1)}, u32[]{:S(2)}, u32[]{:S(2)}) %collective-permute-start.8) | collective-permute-done | bytes 131104 | tf_op jit(solution)/shard_map/ppermute | solution.py:296
  17.7 1.3 %collective-permute-start.11 = (bf16[512,128]{1,0:T(8,128)(2,1)S(1)}, bf16[512,128]{1,0:T(8,128)(2,1)S(1)}, u32[]{:S(2)}, u32[]{:S(2)}) collective-permute-start(bf16[512,128]{1,0:T(8,128)(2,1)S(1)} %get-tuple-element.35.refs_1_.refs_5_), channel_id=1, source_target_pairs={{0,1},{1,2},{2,3},{3,4},{4,5},{5,6},{6,7},{7,0},{8,15},{9,8},{10,9... | collective-permute-start | bytes 393224 | tf_op jit(solution)/shard_map/ppermute | solution.py:307
  19.2 0.6 shard_map.76.refs_2_
  19.8 6.3 %collective-permute-done.11.refs_1_.refs_3_ = bf16[512,128]{1,0:T(8,128)(2,1)S(1)} collective-permute-done((bf16[512,128]{1,0:T(8,128)(2,1)S(1)}, bf16[512,128]{1,0:T(8,128)(2,1)S(1)}, u32[]{:S(2)}, u32[]{:S(2)}) %collective-permute-start.11) | collective-permute-done | bytes 131104 | tf_op jit(solution)/shard_map/ppermute | solution.py:307
  26.8 1.3 %collective-permute-done.12.other_ref = bf16[512,128]{1,0:T(8,128)(2,1)S(1)} collective-permute-done((bf16[512,128]{1,0:T(8,128)(2,1)S(1)}, bf16[512,128]{1,0:T(8,128)(2,1)S(1)}, u32[]{:S(2)}, u32[]{:S(2)}) %collective-permute-start.12) | collective-permute-done | bytes 131104 | tf_op jit(solution)/shard_map/ppermute | solution.py:296
  28.4 1.7 %collective-permute-start.14 = (bf16[512,128]{1,0:T(8,128)(2,1)S(1)}, bf16[512,128]{1,0:T(8,128)(2,1)S(1)}, u32[]{:S(2)}, u32[]{:S(2)}) collective-permute-start(bf16[512,128]{1,0:T(8,128)(2,1)S(1)} %get-tuple-element.38.refs_1_.refs_5_.refs_2_), channel_id=1, source_target_pairs={{0,1},{1,2},{2,3},{3,4},{4,5},{5,6},{6,7},{7,0},{8,15},{9,8},{10,9... | collective-permute-start | bytes 393224 | tf_op jit(solution)/shard_map/ppermute | solution.py:307
  30.5 0.6 shard_map.80.refs_2_
  31.1 5.0 %collective-permute-done.14.refs_1_.refs_3_ = bf16[512,128]{1,0:T(8,128)(2,1)S(1)} collective-permute-done((bf16[512,128]{1,0:T(8,128)(2,1)S(1)}, bf16[512,128]{1,0:T(8,128)(2,1)S(1)}, u32[]{:S(2)}, u32[]{:S(2)}) %collective-permute-start.14) | collective-permute-done | bytes 131104 | tf_op jit(solution)/shard_map/ppermute | solution.py:307
  36.4 0.7 collective-permute-done.13.second_ref.refs_4_
  37.5 1.3 %collective-permute-done.16.other_ref = bf16[512,128]{1,0:T(8,128)(2,1)S(1)} collective-permute-done((bf16[512,128]{1,0:T(8,128)(2,1)S(1)}, bf16[512,128]{1,0:T(8,128)(2,1)S(1)}, u32[]{:S(2)}, u32[]{:S(2)}) %collective-permute-start.16) | collective-permute-done | bytes 131104 | tf_op jit(solution)/shard_map/ppermute | solution.py:296
  39.0 1.0 %collective-permute-start.18 = (bf16[512,128]{1,0:T(8,128)(2,1)S(1)}, bf16[512,128]{1,0:T(8,128)(2,1)S(1)}, u32[]{:S(2)}, u32[]{:S(2)}) collective-permute-start(bf16[512,128]{1,0:T(8,128)(2,1)S(1)} %get-tuple-element.40.refs_1_.refs_5_.refs_3_), channel_id=1, source_target_pairs={{0,1},{1,2},{2,3},{3,4},{4,5},{5,6},{6,7},{7,0},{8,15},{9,8},{10,9... | collective-permute-start | bytes 393224 | tf_op jit(solution)/shard_map/ppermute | solution.py:307
  40.0 0.6 shard_map.84.refs_2_
  40.6 6.1 %collective-permute-done.18.refs_1_.refs_3_ = bf16[512,128]{1,0:T(8,128)(2,1)S(1)} collective-permute-done((bf16[512,128]{1,0:T(8,128)(2,1)S(1)}, bf16[512,128]{1,0:T(8,128)(2,1)S(1)}, u32[]{:S(2)}, u32[]{:S(2)}) %collective-permute-start.18) | collective-permute-done | bytes 131104 | tf_op jit(solution)/shard_map/ppermute | solution.py:307
  47.5 1.3 %collective-permute-done.20.other_ref = bf16[512,128]{1,0:T(8,128)(2,1)S(1)} collective-permute-done((bf16[512,128]{1,0:T(8,128)(2,1)S(1)}, bf16[512,128]{1,0:T(8,128)(2,1)S(1)}, u32[]{:S(2)}, u32[]{:S(2)}) %collective-permute-start.20) | collective-permute-done | bytes 131104 | tf_op jit(solution)/shard_map/ppermute | solution.py:296
  49.0 1.6 %collective-permute-start.22 = (bf16[512,128]{1,0:T(8,128)(2,1)S(1)}, bf16[512,128]{1,0:T(8,128)(2,1)S(1)}, u32[]{:S(2)}, u32[]{:S(2)}) collective-permute-start(bf16[512,128]{1,0:T(8,128)(2,1)S(1)} %get-tuple-element.42.refs_1_.refs_4_.refs_5_), channel_id=1, source_target_pairs={{0,1},{1,2},{2,3},{3,4},{4,5},{5,6},{6,7},{7,0},{8,15},{9,8},{10,9... | collective-permute-start | bytes 393224 | tf_op jit(solution)/shard_map/ppermute | solution.py:307
  51.1 0.6 shard_map.88.refs_2_
  51.6 5.5 %collective-permute-done.22.refs_1_.refs_3_ = bf16[512,128]{1,0:T(8,128)(2,1)S(1)} collective-permute-done((bf16[512,128]{1,0:T(8,128)(2,1)S(1)}, bf16[512,128]{1,0:T(8,128)(2,1)S(1)}, u32[]{:S(2)}, u32[]{:S(2)}) %collective-permute-start.22) | collective-permute-done | bytes 131104 | tf_op jit(solution)/shard_map/ppermute | solution.py:307
  58.1 1.3 %collective-permute-done.24.other_ref = bf16[512,128]{1,0:T(8,128)(2,1)S(1)} collective-permute-done((bf16[512,128]{1,0:T(8,128)(2,1)S(1)}, bf16[512,128]{1,0:T(8,128)(2,1)S(1)}, u32[]{:S(2)}, u32[]{:S(2)}) %collective-permute-start.24) | collective-permute-done | bytes 131104 | tf_op jit(solution)/shard_map/ppermute | solution.py:296
  59.7 1.4 %collective-permute-start.28 = (bf16[512,128]{1,0:T(8,128)(2,1)S(1)}, bf16[512,128]{1,0:T(8,128)(2,1)S(1)}, u32[]{:S(2)}, u32[]{:S(2)}) collective-permute-start(bf16[512,128]{1,0:T(8,128)(2,1)S(1)} %get-tuple-element.44.refs_5_.refs_1_), channel_id=1, source_target_pairs={{0,1},{1,2},{2,3},{3,4},{4,5},{5,6},{6,7},{7,0},{8,15},{9,8},{10,9... | collective-permute-start | bytes 393224 | tf_op jit(solution)/shard_map/ppermute | solution.py:307
  61.2 0.6 shard_map.99.refs_2_
  61.8 3.5 %collective-permute-done.25.refs_6_.refs_1_.refs_3_ = bf16[512,128]{1,0:T(8,128)(2,1)S(1)} collective-permute-done((bf16[512,128]{1,0:T(8,128)(2,1)S(1)}, bf16[512,128]{1,0:T(8,128)(2,1)S(1)}, u32[]{:S(2)}, u32[]{:S(2)}) %collective-permute-start.25) | collective-permute-done | bytes 131104 | tf_op jit(solution)/shard_map/ppermute | solution.py:299
  65.8 1.7 %collective-permute-done.28.refs_3_.refs_1_ = bf16[512,128]{1,0:T(8,128)(2,1)S(1)} collective-permute-done((bf16[512,128]{1,0:T(8,128)(2,1)S(1)}, bf16[512,128]{1,0:T(8,128)(2,1)S(1)}, u32[]{:S(2)}, u32[]{:S(2)}) %collective-permute-start.28) | collective-permute-done | bytes 131104 | tf_op jit(solution)/shard_map/ppermute | solution.py:307
  68.4 2.6 %collective-permute-start.30 = (bf16[512,128]{1,0:T(8,128)(2,1)S(1)}, bf16[512,128]{1,0:T(8,128)(2,1)S(1)}, u32[]{:S(2)}, u32[]{:S(2)}) collective-permute-start(bf16[512,128]{1,0:T(8,128)(2,1)S(1)} %get-tuple-element.47), channel_id=1, source_target_pairs={{0,16},{1,17},{2,18},{3,19},{4,20},{5,21},{6,22},{7,23},{8,24},{9,... | collective-permute-start | bytes 393224 | tf_op jit(solution)/shard_map/ppermute | solution.py:299
  72.4 1.6 %collective-permute-done.30.rest_0_ = bf16[512,128]{1,0:T(8,128)(2,1)S(1)} collective-permute-done((bf16[512,128]{1,0:T(8,128)(2,1)S(1)}, bf16[512,128]{1,0:T(8,128)(2,1)S(1)}, u32[]{:S(2)}, u32[]{:S(2)}) %collective-permute-start.30) | collective-permute-done | bytes 131104 | tf_op jit(solution)/shard_map/ppermute | solution.py:299
  74.2 1.0 %shard_map.92 = (bf16[6,512,128]{2,1,0:T(8,128)(2,1)}, f32[8,128]{1,0:T(8,128)S(1)}) custom-call(bf16[512,128]{1,0:T(8,128)(2,1)S(1)} %shard_map.69.refs_1_.refs_5_.refs_0_, bf16[512,128]{1,0:T(8,128)(2,1)S(1)} %get-tuple-element.35.refs_1_.refs_5_, bf16[512,128]{1,0:T(8,128)(2,1)S(1)} %get-tuple-element.38.refs_1_.refs_5_.refs_2_, ...), custom_call_target="tpu_custom_call" | custom-call | bytes 1048576 | tf_op jit(solution)/shard_map/pallas_call | solution.py:38
  75.5 0.8 %shard_map.108 = f32[512,128]{1,0:T(8,128)} custom-call(f32[512,128]{1,0:T(8,128)S(1)} %get-tuple-element.48.refs_0_, bf16[512,128]{1,0:T(8,128)(2,1)S(1)} %collective-permute-done.31.refs_1_, f32[512,128]{1,0:T(8,128)S(1)} %shard_map.107.refs_2_, f32[8,128]{1,0:T(8,128)S(1)} %get-tuple-element.53.refs_3_), custom_call_target="tpu_custom_call" | custom-call | bytes 1048576 | tf_op jit(solution)/shard_map/pallas_call | solution.py:38
  (83 shorter events, 11.5 us)
Async XLA Ops:
  0.7 4.0 %collective-permute-start = (f32[512,128]{1,0:T(8,128)}, f32[512,128]{1,0:T(8,128)S(1)}, u32[]{:S(2)}, u32[]{:S(2)}) collective-permute-start(f32[512,128]{1,0:T(8,128)} %bitcast.4), channel_id=1, source_target_pairs={{0,8},{1,9},{2,10},{3,11},{4,12},{5,13},{6,14},{7,15},{8,0},{9,1},... | collective-permute-start | bytes 786440 | tf_op jit(solution)/shard_map/ppermute | solution.py:296
  3.6 4.0 %collective-permute-start.1 = (bf16[128,1024]{1,0:T(8,128)(2,1)S(1)}, bf16[128,1024]{1,0:T(8,128)(2,1)S(1)}, u32[]{:S(2)}, u32[]{:S(2)}) collective-permute-start(bf16[128,1024]{1,0:T(8,128)(2,1)S(1)} %get-tuple-element.29), channel_id=1, source_target_pairs={{0,8},{1,9},{2,10},{3,11},{4,12},{5,13},{6,14},{7,15},{8,0},{9,1},... | collective-permute-start | bytes 786440 | tf_op jit(solution)/shard_map/ppermute | solution.py:296
  3.8 5.4 %collective-permute-start.2 = (bf16[128,1024]{1,0:T(8,128)(2,1)S(1)}, bf16[128,1024]{1,0:T(8,128)(2,1)S(1)}, u32[]{:S(2)}, u32[]{:S(2)}) collective-permute-start(bf16[128,1024]{1,0:T(8,128)(2,1)S(1)} %get-tuple-element.30), channel_id=1, source_target_pairs={{0,8},{1,9},{2,10},{3,11},{4,12},{5,13},{6,14},{7,15},{8,0},{9,1},... | collective-permute-start | bytes 786440 | tf_op jit(solution)/shard_map/ppermute | solution.py:296
  4.2 5.3 %collective-permute-start.3 = (bf16[128,1024]{1,0:T(8,128)(2,1)S(1)}, bf16[128,1024]{1,0:T(8,128)(2,1)S(1)}, u32[]{:S(2)}, u32[]{:S(2)}) collective-permute-start(bf16[128,1024]{1,0:T(8,128)(2,1)S(1)} %get-tuple-element.31), channel_id=1, source_target_pairs={{0,8},{1,9},{2,10},{3,11},{4,12},{5,13},{6,14},{7,15},{8,0},{9,1},... | collective-permute-start | bytes 786440 | tf_op jit(solution)/shard_map/ppermute | solution.py:296
  4.3 5.2 %collective-permute-start.4 = (bf16[128,1024]{1,0:T(8,128)(2,1)S(1)}, bf16[128,1024]{1,0:T(8,128)(2,1)S(1)}, u32[]{:S(2)}, u32[]{:S(2)}) collective-permute-start(bf16[128,1024]{1,0:T(8,128)(2,1)S(1)} %get-tuple-element.32), channel_id=1, source_target_pairs={{0,8},{1,9},{2,10},{3,11},{4,12},{5,13},{6,14},{7,15},{8,0},{9,1},... | collective-permute-start | bytes 786440 | tf_op jit(solution)/shard_map/ppermute | solution.py:296
  4.9 9.9 %collective-permute-start.6 = (bf16[512,128]{1,0:T(8,128)(2,1)S(1)}, bf16[512,128]{1,0:T(8,128)(2,1)S(1)}, u32[]{:S(2)}, u32[]{:S(2)}) collective-permute-start(bf16[512,128]{1,0:T(8,128)(2,1)S(1)} %shard_map.69.refs_1_.refs_5_.refs_0_), channel_id=1, source_target_pairs={{0,1},{1,2},{2,3},{3,4},{4,5},{5,6},{6,7},{7,0},{8,15},{9,8},{10,9... | collective-permute-start | bytes 393224 | tf_op jit(solution)/shard_map/ppermute | solution.py:307
  7.6 8.2 %collective-permute-start.5 = (bf16[512,128]{1,0:T(8,128)(2,1)S(1)}, bf16[512,128]{1,0:T(8,128)(2,1)S(1)}, u32[]{:S(2)}, u32[]{:S(2)}) collective-permute-start(bf16[512,128]{1,0:T(8,128)(2,1)S(1)} %shard_map.69.refs_1_.refs_5_.refs_0_), channel_id=1, source_target_pairs={{0,2},{1,3},{2,4},{3,5},{4,6},{5,7},{6,0},{7,1},{8,14},{9,15},{10,... | collective-permute-start | bytes 393224 | tf_op jit(solution)/shard_map/ppermute | solution.py:307
  9.2 6.6 %collective-permute-start.7 = (bf16[512,128]{1,0:T(8,128)(2,1)S(1)}, bf16[512,128]{1,0:T(8,128)(2,1)S(1)}, u32[]{:S(2)}, u32[]{:S(2)}) collective-permute-start(bf16[512,128]{1,0:T(8,128)(2,1)S(1)} %shard_map.69.refs_1_.refs_5_.refs_0_), channel_id=1, source_target_pairs={{0,16},{1,17},{2,18},{3,19},{4,20},{5,21},{6,22},{7,23},{8,24},{9,... | collective-permute-start | bytes 393224 | tf_op jit(solution)/shard_map/ppermute | solution.py:299
  16.1 1.4 %collective-permute-start.8 = (bf16[512,128]{1,0:T(8,128)(2,1)S(1)}, bf16[512,128]{1,0:T(8,128)(2,1)S(1)}, u32[]{:S(2)}, u32[]{:S(2)}) collective-permute-start(bf16[512,128]{1,0:T(8,128)(2,1)S(1)} %shard_map.74.mine_ref), channel_id=1, source_target_pairs={{0,8},{1,9},{2,10},{3,11},{4,12},{5,13},{6,14},{7,15},{8,0},{9,1},... | collective-permute-start | bytes 393224 | tf_op jit(solution)/shard_map/ppermute | solution.py:296
  17.7 8.4 %collective-permute-start.11 = (bf16[512,128]{1,0:T(8,128)(2,1)S(1)}, bf16[512,128]{1,0:T(8,128)(2,1)S(1)}, u32[]{:S(2)}, u32[]{:S(2)}) collective-permute-start(bf16[512,128]{1,0:T(8,128)(2,1)S(1)} %get-tuple-element.35.refs_1_.refs_5_), channel_id=1, source_target_pairs={{0,1},{1,2},{2,3},{3,4},{4,5},{5,6},{6,7},{7,0},{8,15},{9,8},{10,9... | collective-permute-start | bytes 393224 | tf_op jit(solution)/shard_map/ppermute | solution.py:307
  19.0 7.5 %collective-permute-start.10 = (bf16[512,128]{1,0:T(8,128)(2,1)S(1)}, bf16[512,128]{1,0:T(8,128)(2,1)S(1)}, u32[]{:S(2)}, u32[]{:S(2)}) collective-permute-start(bf16[512,128]{1,0:T(8,128)(2,1)S(1)} %get-tuple-element.35.refs_1_.refs_5_), channel_id=1, source_target_pairs={{0,2},{1,3},{2,4},{3,5},{4,6},{5,7},{6,0},{7,1},{8,14},{9,15},{10,... | collective-permute-start | bytes 393224 | tf_op jit(solution)/shard_map/ppermute | solution.py:307
  19.2 7.2 %collective-permute-start.9 = (bf16[512,128]{1,0:T(8,128)(2,1)S(1)}, bf16[512,128]{1,0:T(8,128)(2,1)S(1)}, u32[]{:S(2)}, u32[]{:S(2)}) collective-permute-start(bf16[512,128]{1,0:T(8,128)(2,1)S(1)} %get-tuple-element.36), channel_id=1, source_target_pairs={{0,16},{1,17},{2,18},{3,19},{4,20},{5,21},{6,22},{7,23},{8,24},{9,... | collective-permute-start | bytes 393224 | tf_op jit(solution)/shard_map/ppermute | solution.py:299
  26.8 1.4 %collective-permute-start.12 = (bf16[512,128]{1,0:T(8,128)(2,1)S(1)}, bf16[512,128]{1,0:T(8,128)(2,1)S(1)}, u32[]{:S(2)}, u32[]{:S(2)}) collective-permute-start(bf16[512,128]{1,0:T(8,128)(2,1)S(1)} %shard_map.78.mine_ref), channel_id=1, source_target_pairs={{0,8},{1,9},{2,10},{3,11},{4,12},{5,13},{6,14},{7,15},{8,0},{9,1},... | collective-permute-start | bytes 393224 | tf_op jit(solution)/shard_map/ppermute | solution.py:296
  28.4 7.7 %collective-permute-start.14 = (bf16[512,128]{1,0:T(8,128)(2,1)S(1)}, bf16[512,128]{1,0:T(8,128)(2,1)S(1)}, u32[]{:S(2)}, u32[]{:S(2)}) collective-permute-start(bf16[512,128]{1,0:T(8,128)(2,1)S(1)} %get-tuple-element.38.refs_1_.refs_5_.refs_2_), channel_id=1, source_target_pairs={{0,1},{1,2},{2,3},{3,4},{4,5},{5,6},{6,7},{7,0},{8,15},{9,8},{10,9... | collective-permute-start | bytes 393224 | tf_op jit(solution)/shard_map/ppermute | solution.py:307
  30.1 7.0 %collective-permute-start.13 = (bf16[512,128]{1,0:T(8,128)(2,1)S(1)}, bf16[512,128]{1,0:T(8,128)(2,1)S(1)}, u32[]{:S(2)}, u32[]{:S(2)}) collective-permute-start(bf16[512,128]{1,0:T(8,128)(2,1)S(1)} %get-tuple-element.38.refs_1_.refs_5_.refs_2_), channel_id=1, source_target_pairs={{0,2},{1,3},{2,4},{3,5},{4,6},{5,7},{6,0},{7,1},{8,14},{9,15},{10,... | collective-permute-start | bytes 393224 | tf_op jit(solution)/shard_map/ppermute | solution.py:307
  30.5 6.6 %collective-permute-start.15 = (bf16[512,128]{1,0:T(8,128)(2,1)S(1)}, bf16[512,128]{1,0:T(8,128)(2,1)S(1)}, u32[]{:S(2)}, u32[]{:S(2)}) collective-permute-start(bf16[512,128]{1,0:T(8,128)(2,1)S(1)} %get-tuple-element.39), channel_id=1, source_target_pairs={{0,16},{1,17},{2,18},{3,19},{4,20},{5,21},{6,22},{7,23},{8,24},{9,... | collective-permute-start | bytes 393224 | tf_op jit(solution)/shard_map/ppermute | solution.py:299
  37.4 1.4 %collective-permute-start.16 = (bf16[512,128]{1,0:T(8,128)(2,1)S(1)}, bf16[512,128]{1,0:T(8,128)(2,1)S(1)}, u32[]{:S(2)}, u32[]{:S(2)}) collective-permute-start(bf16[512,128]{1,0:T(8,128)(2,1)S(1)} %shard_map.82.mine_ref), channel_id=1, source_target_pairs={{0,8},{1,9},{2,10},{3,11},{4,12},{5,13},{6,14},{7,15},{8,0},{9,1},... | collective-permute-start | bytes 393224 | tf_op jit(solution)/shard_map/ppermute | solution.py:296
  39.0 7.7 %collective-permute-start.18 = (bf16[512,128]{1,0:T(8,128)(2,1)S(1)}, bf16[512,128]{1,0:T(8,128)(2,1)S(1)}, u32[]{:S(2)}, u32[]{:S(2)}) collective-permute-start(bf16[512,128]{1,0:T(8,128)(2,1)S(1)} %get-tuple-element.40.refs_1_.refs_5_.refs_3_), channel_id=1, source_target_pairs={{0,1},{1,2},{2,3},{3,4},{4,5},{5,6},{6,7},{7,0},{8,15},{9,8},{10,9... | collective-permute-start | bytes 393224 | tf_op jit(solution)/shard_map/ppermute | solution.py:307
  40.0 7.1 %collective-permute-start.17 = (bf16[512,128]{1,0:T(8,128)(2,1)S(1)}, bf16[512,128]{1,0:T(8,128)(2,1)S(1)}, u32[]{:S(2)}, u32[]{:S(2)}) collective-permute-start(bf16[512,128]{1,0:T(8,128)(2,1)S(1)} %get-tuple-element.40.refs_1_.refs_5_.refs_3_), channel_id=1, source_target_pairs={{0,2},{1,3},{2,4},{3,5},{4,6},{5,7},{6,0},{7,1},{8,14},{9,15},{10,... | collective-permute-start | bytes 393224 | tf_op jit(solution)/shard_map/ppermute | solution.py:307
  40.0 7.1 %collective-permute-start.19 = (bf16[512,128]{1,0:T(8,128)(2,1)S(1)}, bf16[512,128]{1,0:T(8,128)(2,1)S(1)}, u32[]{:S(2)}, u32[]{:S(2)}) collective-permute-start(bf16[512,128]{1,0:T(8,128)(2,1)S(1)} %get-tuple-element.41), channel_id=1, source_target_pairs={{0,16},{1,17},{2,18},{3,19},{4,20},{5,21},{6,22},{7,23},{8,24},{9,... | collective-permute-start | bytes 393224 | tf_op jit(solution)/shard_map/ppermute | solution.py:299
  47.4 1.4 %collective-permute-start.20 = (bf16[512,128]{1,0:T(8,128)(2,1)S(1)}, bf16[512,128]{1,0:T(8,128)(2,1)S(1)}, u32[]{:S(2)}, u32[]{:S(2)}) collective-permute-start(bf16[512,128]{1,0:T(8,128)(2,1)S(1)} %shard_map.86.mine_ref), channel_id=1, source_target_pairs={{0,8},{1,9},{2,10},{3,11},{4,12},{5,13},{6,14},{7,15},{8,0},{9,1},... | collective-permute-start | bytes 393224 | tf_op jit(solution)/shard_map/ppermute | solution.py:296
  49.0 8.1 %collective-permute-start.22 = (bf16[512,128]{1,0:T(8,128)(2,1)S(1)}, bf16[512,128]{1,0:T(8,128)(2,1)S(1)}, u32[]{:S(2)}, u32[]{:S(2)}) collective-permute-start(bf16[512,128]{1,0:T(8,128)(2,1)S(1)} %get-tuple-element.42.refs_1_.refs_4_.refs_5_), channel_id=1, source_target_pairs={{0,1},{1,2},{2,3},{3,4},{4,5},{5,6},{6,7},{7,0},{8,15},{9,8},{10,9... | collective-permute-start | bytes 393224 | tf_op jit(solution)/shard_map/ppermute | solution.py:307
  50.7 7.1 %collective-permute-start.21 = (bf16[512,128]{1,0:T(8,128)(2,1)S(1)}, bf16[512,128]{1,0:T(8,128)(2,1)S(1)}, u32[]{:S(2)}, u32[]{:S(2)}) collective-permute-start(bf16[512,128]{1,0:T(8,128)(2,1)S(1)} %get-tuple-element.42.refs_1_.refs_4_.refs_5_), channel_id=1, source_target_pairs={{0,2},{1,3},{2,4},{3,5},{4,6},{5,7},{6,0},{7,1},{8,14},{9,15},{10,... | collective-permute-start | bytes 393224 | tf_op jit(solution)/shard_map/ppermute | solution.py:307
  51.0 6.7 %collective-permute-start.23 = (bf16[512,128]{1,0:T(8,128)(2,1)S(1)}, bf16[512,128]{1,0:T(8,128)(2,1)S(1)}, u32[]{:S(2)}, u32[]{:S(2)}) collective-permute-start(bf16[512,128]{1,0:T(8,128)(2,1)S(1)} %get-tuple-element.43), channel_id=1, source_target_pairs={{0,16},{1,17},{2,18},{3,19},{4,20},{5,21},{6,22},{7,23},{8,24},{9,... | collective-permute-start | bytes 393224 | tf_op jit(solution)/shard_map/ppermute | solution.py:299
  58.0 1.4 %collective-permute-start.24 = (bf16[512,128]{1,0:T(8,128)(2,1)S(1)}, bf16[512,128]{1,0:T(8,128)(2,1)S(1)}, u32[]{:S(2)}, u32[]{:S(2)}) collective-permute-start(bf16[512,128]{1,0:T(8,128)(2,1)S(1)} %shard_map.90.mine_ref), channel_id=1, source_target_pairs={{0,8},{1,9},{2,10},{3,11},{4,12},{5,13},{6,14},{7,15},{8,0},{9,1},... | collective-permute-start | bytes 393224 | tf_op jit(solution)/shard_map/ppermute | solution.py:296
  59.6 5.6 %collective-permute-start.25 = (bf16[512,128]{1,0:T(8,128)(2,1)S(1)}, bf16[512,128]{1,0:T(8,128)(2,1)S(1)}, u32[]{:S(2)}, u32[]{:S(2)}) collective-permute-start(bf16[512,128]{1,0:T(8,128)(2,1)S(1)} %get-tuple-element.45), channel_id=1, source_target_pairs={{0,16},{1,17},{2,18},{3,19},{4,20},{5,21},{6,22},{7,23},{8,24},{9,... | collective-permute-start | bytes 393224 | tf_op jit(solution)/shard_map/ppermute | solution.py:299
  59.7 7.7 %collective-permute-start.28 = (bf16[512,128]{1,0:T(8,128)(2,1)S(1)}, bf16[512,128]{1,0:T(8,128)(2,1)S(1)}, u32[]{:S(2)}, u32[]{:S(2)}) collective-permute-start(bf16[512,128]{1,0:T(8,128)(2,1)S(1)} %get-tuple-element.44.refs_5_.refs_1_), channel_id=1, source_target_pairs={{0,1},{1,2},{2,3},{3,4},{4,5},{5,6},{6,7},{7,0},{8,15},{9,8},{10,9... | collective-permute-start | bytes 393224 | tf_op jit(solution)/shard_map/ppermute | solution.py:307
  61.2 7.0 %collective-permute-start.29 = (bf16[512,128]{1,0:T(8,128)(2,1)S(1)}, bf16[512,128]{1,0:T(8,128)(2,1)S(1)}, u32[]{:S(2)}, u32[]{:S(2)}) collective-permute-start(bf16[512,128]{1,0:T(8,128)(2,1)S(1)} %get-tuple-element.44.refs_5_.refs_1_), channel_id=1, source_target_pairs={{0,2},{1,3},{2,4},{3,5},{4,6},{5,7},{6,0},{7,1},{8,14},{9,15},{10,... | collective-permute-start | bytes 393224 | tf_op jit(solution)/shard_map/ppermute | solution.py:307
  65.3 7.0 %collective-permute-start.27 = (bf16[512,128]{1,0:T(8,128)(2,1)S(1)}, bf16[512,128]{1,0:T(8,128)(2,1)S(1)}, u32[]{:S(2)}, u32[]{:S(2)}) collective-permute-start(bf16[512,128]{1,0:T(8,128)(2,1)S(1)} %collective-permute-done.25.refs_6_.refs_1_.refs_3_), channel_id=1, source_target_pairs={{0,8},{1,9},{2,10},{3,11},{4,12},{5,13},{6,14},{7,15},{8,0},{9,1},... | collective-permute-start | bytes 393224 | tf_op jit(solution)/shard_map/ppermute | solution.py:307
  65.3 7.1 %collective-permute-start.26 = (bf16[512,128]{1,0:T(8,128)(2,1)S(1)}, bf16[512,128]{1,0:T(8,128)(2,1)S(1)}, u32[]{:S(2)}, u32[]{:S(2)}) collective-permute-start(bf16[512,128]{1,0:T(8,128)(2,1)S(1)} %collective-permute-done.25.refs_6_.refs_1_.refs_3_), channel_id=1, source_target_pairs={{0,8},{1,9},{2,10},{3,11},{4,12},{5,13},{6,14},{7,15},{8,0},{9,1},... | collective-permute-start | bytes 393224 | tf_op jit(solution)/shard_map/ppermute | solution.py:307
  68.4 5.6 %collective-permute-start.30 = (bf16[512,128]{1,0:T(8,128)(2,1)S(1)}, bf16[512,128]{1,0:T(8,128)(2,1)S(1)}, u32[]{:S(2)}, u32[]{:S(2)}) collective-permute-start(bf16[512,128]{1,0:T(8,128)(2,1)S(1)} %get-tuple-element.47), channel_id=1, source_target_pairs={{0,16},{1,17},{2,18},{3,19},{4,20},{5,21},{6,22},{7,23},{8,24},{9,... | collective-permute-start | bytes 393224 | tf_op jit(solution)/shard_map/ppermute | solution.py:299
  72.1 3.2 %collective-permute-start.32 = (bf16[512,128]{1,0:T(8,128)(2,1)S(1)}, bf16[512,128]{1,0:T(8,128)(2,1)S(1)}, u32[]{:S(2)}, u32[]{:S(2)}) collective-permute-start(bf16[512,128]{1,0:T(8,128)(2,1)S(1)} %get-tuple-element.52), channel_id=1, source_target_pairs={{0,8},{1,9},{2,10},{3,11},{4,12},{5,13},{6,14},{7,15},{8,0},{9,1},... | collective-permute-start | bytes 393224 | tf_op jit(solution)/shard_map/ppermute | solution.py:296
  (5 other events, 14.4 us)

commit v11 on v10

--- a/solution.py
+++ b/solution.py
@@ -185,7 +185,7 @@
 def late_body(step, pairs, near_ref, second_ref, early_ref, field_ref, *rest):
     *history, out_ref = rest
     total = early_ref[...] + half(near_ref, second_ref, 1)
-    out_ref[...] = (total + came(step, pairs, field_ref, history)).astype(BF16)
+    out_ref[...] = total + came(step, pairs, field_ref, history)
 
 
 def even_body(step, pairs, near_ref, second_ref, early_ref, *rest):
@@ -268,13 +268,13 @@
 
 def next_body(step, inverse_ref, excitation_ref, mine_ref, other_ref, came_ref, out_ref, going_ref):
     _, pair = place()
-    field = mine_ref[...].astype(F32) + other_ref[...].astype(F32)
+    field = mine_ref[...] + other_ref[...]
     rhs = (excitation_ref[step + 1].astype(F32) - field).astype(BF16)
     first_pair = pair == 0
     size = inverse_ref.shape[1]
     for i, block in enumerate(solve(inverse_ref, rhs, out_ref, first_pair, came_ref)):
         rows = slice(i * size, (i + 1) * size)
-        going_ref[rows, :] = jnp.where(first_pair, block, mine_ref[rows, :])
+        going_ref[rows, :] = jnp.where(first_pair, block, mine_ref[rows, :].astype(BF16))
 
 
 def per_device(lagged_block_entries, pattern, diagonal_block_inverses, excitation, history):
@@ -338,7 +338,7 @@
         if pairs == 2:
             current_in = field_in = pair_moved(going, 1)
         else:
-            current_in, field_in = pair_moved(current, 1), pair_moved(field, -1)
+            current_in, field_in = pair_moved(current, 1), pair_moved(field.astype(BF16), -1)
         last = [far, *previous] if previous else []
         ending = max(step - (steps - 1), 0)
         going_on = functools.partial(only, ending, pairs)
@@ -354,7 +354,7 @@
         if step < steps - 1:
             (field,) = call(
                 functools.partial(late_body, step, pairs),
-                [current_shape],
+                [field_shape],
                 received + [field_in] + past,
                 in_front=len(received) if step == 1 else None,
             )

time: 76.4 us -> 77.4 us (1.013)
    ppermute x12, waiting for transfers between devices: 6.85 us -> 7.78 us  [swapped(): return lax.ppermute(value, AXES, everyone(lambda d, s: (d ^ 1, s)))]
where the time goes in v11:
time: 77.4 us; the launch traced here: 77.2 us
  waiting for transfers between devices  44.2 us (57%)
  starting transfers between devices  18.2 us (24%)
  Pallas kernels  12.9 us (17%)
  between operations  1.09 us (1%)
    ppermute x14, waiting for transfers between devices, halo(): return lax.ppermute(value, AXES, everyone(move))  31.4 us
    ppermute x14, starting transfers between devices, halo(): return lax.ppermute(value, AXES, everyone(move))  13 us
    pallas_call x40, Pallas kernels, call(): pl.pallas_call(body, out_shape=tuple(outs), in_specs=specs, out_specs=tup...  11.2 us
    ppermute x12, waiting for transfers between devices, swapped(): return lax.ppermute(value, AXES, everyone(lambda d, s: (d ^ 1, s)))  7.78 us
    ppermute x7, waiting for transfers between devices, pair_moved(): lax.ppermute(value, AXES, everyone(lambda d, s: ((d + 2 * hop) % lags, s)))  5.05 us
    ppermute x7, starting transfers between devices, pair_moved(): lax.ppermute(value, AXES, everyone(lambda d, s: ((d + 2 * hop) % lags, s)))  3.05 us
    ppermute x12, starting transfers between devices, swapped(): return lax.ppermute(value, AXES, everyone(lambda d, s: (d ^ 1, s)))  2.21 us
    pallas_call x1, Pallas kernels, spread(): pl.pallas_call(functools.partial(spread_body, groups), out_shape=(matrix(...  1.74 us
  transfers between devices with their start and end apart: 33, of which 19 were waited for; matrix products, arithmetic and copies ran while one was open for 0% of the time, Pallas kernels for 13%

profile of v11, /device:TPU:0, one launch (start us, length us, event | category | flops | bytes accessed | tf_op | source)
XLA Modules:
  0.0 77.2 jit_solution(6326422530489248038)
XLA Ops:
  1.2 0.7 copy-done.3
  1.9 1.7 %shard_map.70 = (bf16[512,1024]{1,0:T(8,128)(2,1)S(1)}, bf16[512,512]{1,0:T(8,128)(2,1)S(1)}, bf16[128,1024]{1,0:T(8,128)(2,1)S(1)}, bf16[128,1024]{1,0:T(8,128)...) custom-call(s32[4,16]{1,0:T(4,128)S(1)} %bitcast.8, bf16[4,16,128,128]{3,2,1,0:T(8,128)(2,1)} %bitcast.9), custom_call_target="tpu_custom_call" | custom-call | bytes 1048576 | tf_op jit(solution)/shard_map/pallas_call | solution.py:113
  4.9 2.7 %collective-permute-start.6 = (bf16[512,128]{1,0:T(8,128)(2,1)S(1)}, bf16[512,128]{1,0:T(8,128)(2,1)S(1)}, u32[]{:S(2)}, u32[]{:S(2)}) collective-permute-start(bf16[512,128]{1,0:T(8,128)(2,1)S(1)} %shard_map.69.refs_1_.refs_5_.refs_0_), channel_id=1, source_target_pairs={{0,1},{1,2},{2,3},{3,4},{4,5},{5,6},{6,7},{7,0},{8,15},{9,8},{10,9... | collective-permute-start | bytes 393224 | tf_op jit(solution)/shard_map/ppermute | solution.py:307
  7.6 1.6 %collective-permute-start.5 = (bf16[512,128]{1,0:T(8,128)(2,1)S(1)}, bf16[512,128]{1,0:T(8,128)(2,1)S(1)}, u32[]{:S(2)}, u32[]{:S(2)}) collective-permute-start(bf16[512,128]{1,0:T(8,128)(2,1)S(1)} %shard_map.69.refs_1_.refs_5_.refs_0_), channel_id=1, source_target_pairs={{0,2},{1,3},{2,4},{3,5},{4,6},{5,7},{6,0},{7,1},{8,14},{9,15},{10,... | collective-permute-start | bytes 393224 | tf_op jit(solution)/shard_map/ppermute | solution.py:307
  9.7 5.2 %collective-permute-done.6.refs_1_.refs_3_ = bf16[512,128]{1,0:T(8,128)(2,1)S(1)} collective-permute-done((bf16[512,128]{1,0:T(8,128)(2,1)S(1)}, bf16[512,128]{1,0:T(8,128)(2,1)S(1)}, u32[]{:S(2)}, u32[]{:S(2)}) %collective-permute-start.6) | collective-permute-done | bytes 131104 | tf_op jit(solution)/shard_map/ppermute | solution.py:307
  15.2 0.6 collective-permute-done.5.second_ref.refs_4_
  16.2 1.4 %collective-permute-done.8.other_ref = f32[512,128]{1,0:T(8,128)S(1)} collective-permute-done((f32[512,128]{1,0:T(8,128)S(1)}, f32[512,128]{1,0:T(8,128)S(1)}, u32[]{:S(2)}, u32[]{:S(2)}) %collective-permute-start.8) | collective-permute-done | bytes 262176 | tf_op jit(solution)/shard_map/ppermute | solution.py:296
  17.9 1.3 %collective-permute-start.11 = (bf16[512,128]{1,0:T(8,128)(2,1)S(1)}, bf16[512,128]{1,0:T(8,128)(2,1)S(1)}, u32[]{:S(2)}, u32[]{:S(2)}) collective-permute-start(bf16[512,128]{1,0:T(8,128)(2,1)S(1)} %get-tuple-element.35.refs_1_.refs_5_), channel_id=1, source_target_pairs={{0,1},{1,2},{2,3},{3,4},{4,5},{5,6},{6,7},{7,0},{8,15},{9,8},{10,9... | collective-permute-start | bytes 393224 | tf_op jit(solution)/shard_map/ppermute | solution.py:307
  19.4 0.6 shard_map.76.refs_2_
  20.0 6.3 %collective-permute-done.11.refs_1_.refs_3_ = bf16[512,128]{1,0:T(8,128)(2,1)S(1)} collective-permute-done((bf16[512,128]{1,0:T(8,128)(2,1)S(1)}, bf16[512,128]{1,0:T(8,128)(2,1)S(1)}, u32[]{:S(2)}, u32[]{:S(2)}) %collective-permute-start.11) | collective-permute-done | bytes 131104 | tf_op jit(solution)/shard_map/ppermute | solution.py:307
  27.0 1.5 %collective-permute-done.12.other_ref = f32[512,128]{1,0:T(8,128)S(1)} collective-permute-done((f32[512,128]{1,0:T(8,128)S(1)}, f32[512,128]{1,0:T(8,128)S(1)}, u32[]{:S(2)}, u32[]{:S(2)}) %collective-permute-start.12) | collective-permute-done | bytes 262176 | tf_op jit(solution)/shard_map/ppermute | solution.py:296
  28.7 1.7 %collective-permute-start.14 = (bf16[512,128]{1,0:T(8,128)(2,1)S(1)}, bf16[512,128]{1,0:T(8,128)(2,1)S(1)}, u32[]{:S(2)}, u32[]{:S(2)}) collective-permute-start(bf16[512,128]{1,0:T(8,128)(2,1)S(1)} %get-tuple-element.38.refs_1_.refs_5_.refs_2_), channel_id=1, source_target_pairs={{0,1},{1,2},{2,3},{3,4},{4,5},{5,6},{6,7},{7,0},{8,15},{9,8},{10,9... | collective-permute-start | bytes 393224 | tf_op jit(solution)/shard_map/ppermute | solution.py:307
  30.9 0.6 shard_map.80.refs_2_
  31.5 5.0 %collective-permute-done.14.refs_1_.refs_3_ = bf16[512,128]{1,0:T(8,128)(2,1)S(1)} collective-permute-done((bf16[512,128]{1,0:T(8,128)(2,1)S(1)}, bf16[512,128]{1,0:T(8,128)(2,1)S(1)}, u32[]{:S(2)}, u32[]{:S(2)}) %collective-permute-start.14) | collective-permute-done | bytes 131104 | tf_op jit(solution)/shard_map/ppermute | solution.py:307
  36.8 0.7 collective-permute-done.13.second_ref.refs_4_
  37.8 1.5 %collective-permute-done.16.other_ref = f32[512,128]{1,0:T(8,128)S(1)} collective-permute-done((f32[512,128]{1,0:T(8,128)S(1)}, f32[512,128]{1,0:T(8,128)S(1)}, u32[]{:S(2)}, u32[]{:S(2)}) %collective-permute-start.16) | collective-permute-done | bytes 262176 | tf_op jit(solution)/shard_map/ppermute | solution.py:296
  39.5 1.1 %collective-permute-start.18 = (bf16[512,128]{1,0:T(8,128)(2,1)S(1)}, bf16[512,128]{1,0:T(8,128)(2,1)S(1)}, u32[]{:S(2)}, u32[]{:S(2)}) collective-permute-start(bf16[512,128]{1,0:T(8,128)(2,1)S(1)} %get-tuple-element.40.refs_1_.refs_5_.refs_3_), channel_id=1, source_target_pairs={{0,1},{1,2},{2,3},{3,4},{4,5},{5,6},{6,7},{7,0},{8,15},{9,8},{10,9... | collective-permute-start | bytes 393224 | tf_op jit(solution)/shard_map/ppermute | solution.py:307
  40.9 0.6 shard_map.84.refs_2_
  41.5 5.8 %collective-permute-done.18.refs_1_.refs_3_ = bf16[512,128]{1,0:T(8,128)(2,1)S(1)} collective-permute-done((bf16[512,128]{1,0:T(8,128)(2,1)S(1)}, bf16[512,128]{1,0:T(8,128)(2,1)S(1)}, u32[]{:S(2)}, u32[]{:S(2)}) %collective-permute-start.18) | collective-permute-done | bytes 131104 | tf_op jit(solution)/shard_map/ppermute | solution.py:307
  48.0 1.5 %collective-permute-done.20.other_ref = f32[512,128]{1,0:T(8,128)S(1)} collective-permute-done((f32[512,128]{1,0:T(8,128)S(1)}, f32[512,128]{1,0:T(8,128)S(1)}, u32[]{:S(2)}, u32[]{:S(2)}) %collective-permute-start.20) | collective-permute-done | bytes 262176 | tf_op jit(solution)/shard_map/ppermute | solution.py:296
  49.7 1.7 %collective-permute-start.22 = (bf16[512,128]{1,0:T(8,128)(2,1)S(1)}, bf16[512,128]{1,0:T(8,128)(2,1)S(1)}, u32[]{:S(2)}, u32[]{:S(2)}) collective-permute-start(bf16[512,128]{1,0:T(8,128)(2,1)S(1)} %get-tuple-element.42.refs_1_.refs_4_.refs_5_), channel_id=1, source_target_pairs={{0,1},{1,2},{2,3},{3,4},{4,5},{5,6},{6,7},{7,0},{8,15},{9,8},{10,9... | collective-permute-start | bytes 393224 | tf_op jit(solution)/shard_map/ppermute | solution.py:307
  51.8 0.6 shard_map.88.refs_2_
  52.4 5.5 %collective-permute-done.22.refs_1_.refs_3_ = bf16[512,128]{1,0:T(8,128)(2,1)S(1)} collective-permute-done((bf16[512,128]{1,0:T(8,128)(2,1)S(1)}, bf16[512,128]{1,0:T(8,128)(2,1)S(1)}, u32[]{:S(2)}, u32[]{:S(2)}) %collective-permute-start.22) | collective-permute-done | bytes 131104 | tf_op jit(solution)/shard_map/ppermute | solution.py:307
  58.8 1.5 %collective-permute-done.24.other_ref = f32[512,128]{1,0:T(8,128)S(1)} collective-permute-done((f32[512,128]{1,0:T(8,128)S(1)}, f32[512,128]{1,0:T(8,128)S(1)}, u32[]{:S(2)}, u32[]{:S(2)}) %collective-permute-start.24) | collective-permute-done | bytes 262176 | tf_op jit(solution)/shard_map/ppermute | solution.py:296
  60.6 1.5 %collective-permute-start.28 = (bf16[512,128]{1,0:T(8,128)(2,1)S(1)}, bf16[512,128]{1,0:T(8,128)(2,1)S(1)}, u32[]{:S(2)}, u32[]{:S(2)}) collective-permute-start(bf16[512,128]{1,0:T(8,128)(2,1)S(1)} %get-tuple-element.44.refs_5_.refs_1_), channel_id=1, source_target_pairs={{0,1},{1,2},{2,3},{3,4},{4,5},{5,6},{6,7},{7,0},{8,15},{9,8},{10,9... | collective-permute-start | bytes 393224 | tf_op jit(solution)/shard_map/ppermute | solution.py:307
  62.1 0.6 shard_map.99.refs_2_
  62.7 3.5 %collective-permute-done.25.refs_6_.refs_1_.refs_3_ = bf16[512,128]{1,0:T(8,128)(2,1)S(1)} collective-permute-done((bf16[512,128]{1,0:T(8,128)(2,1)S(1)}, bf16[512,128]{1,0:T(8,128)(2,1)S(1)}, u32[]{:S(2)}, u32[]{:S(2)}) %collective-permute-start.25) | collective-permute-done | bytes 131104 | tf_op jit(solution)/shard_map/ppermute | solution.py:299
  66.6 1.7 %collective-permute-done.28.refs_3_.refs_1_ = bf16[512,128]{1,0:T(8,128)(2,1)S(1)} collective-permute-done((bf16[512,128]{1,0:T(8,128)(2,1)S(1)}, bf16[512,128]{1,0:T(8,128)(2,1)S(1)}, u32[]{:S(2)}, u32[]{:S(2)}) %collective-permute-start.28) | collective-permute-done | bytes 131104 | tf_op jit(solution)/shard_map/ppermute | solution.py:307
  69.3 2.6 %collective-permute-start.30 = (bf16[512,128]{1,0:T(8,128)(2,1)S(1)}, bf16[512,128]{1,0:T(8,128)(2,1)S(1)}, u32[]{:S(2)}, u32[]{:S(2)}) collective-permute-start(bf16[512,128]{1,0:T(8,128)(2,1)S(1)} %get-tuple-element.47), channel_id=1, source_target_pairs={{0,16},{1,17},{2,18},{3,19},{4,20},{5,21},{6,22},{7,23},{8,24},{9,... | collective-permute-start | bytes 393224 | tf_op jit(solution)/shard_map/ppermute | solution.py:299
  73.4 1.6 %collective-permute-done.30.rest_0_ = bf16[512,128]{1,0:T(8,128)(2,1)S(1)} collective-permute-done((bf16[512,128]{1,0:T(8,128)(2,1)S(1)}, bf16[512,128]{1,0:T(8,128)(2,1)S(1)}, u32[]{:S(2)}, u32[]{:S(2)}) %collective-permute-start.30) | collective-permute-done | bytes 131104 | tf_op jit(solution)/shard_map/ppermute | solution.py:299
  75.1 1.0 %shard_map.92 = (bf16[6,512,128]{2,1,0:T(8,128)(2,1)}, f32[8,128]{1,0:T(8,128)S(1)}) custom-call(bf16[512,128]{1,0:T(8,128)(2,1)S(1)} %shard_map.69.refs_1_.refs_5_.refs_0_, bf16[512,128]{1,0:T(8,128)(2,1)S(1)} %get-tuple-element.35.refs_1_.refs_5_, bf16[512,128]{1,0:T(8,128)(2,1)S(1)} %get-tuple-element.38.refs_1_.refs_5_.refs_2_, ...), custom_call_target="tpu_custom_call" | custom-call | bytes 1048576 | tf_op jit(solution)/shard_map/pallas_call | solution.py:38
  76.4 0.8 shard_map.108
  (83 shorter events, 11.8 us)
Async XLA Ops:
  0.7 4.0 %collective-permute-start = (f32[512,128]{1,0:T(8,128)}, f32[512,128]{1,0:T(8,128)S(1)}, u32[]{:S(2)}, u32[]{:S(2)}) collective-permute-start(f32[512,128]{1,0:T(8,128)} %bitcast.4), channel_id=1, source_target_pairs={{0,8},{1,9},{2,10},{3,11},{4,12},{5,13},{6,14},{7,15},{8,0},{9,1},... | collective-permute-start | bytes 786440 | tf_op jit(solution)/shard_map/ppermute | solution.py:296
  3.6 4.0 %collective-permute-start.1 = (bf16[128,1024]{1,0:T(8,128)(2,1)S(1)}, bf16[128,1024]{1,0:T(8,128)(2,1)S(1)}, u32[]{:S(2)}, u32[]{:S(2)}) collective-permute-start(bf16[128,1024]{1,0:T(8,128)(2,1)S(1)} %get-tuple-element.29), channel_id=1, source_target_pairs={{0,8},{1,9},{2,10},{3,11},{4,12},{5,13},{6,14},{7,15},{8,0},{9,1},... | collective-permute-start | bytes 786440 | tf_op jit(solution)/shard_map/ppermute | solution.py:296
  3.8 5.4 %collective-permute-start.2 = (bf16[128,1024]{1,0:T(8,128)(2,1)S(1)}, bf16[128,1024]{1,0:T(8,128)(2,1)S(1)}, u32[]{:S(2)}, u32[]{:S(2)}) collective-permute-start(bf16[128,1024]{1,0:T(8,128)(2,1)S(1)} %get-tuple-element.30), channel_id=1, source_target_pairs={{0,8},{1,9},{2,10},{3,11},{4,12},{5,13},{6,14},{7,15},{8,0},{9,1},... | collective-permute-start | bytes 786440 | tf_op jit(solution)/shard_map/ppermute | solution.py:296
  4.2 5.3 %collective-permute-start.3 = (bf16[128,1024]{1,0:T(8,128)(2,1)S(1)}, bf16[128,1024]{1,0:T(8,128)(2,1)S(1)}, u32[]{:S(2)}, u32[]{:S(2)}) collective-permute-start(bf16[128,1024]{1,0:T(8,128)(2,1)S(1)} %get-tuple-element.31), channel_id=1, source_target_pairs={{0,8},{1,9},{2,10},{3,11},{4,12},{5,13},{6,14},{7,15},{8,0},{9,1},... | collective-permute-start | bytes 786440 | tf_op jit(solution)/shard_map/ppermute | solution.py:296
  4.3 5.2 %collective-permute-start.4 = (bf16[128,1024]{1,0:T(8,128)(2,1)S(1)}, bf16[128,1024]{1,0:T(8,128)(2,1)S(1)}, u32[]{:S(2)}, u32[]{:S(2)}) collective-permute-start(bf16[128,1024]{1,0:T(8,128)(2,1)S(1)} %get-tuple-element.32), channel_id=1, source_target_pairs={{0,8},{1,9},{2,10},{3,11},{4,12},{5,13},{6,14},{7,15},{8,0},{9,1},... | collective-permute-start | bytes 786440 | tf_op jit(solution)/shard_map/ppermute | solution.py:296
  4.9 9.9 %collective-permute-start.6 = (bf16[512,128]{1,0:T(8,128)(2,1)S(1)}, bf16[512,128]{1,0:T(8,128)(2,1)S(1)}, u32[]{:S(2)}, u32[]{:S(2)}) collective-permute-start(bf16[512,128]{1,0:T(8,128)(2,1)S(1)} %shard_map.69.refs_1_.refs_5_.refs_0_), channel_id=1, source_target_pairs={{0,1},{1,2},{2,3},{3,4},{4,5},{5,6},{6,7},{7,0},{8,15},{9,8},{10,9... | collective-permute-start | bytes 393224 | tf_op jit(solution)/shard_map/ppermute | solution.py:307
  7.6 8.2 %collective-permute-start.5 = (bf16[512,128]{1,0:T(8,128)(2,1)S(1)}, bf16[512,128]{1,0:T(8,128)(2,1)S(1)}, u32[]{:S(2)}, u32[]{:S(2)}) collective-permute-start(bf16[512,128]{1,0:T(8,128)(2,1)S(1)} %shard_map.69.refs_1_.refs_5_.refs_0_), channel_id=1, source_target_pairs={{0,2},{1,3},{2,4},{3,5},{4,6},{5,7},{6,0},{7,1},{8,14},{9,15},{10,... | collective-permute-start | bytes 393224 | tf_op jit(solution)/shard_map/ppermute | solution.py:307
  9.2 6.6 %collective-permute-start.7 = (bf16[512,128]{1,0:T(8,128)(2,1)S(1)}, bf16[512,128]{1,0:T(8,128)(2,1)S(1)}, u32[]{:S(2)}, u32[]{:S(2)}) collective-permute-start(bf16[512,128]{1,0:T(8,128)(2,1)S(1)} %shard_map.69.refs_1_.refs_5_.refs_0_), channel_id=1, source_target_pairs={{0,16},{1,17},{2,18},{3,19},{4,20},{5,21},{6,22},{7,23},{8,24},{9,... | collective-permute-start | bytes 393224 | tf_op jit(solution)/shard_map/ppermute | solution.py:299
  16.1 1.6 %collective-permute-start.8 = (f32[512,128]{1,0:T(8,128)S(1)}, f32[512,128]{1,0:T(8,128)S(1)}, u32[]{:S(2)}, u32[]{:S(2)}) collective-permute-start(f32[512,128]{1,0:T(8,128)S(1)} %shard_map.74.mine_ref), channel_id=1, source_target_pairs={{0,8},{1,9},{2,10},{3,11},{4,12},{5,13},{6,14},{7,15},{8,0},{9,1},... | collective-permute-start | bytes 786440 | tf_op jit(solution)/shard_map/ppermute | solution.py:296
  17.9 8.4 %collective-permute-start.11 = (bf16[512,128]{1,0:T(8,128)(2,1)S(1)}, bf16[512,128]{1,0:T(8,128)(2,1)S(1)}, u32[]{:S(2)}, u32[]{:S(2)}) collective-permute-start(bf16[512,128]{1,0:T(8,128)(2,1)S(1)} %get-tuple-element.35.refs_1_.refs_5_), channel_id=1, source_target_pairs={{0,1},{1,2},{2,3},{3,4},{4,5},{5,6},{6,7},{7,0},{8,15},{9,8},{10,9... | collective-permute-start | bytes 393224 | tf_op jit(solution)/shard_map/ppermute | solution.py:307
  19.1 7.5 %collective-permute-start.10 = (bf16[512,128]{1,0:T(8,128)(2,1)S(1)}, bf16[512,128]{1,0:T(8,128)(2,1)S(1)}, u32[]{:S(2)}, u32[]{:S(2)}) collective-permute-start(bf16[512,128]{1,0:T(8,128)(2,1)S(1)} %get-tuple-element.35.refs_1_.refs_5_), channel_id=1, source_target_pairs={{0,2},{1,3},{2,4},{3,5},{4,6},{5,7},{6,0},{7,1},{8,14},{9,15},{10,... | collective-permute-start | bytes 393224 | tf_op jit(solution)/shard_map/ppermute | solution.py:307
  19.4 7.2 %collective-permute-start.9 = (bf16[512,128]{1,0:T(8,128)(2,1)S(1)}, bf16[512,128]{1,0:T(8,128)(2,1)S(1)}, u32[]{:S(2)}, u32[]{:S(2)}) collective-permute-start(bf16[512,128]{1,0:T(8,128)(2,1)S(1)} %get-tuple-element.36), channel_id=1, source_target_pairs={{0,16},{1,17},{2,18},{3,19},{4,20},{5,21},{6,22},{7,23},{8,24},{9,... | collective-permute-start | bytes 393224 | tf_op jit(solution)/shard_map/ppermute | solution.py:299
  26.9 1.6 %collective-permute-start.12 = (f32[512,128]{1,0:T(8,128)S(1)}, f32[512,128]{1,0:T(8,128)S(1)}, u32[]{:S(2)}, u32[]{:S(2)}) collective-permute-start(f32[512,128]{1,0:T(8,128)S(1)} %shard_map.78.mine_ref), channel_id=1, source_target_pairs={{0,8},{1,9},{2,10},{3,11},{4,12},{5,13},{6,14},{7,15},{8,0},{9,1},... | collective-permute-start | bytes 786440 | tf_op jit(solution)/shard_map/ppermute | solution.py:296
  28.7 7.7 %collective-permute-start.14 = (bf16[512,128]{1,0:T(8,128)(2,1)S(1)}, bf16[512,128]{1,0:T(8,128)(2,1)S(1)}, u32[]{:S(2)}, u32[]{:S(2)}) collective-permute-start(bf16[512,128]{1,0:T(8,128)(2,1)S(1)} %get-tuple-element.38.refs_1_.refs_5_.refs_2_), channel_id=1, source_target_pairs={{0,1},{1,2},{2,3},{3,4},{4,5},{5,6},{6,7},{7,0},{8,15},{9,8},{10,9... | collective-permute-start | bytes 393224 | tf_op jit(solution)/shard_map/ppermute | solution.py:307
  30.4 7.0 %collective-permute-start.13 = (bf16[512,128]{1,0:T(8,128)(2,1)S(1)}, bf16[512,128]{1,0:T(8,128)(2,1)S(1)}, u32[]{:S(2)}, u32[]{:S(2)}) collective-permute-start(bf16[512,128]{1,0:T(8,128)(2,1)S(1)} %get-tuple-element.38.refs_1_.refs_5_.refs_2_), channel_id=1, source_target_pairs={{0,2},{1,3},{2,4},{3,5},{4,6},{5,7},{6,0},{7,1},{8,14},{9,15},{10,... | collective-permute-start | bytes 393224 | tf_op jit(solution)/shard_map/ppermute | solution.py:307
  30.9 6.5 %collective-permute-start.15 = (bf16[512,128]{1,0:T(8,128)(2,1)S(1)}, bf16[512,128]{1,0:T(8,128)(2,1)S(1)}, u32[]{:S(2)}, u32[]{:S(2)}) collective-permute-start(bf16[512,128]{1,0:T(8,128)(2,1)S(1)} %get-tuple-element.39), channel_id=1, source_target_pairs={{0,16},{1,17},{2,18},{3,19},{4,20},{5,21},{6,22},{7,23},{8,24},{9,... | collective-permute-start | bytes 393224 | tf_op jit(solution)/shard_map/ppermute | solution.py:299
  37.7 1.6 %collective-permute-start.16 = (f32[512,128]{1,0:T(8,128)S(1)}, f32[512,128]{1,0:T(8,128)S(1)}, u32[]{:S(2)}, u32[]{:S(2)}) collective-permute-start(f32[512,128]{1,0:T(8,128)S(1)} %shard_map.82.mine_ref), channel_id=1, source_target_pairs={{0,8},{1,9},{2,10},{3,11},{4,12},{5,13},{6,14},{7,15},{8,0},{9,1},... | collective-permute-start | bytes 786440 | tf_op jit(solution)/shard_map/ppermute | solution.py:296
  39.5 7.7 %collective-permute-start.18 = (bf16[512,128]{1,0:T(8,128)(2,1)S(1)}, bf16[512,128]{1,0:T(8,128)(2,1)S(1)}, u32[]{:S(2)}, u32[]{:S(2)}) collective-permute-start(bf16[512,128]{1,0:T(8,128)(2,1)S(1)} %get-tuple-element.40.refs_1_.refs_5_.refs_3_), channel_id=1, source_target_pairs={{0,1},{1,2},{2,3},{3,4},{4,5},{5,6},{6,7},{7,0},{8,15},{9,8},{10,9... | collective-permute-start | bytes 393224 | tf_op jit(solution)/shard_map/ppermute | solution.py:307
  40.6 7.0 %collective-permute-start.17 = (bf16[512,128]{1,0:T(8,128)(2,1)S(1)}, bf16[512,128]{1,0:T(8,128)(2,1)S(1)}, u32[]{:S(2)}, u32[]{:S(2)}) collective-permute-start(bf16[512,128]{1,0:T(8,128)(2,1)S(1)} %get-tuple-element.40.refs_1_.refs_5_.refs_3_), channel_id=1, source_target_pairs={{0,2},{1,3},{2,4},{3,5},{4,6},{5,7},{6,0},{7,1},{8,14},{9,15},{10,... | collective-permute-start | bytes 393224 | tf_op jit(solution)/shard_map/ppermute | solution.py:307
  40.6 7.0 %collective-permute-start.19 = (bf16[512,128]{1,0:T(8,128)(2,1)S(1)}, bf16[512,128]{1,0:T(8,128)(2,1)S(1)}, u32[]{:S(2)}, u32[]{:S(2)}) collective-permute-start(bf16[512,128]{1,0:T(8,128)(2,1)S(1)} %get-tuple-element.41), channel_id=1, source_target_pairs={{0,16},{1,17},{2,18},{3,19},{4,20},{5,21},{6,22},{7,23},{8,24},{9,... | collective-permute-start | bytes 393224 | tf_op jit(solution)/shard_map/ppermute | solution.py:299
  47.9 1.6 %collective-permute-start.20 = (f32[512,128]{1,0:T(8,128)S(1)}, f32[512,128]{1,0:T(8,128)S(1)}, u32[]{:S(2)}, u32[]{:S(2)}) collective-permute-start(f32[512,128]{1,0:T(8,128)S(1)} %shard_map.86.mine_ref), channel_id=1, source_target_pairs={{0,8},{1,9},{2,10},{3,11},{4,12},{5,13},{6,14},{7,15},{8,0},{9,1},... | collective-permute-start | bytes 786440 | tf_op jit(solution)/shard_map/ppermute | solution.py:296
  49.7 8.1 %collective-permute-start.22 = (bf16[512,128]{1,0:T(8,128)(2,1)S(1)}, bf16[512,128]{1,0:T(8,128)(2,1)S(1)}, u32[]{:S(2)}, u32[]{:S(2)}) collective-permute-start(bf16[512,128]{1,0:T(8,128)(2,1)S(1)} %get-tuple-element.42.refs_1_.refs_4_.refs_5_), channel_id=1, source_target_pairs={{0,1},{1,2},{2,3},{3,4},{4,5},{5,6},{6,7},{7,0},{8,15},{9,8},{10,9... | collective-permute-start | bytes 393224 | tf_op jit(solution)/shard_map/ppermute | solution.py:307
  51.4 7.0 %collective-permute-start.21 = (bf16[512,128]{1,0:T(8,128)(2,1)S(1)}, bf16[512,128]{1,0:T(8,128)(2,1)S(1)}, u32[]{:S(2)}, u32[]{:S(2)}) collective-permute-start(bf16[512,128]{1,0:T(8,128)(2,1)S(1)} %get-tuple-element.42.refs_1_.refs_4_.refs_5_), channel_id=1, source_target_pairs={{0,2},{1,3},{2,4},{3,5},{4,6},{5,7},{6,0},{7,1},{8,14},{9,15},{10,... | collective-permute-start | bytes 393224 | tf_op jit(solution)/shard_map/ppermute | solution.py:307
  51.8 6.6 %collective-permute-start.23 = (bf16[512,128]{1,0:T(8,128)(2,1)S(1)}, bf16[512,128]{1,0:T(8,128)(2,1)S(1)}, u32[]{:S(2)}, u32[]{:S(2)}) collective-permute-start(bf16[512,128]{1,0:T(8,128)(2,1)S(1)} %get-tuple-element.43), channel_id=1, source_target_pairs={{0,16},{1,17},{2,18},{3,19},{4,20},{5,21},{6,22},{7,23},{8,24},{9,... | collective-permute-start | bytes 393224 | tf_op jit(solution)/shard_map/ppermute | solution.py:299
  58.7 1.6 %collective-permute-start.24 = (f32[512,128]{1,0:T(8,128)S(1)}, f32[512,128]{1,0:T(8,128)S(1)}, u32[]{:S(2)}, u32[]{:S(2)}) collective-permute-start(f32[512,128]{1,0:T(8,128)S(1)} %shard_map.90.mine_ref), channel_id=1, source_target_pairs={{0,8},{1,9},{2,10},{3,11},{4,12},{5,13},{6,14},{7,15},{8,0},{9,1},... | collective-permute-start | bytes 786440 | tf_op jit(solution)/shard_map/ppermute | solution.py:296
  60.5 5.6 %collective-permute-start.25 = (bf16[512,128]{1,0:T(8,128)(2,1)S(1)}, bf16[512,128]{1,0:T(8,128)(2,1)S(1)}, u32[]{:S(2)}, u32[]{:S(2)}) collective-permute-start(bf16[512,128]{1,0:T(8,128)(2,1)S(1)} %get-tuple-element.45), channel_id=1, source_target_pairs={{0,16},{1,17},{2,18},{3,19},{4,20},{5,21},{6,22},{7,23},{8,24},{9,... | collective-permute-start | bytes 393224 | tf_op jit(solution)/shard_map/ppermute | solution.py:299
  60.6 7.7 %collective-permute-start.28 = (bf16[512,128]{1,0:T(8,128)(2,1)S(1)}, bf16[512,128]{1,0:T(8,128)(2,1)S(1)}, u32[]{:S(2)}, u32[]{:S(2)}) collective-permute-start(bf16[512,128]{1,0:T(8,128)(2,1)S(1)} %get-tuple-element.44.refs_5_.refs_1_), channel_id=1, source_target_pairs={{0,1},{1,2},{2,3},{3,4},{4,5},{5,6},{6,7},{7,0},{8,15},{9,8},{10,9... | collective-permute-start | bytes 393224 | tf_op jit(solution)/shard_map/ppermute | solution.py:307
  62.1 7.0 %collective-permute-start.29 = (bf16[512,128]{1,0:T(8,128)(2,1)S(1)}, bf16[512,128]{1,0:T(8,128)(2,1)S(1)}, u32[]{:S(2)}, u32[]{:S(2)}) collective-permute-start(bf16[512,128]{1,0:T(8,128)(2,1)S(1)} %get-tuple-element.44.refs_5_.refs_1_), channel_id=1, source_target_pairs={{0,2},{1,3},{2,4},{3,5},{4,6},{5,7},{6,0},{7,1},{8,14},{9,15},{10,... | collective-permute-start | bytes 393224 | tf_op jit(solution)/shard_map/ppermute | solution.py:307
  66.1 7.0 %collective-permute-start.27 = (bf16[512,128]{1,0:T(8,128)(2,1)S(1)}, bf16[512,128]{1,0:T(8,128)(2,1)S(1)}, u32[]{:S(2)}, u32[]{:S(2)}) collective-permute-start(bf16[512,128]{1,0:T(8,128)(2,1)S(1)} %collective-permute-done.25.refs_6_.refs_1_.refs_3_), channel_id=1, source_target_pairs={{0,8},{1,9},{2,10},{3,11},{4,12},{5,13},{6,14},{7,15},{8,0},{9,1},... | collective-permute-start | bytes 393224 | tf_op jit(solution)/shard_map/ppermute | solution.py:307
  66.1 7.1 %collective-permute-start.26 = (bf16[512,128]{1,0:T(8,128)(2,1)S(1)}, bf16[512,128]{1,0:T(8,128)(2,1)S(1)}, u32[]{:S(2)}, u32[]{:S(2)}) collective-permute-start(bf16[512,128]{1,0:T(8,128)(2,1)S(1)} %collective-permute-done.25.refs_6_.refs_1_.refs_3_), channel_id=1, source_target_pairs={{0,8},{1,9},{2,10},{3,11},{4,12},{5,13},{6,14},{7,15},{8,0},{9,1},... | collective-permute-start | bytes 393224 | tf_op jit(solution)/shard_map/ppermute | solution.py:307
  69.3 5.6 %collective-permute-start.30 = (bf16[512,128]{1,0:T(8,128)(2,1)S(1)}, bf16[512,128]{1,0:T(8,128)(2,1)S(1)}, u32[]{:S(2)}, u32[]{:S(2)}) collective-permute-start(bf16[512,128]{1,0:T(8,128)(2,1)S(1)} %get-tuple-element.47), channel_id=1, source_target_pairs={{0,16},{1,17},{2,18},{3,19},{4,20},{5,21},{6,22},{7,23},{8,24},{9,... | collective-permute-start | bytes 393224 | tf_op jit(solution)/shard_map/ppermute | solution.py:299
  73.0 3.2 %collective-permute-start.32 = (bf16[512,128]{1,0:T(8,128)(2,1)S(1)}, bf16[512,128]{1,0:T(8,128)(2,1)S(1)}, u32[]{:S(2)}, u32[]{:S(2)}) collective-permute-start(bf16[512,128]{1,0:T(8,128)(2,1)S(1)} %get-tuple-element.52), channel_id=1, source_target_pairs={{0,8},{1,9},{2,10},{3,11},{4,12},{5,13},{6,14},{7,15},{8,0},{9,1},... | collective-permute-start | bytes 393224 | tf_op jit(solution)/shard_map/ppermute | solution.py:296
  (5 other events, 14.4 us)

commit v12 on v10

--- a/solution.py
+++ b/solution.py
@@ -12,6 +12,7 @@
 AXES = ("delay", "surface")
 VMEM = pl.BlockSpec(memory_space=pltpu.VMEM)
 MIB = 1024 * 1024
+CHUNKS = 2
 TOKEN = jax.ShapeDtypeStruct((8, 128), F32)
 
 
@@ -178,14 +179,31 @@
     return value
 
 
+def add_half(matrix_ref, block_ref, which, early_ref, put):
+    rows = block_ref.shape[0]
+    size = rows // CHUNKS
+    block = block_ref[...]
+    columns = slice(which * rows, (which + 1) * rows)
+    for i in range(CHUNKS):
+        part = slice(i * size, (i + 1) * size)
+        put(part, early_ref[part, :] + dot(matrix_ref[part, columns], block))
+
+
 def first_body(near_ref, first_ref, early_ref, out_ref):
-    out_ref[...] = early_ref[...] + half(near_ref, first_ref, 0)
+    def put(part, total):
+        out_ref[part, :] = total
+
+    add_half(near_ref, first_ref, 0, early_ref, put)
 
 
 def late_body(step, pairs, near_ref, second_ref, early_ref, field_ref, *rest):
     *history, out_ref = rest
-    total = early_ref[...] + half(near_ref, second_ref, 1)
-    out_ref[...] = (total + came(step, pairs, field_ref, history)).astype(BF16)
+    value = came(step, pairs, field_ref, history)
+
+    def put(part, total):
+        out_ref[part, :] = (total + value[part]).astype(BF16)
+
+    add_half(near_ref, second_ref, 1, early_ref, put)
 
 
 def even_body(step, pairs, near_ref, second_ref, early_ref, *rest):

time: 76.4 us -> 76.4 us (level)
  no operation moved by 1% of the time
where the time goes in v12:
time: 76.4 us; the launch traced here: 76.2 us
  waiting for transfers between devices  43.8 us (57%)
  starting transfers between devices  17.8 us (23%)
  Pallas kernels  12.8 us (17%)
  between operations  1.09 us (1%)
    ppermute x14, waiting for transfers between devices, halo(): return lax.ppermute(value, AXES, everyone(move))  31.8 us
    ppermute x14, starting transfers between devices, halo(): return lax.ppermute(value, AXES, everyone(move))  12.9 us
    pallas_call x40, Pallas kernels, call(): pl.pallas_call(body, out_shape=tuple(outs), in_specs=specs, out_specs=tup...  11.1 us
    ppermute x12, waiting for transfers between devices, swapped(): return lax.ppermute(value, AXES, everyone(lambda d, s: (d ^ 1, s)))  6.85 us
    ppermute x7, waiting for transfers between devices, pair_moved(): lax.ppermute(value, AXES, everyone(lambda d, s: ((d + 2 * hop) % lags, s)))  5.09 us
    ppermute x7, starting transfers between devices, pair_moved(): lax.ppermute(value, AXES, everyone(lambda d, s: ((d + 2 * hop) % lags, s)))  2.7 us
    ppermute x12, starting transfers between devices, swapped(): return lax.ppermute(value, AXES, everyone(lambda d, s: (d ^ 1, s)))  2.2 us
    pallas_call x1, Pallas kernels, spread(): pl.pallas_call(functools.partial(spread_body, groups), out_shape=(matrix(...  1.74 us
  transfers between devices with their start and end apart: 33, of which 19 were waited for; matrix products, arithmetic and copies ran while one was open for 0% of the time, Pallas kernels for 13%

profile of v12, /device:TPU:0, one launch (start us, length us, event | category | flops | bytes accessed | tf_op | source)
XLA Modules:
  0.0 76.2 jit_solution(2005838819023872726)
XLA Ops:
  1.2 0.7 copy-done.3
  1.9 1.7 %shard_map.70 = (bf16[512,1024]{1,0:T(8,128)(2,1)S(1)}, bf16[512,512]{1,0:T(8,128)(2,1)S(1)}, bf16[128,1024]{1,0:T(8,128)(2,1)S(1)}, bf16[128,1024]{1,0:T(8,128)...) custom-call(s32[4,16]{1,0:T(4,128)S(1)} %bitcast.8, bf16[4,16,128,128]{3,2,1,0:T(8,128)(2,1)} %bitcast.9), custom_call_target="tpu_custom_call" | custom-call | bytes 1048576 | tf_op jit(solution)/shard_map/pallas_call | solution.py:114
  4.9 2.7 %collective-permute-start.6 = (bf16[512,128]{1,0:T(8,128)(2,1)S(1)}, bf16[512,128]{1,0:T(8,128)(2,1)S(1)}, u32[]{:S(2)}, u32[]{:S(2)}) collective-permute-start(bf16[512,128]{1,0:T(8,128)(2,1)S(1)} %shard_map.69.refs_1_.refs_5_.refs_0_), channel_id=1, source_target_pairs={{0,1},{1,2},{2,3},{3,4},{4,5},{5,6},{6,7},{7,0},{8,15},{9,8},{10,9... | collective-permute-start | bytes 393224 | tf_op jit(solution)/shard_map/ppermute | solution.py:325
  7.6 1.6 %collective-permute-start.5 = (bf16[512,128]{1,0:T(8,128)(2,1)S(1)}, bf16[512,128]{1,0:T(8,128)(2,1)S(1)}, u32[]{:S(2)}, u32[]{:S(2)}) collective-permute-start(bf16[512,128]{1,0:T(8,128)(2,1)S(1)} %shard_map.69.refs_1_.refs_5_.refs_0_), channel_id=1, source_target_pairs={{0,2},{1,3},{2,4},{3,5},{4,6},{5,7},{6,0},{7,1},{8,14},{9,15},{10,... | collective-permute-start | bytes 393224 | tf_op jit(solution)/shard_map/ppermute | solution.py:325
  9.7 5.2 %collective-permute-done.6.refs_1_.refs_3_ = bf16[512,128]{1,0:T(8,128)(2,1)S(1)} collective-permute-done((bf16[512,128]{1,0:T(8,128)(2,1)S(1)}, bf16[512,128]{1,0:T(8,128)(2,1)S(1)}, u32[]{:S(2)}, u32[]{:S(2)}) %collective-permute-start.6) | collective-permute-done | bytes 131104 | tf_op jit(solution)/shard_map/ppermute | solution.py:325
  15.2 0.6 collective-permute-done.5.second_ref.refs_4_
  16.2 1.2 %collective-permute-done.8.other_ref = bf16[512,128]{1,0:T(8,128)(2,1)S(1)} collective-permute-done((bf16[512,128]{1,0:T(8,128)(2,1)S(1)}, bf16[512,128]{1,0:T(8,128)(2,1)S(1)}, u32[]{:S(2)}, u32[]{:S(2)}) %collective-permute-start.8) | collective-permute-done | bytes 131104 | tf_op jit(solution)/shard_map/ppermute | solution.py:314
  17.7 1.3 %collective-permute-start.11 = (bf16[512,128]{1,0:T(8,128)(2,1)S(1)}, bf16[512,128]{1,0:T(8,128)(2,1)S(1)}, u32[]{:S(2)}, u32[]{:S(2)}) collective-permute-start(bf16[512,128]{1,0:T(8,128)(2,1)S(1)} %get-tuple-element.35.refs_1_.refs_5_), channel_id=1, source_target_pairs={{0,1},{1,2},{2,3},{3,4},{4,5},{5,6},{6,7},{7,0},{8,15},{9,8},{10,9... | collective-permute-start | bytes 393224 | tf_op jit(solution)/shard_map/ppermute | solution.py:325
  19.2 0.6 shard_map.76.refs_2_
  19.8 6.3 %collective-permute-done.11.refs_1_.refs_3_ = bf16[512,128]{1,0:T(8,128)(2,1)S(1)} collective-permute-done((bf16[512,128]{1,0:T(8,128)(2,1)S(1)}, bf16[512,128]{1,0:T(8,128)(2,1)S(1)}, u32[]{:S(2)}, u32[]{:S(2)}) %collective-permute-start.11) | collective-permute-done | bytes 131104 | tf_op jit(solution)/shard_map/ppermute | solution.py:325
  26.8 1.3 %collective-permute-done.12.other_ref = bf16[512,128]{1,0:T(8,128)(2,1)S(1)} collective-permute-done((bf16[512,128]{1,0:T(8,128)(2,1)S(1)}, bf16[512,128]{1,0:T(8,128)(2,1)S(1)}, u32[]{:S(2)}, u32[]{:S(2)}) %collective-permute-start.12) | collective-permute-done | bytes 131104 | tf_op jit(solution)/shard_map/ppermute | solution.py:314
  28.3 1.7 %collective-permute-start.14 = (bf16[512,128]{1,0:T(8,128)(2,1)S(1)}, bf16[512,128]{1,0:T(8,128)(2,1)S(1)}, u32[]{:S(2)}, u32[]{:S(2)}) collective-permute-start(bf16[512,128]{1,0:T(8,128)(2,1)S(1)} %get-tuple-element.38.refs_1_.refs_5_.refs_2_), channel_id=1, source_target_pairs={{0,1},{1,2},{2,3},{3,4},{4,5},{5,6},{6,7},{7,0},{8,15},{9,8},{10,9... | collective-permute-start | bytes 393224 | tf_op jit(solution)/shard_map/ppermute | solution.py:325
  30.5 0.6 shard_map.80.refs_2_
  31.1 5.0 %collective-permute-done.14.refs_1_.refs_3_ = bf16[512,128]{1,0:T(8,128)(2,1)S(1)} collective-permute-done((bf16[512,128]{1,0:T(8,128)(2,1)S(1)}, bf16[512,128]{1,0:T(8,128)(2,1)S(1)}, u32[]{:S(2)}, u32[]{:S(2)}) %collective-permute-start.14) | collective-permute-done | bytes 131104 | tf_op jit(solution)/shard_map/ppermute | solution.py:325
  36.4 0.7 collective-permute-done.13.second_ref.refs_4_
  37.4 1.3 %collective-permute-done.16.other_ref = bf16[512,128]{1,0:T(8,128)(2,1)S(1)} collective-permute-done((bf16[512,128]{1,0:T(8,128)(2,1)S(1)}, bf16[512,128]{1,0:T(8,128)(2,1)S(1)}, u32[]{:S(2)}, u32[]{:S(2)}) %collective-permute-start.16) | collective-permute-done | bytes 131104 | tf_op jit(solution)/shard_map/ppermute | solution.py:314
  39.0 1.0 %collective-permute-start.18 = (bf16[512,128]{1,0:T(8,128)(2,1)S(1)}, bf16[512,128]{1,0:T(8,128)(2,1)S(1)}, u32[]{:S(2)}, u32[]{:S(2)}) collective-permute-start(bf16[512,128]{1,0:T(8,128)(2,1)S(1)} %get-tuple-element.40.refs_1_.refs_5_.refs_3_), channel_id=1, source_target_pairs={{0,1},{1,2},{2,3},{3,4},{4,5},{5,6},{6,7},{7,0},{8,15},{9,8},{10,9... | collective-permute-start | bytes 393224 | tf_op jit(solution)/shard_map/ppermute | solution.py:325
  40.0 0.6 shard_map.84.refs_2_
  40.6 6.1 %collective-permute-done.18.refs_1_.refs_3_ = bf16[512,128]{1,0:T(8,128)(2,1)S(1)} collective-permute-done((bf16[512,128]{1,0:T(8,128)(2,1)S(1)}, bf16[512,128]{1,0:T(8,128)(2,1)S(1)}, u32[]{:S(2)}, u32[]{:S(2)}) %collective-permute-start.18) | collective-permute-done | bytes 131104 | tf_op jit(solution)/shard_map/ppermute | solution.py:325
  47.4 1.3 %collective-permute-done.20.other_ref = bf16[512,128]{1,0:T(8,128)(2,1)S(1)} collective-permute-done((bf16[512,128]{1,0:T(8,128)(2,1)S(1)}, bf16[512,128]{1,0:T(8,128)(2,1)S(1)}, u32[]{:S(2)}, u32[]{:S(2)}) %collective-permute-start.20) | collective-permute-done | bytes 131104 | tf_op jit(solution)/shard_map/ppermute | solution.py:314
  49.0 1.7 %collective-permute-start.22 = (bf16[512,128]{1,0:T(8,128)(2,1)S(1)}, bf16[512,128]{1,0:T(8,128)(2,1)S(1)}, u32[]{:S(2)}, u32[]{:S(2)}) collective-permute-start(bf16[512,128]{1,0:T(8,128)(2,1)S(1)} %get-tuple-element.42.refs_1_.refs_4_.refs_5_), channel_id=1, source_target_pairs={{0,1},{1,2},{2,3},{3,4},{4,5},{5,6},{6,7},{7,0},{8,15},{9,8},{10,9... | collective-permute-start | bytes 393224 | tf_op jit(solution)/shard_map/ppermute | solution.py:325
  51.0 0.6 shard_map.88.refs_2_
  51.6 5.5 %collective-permute-done.22.refs_1_.refs_3_ = bf16[512,128]{1,0:T(8,128)(2,1)S(1)} collective-permute-done((bf16[512,128]{1,0:T(8,128)(2,1)S(1)}, bf16[512,128]{1,0:T(8,128)(2,1)S(1)}, u32[]{:S(2)}, u32[]{:S(2)}) %collective-permute-start.22) | collective-permute-done | bytes 131104 | tf_op jit(solution)/shard_map/ppermute | solution.py:325
  58.0 1.3 %collective-permute-done.24.other_ref = bf16[512,128]{1,0:T(8,128)(2,1)S(1)} collective-permute-done((bf16[512,128]{1,0:T(8,128)(2,1)S(1)}, bf16[512,128]{1,0:T(8,128)(2,1)S(1)}, u32[]{:S(2)}, u32[]{:S(2)}) %collective-permute-start.24) | collective-permute-done | bytes 131104 | tf_op jit(solution)/shard_map/ppermute | solution.py:314
  59.7 1.4 %collective-permute-start.28 = (bf16[512,128]{1,0:T(8,128)(2,1)S(1)}, bf16[512,128]{1,0:T(8,128)(2,1)S(1)}, u32[]{:S(2)}, u32[]{:S(2)}) collective-permute-start(bf16[512,128]{1,0:T(8,128)(2,1)S(1)} %get-tuple-element.44.refs_5_.refs_1_), channel_id=1, source_target_pairs={{0,1},{1,2},{2,3},{3,4},{4,5},{5,6},{6,7},{7,0},{8,15},{9,8},{10,9... | collective-permute-start | bytes 393224 | tf_op jit(solution)/shard_map/ppermute | solution.py:325
  61.1 0.6 shard_map.99.refs_2_
  61.7 3.5 %collective-permute-done.25.refs_6_.refs_1_.refs_3_ = bf16[512,128]{1,0:T(8,128)(2,1)S(1)} collective-permute-done((bf16[512,128]{1,0:T(8,128)(2,1)S(1)}, bf16[512,128]{1,0:T(8,128)(2,1)S(1)}, u32[]{:S(2)}, u32[]{:S(2)}) %collective-permute-start.25) | collective-permute-done | bytes 131104 | tf_op jit(solution)/shard_map/ppermute | solution.py:317
  65.7 1.7 %collective-permute-done.28.refs_3_.refs_1_ = bf16[512,128]{1,0:T(8,128)(2,1)S(1)} collective-permute-done((bf16[512,128]{1,0:T(8,128)(2,1)S(1)}, bf16[512,128]{1,0:T(8,128)(2,1)S(1)}, u32[]{:S(2)}, u32[]{:S(2)}) %collective-permute-start.28) | collective-permute-done | bytes 131104 | tf_op jit(solution)/shard_map/ppermute | solution.py:325
  68.4 2.6 %collective-permute-start.30 = (bf16[512,128]{1,0:T(8,128)(2,1)S(1)}, bf16[512,128]{1,0:T(8,128)(2,1)S(1)}, u32[]{:S(2)}, u32[]{:S(2)}) collective-permute-start(bf16[512,128]{1,0:T(8,128)(2,1)S(1)} %get-tuple-element.47), channel_id=1, source_target_pairs={{0,16},{1,17},{2,18},{3,19},{4,20},{5,21},{6,22},{7,23},{8,24},{9,... | collective-permute-start | bytes 393224 | tf_op jit(solution)/shard_map/ppermute | solution.py:317
  72.4 1.6 %collective-permute-done.30.rest_0_ = bf16[512,128]{1,0:T(8,128)(2,1)S(1)} collective-permute-done((bf16[512,128]{1,0:T(8,128)(2,1)S(1)}, bf16[512,128]{1,0:T(8,128)(2,1)S(1)}, u32[]{:S(2)}, u32[]{:S(2)}) %collective-permute-start.30) | collective-permute-done | bytes 131104 | tf_op jit(solution)/shard_map/ppermute | solution.py:317
  74.1 1.0 %shard_map.92 = (bf16[6,512,128]{2,1,0:T(8,128)(2,1)}, f32[8,128]{1,0:T(8,128)S(1)}) custom-call(bf16[512,128]{1,0:T(8,128)(2,1)S(1)} %shard_map.69.refs_1_.refs_5_.refs_0_, bf16[512,128]{1,0:T(8,128)(2,1)S(1)} %get-tuple-element.35.refs_1_.refs_5_, bf16[512,128]{1,0:T(8,128)(2,1)S(1)} %get-tuple-element.38.refs_1_.refs_5_.refs_2_, ...), custom_call_target="tpu_custom_call" | custom-call | bytes 1048576 | tf_op jit(solution)/shard_map/pallas_call | solution.py:39
  75.4 0.8 %shard_map.108 = f32[512,128]{1,0:T(8,128)} custom-call(f32[512,128]{1,0:T(8,128)S(1)} %get-tuple-element.48.refs_0_, bf16[512,128]{1,0:T(8,128)(2,1)S(1)} %collective-permute-done.31.refs_1_, f32[512,128]{1,0:T(8,128)S(1)} %shard_map.107.refs_2_, f32[8,128]{1,0:T(8,128)S(1)} %get-tuple-element.53.refs_3_), custom_call_target="tpu_custom_call" | custom-call | bytes 1048576 | tf_op jit(solution)/shard_map/pallas_call | solution.py:39
  (83 shorter events, 11.4 us)
Async XLA Ops:
  0.7 4.0 %collective-permute-start = (f32[512,128]{1,0:T(8,128)}, f32[512,128]{1,0:T(8,128)S(1)}, u32[]{:S(2)}, u32[]{:S(2)}) collective-permute-start(f32[512,128]{1,0:T(8,128)} %bitcast.4), channel_id=1, source_target_pairs={{0,8},{1,9},{2,10},{3,11},{4,12},{5,13},{6,14},{7,15},{8,0},{9,1},... | collective-permute-start | bytes 786440 | tf_op jit(solution)/shard_map/ppermute | solution.py:314
  3.6 4.0 %collective-permute-start.1 = (bf16[128,1024]{1,0:T(8,128)(2,1)S(1)}, bf16[128,1024]{1,0:T(8,128)(2,1)S(1)}, u32[]{:S(2)}, u32[]{:S(2)}) collective-permute-start(bf16[128,1024]{1,0:T(8,128)(2,1)S(1)} %get-tuple-element.29), channel_id=1, source_target_pairs={{0,8},{1,9},{2,10},{3,11},{4,12},{5,13},{6,14},{7,15},{8,0},{9,1},... | collective-permute-start | bytes 786440 | tf_op jit(solution)/shard_map/ppermute | solution.py:314
  3.8 5.3 %collective-permute-start.2 = (bf16[128,1024]{1,0:T(8,128)(2,1)S(1)}, bf16[128,1024]{1,0:T(8,128)(2,1)S(1)}, u32[]{:S(2)}, u32[]{:S(2)}) collective-permute-start(bf16[128,1024]{1,0:T(8,128)(2,1)S(1)} %get-tuple-element.30), channel_id=1, source_target_pairs={{0,8},{1,9},{2,10},{3,11},{4,12},{5,13},{6,14},{7,15},{8,0},{9,1},... | collective-permute-start | bytes 786440 | tf_op jit(solution)/shard_map/ppermute | solution.py:314
  4.2 5.3 %collective-permute-start.3 = (bf16[128,1024]{1,0:T(8,128)(2,1)S(1)}, bf16[128,1024]{1,0:T(8,128)(2,1)S(1)}, u32[]{:S(2)}, u32[]{:S(2)}) collective-permute-start(bf16[128,1024]{1,0:T(8,128)(2,1)S(1)} %get-tuple-element.31), channel_id=1, source_target_pairs={{0,8},{1,9},{2,10},{3,11},{4,12},{5,13},{6,14},{7,15},{8,0},{9,1},... | collective-permute-start | bytes 786440 | tf_op jit(solution)/shard_map/ppermute | solution.py:314
  4.3 5.2 %collective-permute-start.4 = (bf16[128,1024]{1,0:T(8,128)(2,1)S(1)}, bf16[128,1024]{1,0:T(8,128)(2,1)S(1)}, u32[]{:S(2)}, u32[]{:S(2)}) collective-permute-start(bf16[128,1024]{1,0:T(8,128)(2,1)S(1)} %get-tuple-element.32), channel_id=1, source_target_pairs={{0,8},{1,9},{2,10},{3,11},{4,12},{5,13},{6,14},{7,15},{8,0},{9,1},... | collective-permute-start | bytes 786440 | tf_op jit(solution)/shard_map/ppermute | solution.py:314
  4.9 9.9 %collective-permute-start.6 = (bf16[512,128]{1,0:T(8,128)(2,1)S(1)}, bf16[512,128]{1,0:T(8,128)(2,1)S(1)}, u32[]{:S(2)}, u32[]{:S(2)}) collective-permute-start(bf16[512,128]{1,0:T(8,128)(2,1)S(1)} %shard_map.69.refs_1_.refs_5_.refs_0_), channel_id=1, source_target_pairs={{0,1},{1,2},{2,3},{3,4},{4,5},{5,6},{6,7},{7,0},{8,15},{9,8},{10,9... | collective-permute-start | bytes 393224 | tf_op jit(solution)/shard_map/ppermute | solution.py:325
  7.6 8.2 %collective-permute-start.5 = (bf16[512,128]{1,0:T(8,128)(2,1)S(1)}, bf16[512,128]{1,0:T(8,128)(2,1)S(1)}, u32[]{:S(2)}, u32[]{:S(2)}) collective-permute-start(bf16[512,128]{1,0:T(8,128)(2,1)S(1)} %shard_map.69.refs_1_.refs_5_.refs_0_), channel_id=1, source_target_pairs={{0,2},{1,3},{2,4},{3,5},{4,6},{5,7},{6,0},{7,1},{8,14},{9,15},{10,... | collective-permute-start | bytes 393224 | tf_op jit(solution)/shard_map/ppermute | solution.py:325
  9.2 6.6 %collective-permute-start.7 = (bf16[512,128]{1,0:T(8,128)(2,1)S(1)}, bf16[512,128]{1,0:T(8,128)(2,1)S(1)}, u32[]{:S(2)}, u32[]{:S(2)}) collective-permute-start(bf16[512,128]{1,0:T(8,128)(2,1)S(1)} %shard_map.69.refs_1_.refs_5_.refs_0_), channel_id=1, source_target_pairs={{0,16},{1,17},{2,18},{3,19},{4,20},{5,21},{6,22},{7,23},{8,24},{9,... | collective-permute-start | bytes 393224 | tf_op jit(solution)/shard_map/ppermute | solution.py:317
  16.1 1.4 %collective-permute-start.8 = (bf16[512,128]{1,0:T(8,128)(2,1)S(1)}, bf16[512,128]{1,0:T(8,128)(2,1)S(1)}, u32[]{:S(2)}, u32[]{:S(2)}) collective-permute-start(bf16[512,128]{1,0:T(8,128)(2,1)S(1)} %shard_map.74.mine_ref), channel_id=1, source_target_pairs={{0,8},{1,9},{2,10},{3,11},{4,12},{5,13},{6,14},{7,15},{8,0},{9,1},... | collective-permute-start | bytes 393224 | tf_op jit(solution)/shard_map/ppermute | solution.py:314
  17.7 8.4 %collective-permute-start.11 = (bf16[512,128]{1,0:T(8,128)(2,1)S(1)}, bf16[512,128]{1,0:T(8,128)(2,1)S(1)}, u32[]{:S(2)}, u32[]{:S(2)}) collective-permute-start(bf16[512,128]{1,0:T(8,128)(2,1)S(1)} %get-tuple-element.35.refs_1_.refs_5_), channel_id=1, source_target_pairs={{0,1},{1,2},{2,3},{3,4},{4,5},{5,6},{6,7},{7,0},{8,15},{9,8},{10,9... | collective-permute-start | bytes 393224 | tf_op jit(solution)/shard_map/ppermute | solution.py:325
  18.9 7.5 %collective-permute-start.10 = (bf16[512,128]{1,0:T(8,128)(2,1)S(1)}, bf16[512,128]{1,0:T(8,128)(2,1)S(1)}, u32[]{:S(2)}, u32[]{:S(2)}) collective-permute-start(bf16[512,128]{1,0:T(8,128)(2,1)S(1)} %get-tuple-element.35.refs_1_.refs_5_), channel_id=1, source_target_pairs={{0,2},{1,3},{2,4},{3,5},{4,6},{5,7},{6,0},{7,1},{8,14},{9,15},{10,... | collective-permute-start | bytes 393224 | tf_op jit(solution)/shard_map/ppermute | solution.py:325
  19.2 7.2 %collective-permute-start.9 = (bf16[512,128]{1,0:T(8,128)(2,1)S(1)}, bf16[512,128]{1,0:T(8,128)(2,1)S(1)}, u32[]{:S(2)}, u32[]{:S(2)}) collective-permute-start(bf16[512,128]{1,0:T(8,128)(2,1)S(1)} %get-tuple-element.36), channel_id=1, source_target_pairs={{0,16},{1,17},{2,18},{3,19},{4,20},{5,21},{6,22},{7,23},{8,24},{9,... | collective-permute-start | bytes 393224 | tf_op jit(solution)/shard_map/ppermute | solution.py:317
  26.7 1.4 %collective-permute-start.12 = (bf16[512,128]{1,0:T(8,128)(2,1)S(1)}, bf16[512,128]{1,0:T(8,128)(2,1)S(1)}, u32[]{:S(2)}, u32[]{:S(2)}) collective-permute-start(bf16[512,128]{1,0:T(8,128)(2,1)S(1)} %shard_map.78.mine_ref), channel_id=1, source_target_pairs={{0,8},{1,9},{2,10},{3,11},{4,12},{5,13},{6,14},{7,15},{8,0},{9,1},... | collective-permute-start | bytes 393224 | tf_op jit(solution)/shard_map/ppermute | solution.py:314
  28.3 7.7 %collective-permute-start.14 = (bf16[512,128]{1,0:T(8,128)(2,1)S(1)}, bf16[512,128]{1,0:T(8,128)(2,1)S(1)}, u32[]{:S(2)}, u32[]{:S(2)}) collective-permute-start(bf16[512,128]{1,0:T(8,128)(2,1)S(1)} %get-tuple-element.38.refs_1_.refs_5_.refs_2_), channel_id=1, source_target_pairs={{0,1},{1,2},{2,3},{3,4},{4,5},{5,6},{6,7},{7,0},{8,15},{9,8},{10,9... | collective-permute-start | bytes 393224 | tf_op jit(solution)/shard_map/ppermute | solution.py:325
  30.1 7.0 %collective-permute-start.13 = (bf16[512,128]{1,0:T(8,128)(2,1)S(1)}, bf16[512,128]{1,0:T(8,128)(2,1)S(1)}, u32[]{:S(2)}, u32[]{:S(2)}) collective-permute-start(bf16[512,128]{1,0:T(8,128)(2,1)S(1)} %get-tuple-element.38.refs_1_.refs_5_.refs_2_), channel_id=1, source_target_pairs={{0,2},{1,3},{2,4},{3,5},{4,6},{5,7},{6,0},{7,1},{8,14},{9,15},{10,... | collective-permute-start | bytes 393224 | tf_op jit(solution)/shard_map/ppermute | solution.py:325
  30.5 6.6 %collective-permute-start.15 = (bf16[512,128]{1,0:T(8,128)(2,1)S(1)}, bf16[512,128]{1,0:T(8,128)(2,1)S(1)}, u32[]{:S(2)}, u32[]{:S(2)}) collective-permute-start(bf16[512,128]{1,0:T(8,128)(2,1)S(1)} %get-tuple-element.39), channel_id=1, source_target_pairs={{0,16},{1,17},{2,18},{3,19},{4,20},{5,21},{6,22},{7,23},{8,24},{9,... | collective-permute-start | bytes 393224 | tf_op jit(solution)/shard_map/ppermute | solution.py:317
  37.3 1.4 %collective-permute-start.16 = (bf16[512,128]{1,0:T(8,128)(2,1)S(1)}, bf16[512,128]{1,0:T(8,128)(2,1)S(1)}, u32[]{:S(2)}, u32[]{:S(2)}) collective-permute-start(bf16[512,128]{1,0:T(8,128)(2,1)S(1)} %shard_map.82.mine_ref), channel_id=1, source_target_pairs={{0,8},{1,9},{2,10},{3,11},{4,12},{5,13},{6,14},{7,15},{8,0},{9,1},... | collective-permute-start | bytes 393224 | tf_op jit(solution)/shard_map/ppermute | solution.py:314
  39.0 7.7 %collective-permute-start.18 = (bf16[512,128]{1,0:T(8,128)(2,1)S(1)}, bf16[512,128]{1,0:T(8,128)(2,1)S(1)}, u32[]{:S(2)}, u32[]{:S(2)}) collective-permute-start(bf16[512,128]{1,0:T(8,128)(2,1)S(1)} %get-tuple-element.40.refs_1_.refs_5_.refs_3_), channel_id=1, source_target_pairs={{0,1},{1,2},{2,3},{3,4},{4,5},{5,6},{6,7},{7,0},{8,15},{9,8},{10,9... | collective-permute-start | bytes 393224 | tf_op jit(solution)/shard_map/ppermute | solution.py:325
  40.0 7.0 %collective-permute-start.17 = (bf16[512,128]{1,0:T(8,128)(2,1)S(1)}, bf16[512,128]{1,0:T(8,128)(2,1)S(1)}, u32[]{:S(2)}, u32[]{:S(2)}) collective-permute-start(bf16[512,128]{1,0:T(8,128)(2,1)S(1)} %get-tuple-element.40.refs_1_.refs_5_.refs_3_), channel_id=1, source_target_pairs={{0,2},{1,3},{2,4},{3,5},{4,6},{5,7},{6,0},{7,1},{8,14},{9,15},{10,... | collective-permute-start | bytes 393224 | tf_op jit(solution)/shard_map/ppermute | solution.py:325
  40.0 7.0 %collective-permute-start.19 = (bf16[512,128]{1,0:T(8,128)(2,1)S(1)}, bf16[512,128]{1,0:T(8,128)(2,1)S(1)}, u32[]{:S(2)}, u32[]{:S(2)}) collective-permute-start(bf16[512,128]{1,0:T(8,128)(2,1)S(1)} %get-tuple-element.41), channel_id=1, source_target_pairs={{0,16},{1,17},{2,18},{3,19},{4,20},{5,21},{6,22},{7,23},{8,24},{9,... | collective-permute-start | bytes 393224 | tf_op jit(solution)/shard_map/ppermute | solution.py:317
  47.3 1.4 %collective-permute-start.20 = (bf16[512,128]{1,0:T(8,128)(2,1)S(1)}, bf16[512,128]{1,0:T(8,128)(2,1)S(1)}, u32[]{:S(2)}, u32[]{:S(2)}) collective-permute-start(bf16[512,128]{1,0:T(8,128)(2,1)S(1)} %shard_map.86.mine_ref), channel_id=1, source_target_pairs={{0,8},{1,9},{2,10},{3,11},{4,12},{5,13},{6,14},{7,15},{8,0},{9,1},... | collective-permute-start | bytes 393224 | tf_op jit(solution)/shard_map/ppermute | solution.py:314
  49.0 8.1 %collective-permute-start.22 = (bf16[512,128]{1,0:T(8,128)(2,1)S(1)}, bf16[512,128]{1,0:T(8,128)(2,1)S(1)}, u32[]{:S(2)}, u32[]{:S(2)}) collective-permute-start(bf16[512,128]{1,0:T(8,128)(2,1)S(1)} %get-tuple-element.42.refs_1_.refs_4_.refs_5_), channel_id=1, source_target_pairs={{0,1},{1,2},{2,3},{3,4},{4,5},{5,6},{6,7},{7,0},{8,15},{9,8},{10,9... | collective-permute-start | bytes 393224 | tf_op jit(solution)/shard_map/ppermute | solution.py:325
  50.6 7.0 %collective-permute-start.21 = (bf16[512,128]{1,0:T(8,128)(2,1)S(1)}, bf16[512,128]{1,0:T(8,128)(2,1)S(1)}, u32[]{:S(2)}, u32[]{:S(2)}) collective-permute-start(bf16[512,128]{1,0:T(8,128)(2,1)S(1)} %get-tuple-element.42.refs_1_.refs_4_.refs_5_), channel_id=1, source_target_pairs={{0,2},{1,3},{2,4},{3,5},{4,6},{5,7},{6,0},{7,1},{8,14},{9,15},{10,... | collective-permute-start | bytes 393224 | tf_op jit(solution)/shard_map/ppermute | solution.py:325
  51.0 6.7 %collective-permute-start.23 = (bf16[512,128]{1,0:T(8,128)(2,1)S(1)}, bf16[512,128]{1,0:T(8,128)(2,1)S(1)}, u32[]{:S(2)}, u32[]{:S(2)}) collective-permute-start(bf16[512,128]{1,0:T(8,128)(2,1)S(1)} %get-tuple-element.43), channel_id=1, source_target_pairs={{0,16},{1,17},{2,18},{3,19},{4,20},{5,21},{6,22},{7,23},{8,24},{9,... | collective-permute-start | bytes 393224 | tf_op jit(solution)/shard_map/ppermute | solution.py:317
  58.0 1.4 %collective-permute-start.24 = (bf16[512,128]{1,0:T(8,128)(2,1)S(1)}, bf16[512,128]{1,0:T(8,128)(2,1)S(1)}, u32[]{:S(2)}, u32[]{:S(2)}) collective-permute-start(bf16[512,128]{1,0:T(8,128)(2,1)S(1)} %shard_map.90.mine_ref), channel_id=1, source_target_pairs={{0,8},{1,9},{2,10},{3,11},{4,12},{5,13},{6,14},{7,15},{8,0},{9,1},... | collective-permute-start | bytes 393224 | tf_op jit(solution)/shard_map/ppermute | solution.py:314
  59.6 5.6 %collective-permute-start.25 = (bf16[512,128]{1,0:T(8,128)(2,1)S(1)}, bf16[512,128]{1,0:T(8,128)(2,1)S(1)}, u32[]{:S(2)}, u32[]{:S(2)}) collective-permute-start(bf16[512,128]{1,0:T(8,128)(2,1)S(1)} %get-tuple-element.45), channel_id=1, source_target_pairs={{0,16},{1,17},{2,18},{3,19},{4,20},{5,21},{6,22},{7,23},{8,24},{9,... | collective-permute-start | bytes 393224 | tf_op jit(solution)/shard_map/ppermute | solution.py:317
  59.7 7.7 %collective-permute-start.28 = (bf16[512,128]{1,0:T(8,128)(2,1)S(1)}, bf16[512,128]{1,0:T(8,128)(2,1)S(1)}, u32[]{:S(2)}, u32[]{:S(2)}) collective-permute-start(bf16[512,128]{1,0:T(8,128)(2,1)S(1)} %get-tuple-element.44.refs_5_.refs_1_), channel_id=1, source_target_pairs={{0,1},{1,2},{2,3},{3,4},{4,5},{5,6},{6,7},{7,0},{8,15},{9,8},{10,9... | collective-permute-start | bytes 393224 | tf_op jit(solution)/shard_map/ppermute | solution.py:325
  61.1 7.0 %collective-permute-start.29 = (bf16[512,128]{1,0:T(8,128)(2,1)S(1)}, bf16[512,128]{1,0:T(8,128)(2,1)S(1)}, u32[]{:S(2)}, u32[]{:S(2)}) collective-permute-start(bf16[512,128]{1,0:T(8,128)(2,1)S(1)} %get-tuple-element.44.refs_5_.refs_1_), channel_id=1, source_target_pairs={{0,2},{1,3},{2,4},{3,5},{4,6},{5,7},{6,0},{7,1},{8,14},{9,15},{10,... | collective-permute-start | bytes 393224 | tf_op jit(solution)/shard_map/ppermute | solution.py:325
  65.2 7.0 %collective-permute-start.27 = (bf16[512,128]{1,0:T(8,128)(2,1)S(1)}, bf16[512,128]{1,0:T(8,128)(2,1)S(1)}, u32[]{:S(2)}, u32[]{:S(2)}) collective-permute-start(bf16[512,128]{1,0:T(8,128)(2,1)S(1)} %collective-permute-done.25.refs_6_.refs_1_.refs_3_), channel_id=1, source_target_pairs={{0,8},{1,9},{2,10},{3,11},{4,12},{5,13},{6,14},{7,15},{8,0},{9,1},... | collective-permute-start | bytes 393224 | tf_op jit(solution)/shard_map/ppermute | solution.py:325
  65.2 7.1 %collective-permute-start.26 = (bf16[512,128]{1,0:T(8,128)(2,1)S(1)}, bf16[512,128]{1,0:T(8,128)(2,1)S(1)}, u32[]{:S(2)}, u32[]{:S(2)}) collective-permute-start(bf16[512,128]{1,0:T(8,128)(2,1)S(1)} %collective-permute-done.25.refs_6_.refs_1_.refs_3_), channel_id=1, source_target_pairs={{0,8},{1,9},{2,10},{3,11},{4,12},{5,13},{6,14},{7,15},{8,0},{9,1},... | collective-permute-start | bytes 393224 | tf_op jit(solution)/shard_map/ppermute | solution.py:325
  68.4 5.6 %collective-permute-start.30 = (bf16[512,128]{1,0:T(8,128)(2,1)S(1)}, bf16[512,128]{1,0:T(8,128)(2,1)S(1)}, u32[]{:S(2)}, u32[]{:S(2)}) collective-permute-start(bf16[512,128]{1,0:T(8,128)(2,1)S(1)} %get-tuple-element.47), channel_id=1, source_target_pairs={{0,16},{1,17},{2,18},{3,19},{4,20},{5,21},{6,22},{7,23},{8,24},{9,... | collective-permute-start | bytes 393224 | tf_op jit(solution)/shard_map/ppermute | solution.py:317
  72.0 3.1 %collective-permute-start.32 = (bf16[512,128]{1,0:T(8,128)(2,1)S(1)}, bf16[512,128]{1,0:T(8,128)(2,1)S(1)}, u32[]{:S(2)}, u32[]{:S(2)}) collective-permute-start(bf16[512,128]{1,0:T(8,128)(2,1)S(1)} %get-tuple-element.52), channel_id=1, source_target_pairs={{0,8},{1,9},{2,10},{3,11},{4,12},{5,13},{6,14},{7,15},{8,0},{9,1},... | collective-permute-start | bytes 393224 | tf_op jit(solution)/shard_map/ppermute | solution.py:314
  (5 other events, 14.4 us)

commit v13 on v12

--- a/solution.py
+++ b/solution.py
@@ -226,6 +226,11 @@
     out_ref[...] = early_ref[...] + half(far_ref, block_ref, which)
 
 
+def both_body(which, near_ref, far_ref, block_ref, even_in_ref, odd_in_ref, even_ref, odd_ref):
+    even_ref[...] = even_in_ref[...] + half(near_ref, block_ref, which)
+    odd_ref[...] = odd_in_ref[...] + half(far_ref, block_ref, which)
+
+
 def share_body(step, steps, even_ref, odd_ref, *rest):
     *field, keep_ref, send_ref = rest
     core, pair = place()
@@ -386,21 +391,32 @@
                 done = step + 2 - steps
                 windows = halo(current_in, 1, done), halo(current_in, 2, done)
             more = step < rounds - 1
-            even, *next_field = call(
-                functools.partial(going_on, 1 + more, functools.partial(even_body, step, pairs)),
-                [field_shape] + [current_shape] * more,
-                received + ([field_in] + past) * more,
-            )
             alone = functools.partial(only, ending, ending, 1)
             (odd_early,) = call(
                 functools.partial(alone, odd_early_body), [field_shape], [own, current]
             )
-            for which, block in enumerate((first, second)):
-                (odd_early,) = call(
-                    functools.partial(alone, functools.partial(odd_body, which)),
-                    [field_shape],
-                    [far, block, odd_early],
+            if more:
+                even, *next_field = call(
+                    functools.partial(going_on, 1 + more, functools.partial(even_body, step, pairs)),
+                    [field_shape] + [current_shape] * more,
+                    received + ([field_in] + past) * more,
                 )
+                for which, block in enumerate((first, second)):
+                    (odd_early,) = call(
+                        functools.partial(alone, functools.partial(odd_body, which)),
+                        [field_shape],
+                        [far, block, odd_early],
+                    )
+            else:
+                even, next_field = early, []
+                for which, block in enumerate((first, second)):
+                    even, odd_early = call(
+                        functools.partial(
+                            only, ending, ending, 2, functools.partial(both_body, which)
+                        ),
+                        [field_shape, field_shape],
+                        [near, far, block, even, odd_early],
+                    )
             mine, send = call(
                 functools.partial(share_body, step, steps),
                 [field_shape, current_shape],
@@ -412,7 +428,7 @@
                 [mine, swapped(send)] + [result] * (step >= steps),
                 after=collected,
             )
-            field = next_field[0] if more else None
+            field = next_field[0] if next_field else None
             current, going = current_in, field
     return (out, result[None])
 

time: 76.4 us -> 76.4 us (level)
    pallas_call x40 -> x38, Pallas kernels: 11.1 us -> 11 us  [call(): pl.pallas_call(body, out_shape=tuple(outs), in_specs=specs, out_specs=tup...]
where the time goes in v13:
time: 76.4 us; the launch traced here: 76.2 us
  waiting for transfers between devices  43.8 us (57%)
  starting transfers between devices  17.8 us (23%)
  Pallas kernels  12.8 us (17%)
  between operations  1.07 us (1%)
    ppermute x14, waiting for transfers between devices, halo(): return lax.ppermute(value, AXES, everyone(move))  31.8 us
    ppermute x14, starting transfers between devices, halo(): return lax.ppermute(value, AXES, everyone(move))  12.9 us
    pallas_call x38, Pallas kernels, call(): pl.pallas_call(body, out_shape=tuple(outs), in_specs=specs, out_specs=tup...  11 us
    ppermute x12, waiting for transfers between devices, swapped(): return lax.ppermute(value, AXES, everyone(lambda d, s: (d ^ 1, s)))  6.85 us
    ppermute x7, waiting for transfers between devices, pair_moved(): lax.ppermute(value, AXES, everyone(lambda d, s: ((d + 2 * hop) % lags, s)))  5.14 us
    ppermute x7, starting transfers between devices, pair_moved(): lax.ppermute(value, AXES, everyone(lambda d, s: ((d + 2 * hop) % lags, s)))  2.7 us
    ppermute x12, starting transfers between devices, swapped(): return lax.ppermute(value, AXES, everyone(lambda d, s: (d ^ 1, s)))  2.21 us
    pallas_call x1, Pallas kernels, spread(): pl.pallas_call(functools.partial(spread_body, groups), out_shape=(matrix(...  1.74 us
  transfers between devices with their start and end apart: 33, of which 19 were waited for; matrix products, arithmetic and copies ran while one was open for 0% of the time, Pallas kernels for 13%

profile of v13, /device:TPU:0, one launch (start us, length us, event | category | flops | bytes accessed | tf_op | source)
XLA Modules:
  0.0 76.2 jit_solution(14417907276287711471)
XLA Ops:
  1.2 0.7 copy-done.3
  1.9 1.7 %shard_map.70 = (bf16[512,1024]{1,0:T(8,128)(2,1)S(1)}, bf16[512,512]{1,0:T(8,128)(2,1)S(1)}, bf16[128,1024]{1,0:T(8,128)(2,1)S(1)}, bf16[128,1024]{1,0:T(8,128)...) custom-call(s32[4,16]{1,0:T(4,128)S(1)} %bitcast.8, bf16[4,16,128,128]{3,2,1,0:T(8,128)(2,1)} %bitcast.9), custom_call_target="tpu_custom_call" | custom-call | bytes 1048576 | tf_op jit(solution)/shard_map/pallas_call | solution.py:114
  4.9 2.7 %collective-permute-start.6 = (bf16[512,128]{1,0:T(8,128)(2,1)S(1)}, bf16[512,128]{1,0:T(8,128)(2,1)S(1)}, u32[]{:S(2)}, u32[]{:S(2)}) collective-permute-start(bf16[512,128]{1,0:T(8,128)(2,1)S(1)} %shard_map.69.refs_1_.refs_5_.refs_0_), channel_id=1, source_target_pairs={{0,1},{1,2},{2,3},{3,4},{4,5},{5,6},{6,7},{7,0},{8,15},{9,8},{10,9... | collective-permute-start | bytes 393224 | tf_op jit(solution)/shard_map/ppermute | solution.py:330
  7.6 1.6 %collective-permute-start.5 = (bf16[512,128]{1,0:T(8,128)(2,1)S(1)}, bf16[512,128]{1,0:T(8,128)(2,1)S(1)}, u32[]{:S(2)}, u32[]{:S(2)}) collective-permute-start(bf16[512,128]{1,0:T(8,128)(2,1)S(1)} %shard_map.69.refs_1_.refs_5_.refs_0_), channel_id=1, source_target_pairs={{0,2},{1,3},{2,4},{3,5},{4,6},{5,7},{6,0},{7,1},{8,14},{9,15},{10,... | collective-permute-start | bytes 393224 | tf_op jit(solution)/shard_map/ppermute | solution.py:330
  9.7 5.2 %collective-permute-done.6.refs_1_.refs_3_ = bf16[512,128]{1,0:T(8,128)(2,1)S(1)} collective-permute-done((bf16[512,128]{1,0:T(8,128)(2,1)S(1)}, bf16[512,128]{1,0:T(8,128)(2,1)S(1)}, u32[]{:S(2)}, u32[]{:S(2)}) %collective-permute-start.6) | collective-permute-done | bytes 131104 | tf_op jit(solution)/shard_map/ppermute | solution.py:330
  15.2 0.6 collective-permute-done.5.second_ref.refs_4_
  16.2 1.2 %collective-permute-done.8.other_ref = bf16[512,128]{1,0:T(8,128)(2,1)S(1)} collective-permute-done((bf16[512,128]{1,0:T(8,128)(2,1)S(1)}, bf16[512,128]{1,0:T(8,128)(2,1)S(1)}, u32[]{:S(2)}, u32[]{:S(2)}) %collective-permute-start.8) | collective-permute-done | bytes 131104 | tf_op jit(solution)/shard_map/ppermute | solution.py:319
  17.7 1.3 %collective-permute-start.11 = (bf16[512,128]{1,0:T(8,128)(2,1)S(1)}, bf16[512,128]{1,0:T(8,128)(2,1)S(1)}, u32[]{:S(2)}, u32[]{:S(2)}) collective-permute-start(bf16[512,128]{1,0:T(8,128)(2,1)S(1)} %get-tuple-element.39.refs_1_.refs_5_), channel_id=1, source_target_pairs={{0,1},{1,2},{2,3},{3,4},{4,5},{5,6},{6,7},{7,0},{8,15},{9,8},{10,9... | collective-permute-start | bytes 393224 | tf_op jit(solution)/shard_map/ppermute | solution.py:330
  19.2 0.6 shard_map.76.refs_2_
  19.8 6.3 %collective-permute-done.11.refs_1_.refs_3_ = bf16[512,128]{1,0:T(8,128)(2,1)S(1)} collective-permute-done((bf16[512,128]{1,0:T(8,128)(2,1)S(1)}, bf16[512,128]{1,0:T(8,128)(2,1)S(1)}, u32[]{:S(2)}, u32[]{:S(2)}) %collective-permute-start.11) | collective-permute-done | bytes 131104 | tf_op jit(solution)/shard_map/ppermute | solution.py:330
  26.8 1.3 %collective-permute-done.12.other_ref = bf16[512,128]{1,0:T(8,128)(2,1)S(1)} collective-permute-done((bf16[512,128]{1,0:T(8,128)(2,1)S(1)}, bf16[512,128]{1,0:T(8,128)(2,1)S(1)}, u32[]{:S(2)}, u32[]{:S(2)}) %collective-permute-start.12) | collective-permute-done | bytes 131104 | tf_op jit(solution)/shard_map/ppermute | solution.py:319
  28.3 1.7 %collective-permute-start.14 = (bf16[512,128]{1,0:T(8,128)(2,1)S(1)}, bf16[512,128]{1,0:T(8,128)(2,1)S(1)}, u32[]{:S(2)}, u32[]{:S(2)}) collective-permute-start(bf16[512,128]{1,0:T(8,128)(2,1)S(1)} %get-tuple-element.42.refs_1_.refs_5_.refs_2_), channel_id=1, source_target_pairs={{0,1},{1,2},{2,3},{3,4},{4,5},{5,6},{6,7},{7,0},{8,15},{9,8},{10,9... | collective-permute-start | bytes 393224 | tf_op jit(solution)/shard_map/ppermute | solution.py:330
  30.5 0.6 shard_map.80.refs_2_
  31.1 5.0 %collective-permute-done.14.refs_1_.refs_3_ = bf16[512,128]{1,0:T(8,128)(2,1)S(1)} collective-permute-done((bf16[512,128]{1,0:T(8,128)(2,1)S(1)}, bf16[512,128]{1,0:T(8,128)(2,1)S(1)}, u32[]{:S(2)}, u32[]{:S(2)}) %collective-permute-start.14) | collective-permute-done | bytes 131104 | tf_op jit(solution)/shard_map/ppermute | solution.py:330
  36.4 0.7 collective-permute-done.13.second_ref.refs_4_
  37.4 1.3 %collective-permute-done.16.other_ref = bf16[512,128]{1,0:T(8,128)(2,1)S(1)} collective-permute-done((bf16[512,128]{1,0:T(8,128)(2,1)S(1)}, bf16[512,128]{1,0:T(8,128)(2,1)S(1)}, u32[]{:S(2)}, u32[]{:S(2)}) %collective-permute-start.16) | collective-permute-done | bytes 131104 | tf_op jit(solution)/shard_map/ppermute | solution.py:319
  39.0 1.0 %collective-permute-start.18 = (bf16[512,128]{1,0:T(8,128)(2,1)S(1)}, bf16[512,128]{1,0:T(8,128)(2,1)S(1)}, u32[]{:S(2)}, u32[]{:S(2)}) collective-permute-start(bf16[512,128]{1,0:T(8,128)(2,1)S(1)} %get-tuple-element.44.refs_1_.refs_5_.refs_3_), channel_id=1, source_target_pairs={{0,1},{1,2},{2,3},{3,4},{4,5},{5,6},{6,7},{7,0},{8,15},{9,8},{10,9... | collective-permute-start | bytes 393224 | tf_op jit(solution)/shard_map/ppermute | solution.py:330
  40.0 0.6 shard_map.84.refs_2_
  40.6 6.1 %collective-permute-done.18.refs_1_.refs_3_ = bf16[512,128]{1,0:T(8,128)(2,1)S(1)} collective-permute-done((bf16[512,128]{1,0:T(8,128)(2,1)S(1)}, bf16[512,128]{1,0:T(8,128)(2,1)S(1)}, u32[]{:S(2)}, u32[]{:S(2)}) %collective-permute-start.18) | collective-permute-done | bytes 131104 | tf_op jit(solution)/shard_map/ppermute | solution.py:330
  47.4 1.3 %collective-permute-done.20.other_ref = bf16[512,128]{1,0:T(8,128)(2,1)S(1)} collective-permute-done((bf16[512,128]{1,0:T(8,128)(2,1)S(1)}, bf16[512,128]{1,0:T(8,128)(2,1)S(1)}, u32[]{:S(2)}, u32[]{:S(2)}) %collective-permute-start.20) | collective-permute-done | bytes 131104 | tf_op jit(solution)/shard_map/ppermute | solution.py:319
  49.0 1.7 %collective-permute-start.22 = (bf16[512,128]{1,0:T(8,128)(2,1)S(1)}, bf16[512,128]{1,0:T(8,128)(2,1)S(1)}, u32[]{:S(2)}, u32[]{:S(2)}) collective-permute-start(bf16[512,128]{1,0:T(8,128)(2,1)S(1)} %get-tuple-element.46.refs_1_.refs_4_.refs_5_), channel_id=1, source_target_pairs={{0,1},{1,2},{2,3},{3,4},{4,5},{5,6},{6,7},{7,0},{8,15},{9,8},{10,9... | collective-permute-start | bytes 393224 | tf_op jit(solution)/shard_map/ppermute | solution.py:330
  51.0 0.6 shard_map.88.refs_2_
  51.6 5.5 %collective-permute-done.22.refs_1_.refs_3_ = bf16[512,128]{1,0:T(8,128)(2,1)S(1)} collective-permute-done((bf16[512,128]{1,0:T(8,128)(2,1)S(1)}, bf16[512,128]{1,0:T(8,128)(2,1)S(1)}, u32[]{:S(2)}, u32[]{:S(2)}) %collective-permute-start.22) | collective-permute-done | bytes 131104 | tf_op jit(solution)/shard_map/ppermute | solution.py:330
  58.0 1.3 %collective-permute-done.24.other_ref = bf16[512,128]{1,0:T(8,128)(2,1)S(1)} collective-permute-done((bf16[512,128]{1,0:T(8,128)(2,1)S(1)}, bf16[512,128]{1,0:T(8,128)(2,1)S(1)}, u32[]{:S(2)}, u32[]{:S(2)}) %collective-permute-start.24) | collective-permute-done | bytes 131104 | tf_op jit(solution)/shard_map/ppermute | solution.py:319
  59.7 1.4 %collective-permute-start.28 = (bf16[512,128]{1,0:T(8,128)(2,1)S(1)}, bf16[512,128]{1,0:T(8,128)(2,1)S(1)}, u32[]{:S(2)}, u32[]{:S(2)}) collective-permute-start(bf16[512,128]{1,0:T(8,128)(2,1)S(1)} %get-tuple-element.48.refs_5_.refs_1_), channel_id=1, source_target_pairs={{0,1},{1,2},{2,3},{3,4},{4,5},{5,6},{6,7},{7,0},{8,15},{9,8},{10,9... | collective-permute-start | bytes 393224 | tf_op jit(solution)/shard_map/ppermute | solution.py:330
  61.1 0.6 shard_map.97.refs_2_
  61.7 3.5 %collective-permute-done.25.refs_6_.refs_1_.refs_3_ = bf16[512,128]{1,0:T(8,128)(2,1)S(1)} collective-permute-done((bf16[512,128]{1,0:T(8,128)(2,1)S(1)}, bf16[512,128]{1,0:T(8,128)(2,1)S(1)}, u32[]{:S(2)}, u32[]{:S(2)}) %collective-permute-start.25) | collective-permute-done | bytes 131104 | tf_op jit(solution)/shard_map/ppermute | solution.py:322
  65.7 1.7 %collective-permute-done.28.refs_3_.refs_1_ = bf16[512,128]{1,0:T(8,128)(2,1)S(1)} collective-permute-done((bf16[512,128]{1,0:T(8,128)(2,1)S(1)}, bf16[512,128]{1,0:T(8,128)(2,1)S(1)}, u32[]{:S(2)}, u32[]{:S(2)}) %collective-permute-start.28) | collective-permute-done | bytes 131104 | tf_op jit(solution)/shard_map/ppermute | solution.py:330
  68.4 2.6 %collective-permute-start.30 = (bf16[512,128]{1,0:T(8,128)(2,1)S(1)}, bf16[512,128]{1,0:T(8,128)(2,1)S(1)}, u32[]{:S(2)}, u32[]{:S(2)}) collective-permute-start(bf16[512,128]{1,0:T(8,128)(2,1)S(1)} %get-tuple-element.55), channel_id=1, source_target_pairs={{0,16},{1,17},{2,18},{3,19},{4,20},{5,21},{6,22},{7,23},{8,24},{9,... | collective-permute-start | bytes 393224 | tf_op jit(solution)/shard_map/ppermute | solution.py:322
  72.3 1.6 %collective-permute-done.30.rest_0_ = bf16[512,128]{1,0:T(8,128)(2,1)S(1)} collective-permute-done((bf16[512,128]{1,0:T(8,128)(2,1)S(1)}, bf16[512,128]{1,0:T(8,128)(2,1)S(1)}, u32[]{:S(2)}, u32[]{:S(2)}) %collective-permute-start.30) | collective-permute-done | bytes 131104 | tf_op jit(solution)/shard_map/ppermute | solution.py:322
  74.1 1.0 %shard_map.92 = (bf16[6,512,128]{2,1,0:T(8,128)(2,1)}, f32[8,128]{1,0:T(8,128)S(1)}) custom-call(bf16[512,128]{1,0:T(8,128)(2,1)S(1)} %shard_map.69.refs_1_.refs_5_.refs_0_, bf16[512,128]{1,0:T(8,128)(2,1)S(1)} %get-tuple-element.39.refs_1_.refs_5_, bf16[512,128]{1,0:T(8,128)(2,1)S(1)} %get-tuple-element.42.refs_1_.refs_5_.refs_2_, ...), custom_call_target="tpu_custom_call" | custom-call | bytes 1048576 | tf_op jit(solution)/shard_map/pallas_call | solution.py:39
  75.4 0.8 %shard_map.106 = f32[512,128]{1,0:T(8,128)} custom-call(f32[512,128]{1,0:T(8,128)S(1)} %get-tuple-element.56.refs_0_, bf16[512,128]{1,0:T(8,128)(2,1)S(1)} %collective-permute-done.31.refs_1_, f32[512,128]{1,0:T(8,128)S(1)} %shard_map.105.refs_2_, f32[8,128]{1,0:T(8,128)S(1)} %get-tuple-element.61.refs_3_), custom_call_target="tpu_custom_call" | custom-call | bytes 1048576 | tf_op jit(solution)/shard_map/pallas_call | solution.py:39
  (81 shorter events, 11.3 us)
Async XLA Ops:
  0.7 4.0 %collective-permute-start = (f32[512,128]{1,0:T(8,128)}, f32[512,128]{1,0:T(8,128)S(1)}, u32[]{:S(2)}, u32[]{:S(2)}) collective-permute-start(f32[512,128]{1,0:T(8,128)} %bitcast.4), channel_id=1, source_target_pairs={{0,8},{1,9},{2,10},{3,11},{4,12},{5,13},{6,14},{7,15},{8,0},{9,1},... | collective-permute-start | bytes 786440 | tf_op jit(solution)/shard_map/ppermute | solution.py:319
  3.6 4.0 %collective-permute-start.1 = (bf16[128,1024]{1,0:T(8,128)(2,1)S(1)}, bf16[128,1024]{1,0:T(8,128)(2,1)S(1)}, u32[]{:S(2)}, u32[]{:S(2)}) collective-permute-start(bf16[128,1024]{1,0:T(8,128)(2,1)S(1)} %get-tuple-element.33), channel_id=1, source_target_pairs={{0,8},{1,9},{2,10},{3,11},{4,12},{5,13},{6,14},{7,15},{8,0},{9,1},... | collective-permute-start | bytes 786440 | tf_op jit(solution)/shard_map/ppermute | solution.py:319
  3.8 5.4 %collective-permute-start.2 = (bf16[128,1024]{1,0:T(8,128)(2,1)S(1)}, bf16[128,1024]{1,0:T(8,128)(2,1)S(1)}, u32[]{:S(2)}, u32[]{:S(2)}) collective-permute-start(bf16[128,1024]{1,0:T(8,128)(2,1)S(1)} %get-tuple-element.34), channel_id=1, source_target_pairs={{0,8},{1,9},{2,10},{3,11},{4,12},{5,13},{6,14},{7,15},{8,0},{9,1},... | collective-permute-start | bytes 786440 | tf_op jit(solution)/shard_map/ppermute | solution.py:319
  4.2 5.3 %collective-permute-start.3 = (bf16[128,1024]{1,0:T(8,128)(2,1)S(1)}, bf16[128,1024]{1,0:T(8,128)(2,1)S(1)}, u32[]{:S(2)}, u32[]{:S(2)}) collective-permute-start(bf16[128,1024]{1,0:T(8,128)(2,1)S(1)} %get-tuple-element.35), channel_id=1, source_target_pairs={{0,8},{1,9},{2,10},{3,11},{4,12},{5,13},{6,14},{7,15},{8,0},{9,1},... | collective-permute-start | bytes 786440 | tf_op jit(solution)/shard_map/ppermute | solution.py:319
  4.3 5.2 %collective-permute-start.4 = (bf16[128,1024]{1,0:T(8,128)(2,1)S(1)}, bf16[128,1024]{1,0:T(8,128)(2,1)S(1)}, u32[]{:S(2)}, u32[]{:S(2)}) collective-permute-start(bf16[128,1024]{1,0:T(8,128)(2,1)S(1)} %get-tuple-element.36), channel_id=1, source_target_pairs={{0,8},{1,9},{2,10},{3,11},{4,12},{5,13},{6,14},{7,15},{8,0},{9,1},... | collective-permute-start | bytes 786440 | tf_op jit(solution)/shard_map/ppermute | solution.py:319
  4.9 9.9 %collective-permute-start.6 = (bf16[512,128]{1,0:T(8,128)(2,1)S(1)}, bf16[512,128]{1,0:T(8,128)(2,1)S(1)}, u32[]{:S(2)}, u32[]{:S(2)}) collective-permute-start(bf16[512,128]{1,0:T(8,128)(2,1)S(1)} %shard_map.69.refs_1_.refs_5_.refs_0_), channel_id=1, source_target_pairs={{0,1},{1,2},{2,3},{3,4},{4,5},{5,6},{6,7},{7,0},{8,15},{9,8},{10,9... | collective-permute-start | bytes 393224 | tf_op jit(solution)/shard_map/ppermute | solution.py:330
  7.6 8.2 %collective-permute-start.5 = (bf16[512,128]{1,0:T(8,128)(2,1)S(1)}, bf16[512,128]{1,0:T(8,128)(2,1)S(1)}, u32[]{:S(2)}, u32[]{:S(2)}) collective-permute-start(bf16[512,128]{1,0:T(8,128)(2,1)S(1)} %shard_map.69.refs_1_.refs_5_.refs_0_), channel_id=1, source_target_pairs={{0,2},{1,3},{2,4},{3,5},{4,6},{5,7},{6,0},{7,1},{8,14},{9,15},{10,... | collective-permute-start | bytes 393224 | tf_op jit(solution)/shard_map/ppermute | solution.py:330
  9.2 6.6 %collective-permute-start.7 = (bf16[512,128]{1,0:T(8,128)(2,1)S(1)}, bf16[512,128]{1,0:T(8,128)(2,1)S(1)}, u32[]{:S(2)}, u32[]{:S(2)}) collective-permute-start(bf16[512,128]{1,0:T(8,128)(2,1)S(1)} %shard_map.69.refs_1_.refs_5_.refs_0_), channel_id=1, source_target_pairs={{0,16},{1,17},{2,18},{3,19},{4,20},{5,21},{6,22},{7,23},{8,24},{9,... | collective-permute-start | bytes 393224 | tf_op jit(solution)/shard_map/ppermute | solution.py:322
  16.1 1.4 %collective-permute-start.8 = (bf16[512,128]{1,0:T(8,128)(2,1)S(1)}, bf16[512,128]{1,0:T(8,128)(2,1)S(1)}, u32[]{:S(2)}, u32[]{:S(2)}) collective-permute-start(bf16[512,128]{1,0:T(8,128)(2,1)S(1)} %shard_map.74.mine_ref), channel_id=1, source_target_pairs={{0,8},{1,9},{2,10},{3,11},{4,12},{5,13},{6,14},{7,15},{8,0},{9,1},... | collective-permute-start | bytes 393224 | tf_op jit(solution)/shard_map/ppermute | solution.py:319
  17.7 8.4 %collective-permute-start.11 = (bf16[512,128]{1,0:T(8,128)(2,1)S(1)}, bf16[512,128]{1,0:T(8,128)(2,1)S(1)}, u32[]{:S(2)}, u32[]{:S(2)}) collective-permute-start(bf16[512,128]{1,0:T(8,128)(2,1)S(1)} %get-tuple-element.39.refs_1_.refs_5_), channel_id=1, source_target_pairs={{0,1},{1,2},{2,3},{3,4},{4,5},{5,6},{6,7},{7,0},{8,15},{9,8},{10,9... | collective-permute-start | bytes 393224 | tf_op jit(solution)/shard_map/ppermute | solution.py:330
  18.9 7.5 %collective-permute-start.10 = (bf16[512,128]{1,0:T(8,128)(2,1)S(1)}, bf16[512,128]{1,0:T(8,128)(2,1)S(1)}, u32[]{:S(2)}, u32[]{:S(2)}) collective-permute-start(bf16[512,128]{1,0:T(8,128)(2,1)S(1)} %get-tuple-element.39.refs_1_.refs_5_), channel_id=1, source_target_pairs={{0,2},{1,3},{2,4},{3,5},{4,6},{5,7},{6,0},{7,1},{8,14},{9,15},{10,... | collective-permute-start | bytes 393224 | tf_op jit(solution)/shard_map/ppermute | solution.py:330
  19.2 7.2 %collective-permute-start.9 = (bf16[512,128]{1,0:T(8,128)(2,1)S(1)}, bf16[512,128]{1,0:T(8,128)(2,1)S(1)}, u32[]{:S(2)}, u32[]{:S(2)}) collective-permute-start(bf16[512,128]{1,0:T(8,128)(2,1)S(1)} %get-tuple-element.40), channel_id=1, source_target_pairs={{0,16},{1,17},{2,18},{3,19},{4,20},{5,21},{6,22},{7,23},{8,24},{9,... | collective-permute-start | bytes 393224 | tf_op jit(solution)/shard_map/ppermute | solution.py:322
  26.7 1.4 %collective-permute-start.12 = (bf16[512,128]{1,0:T(8,128)(2,1)S(1)}, bf16[512,128]{1,0:T(8,128)(2,1)S(1)}, u32[]{:S(2)}, u32[]{:S(2)}) collective-permute-start(bf16[512,128]{1,0:T(8,128)(2,1)S(1)} %shard_map.78.mine_ref), channel_id=1, source_target_pairs={{0,8},{1,9},{2,10},{3,11},{4,12},{5,13},{6,14},{7,15},{8,0},{9,1},... | collective-permute-start | bytes 393224 | tf_op jit(solution)/shard_map/ppermute | solution.py:319
  28.3 7.7 %collective-permute-start.14 = (bf16[512,128]{1,0:T(8,128)(2,1)S(1)}, bf16[512,128]{1,0:T(8,128)(2,1)S(1)}, u32[]{:S(2)}, u32[]{:S(2)}) collective-permute-start(bf16[512,128]{1,0:T(8,128)(2,1)S(1)} %get-tuple-element.42.refs_1_.refs_5_.refs_2_), channel_id=1, source_target_pairs={{0,1},{1,2},{2,3},{3,4},{4,5},{5,6},{6,7},{7,0},{8,15},{9,8},{10,9... | collective-permute-start | bytes 393224 | tf_op jit(solution)/shard_map/ppermute | solution.py:330
  30.1 7.0 %collective-permute-start.13 = (bf16[512,128]{1,0:T(8,128)(2,1)S(1)}, bf16[512,128]{1,0:T(8,128)(2,1)S(1)}, u32[]{:S(2)}, u32[]{:S(2)}) collective-permute-start(bf16[512,128]{1,0:T(8,128)(2,1)S(1)} %get-tuple-element.42.refs_1_.refs_5_.refs_2_), channel_id=1, source_target_pairs={{0,2},{1,3},{2,4},{3,5},{4,6},{5,7},{6,0},{7,1},{8,14},{9,15},{10,... | collective-permute-start | bytes 393224 | tf_op jit(solution)/shard_map/ppermute | solution.py:330
  30.5 6.6 %collective-permute-start.15 = (bf16[512,128]{1,0:T(8,128)(2,1)S(1)}, bf16[512,128]{1,0:T(8,128)(2,1)S(1)}, u32[]{:S(2)}, u32[]{:S(2)}) collective-permute-start(bf16[512,128]{1,0:T(8,128)(2,1)S(1)} %get-tuple-element.43), channel_id=1, source_target_pairs={{0,16},{1,17},{2,18},{3,19},{4,20},{5,21},{6,22},{7,23},{8,24},{9,... | collective-permute-start | bytes 393224 | tf_op jit(solution)/shard_map/ppermute | solution.py:322
  37.3 1.4 %collective-permute-start.16 = (bf16[512,128]{1,0:T(8,128)(2,1)S(1)}, bf16[512,128]{1,0:T(8,128)(2,1)S(1)}, u32[]{:S(2)}, u32[]{:S(2)}) collective-permute-start(bf16[512,128]{1,0:T(8,128)(2,1)S(1)} %shard_map.82.mine_ref), channel_id=1, source_target_pairs={{0,8},{1,9},{2,10},{3,11},{4,12},{5,13},{6,14},{7,15},{8,0},{9,1},... | collective-permute-start | bytes 393224 | tf_op jit(solution)/shard_map/ppermute | solution.py:319
  39.0 7.7 %collective-permute-start.18 = (bf16[512,128]{1,0:T(8,128)(2,1)S(1)}, bf16[512,128]{1,0:T(8,128)(2,1)S(1)}, u32[]{:S(2)}, u32[]{:S(2)}) collective-permute-start(bf16[512,128]{1,0:T(8,128)(2,1)S(1)} %get-tuple-element.44.refs_1_.refs_5_.refs_3_), channel_id=1, source_target_pairs={{0,1},{1,2},{2,3},{3,4},{4,5},{5,6},{6,7},{7,0},{8,15},{9,8},{10,9... | collective-permute-start | bytes 393224 | tf_op jit(solution)/shard_map/ppermute | solution.py:330
  40.0 7.0 %collective-permute-start.17 = (bf16[512,128]{1,0:T(8,128)(2,1)S(1)}, bf16[512,128]{1,0:T(8,128)(2,1)S(1)}, u32[]{:S(2)}, u32[]{:S(2)}) collective-permute-start(bf16[512,128]{1,0:T(8,128)(2,1)S(1)} %get-tuple-element.44.refs_1_.refs_5_.refs_3_), channel_id=1, source_target_pairs={{0,2},{1,3},{2,4},{3,5},{4,6},{5,7},{6,0},{7,1},{8,14},{9,15},{10,... | collective-permute-start | bytes 393224 | tf_op jit(solution)/shard_map/ppermute | solution.py:330
  40.0 7.0 %collective-permute-start.19 = (bf16[512,128]{1,0:T(8,128)(2,1)S(1)}, bf16[512,128]{1,0:T(8,128)(2,1)S(1)}, u32[]{:S(2)}, u32[]{:S(2)}) collective-permute-start(bf16[512,128]{1,0:T(8,128)(2,1)S(1)} %get-tuple-element.45), channel_id=1, source_target_pairs={{0,16},{1,17},{2,18},{3,19},{4,20},{5,21},{6,22},{7,23},{8,24},{9,... | collective-permute-start | bytes 393224 | tf_op jit(solution)/shard_map/ppermute | solution.py:322
  47.3 1.4 %collective-permute-start.20 = (bf16[512,128]{1,0:T(8,128)(2,1)S(1)}, bf16[512,128]{1,0:T(8,128)(2,1)S(1)}, u32[]{:S(2)}, u32[]{:S(2)}) collective-permute-start(bf16[512,128]{1,0:T(8,128)(2,1)S(1)} %shard_map.86.mine_ref), channel_id=1, source_target_pairs={{0,8},{1,9},{2,10},{3,11},{4,12},{5,13},{6,14},{7,15},{8,0},{9,1},... | collective-permute-start | bytes 393224 | tf_op jit(solution)/shard_map/ppermute | solution.py:319
  49.0 8.1 %collective-permute-start.22 = (bf16[512,128]{1,0:T(8,128)(2,1)S(1)}, bf16[512,128]{1,0:T(8,128)(2,1)S(1)}, u32[]{:S(2)}, u32[]{:S(2)}) collective-permute-start(bf16[512,128]{1,0:T(8,128)(2,1)S(1)} %get-tuple-element.46.refs_1_.refs_4_.refs_5_), channel_id=1, source_target_pairs={{0,1},{1,2},{2,3},{3,4},{4,5},{5,6},{6,7},{7,0},{8,15},{9,8},{10,9... | collective-permute-start | bytes 393224 | tf_op jit(solution)/shard_map/ppermute | solution.py:330
  50.6 7.0 %collective-permute-start.21 = (bf16[512,128]{1,0:T(8,128)(2,1)S(1)}, bf16[512,128]{1,0:T(8,128)(2,1)S(1)}, u32[]{:S(2)}, u32[]{:S(2)}) collective-permute-start(bf16[512,128]{1,0:T(8,128)(2,1)S(1)} %get-tuple-element.46.refs_1_.refs_4_.refs_5_), channel_id=1, source_target_pairs={{0,2},{1,3},{2,4},{3,5},{4,6},{5,7},{6,0},{7,1},{8,14},{9,15},{10,... | collective-permute-start | bytes 393224 | tf_op jit(solution)/shard_map/ppermute | solution.py:330
  51.0 6.7 %collective-permute-start.23 = (bf16[512,128]{1,0:T(8,128)(2,1)S(1)}, bf16[512,128]{1,0:T(8,128)(2,1)S(1)}, u32[]{:S(2)}, u32[]{:S(2)}) collective-permute-start(bf16[512,128]{1,0:T(8,128)(2,1)S(1)} %get-tuple-element.47), channel_id=1, source_target_pairs={{0,16},{1,17},{2,18},{3,19},{4,20},{5,21},{6,22},{7,23},{8,24},{9,... | collective-permute-start | bytes 393224 | tf_op jit(solution)/shard_map/ppermute | solution.py:322
  58.0 1.4 %collective-permute-start.24 = (bf16[512,128]{1,0:T(8,128)(2,1)S(1)}, bf16[512,128]{1,0:T(8,128)(2,1)S(1)}, u32[]{:S(2)}, u32[]{:S(2)}) collective-permute-start(bf16[512,128]{1,0:T(8,128)(2,1)S(1)} %shard_map.90.mine_ref), channel_id=1, source_target_pairs={{0,8},{1,9},{2,10},{3,11},{4,12},{5,13},{6,14},{7,15},{8,0},{9,1},... | collective-permute-start | bytes 393224 | tf_op jit(solution)/shard_map/ppermute | solution.py:319
  59.6 5.6 %collective-permute-start.25 = (bf16[512,128]{1,0:T(8,128)(2,1)S(1)}, bf16[512,128]{1,0:T(8,128)(2,1)S(1)}, u32[]{:S(2)}, u32[]{:S(2)}) collective-permute-start(bf16[512,128]{1,0:T(8,128)(2,1)S(1)} %get-tuple-element.49), channel_id=1, source_target_pairs={{0,16},{1,17},{2,18},{3,19},{4,20},{5,21},{6,22},{7,23},{8,24},{9,... | collective-permute-start | bytes 393224 | tf_op jit(solution)/shard_map/ppermute | solution.py:322
  59.7 7.7 %collective-permute-start.28 = (bf16[512,128]{1,0:T(8,128)(2,1)S(1)}, bf16[512,128]{1,0:T(8,128)(2,1)S(1)}, u32[]{:S(2)}, u32[]{:S(2)}) collective-permute-start(bf16[512,128]{1,0:T(8,128)(2,1)S(1)} %get-tuple-element.48.refs_5_.refs_1_), channel_id=1, source_target_pairs={{0,1},{1,2},{2,3},{3,4},{4,5},{5,6},{6,7},{7,0},{8,15},{9,8},{10,9... | collective-permute-start | bytes 393224 | tf_op jit(solution)/shard_map/ppermute | solution.py:330
  61.1 7.0 %collective-permute-start.29 = (bf16[512,128]{1,0:T(8,128)(2,1)S(1)}, bf16[512,128]{1,0:T(8,128)(2,1)S(1)}, u32[]{:S(2)}, u32[]{:S(2)}) collective-permute-start(bf16[512,128]{1,0:T(8,128)(2,1)S(1)} %get-tuple-element.48.refs_5_.refs_1_), channel_id=1, source_target_pairs={{0,2},{1,3},{2,4},{3,5},{4,6},{5,7},{6,0},{7,1},{8,14},{9,15},{10,... | collective-permute-start | bytes 393224 | tf_op jit(solution)/shard_map/ppermute | solution.py:330
  65.2 7.0 %collective-permute-start.27 = (bf16[512,128]{1,0:T(8,128)(2,1)S(1)}, bf16[512,128]{1,0:T(8,128)(2,1)S(1)}, u32[]{:S(2)}, u32[]{:S(2)}) collective-permute-start(bf16[512,128]{1,0:T(8,128)(2,1)S(1)} %collective-permute-done.25.refs_6_.refs_1_.refs_3_), channel_id=1, source_target_pairs={{0,8},{1,9},{2,10},{3,11},{4,12},{5,13},{6,14},{7,15},{8,0},{9,1},... | collective-permute-start | bytes 393224 | tf_op jit(solution)/shard_map/ppermute | solution.py:330
  65.2 7.1 %collective-permute-start.26 = (bf16[512,128]{1,0:T(8,128)(2,1)S(1)}, bf16[512,128]{1,0:T(8,128)(2,1)S(1)}, u32[]{:S(2)}, u32[]{:S(2)}) collective-permute-start(bf16[512,128]{1,0:T(8,128)(2,1)S(1)} %collective-permute-done.25.refs_6_.refs_1_.refs_3_), channel_id=1, source_target_pairs={{0,8},{1,9},{2,10},{3,11},{4,12},{5,13},{6,14},{7,15},{8,0},{9,1},... | collective-permute-start | bytes 393224 | tf_op jit(solution)/shard_map/ppermute | solution.py:330
  68.4 5.6 %collective-permute-start.30 = (bf16[512,128]{1,0:T(8,128)(2,1)S(1)}, bf16[512,128]{1,0:T(8,128)(2,1)S(1)}, u32[]{:S(2)}, u32[]{:S(2)}) collective-permute-start(bf16[512,128]{1,0:T(8,128)(2,1)S(1)} %get-tuple-element.55), channel_id=1, source_target_pairs={{0,16},{1,17},{2,18},{3,19},{4,20},{5,21},{6,22},{7,23},{8,24},{9,... | collective-permute-start | bytes 393224 | tf_op jit(solution)/shard_map/ppermute | solution.py:322
  72.0 3.1 %collective-permute-start.32 = (bf16[512,128]{1,0:T(8,128)(2,1)S(1)}, bf16[512,128]{1,0:T(8,128)(2,1)S(1)}, u32[]{:S(2)}, u32[]{:S(2)}) collective-permute-start(bf16[512,128]{1,0:T(8,128)(2,1)S(1)} %get-tuple-element.60), channel_id=1, source_target_pairs={{0,8},{1,9},{2,10},{3,11},{4,12},{5,13},{6,14},{7,15},{8,0},{9,1},... | collective-permute-start | bytes 393224 | tf_op jit(solution)/shard_map/ppermute | solution.py:319
  (5 other events, 14.4 us)

commit v14 on v12

--- a/solution.py
+++ b/solution.py
@@ -273,14 +273,10 @@
     return fresh
 
 
-def first_history_body(history_ref, other_history_ref, out_ref):
-    core, _ = place()
-    out_ref[...] = jnp.where(core == 0, history_ref[...], other_history_ref[...])
-
-
-def start_body(inverse_ref, excitation_ref, history_ref, out_ref):
-    _, pair = place()
-    rhs = (excitation_ref[0].astype(F32) - history_ref[...]).astype(BF16)
+def start_body(inverse_ref, excitation_ref, history_ref, other_history_ref, out_ref):
+    core, pair = place()
+    history = jnp.where(core == 0, history_ref[...], other_history_ref[...])
+    rhs = (excitation_ref[0].astype(F32) - history).astype(BF16)
     solve(inverse_ref, rhs, out_ref, pair == 0, jnp.zeros_like(rhs))
 
 
@@ -328,11 +324,10 @@
     field_shape = jax.ShapeDtypeStruct((rows, columns), F32)
     current_shape = jax.ShapeDtypeStruct((rows, columns), BF16)
     kept, own, *sent = spread(entries, pattern[0], groups)
-    (first_history,) = call(first_history_body, [field_shape], [history[0], other_history])
     (current,) = call(
         start_body,
         [current_shape],
-        [diagonal_block_inverses, excitation, first_history],
+        [diagonal_block_inverses, excitation, history[0], other_history],
     )
     matrix_shape = jax.ShapeDtypeStruct((rows, 2 * rows), kept.dtype)
     near, far = call(arrange_body, [matrix_shape, matrix_shape], [kept] + [swapped(part) for part in sent])

time: 76.4 us -> 76.4 us (level)
    pallas_call x40 -> x39, Pallas kernels: 11.1 us -> 11.1 us  [call(): pl.pallas_call(body, out_shape=tuple(outs), in_specs=specs, out_specs=tup...]
where the time goes in v14:
time: 76.4 us; the launch traced here: 76.2 us
  waiting for transfers between devices  43.4 us (57%)
  starting transfers between devices  18.2 us (24%)
  Pallas kernels  12.8 us (17%)
  between operations  1.08 us (1%)
    ppermute x14, waiting for transfers between devices, halo(): return lax.ppermute(value, AXES, everyone(move))  31.4 us
    ppermute x14, starting transfers between devices, halo(): return lax.ppermute(value, AXES, everyone(move))  12.9 us
    pallas_call x39, Pallas kernels, call(): pl.pallas_call(body, out_shape=tuple(outs), in_specs=specs, out_specs=tup...  11.1 us
    ppermute x12, waiting for transfers between devices, swapped(): return lax.ppermute(value, AXES, everyone(lambda d, s: (d ^ 1, s)))  6.85 us
    ppermute x7, waiting for transfers between devices, pair_moved(): lax.ppermute(value, AXES, everyone(lambda d, s: ((d + 2 * hop) % lags, s)))  5.08 us
    ppermute x7, starting transfers between devices, pair_moved(): lax.ppermute(value, AXES, everyone(lambda d, s: ((d + 2 * hop) % lags, s)))  3.08 us
    ppermute x12, starting transfers between devices, swapped(): return lax.ppermute(value, AXES, everyone(lambda d, s: (d ^ 1, s)))  2.2 us
    pallas_call x1, Pallas kernels, spread(): pl.pallas_call(functools.partial(spread_body, groups), out_shape=(matrix(...  1.74 us
  transfers between devices with their start and end apart: 33, of which 19 were waited for; matrix products, arithmetic and copies ran while one was open for 0% of the time, Pallas kernels for 13%

profile of v14, /device:TPU:0, one launch (start us, length us, event | category | flops | bytes accessed | tf_op | source)
XLA Modules:
  0.0 76.2 jit_solution(10864668943038107672)
XLA Ops:
  1.2 0.7 copy-done.3
  1.9 1.7 %shard_map.69 = (bf16[512,1024]{1,0:T(8,128)(2,1)S(1)}, bf16[512,512]{1,0:T(8,128)(2,1)S(1)}, bf16[128,1024]{1,0:T(8,128)(2,1)S(1)}, bf16[128,1024]{1,0:T(8,128)...) custom-call(s32[4,16]{1,0:T(4,128)S(1)} %bitcast.8, bf16[4,16,128,128]{3,2,1,0:T(8,128)(2,1)} %bitcast.9), custom_call_target="tpu_custom_call" | custom-call | bytes 1048576 | tf_op jit(solution)/shard_map/pallas_call | solution.py:114
  4.9 2.7 %collective-permute-start.6 = (bf16[512,128]{1,0:T(8,128)(2,1)S(1)}, bf16[512,128]{1,0:T(8,128)(2,1)S(1)}, u32[]{:S(2)}, u32[]{:S(2)}) collective-permute-start(bf16[512,128]{1,0:T(8,128)(2,1)S(1)} %shard_map.68.refs_1_.refs_5_.refs_0_), channel_id=1, source_target_pairs={{0,1},{1,2},{2,3},{3,4},{4,5},{5,6},{6,7},{7,0},{8,15},{9,8},{10,9... | collective-permute-start | bytes 393224 | tf_op jit(solution)/shard_map/ppermute | solution.py:321
  7.6 1.6 %collective-permute-start.5 = (bf16[512,128]{1,0:T(8,128)(2,1)S(1)}, bf16[512,128]{1,0:T(8,128)(2,1)S(1)}, u32[]{:S(2)}, u32[]{:S(2)}) collective-permute-start(bf16[512,128]{1,0:T(8,128)(2,1)S(1)} %shard_map.68.refs_1_.refs_5_.refs_0_), channel_id=1, source_target_pairs={{0,2},{1,3},{2,4},{3,5},{4,6},{5,7},{6,0},{7,1},{8,14},{9,15},{10,... | collective-permute-start | bytes 393224 | tf_op jit(solution)/shard_map/ppermute | solution.py:321
  9.6 5.2 %collective-permute-done.6.refs_1_.refs_3_ = bf16[512,128]{1,0:T(8,128)(2,1)S(1)} collective-permute-done((bf16[512,128]{1,0:T(8,128)(2,1)S(1)}, bf16[512,128]{1,0:T(8,128)(2,1)S(1)}, u32[]{:S(2)}, u32[]{:S(2)}) %collective-permute-start.6) | collective-permute-done | bytes 131104 | tf_op jit(solution)/shard_map/ppermute | solution.py:321
  15.1 0.6 collective-permute-done.5.second_ref.refs_4_
  16.2 1.2 %collective-permute-done.8.other_ref = bf16[512,128]{1,0:T(8,128)(2,1)S(1)} collective-permute-done((bf16[512,128]{1,0:T(8,128)(2,1)S(1)}, bf16[512,128]{1,0:T(8,128)(2,1)S(1)}, u32[]{:S(2)}, u32[]{:S(2)}) %collective-permute-start.8) | collective-permute-done | bytes 131104 | tf_op jit(solution)/shard_map/ppermute | solution.py:310
  17.6 1.3 %collective-permute-start.11 = (bf16[512,128]{1,0:T(8,128)(2,1)S(1)}, bf16[512,128]{1,0:T(8,128)(2,1)S(1)}, u32[]{:S(2)}, u32[]{:S(2)}) collective-permute-start(bf16[512,128]{1,0:T(8,128)(2,1)S(1)} %get-tuple-element.35.refs_1_.refs_5_), channel_id=1, source_target_pairs={{0,1},{1,2},{2,3},{3,4},{4,5},{5,6},{6,7},{7,0},{8,15},{9,8},{10,9... | collective-permute-start | bytes 393224 | tf_op jit(solution)/shard_map/ppermute | solution.py:321
  19.2 0.6 shard_map.75.refs_2_
  19.8 6.3 %collective-permute-done.11.refs_1_.refs_3_ = bf16[512,128]{1,0:T(8,128)(2,1)S(1)} collective-permute-done((bf16[512,128]{1,0:T(8,128)(2,1)S(1)}, bf16[512,128]{1,0:T(8,128)(2,1)S(1)}, u32[]{:S(2)}, u32[]{:S(2)}) %collective-permute-start.11) | collective-permute-done | bytes 131104 | tf_op jit(solution)/shard_map/ppermute | solution.py:321
  26.8 1.3 %collective-permute-done.12.other_ref = bf16[512,128]{1,0:T(8,128)(2,1)S(1)} collective-permute-done((bf16[512,128]{1,0:T(8,128)(2,1)S(1)}, bf16[512,128]{1,0:T(8,128)(2,1)S(1)}, u32[]{:S(2)}, u32[]{:S(2)}) %collective-permute-start.12) | collective-permute-done | bytes 131104 | tf_op jit(solution)/shard_map/ppermute | solution.py:310
  28.3 1.7 %collective-permute-start.14 = (bf16[512,128]{1,0:T(8,128)(2,1)S(1)}, bf16[512,128]{1,0:T(8,128)(2,1)S(1)}, u32[]{:S(2)}, u32[]{:S(2)}) collective-permute-start(bf16[512,128]{1,0:T(8,128)(2,1)S(1)} %get-tuple-element.38.refs_1_.refs_5_.refs_2_), channel_id=1, source_target_pairs={{0,1},{1,2},{2,3},{3,4},{4,5},{5,6},{6,7},{7,0},{8,15},{9,8},{10,9... | collective-permute-start | bytes 393224 | tf_op jit(solution)/shard_map/ppermute | solution.py:321
  30.5 0.6 shard_map.79.refs_2_
  31.0 5.0 %collective-permute-done.14.refs_1_.refs_3_ = bf16[512,128]{1,0:T(8,128)(2,1)S(1)} collective-permute-done((bf16[512,128]{1,0:T(8,128)(2,1)S(1)}, bf16[512,128]{1,0:T(8,128)(2,1)S(1)}, u32[]{:S(2)}, u32[]{:S(2)}) %collective-permute-start.14) | collective-permute-done | bytes 131104 | tf_op jit(solution)/shard_map/ppermute | solution.py:321
  36.3 0.7 collective-permute-done.13.second_ref.refs_4_
  37.4 1.3 %collective-permute-done.16.other_ref = bf16[512,128]{1,0:T(8,128)(2,1)S(1)} collective-permute-done((bf16[512,128]{1,0:T(8,128)(2,1)S(1)}, bf16[512,128]{1,0:T(8,128)(2,1)S(1)}, u32[]{:S(2)}, u32[]{:S(2)}) %collective-permute-start.16) | collective-permute-done | bytes 131104 | tf_op jit(solution)/shard_map/ppermute | solution.py:310
  38.9 1.0 %collective-permute-start.18 = (bf16[512,128]{1,0:T(8,128)(2,1)S(1)}, bf16[512,128]{1,0:T(8,128)(2,1)S(1)}, u32[]{:S(2)}, u32[]{:S(2)}) collective-permute-start(bf16[512,128]{1,0:T(8,128)(2,1)S(1)} %get-tuple-element.40.refs_1_.refs_5_.refs_3_), channel_id=1, source_target_pairs={{0,1},{1,2},{2,3},{3,4},{4,5},{5,6},{6,7},{7,0},{8,15},{9,8},{10,9... | collective-permute-start | bytes 393224 | tf_op jit(solution)/shard_map/ppermute | solution.py:321
  40.3 0.6 shard_map.83.refs_2_
  40.9 5.7 %collective-permute-done.18.refs_1_.refs_3_ = bf16[512,128]{1,0:T(8,128)(2,1)S(1)} collective-permute-done((bf16[512,128]{1,0:T(8,128)(2,1)S(1)}, bf16[512,128]{1,0:T(8,128)(2,1)S(1)}, u32[]{:S(2)}, u32[]{:S(2)}) %collective-permute-start.18) | collective-permute-done | bytes 131104 | tf_op jit(solution)/shard_map/ppermute | solution.py:321
  47.4 1.3 %collective-permute-done.20.other_ref = bf16[512,128]{1,0:T(8,128)(2,1)S(1)} collective-permute-done((bf16[512,128]{1,0:T(8,128)(2,1)S(1)}, bf16[512,128]{1,0:T(8,128)(2,1)S(1)}, u32[]{:S(2)}, u32[]{:S(2)}) %collective-permute-start.20) | collective-permute-done | bytes 131104 | tf_op jit(solution)/shard_map/ppermute | solution.py:310
  48.9 1.7 %collective-permute-start.22 = (bf16[512,128]{1,0:T(8,128)(2,1)S(1)}, bf16[512,128]{1,0:T(8,128)(2,1)S(1)}, u32[]{:S(2)}, u32[]{:S(2)}) collective-permute-start(bf16[512,128]{1,0:T(8,128)(2,1)S(1)} %get-tuple-element.42.refs_1_.refs_4_.refs_5_), channel_id=1, source_target_pairs={{0,1},{1,2},{2,3},{3,4},{4,5},{5,6},{6,7},{7,0},{8,15},{9,8},{10,9... | collective-permute-start | bytes 393224 | tf_op jit(solution)/shard_map/ppermute | solution.py:321
  51.0 0.6 shard_map.87.refs_2_
  51.6 5.5 %collective-permute-done.22.refs_1_.refs_3_ = bf16[512,128]{1,0:T(8,128)(2,1)S(1)} collective-permute-done((bf16[512,128]{1,0:T(8,128)(2,1)S(1)}, bf16[512,128]{1,0:T(8,128)(2,1)S(1)}, u32[]{:S(2)}, u32[]{:S(2)}) %collective-permute-start.22) | collective-permute-done | bytes 131104 | tf_op jit(solution)/shard_map/ppermute | solution.py:321
  58.0 1.3 %collective-permute-done.24.other_ref = bf16[512,128]{1,0:T(8,128)(2,1)S(1)} collective-permute-done((bf16[512,128]{1,0:T(8,128)(2,1)S(1)}, bf16[512,128]{1,0:T(8,128)(2,1)S(1)}, u32[]{:S(2)}, u32[]{:S(2)}) %collective-permute-start.24) | collective-permute-done | bytes 131104 | tf_op jit(solution)/shard_map/ppermute | solution.py:310
  59.6 1.4 %collective-permute-start.28 = (bf16[512,128]{1,0:T(8,128)(2,1)S(1)}, bf16[512,128]{1,0:T(8,128)(2,1)S(1)}, u32[]{:S(2)}, u32[]{:S(2)}) collective-permute-start(bf16[512,128]{1,0:T(8,128)(2,1)S(1)} %get-tuple-element.44.refs_5_.refs_1_), channel_id=1, source_target_pairs={{0,1},{1,2},{2,3},{3,4},{4,5},{5,6},{6,7},{7,0},{8,15},{9,8},{10,9... | collective-permute-start | bytes 393224 | tf_op jit(solution)/shard_map/ppermute | solution.py:321
  61.1 0.6 shard_map.98.refs_2_
  61.7 3.5 %collective-permute-done.25.refs_6_.refs_1_.refs_3_ = bf16[512,128]{1,0:T(8,128)(2,1)S(1)} collective-permute-done((bf16[512,128]{1,0:T(8,128)(2,1)S(1)}, bf16[512,128]{1,0:T(8,128)(2,1)S(1)}, u32[]{:S(2)}, u32[]{:S(2)}) %collective-permute-start.25) | collective-permute-done | bytes 131104 | tf_op jit(solution)/shard_map/ppermute | solution.py:313
  65.7 1.7 %collective-permute-done.28.refs_3_.refs_1_ = bf16[512,128]{1,0:T(8,128)(2,1)S(1)} collective-permute-done((bf16[512,128]{1,0:T(8,128)(2,1)S(1)}, bf16[512,128]{1,0:T(8,128)(2,1)S(1)}, u32[]{:S(2)}, u32[]{:S(2)}) %collective-permute-start.28) | collective-permute-done | bytes 131104 | tf_op jit(solution)/shard_map/ppermute | solution.py:321
  68.3 2.6 %collective-permute-start.30 = (bf16[512,128]{1,0:T(8,128)(2,1)S(1)}, bf16[512,128]{1,0:T(8,128)(2,1)S(1)}, u32[]{:S(2)}, u32[]{:S(2)}) collective-permute-start(bf16[512,128]{1,0:T(8,128)(2,1)S(1)} %get-tuple-element.47), channel_id=1, source_target_pairs={{0,16},{1,17},{2,18},{3,19},{4,20},{5,21},{6,22},{7,23},{8,24},{9,... | collective-permute-start | bytes 393224 | tf_op jit(solution)/shard_map/ppermute | solution.py:313
  72.3 1.6 %collective-permute-done.30.rest_0_ = bf16[512,128]{1,0:T(8,128)(2,1)S(1)} collective-permute-done((bf16[512,128]{1,0:T(8,128)(2,1)S(1)}, bf16[512,128]{1,0:T(8,128)(2,1)S(1)}, u32[]{:S(2)}, u32[]{:S(2)}) %collective-permute-start.30) | collective-permute-done | bytes 131104 | tf_op jit(solution)/shard_map/ppermute | solution.py:313
  74.1 1.0 %shard_map.91 = (bf16[6,512,128]{2,1,0:T(8,128)(2,1)}, f32[8,128]{1,0:T(8,128)S(1)}) custom-call(bf16[512,128]{1,0:T(8,128)(2,1)S(1)} %shard_map.68.refs_1_.refs_5_.refs_0_, bf16[512,128]{1,0:T(8,128)(2,1)S(1)} %get-tuple-element.35.refs_1_.refs_5_, bf16[512,128]{1,0:T(8,128)(2,1)S(1)} %get-tuple-element.38.refs_1_.refs_5_.refs_2_, ...), custom_call_target="tpu_custom_call" | custom-call | bytes 1048576 | tf_op jit(solution)/shard_map/pallas_call | solution.py:39
  75.4 0.8 %shard_map.107 = f32[512,128]{1,0:T(8,128)} custom-call(f32[512,128]{1,0:T(8,128)S(1)} %get-tuple-element.48.refs_0_, bf16[512,128]{1,0:T(8,128)(2,1)S(1)} %collective-permute-done.31.refs_1_, f32[512,128]{1,0:T(8,128)S(1)} %shard_map.106.refs_2_, f32[8,128]{1,0:T(8,128)S(1)} %get-tuple-element.53.refs_3_), custom_call_target="tpu_custom_call" | custom-call | bytes 1048576 | tf_op jit(solution)/shard_map/pallas_call | solution.py:39
  (82 shorter events, 11.7 us)
Async XLA Ops:
  0.7 4.0 %collective-permute-start = (f32[512,128]{1,0:T(8,128)}, f32[512,128]{1,0:T(8,128)S(1)}, u32[]{:S(2)}, u32[]{:S(2)}) collective-permute-start(f32[512,128]{1,0:T(8,128)} %bitcast.4), channel_id=1, source_target_pairs={{0,8},{1,9},{2,10},{3,11},{4,12},{5,13},{6,14},{7,15},{8,0},{9,1},... | collective-permute-start | bytes 786440 | tf_op jit(solution)/shard_map/ppermute | solution.py:310
  3.6 4.0 %collective-permute-start.1 = (bf16[128,1024]{1,0:T(8,128)(2,1)S(1)}, bf16[128,1024]{1,0:T(8,128)(2,1)S(1)}, u32[]{:S(2)}, u32[]{:S(2)}) collective-permute-start(bf16[128,1024]{1,0:T(8,128)(2,1)S(1)} %get-tuple-element.29), channel_id=1, source_target_pairs={{0,8},{1,9},{2,10},{3,11},{4,12},{5,13},{6,14},{7,15},{8,0},{9,1},... | collective-permute-start | bytes 786440 | tf_op jit(solution)/shard_map/ppermute | solution.py:310
  3.8 5.3 %collective-permute-start.2 = (bf16[128,1024]{1,0:T(8,128)(2,1)S(1)}, bf16[128,1024]{1,0:T(8,128)(2,1)S(1)}, u32[]{:S(2)}, u32[]{:S(2)}) collective-permute-start(bf16[128,1024]{1,0:T(8,128)(2,1)S(1)} %get-tuple-element.30), channel_id=1, source_target_pairs={{0,8},{1,9},{2,10},{3,11},{4,12},{5,13},{6,14},{7,15},{8,0},{9,1},... | collective-permute-start | bytes 786440 | tf_op jit(solution)/shard_map/ppermute | solution.py:310
  4.2 5.3 %collective-permute-start.3 = (bf16[128,1024]{1,0:T(8,128)(2,1)S(1)}, bf16[128,1024]{1,0:T(8,128)(2,1)S(1)}, u32[]{:S(2)}, u32[]{:S(2)}) collective-permute-start(bf16[128,1024]{1,0:T(8,128)(2,1)S(1)} %get-tuple-element.31), channel_id=1, source_target_pairs={{0,8},{1,9},{2,10},{3,11},{4,12},{5,13},{6,14},{7,15},{8,0},{9,1},... | collective-permute-start | bytes 786440 | tf_op jit(solution)/shard_map/ppermute | solution.py:310
  4.3 5.1 %collective-permute-start.4 = (bf16[128,1024]{1,0:T(8,128)(2,1)S(1)}, bf16[128,1024]{1,0:T(8,128)(2,1)S(1)}, u32[]{:S(2)}, u32[]{:S(2)}) collective-permute-start(bf16[128,1024]{1,0:T(8,128)(2,1)S(1)} %get-tuple-element.32), channel_id=1, source_target_pairs={{0,8},{1,9},{2,10},{3,11},{4,12},{5,13},{6,14},{7,15},{8,0},{9,1},... | collective-permute-start | bytes 786440 | tf_op jit(solution)/shard_map/ppermute | solution.py:310
  4.9 9.9 %collective-permute-start.6 = (bf16[512,128]{1,0:T(8,128)(2,1)S(1)}, bf16[512,128]{1,0:T(8,128)(2,1)S(1)}, u32[]{:S(2)}, u32[]{:S(2)}) collective-permute-start(bf16[512,128]{1,0:T(8,128)(2,1)S(1)} %shard_map.68.refs_1_.refs_5_.refs_0_), channel_id=1, source_target_pairs={{0,1},{1,2},{2,3},{3,4},{4,5},{5,6},{6,7},{7,0},{8,15},{9,8},{10,9... | collective-permute-start | bytes 393224 | tf_op jit(solution)/shard_map/ppermute | solution.py:321
  7.6 8.2 %collective-permute-start.5 = (bf16[512,128]{1,0:T(8,128)(2,1)S(1)}, bf16[512,128]{1,0:T(8,128)(2,1)S(1)}, u32[]{:S(2)}, u32[]{:S(2)}) collective-permute-start(bf16[512,128]{1,0:T(8,128)(2,1)S(1)} %shard_map.68.refs_1_.refs_5_.refs_0_), channel_id=1, source_target_pairs={{0,2},{1,3},{2,4},{3,5},{4,6},{5,7},{6,0},{7,1},{8,14},{9,15},{10,... | collective-permute-start | bytes 393224 | tf_op jit(solution)/shard_map/ppermute | solution.py:321
  9.2 6.6 %collective-permute-start.7 = (bf16[512,128]{1,0:T(8,128)(2,1)S(1)}, bf16[512,128]{1,0:T(8,128)(2,1)S(1)}, u32[]{:S(2)}, u32[]{:S(2)}) collective-permute-start(bf16[512,128]{1,0:T(8,128)(2,1)S(1)} %shard_map.68.refs_1_.refs_5_.refs_0_), channel_id=1, source_target_pairs={{0,16},{1,17},{2,18},{3,19},{4,20},{5,21},{6,22},{7,23},{8,24},{9,... | collective-permute-start | bytes 393224 | tf_op jit(solution)/shard_map/ppermute | solution.py:313
  16.0 1.4 %collective-permute-start.8 = (bf16[512,128]{1,0:T(8,128)(2,1)S(1)}, bf16[512,128]{1,0:T(8,128)(2,1)S(1)}, u32[]{:S(2)}, u32[]{:S(2)}) collective-permute-start(bf16[512,128]{1,0:T(8,128)(2,1)S(1)} %shard_map.73.mine_ref), channel_id=1, source_target_pairs={{0,8},{1,9},{2,10},{3,11},{4,12},{5,13},{6,14},{7,15},{8,0},{9,1},... | collective-permute-start | bytes 393224 | tf_op jit(solution)/shard_map/ppermute | solution.py:310
  17.6 8.4 %collective-permute-start.11 = (bf16[512,128]{1,0:T(8,128)(2,1)S(1)}, bf16[512,128]{1,0:T(8,128)(2,1)S(1)}, u32[]{:S(2)}, u32[]{:S(2)}) collective-permute-start(bf16[512,128]{1,0:T(8,128)(2,1)S(1)} %get-tuple-element.35.refs_1_.refs_5_), channel_id=1, source_target_pairs={{0,1},{1,2},{2,3},{3,4},{4,5},{5,6},{6,7},{7,0},{8,15},{9,8},{10,9... | collective-permute-start | bytes 393224 | tf_op jit(solution)/shard_map/ppermute | solution.py:321
  18.9 7.4 %collective-permute-start.10 = (bf16[512,128]{1,0:T(8,128)(2,1)S(1)}, bf16[512,128]{1,0:T(8,128)(2,1)S(1)}, u32[]{:S(2)}, u32[]{:S(2)}) collective-permute-start(bf16[512,128]{1,0:T(8,128)(2,1)S(1)} %get-tuple-element.35.refs_1_.refs_5_), channel_id=1, source_target_pairs={{0,2},{1,3},{2,4},{3,5},{4,6},{5,7},{6,0},{7,1},{8,14},{9,15},{10,... | collective-permute-start | bytes 393224 | tf_op jit(solution)/shard_map/ppermute | solution.py:321
  19.2 7.2 %collective-permute-start.9 = (bf16[512,128]{1,0:T(8,128)(2,1)S(1)}, bf16[512,128]{1,0:T(8,128)(2,1)S(1)}, u32[]{:S(2)}, u32[]{:S(2)}) collective-permute-start(bf16[512,128]{1,0:T(8,128)(2,1)S(1)} %get-tuple-element.36), channel_id=1, source_target_pairs={{0,16},{1,17},{2,18},{3,19},{4,20},{5,21},{6,22},{7,23},{8,24},{9,... | collective-permute-start | bytes 393224 | tf_op jit(solution)/shard_map/ppermute | solution.py:313
  26.7 1.4 %collective-permute-start.12 = (bf16[512,128]{1,0:T(8,128)(2,1)S(1)}, bf16[512,128]{1,0:T(8,128)(2,1)S(1)}, u32[]{:S(2)}, u32[]{:S(2)}) collective-permute-start(bf16[512,128]{1,0:T(8,128)(2,1)S(1)} %shard_map.77.mine_ref), channel_id=1, source_target_pairs={{0,8},{1,9},{2,10},{3,11},{4,12},{5,13},{6,14},{7,15},{8,0},{9,1},... | collective-permute-start | bytes 393224 | tf_op jit(solution)/shard_map/ppermute | solution.py:310
  28.3 7.7 %collective-permute-start.14 = (bf16[512,128]{1,0:T(8,128)(2,1)S(1)}, bf16[512,128]{1,0:T(8,128)(2,1)S(1)}, u32[]{:S(2)}, u32[]{:S(2)}) collective-permute-start(bf16[512,128]{1,0:T(8,128)(2,1)S(1)} %get-tuple-element.38.refs_1_.refs_5_.refs_2_), channel_id=1, source_target_pairs={{0,1},{1,2},{2,3},{3,4},{4,5},{5,6},{6,7},{7,0},{8,15},{9,8},{10,9... | collective-permute-start | bytes 393224 | tf_op jit(solution)/shard_map/ppermute | solution.py:321
  30.0 7.0 %collective-permute-start.13 = (bf16[512,128]{1,0:T(8,128)(2,1)S(1)}, bf16[512,128]{1,0:T(8,128)(2,1)S(1)}, u32[]{:S(2)}, u32[]{:S(2)}) collective-permute-start(bf16[512,128]{1,0:T(8,128)(2,1)S(1)} %get-tuple-element.38.refs_1_.refs_5_.refs_2_), channel_id=1, source_target_pairs={{0,2},{1,3},{2,4},{3,5},{4,6},{5,7},{6,0},{7,1},{8,14},{9,15},{10,... | collective-permute-start | bytes 393224 | tf_op jit(solution)/shard_map/ppermute | solution.py:321
  30.4 6.6 %collective-permute-start.15 = (bf16[512,128]{1,0:T(8,128)(2,1)S(1)}, bf16[512,128]{1,0:T(8,128)(2,1)S(1)}, u32[]{:S(2)}, u32[]{:S(2)}) collective-permute-start(bf16[512,128]{1,0:T(8,128)(2,1)S(1)} %get-tuple-element.39), channel_id=1, source_target_pairs={{0,16},{1,17},{2,18},{3,19},{4,20},{5,21},{6,22},{7,23},{8,24},{9,... | collective-permute-start | bytes 393224 | tf_op jit(solution)/shard_map/ppermute | solution.py:313
  37.3 1.4 %collective-permute-start.16 = (bf16[512,128]{1,0:T(8,128)(2,1)S(1)}, bf16[512,128]{1,0:T(8,128)(2,1)S(1)}, u32[]{:S(2)}, u32[]{:S(2)}) collective-permute-start(bf16[512,128]{1,0:T(8,128)(2,1)S(1)} %shard_map.81.mine_ref), channel_id=1, source_target_pairs={{0,8},{1,9},{2,10},{3,11},{4,12},{5,13},{6,14},{7,15},{8,0},{9,1},... | collective-permute-start | bytes 393224 | tf_op jit(solution)/shard_map/ppermute | solution.py:310
  38.9 7.7 %collective-permute-start.18 = (bf16[512,128]{1,0:T(8,128)(2,1)S(1)}, bf16[512,128]{1,0:T(8,128)(2,1)S(1)}, u32[]{:S(2)}, u32[]{:S(2)}) collective-permute-start(bf16[512,128]{1,0:T(8,128)(2,1)S(1)} %get-tuple-element.40.refs_1_.refs_5_.refs_3_), channel_id=1, source_target_pairs={{0,1},{1,2},{2,3},{3,4},{4,5},{5,6},{6,7},{7,0},{8,15},{9,8},{10,9... | collective-permute-start | bytes 393224 | tf_op jit(solution)/shard_map/ppermute | solution.py:321
  40.0 7.0 %collective-permute-start.17 = (bf16[512,128]{1,0:T(8,128)(2,1)S(1)}, bf16[512,128]{1,0:T(8,128)(2,1)S(1)}, u32[]{:S(2)}, u32[]{:S(2)}) collective-permute-start(bf16[512,128]{1,0:T(8,128)(2,1)S(1)} %get-tuple-element.40.refs_1_.refs_5_.refs_3_), channel_id=1, source_target_pairs={{0,2},{1,3},{2,4},{3,5},{4,6},{5,7},{6,0},{7,1},{8,14},{9,15},{10,... | collective-permute-start | bytes 393224 | tf_op jit(solution)/shard_map/ppermute | solution.py:321
  40.0 7.0 %collective-permute-start.19 = (bf16[512,128]{1,0:T(8,128)(2,1)S(1)}, bf16[512,128]{1,0:T(8,128)(2,1)S(1)}, u32[]{:S(2)}, u32[]{:S(2)}) collective-permute-start(bf16[512,128]{1,0:T(8,128)(2,1)S(1)} %get-tuple-element.41), channel_id=1, source_target_pairs={{0,16},{1,17},{2,18},{3,19},{4,20},{5,21},{6,22},{7,23},{8,24},{9,... | collective-permute-start | bytes 393224 | tf_op jit(solution)/shard_map/ppermute | solution.py:313
  47.3 1.4 %collective-permute-start.20 = (bf16[512,128]{1,0:T(8,128)(2,1)S(1)}, bf16[512,128]{1,0:T(8,128)(2,1)S(1)}, u32[]{:S(2)}, u32[]{:S(2)}) collective-permute-start(bf16[512,128]{1,0:T(8,128)(2,1)S(1)} %shard_map.85.mine_ref), channel_id=1, source_target_pairs={{0,8},{1,9},{2,10},{3,11},{4,12},{5,13},{6,14},{7,15},{8,0},{9,1},... | collective-permute-start | bytes 393224 | tf_op jit(solution)/shard_map/ppermute | solution.py:310
  48.9 8.1 %collective-permute-start.22 = (bf16[512,128]{1,0:T(8,128)(2,1)S(1)}, bf16[512,128]{1,0:T(8,128)(2,1)S(1)}, u32[]{:S(2)}, u32[]{:S(2)}) collective-permute-start(bf16[512,128]{1,0:T(8,128)(2,1)S(1)} %get-tuple-element.42.refs_1_.refs_4_.refs_5_), channel_id=1, source_target_pairs={{0,1},{1,2},{2,3},{3,4},{4,5},{5,6},{6,7},{7,0},{8,15},{9,8},{10,9... | collective-permute-start | bytes 393224 | tf_op jit(solution)/shard_map/ppermute | solution.py:321
  50.6 7.0 %collective-permute-start.21 = (bf16[512,128]{1,0:T(8,128)(2,1)S(1)}, bf16[512,128]{1,0:T(8,128)(2,1)S(1)}, u32[]{:S(2)}, u32[]{:S(2)}) collective-permute-start(bf16[512,128]{1,0:T(8,128)(2,1)S(1)} %get-tuple-element.42.refs_1_.refs_4_.refs_5_), channel_id=1, source_target_pairs={{0,2},{1,3},{2,4},{3,5},{4,6},{5,7},{6,0},{7,1},{8,14},{9,15},{10,... | collective-permute-start | bytes 393224 | tf_op jit(solution)/shard_map/ppermute | solution.py:321
  51.0 6.7 %collective-permute-start.23 = (bf16[512,128]{1,0:T(8,128)(2,1)S(1)}, bf16[512,128]{1,0:T(8,128)(2,1)S(1)}, u32[]{:S(2)}, u32[]{:S(2)}) collective-permute-start(bf16[512,128]{1,0:T(8,128)(2,1)S(1)} %get-tuple-element.43), channel_id=1, source_target_pairs={{0,16},{1,17},{2,18},{3,19},{4,20},{5,21},{6,22},{7,23},{8,24},{9,... | collective-permute-start | bytes 393224 | tf_op jit(solution)/shard_map/ppermute | solution.py:313
  57.9 1.4 %collective-permute-start.24 = (bf16[512,128]{1,0:T(8,128)(2,1)S(1)}, bf16[512,128]{1,0:T(8,128)(2,1)S(1)}, u32[]{:S(2)}, u32[]{:S(2)}) collective-permute-start(bf16[512,128]{1,0:T(8,128)(2,1)S(1)} %shard_map.89.mine_ref), channel_id=1, source_target_pairs={{0,8},{1,9},{2,10},{3,11},{4,12},{5,13},{6,14},{7,15},{8,0},{9,1},... | collective-permute-start | bytes 393224 | tf_op jit(solution)/shard_map/ppermute | solution.py:310
  59.6 5.6 %collective-permute-start.25 = (bf16[512,128]{1,0:T(8,128)(2,1)S(1)}, bf16[512,128]{1,0:T(8,128)(2,1)S(1)}, u32[]{:S(2)}, u32[]{:S(2)}) collective-permute-start(bf16[512,128]{1,0:T(8,128)(2,1)S(1)} %get-tuple-element.45), channel_id=1, source_target_pairs={{0,16},{1,17},{2,18},{3,19},{4,20},{5,21},{6,22},{7,23},{8,24},{9,... | collective-permute-start | bytes 393224 | tf_op jit(solution)/shard_map/ppermute | solution.py:313
  59.6 7.7 %collective-permute-start.28 = (bf16[512,128]{1,0:T(8,128)(2,1)S(1)}, bf16[512,128]{1,0:T(8,128)(2,1)S(1)}, u32[]{:S(2)}, u32[]{:S(2)}) collective-permute-start(bf16[512,128]{1,0:T(8,128)(2,1)S(1)} %get-tuple-element.44.refs_5_.refs_1_), channel_id=1, source_target_pairs={{0,1},{1,2},{2,3},{3,4},{4,5},{5,6},{6,7},{7,0},{8,15},{9,8},{10,9... | collective-permute-start | bytes 393224 | tf_op jit(solution)/shard_map/ppermute | solution.py:321
  61.1 7.0 %collective-permute-start.29 = (bf16[512,128]{1,0:T(8,128)(2,1)S(1)}, bf16[512,128]{1,0:T(8,128)(2,1)S(1)}, u32[]{:S(2)}, u32[]{:S(2)}) collective-permute-start(bf16[512,128]{1,0:T(8,128)(2,1)S(1)} %get-tuple-element.44.refs_5_.refs_1_), channel_id=1, source_target_pairs={{0,2},{1,3},{2,4},{3,5},{4,6},{5,7},{6,0},{7,1},{8,14},{9,15},{10,... | collective-permute-start | bytes 393224 | tf_op jit(solution)/shard_map/ppermute | solution.py:321
  65.2 7.0 %collective-permute-start.27 = (bf16[512,128]{1,0:T(8,128)(2,1)S(1)}, bf16[512,128]{1,0:T(8,128)(2,1)S(1)}, u32[]{:S(2)}, u32[]{:S(2)}) collective-permute-start(bf16[512,128]{1,0:T(8,128)(2,1)S(1)} %collective-permute-done.25.refs_6_.refs_1_.refs_3_), channel_id=1, source_target_pairs={{0,8},{1,9},{2,10},{3,11},{4,12},{5,13},{6,14},{7,15},{8,0},{9,1},... | collective-permute-start | bytes 393224 | tf_op jit(solution)/shard_map/ppermute | solution.py:321
  65.2 7.1 %collective-permute-start.26 = (bf16[512,128]{1,0:T(8,128)(2,1)S(1)}, bf16[512,128]{1,0:T(8,128)(2,1)S(1)}, u32[]{:S(2)}, u32[]{:S(2)}) collective-permute-start(bf16[512,128]{1,0:T(8,128)(2,1)S(1)} %collective-permute-done.25.refs_6_.refs_1_.refs_3_), channel_id=1, source_target_pairs={{0,8},{1,9},{2,10},{3,11},{4,12},{5,13},{6,14},{7,15},{8,0},{9,1},... | collective-permute-start | bytes 393224 | tf_op jit(solution)/shard_map/ppermute | solution.py:321
  68.3 5.6 %collective-permute-start.30 = (bf16[512,128]{1,0:T(8,128)(2,1)S(1)}, bf16[512,128]{1,0:T(8,128)(2,1)S(1)}, u32[]{:S(2)}, u32[]{:S(2)}) collective-permute-start(bf16[512,128]{1,0:T(8,128)(2,1)S(1)} %get-tuple-element.47), channel_id=1, source_target_pairs={{0,16},{1,17},{2,18},{3,19},{4,20},{5,21},{6,22},{7,23},{8,24},{9,... | collective-permute-start | bytes 393224 | tf_op jit(solution)/shard_map/ppermute | solution.py:313
  72.0 3.1 %collective-permute-start.32 = (bf16[512,128]{1,0:T(8,128)(2,1)S(1)}, bf16[512,128]{1,0:T(8,128)(2,1)S(1)}, u32[]{:S(2)}, u32[]{:S(2)}) collective-permute-start(bf16[512,128]{1,0:T(8,128)(2,1)S(1)} %get-tuple-element.52), channel_id=1, source_target_pairs={{0,8},{1,9},{2,10},{3,11},{4,12},{5,13},{6,14},{7,15},{8,0},{9,1},... | collective-permute-start | bytes 393224 | tf_op jit(solution)/shard_map/ppermute | solution.py:310
  (5 other events, 14.3 us)
